TPU v7x, 32 devices: a whole 2x2x4 slice. The times are simulated.
32 devices in a mesh: ctx: 8 (over y, x, core), head: 4 (over z).
Axes of the slice: x: 2, y: 2, z: 4, core: 2. Of those that a mesh axis runs over, the one named last changes fastest.
Arguments:
- query_rows: bfloat16 [4096, 16, 128], P('ctx', 'head'), may hold values from -45 to 45
- key_rows: bfloat16 [4096, 16, 128], P('ctx', 'head'), may hold values from -7 to 7
- value_rows: bfloat16 [4096, 16, 128], P('ctx', 'head'), may hold values from -6 to 6
- out_grad: bfloat16 [4096, 16, 128], P('ctx', 'head'), may hold values from -6 to 6
- global_pos: int32 [256], replicated, may hold values from 0 to 4095, as said below
Outputs:
- attn_out: bfloat16 [4096, 16, 128], P('ctx', 'head')
- query_grad: float32 [4096, 16, 128], P('ctx', 'head')
- key_grad: float32 [4096, 16, 128], P('ctx', 'head')
- value_grad: float32 [4096, 16, 128], P('ctx', 'head')
Inputs may be any that keep to these rules, and one draw needn't show every extreme that they name: `global_pos`: distinct positions; the aligned block of 512 positions that holds the most of them holds exactly 64, and the other blocks hold counts that differ by at most one.
All inputs are finite; a program needn't handle non-finite values.
Results may differ from a plain program's by a relative error of at most 0.03.
Values may be sent and summed in bfloat16 or wider, within the bound.
No kernel may reach another device: no remote copies, remote signals or barrier semaphores. Data moves between devices by JAX's collectives and lax.ppermute only.
A program may use at most 128 MiB of HBM per device.

v0:
```python
import functools
import math

import jax
import jax.numpy as jnp
from jax import lax
from jax.experimental import pallas as pl
from jax.experimental.pallas import tpu as pltpu
from jax.sharding import PartitionSpec as P

HALF = 512
TILE = 256
NEG = -1e30
LOG2E = 1.0 / math.log(2.0)
VMEM_BYTES = 63 * 1024 * 1024
BF = jnp.bfloat16
F32 = jnp.float32


def nt(a, b):
    return lax.dot_general(a, b, (((1,), (1,)), ((), ())), preferred_element_type=F32)


def nn(a, b):
    return lax.dot_general(a, b, (((1,), (0,)), ((), ())), preferred_element_type=F32)


def wide(column, width):
    return jnp.concatenate([column] * (width // column.shape[1]), axis=1)


def iota(shape, dim):
    return lax.broadcasted_iota(jnp.int32, shape, dim)


def params():
    return pltpu.CompilerParams(vmem_limit_bytes=VMEM_BYTES)


def as_column(row):
    return jnp.broadcast_to(row, (128, row.shape[1])).T[:, :1]


def pack_keys_kernel(heads, k, v, kv, *refs):
    parts, wide_rows = refs[:-1], refs[-1]
    group = heads // len(parts)
    toks = k.shape[0] // heads
    for number, source in enumerate((k, v)):
        wide_rows[number] = source[...].astype(F32)
        for head in range(heads):
            rows = wide_rows[number, pl.ds(head, toks, stride=heads), :].astype(BF)
            kv[number, head] = rows
            parts[head // group][number, head % group] = rows


def pack_queries_kernel(heads, slots, q, g, kv, pos_row, qd, slot_rows, wide_rows, acc):
    step = pl.program_id(0)
    toks = q.shape[0] // heads
    row = pos_row[...]
    count = row.shape[1]
    base = lax.axis_index("ctx") * (toks * pl.num_programs(0))
    column = as_column(row)
    tok = iota((count, toks), 1) + (base + step * toks)
    hit = jnp.sum((column == tok).astype(F32), axis=0, keepdims=True)
    rank = jnp.sum(((column >= base) & (column < tok)).astype(F32), axis=0, keepdims=True)
    slot = iota((slots, toks), 0).astype(F32)
    pick = jnp.where((hit > 0) & (rank == slot), 1.0, 0.0).astype(BF)
    tok = iota((toks, count), 0) + (base + step * toks)
    hit_column = jnp.sum((row == tok).astype(F32), axis=1, keepdims=True)
    tables = [[], [kv[0, h] for h in range(heads)], [kv[1, h] for h in range(heads)], []]
    for number, source in ((0, q), (3, g)):
        wide_rows[number // 3] = source[...].astype(F32)
        for head in range(heads):
            rows = wide_rows[number // 3, pl.ds(head, toks, stride=heads), :]
            tables[number].append(rows.astype(BF))
            if number == 0:
                qd[0, head] = rows.astype(BF)
            else:
                qd[1, head] = jnp.where(hit_column > 0, 0.0, rows).astype(BF)
    for number in range(4):
        found = nn(pick, jnp.concatenate(tables[number], axis=1))
        for head in range(heads):
            part = found[:, head * 128 : (head + 1) * 128]
            acc[number, head] = jnp.where(step == 0, part, acc[number, head] + part)

    @pl.when(step == pl.num_programs(0) - 1)
    def _():
        slot_rows[...] = acc[...].astype(BF)


def owner_map(column, owner, toks, slots, shape):
    inside = jnp.sum((column < owner * toks).astype(jnp.int32), axis=0, keepdims=True)
    held = jnp.sum((column < (owner + 1) * toks).astype(jnp.int32), axis=0, keepdims=True) - inside
    slot = iota(shape, 1) % slots
    hot = (iota(shape, 0) == inside + slot) & (slot < held)
    return jnp.where(hot, 1.0, 0.0).astype(BF)


def mask_kernel(order, slots, seq_rows, pos_row, bias, compact, expand, place):
    toks = place.shape[0]
    me = lax.axis_index("ctx")
    base = me * toks
    row = pos_row[...]
    count = row.shape[1]
    column = as_column(row)
    for start in range(0, bias.shape[0], TILE):
        key = iota((TILE, count), 0) + (base - HALF + start)
        hits = jnp.sum((row == key).astype(F32), axis=1, keepdims=True)
        key = key[:, :1]
        out = (hits > 0) | (key < 0) | (key >= seq_rows)
        bias[start : start + TILE, :] = jnp.broadcast_to(jnp.where(out, NEG, 0.0), (TILE, 128))
    tok = iota((toks, count), 0) + base
    hit = jnp.sum((row == tok).astype(F32), axis=1, keepdims=True)
    rank = jnp.sum(((row >= base) & (row < tok)).astype(F32), axis=1, keepdims=True)
    slot = iota((toks, slots), 1).astype(F32)
    place[...] = jnp.where((hit > 0) & (rank == slot), 1.0, 0.0).astype(BF)
    part = iota((1, compact.shape[1]), 1) // slots
    owner = jnp.zeros_like(part)
    for number, relative in enumerate(order):
        owner = jnp.where(part == number, me ^ relative, owner)
    compact[...] = owner_map(column, owner, toks, slots, compact.shape)
    owner = iota((1, compact.shape[1]), 1) // slots
    hot = owner_map(column, owner, toks, slots, compact.shape)
    expand[...] = hot.astype(F32).T.astype(BF)


def stats_kernel(scale2, compact, *refs):
    parts, (kv, rows, stats) = refs[:-3], refs[-3:]
    pieces = []
    for part in parts:
        for i in range(part.shape[0]):
            pieces.append(jnp.concatenate([part[i, number, 0] for number in range(4)], axis=1))
    packed = nn(compact[...], jnp.concatenate(pieces, axis=0)).astype(BF)
    width = kv.shape[3]
    table = [packed[:, number * width : (number + 1) * width] for number in range(4)]
    for number in range(4):
        rows[number, 0] = table[number]
    queries, _, _, grads = table
    scores = nt(kv[0, 0], queries) * scale2
    top = jnp.max(scores, axis=0, keepdims=True)
    weights = jnp.exp2(scores - top)
    stats[0, 0, 0:1, :] = top
    stats[0, 0, 1:2, :] = jnp.sum(weights, axis=0, keepdims=True)
    stats[0, 0, 2:3, :] = jnp.sum(weights * nt(kv[1, 0], grads), axis=0, keepdims=True)


def band(scores, low):
    rows, columns = iota(scores.shape, 0), iota(scores.shape, 1)
    return jnp.where(rows <= columns if low else rows >= columns, scores, NEG)


def join(blocks, number, buf):
    toks = blocks[0].shape[2]
    for place, block in enumerate(blocks):
        buf[place * toks : (place + 1) * toks, :] = block[number, 0]


def put_in_slots(expand, tables, sums):
    owners, kinds, _, slots, width = sums.shape
    spread = nn(expand, jnp.concatenate(tables, axis=1)).astype(BF)
    for owner in range(owners):
        for kind in range(kinds):
            sums[owner, kind, 0] = spread[
                owner * slots : (owner + 1) * slots, kind * width : (kind + 1) * width
            ]


def global_kernel(scale, scale2, kv, rows, stats, expand, dkv, ends):
    g_query, g_grad = rows[0, 0], rows[3, 0]
    tops = stats[:, 0, 0:1, :]
    top = jnp.max(tops, axis=0)
    factor = jnp.exp2(tops - top[None])
    total = jnp.sum(stats[:, 0, 1:2, :] * factor, axis=0)
    g_dot = jnp.sum(stats[:, 0, 2:3, :] * factor, axis=0) / total
    g_log = top + jnp.log2(total)
    weights = jnp.exp2(nt(kv[0, 0], g_query) * scale2 - g_log)
    narrow = weights.astype(BF)
    slopes = (weights * (nt(kv[1, 0], g_grad) - g_dot)).astype(BF)
    dkv[0, 0] = (nt(g_query.T, slopes) * scale).T
    dkv[1, 0] = nt(g_grad.T, narrow).T
    out = nn(kv[1, 0].T, narrow).T.astype(BF)
    dq = (nn(kv[0, 0].T, slopes) * scale).T.astype(BF)
    put_in_slots(expand[...], (out, dq), ends)


def local_kernel(scale, scale2, halves, group, qd, kv, *refs):
    lows, highs, refs = refs[:halves], refs[halves : 2 * halves], refs[2 * halves :]
    rows, bias, expand, out, log_dot, dq, dkv, sums, keys, values, score_buf, probs, slopes = refs
    toks = kv.shape[2]
    reach = 2 * HALF + TILE
    span = keys.shape[0] - rows.shape[2]
    for part in range(halves):

        @pl.when(pl.program_id(0) // group == part)
        def _():
            join((lows[part], kv, highs[part]), 0, keys)
            join((lows[part], kv, highs[part]), 1, values)

    keys[span:, :] = rows[1, 0]
    values[span:, :] = rows[2, 0]
    key_t, value_t = keys[...].T, values[...].T
    query_t, grad_t = qd[0, 0].T, qd[1, 0].T
    tiles = range(toks // TILE)
    lanes = [slice(tile * TILE, (tile + 1) * TILE) for tile in tiles]
    windows = [slice(tile * TILE, tile * TILE + reach) for tile in tiles]
    starts = [
        list(range(tile * TILE, tile * TILE + reach, TILE)) + list(range(span, keys.shape[0], TILE))
        for tile in tiles
    ]
    best, top, total, scaled, dots = ([None] * len(tiles) for _ in range(5))

    def score(tile, piece):
        start = starts[tile][piece]
        scores = nn(keys[start : start + TILE, :], query_t[:, lanes[tile]]) * scale2
        if start < span:
            scores = scores + wide(bias[start : start + TILE, :], TILE)
        if piece == 0:
            scores = band(scores, False)
        elif piece == reach // TILE - 1:
            scores = band(scores, True)
        score_buf[tile, piece * TILE : (piece + 1) * TILE, :] = scores
        part = jnp.max(scores.reshape(TILE // 8, 8, TILE), axis=0)
        best[tile] = part if best[tile] is None else jnp.maximum(best[tile], part)

    def weigh(tile, piece):
        if top[tile] is None:
            top[tile] = jnp.max(best[tile], axis=0, keepdims=True)
        start = starts[tile][piece]
        weights = jnp.exp2(score_buf[tile, piece * TILE : (piece + 1) * TILE, :] - top[tile])
        probs[start : start + TILE, lanes[tile]] = weights.astype(BF)
        part = jnp.sum(weights.reshape(TILE // 8, 8, TILE), axis=0)
        total[tile] = part if total[tile] is None else total[tile] + part

    def attend(tile):
        whole_sum = jnp.sum(total[tile], axis=0, keepdims=True)
        inverse = 1.0 / whole_sum
        grads = grad_t[:, lanes[tile]].astype(F32)
        acc = nn(value_t[:, windows[tile]], probs[windows[tile], lanes[tile]])
        acc = (acc + nn(value_t[:, span:], probs[span:, lanes[tile]])) * inverse
        dot = jnp.sum(grads * acc, axis=0, keepdims=True)
        log_dot[0, 0:1, lanes[tile]] = top[tile] + jnp.log2(whole_sum)
        log_dot[0, 1:2, lanes[tile]] = dot
        out[0, lanes[tile], :] = acc.T.astype(BF)
        scaled[tile] = (grads * inverse).astype(BF)
        dots[tile] = dot * inverse

    def slope(tile, piece):
        start = starts[tile][piece]
        rise = nn(values[start : start + TILE, :], scaled[tile]) - dots[tile]
        weights = probs[start : start + TILE, lanes[tile]].astype(F32)
        slopes[start : start + TILE, lanes[tile]] = (weights * rise).astype(BF)

    def query_gradient(tile):
        acc = nn(key_t[:, windows[tile]], slopes[windows[tile], lanes[tile]])
        acc = acc + nn(key_t[:, span:], slopes[span:, lanes[tile]])
        dq[0, lanes[tile], :] = (acc * scale).T

    for step in range(len(tiles) + 2):
        for piece in range(len(starts[0])):
            if 0 <= step - 2:
                slope(step - 2, piece)
            if 0 <= step - 1 < len(tiles):
                weigh(step - 1, piece)
            if step < len(tiles):
                score(step, piece)
        if 0 <= step - 2:
            query_gradient(step - 2)
        if 0 <= step - 1 < len(tiles):
            attend(step - 1)
    own = slice(HALF, HALF + toks)
    grads = jnp.concatenate(scaled, axis=1)
    dkv[0, 0] = (nt(query_t, slopes[own, :]) * scale).T
    dkv[1, 0] = nt(grads, probs[own, :]).T
    g_dk = (nt(query_t, slopes[span:, :]) * scale).T.astype(BF)
    g_dv = nt(grads, probs[span:, :]).T.astype(BF)
    put_in_slots(expand[...], (g_dk, g_dv), sums)


def rim_kernel(
    scale, scale2, kv, bias, qd_low, qd_high, log_low, log_high, partial, dkv, probs, slopes
):
    toks = kv.shape[2]
    reach = toks + TILE
    query_t = jnp.concatenate([qd_low[0, 0].T, qd_high[0, 0].T], axis=1)
    grad_t = jnp.concatenate([qd_low[1, 0].T, qd_high[1, 0].T], axis=1)
    for k_tile in range(toks // TILE):
        span = slice(k_tile * TILE, (k_tile + 1) * TILE)
        key = kv[0, 0, span, :]
        value = kv[1, 0, span, :]
        key_bias = wide(bias[HALF + k_tile * TILE : HALF + (k_tile + 1) * TILE, :], TILE)
        for piece in range(reach // TILE):
            start = (k_tile + piece) * TILE
            log_dot, offset = (log_low, start) if start < toks else (log_high, start - toks)
            lanes = slice(offset, offset + TILE)
            scores = nn(key, query_t[:, start : start + TILE]) * scale2 + key_bias
            if piece == 0:
                scores = band(scores, True)
            elif piece == reach // TILE - 1:
                scores = band(scores, False)
            weights = jnp.exp2(scores - log_dot[0, 0:1, lanes])
            rise = nn(value, grad_t[:, start : start + TILE]) - log_dot[0, 1:2, lanes]
            spot = slice(piece * TILE, (piece + 1) * TILE)
            probs[span, spot] = weights.astype(BF)
            slopes[span, spot] = (weights * rise).astype(BF)
    for k_tile in range(toks // TILE):
        span = slice(k_tile * TILE, (k_tile + 1) * TILE)
        window = slice(k_tile * TILE, k_tile * TILE + reach)
        dk = (nt(query_t[:, window], slopes[span, :]) * scale).T
        dkv[0, 0, span, :] = partial[0, 0, span, :] + dk
        dkv[1, 0, span, :] = partial[1, 0, span, :] + nt(grad_t[:, window], probs[span, :]).T


def final_kernel(
    place, out, ends, sums, dq, dkv, extra, attn, query_grad, key_grad, value_grad, wide_rows
):
    heads, toks = out.shape[0], out.shape[1]
    hot = place[...]
    is_global = jnp.sum(hot.astype(F32), axis=1, keepdims=True) > 0
    for head in range(heads):
        rows = pl.ds(head, toks, stride=heads)
        tables = []
        for source, kind in ((ends, 0), (ends, 1), (sums, 0), (sums, 1)):
            table = source[0, kind, head].astype(F32)
            for device in range(1, source.shape[0]):
                table = table + source[device, kind, head].astype(F32)
            tables.append(table.astype(BF))
        width = out.shape[2]
        added = nn(hot, jnp.concatenate(tables, axis=1))
        added = [added[:, i * width : (i + 1) * width] for i in range(4)]
        wide_rows[rows, :] = jnp.where(is_global, added[0], out[head].astype(F32))
        query_grad[rows, :] = dq[head] + added[1]
        key_grad[rows, :] = dkv[0, head] + extra[0, head] + added[2]
        value_grad[rows, :] = dkv[1, head] + extra[1, head] + added[3]
    attn[...] = wide_rows[...].astype(BF)


def cost(flops, moved, exps=0):
    return pl.CostEstimate(flops=int(flops), bytes_accessed=int(moved), transcendentals=int(exps))


def struct(shape, dtype):
    return jax.ShapeDtypeStruct(shape, dtype)


def whole(shape):
    return pl.BlockSpec(shape, lambda head: (0,) * len(shape))


def per_head(shape, dim, first=0):
    block = tuple(1 if i == dim else size for i, size in enumerate(shape))
    return pl.BlockSpec(
        block, lambda head: tuple(head + first if i == dim else 0 for i in range(len(shape)))
    )


def shards(query_rows, key_rows, value_rows, out_grad, global_pos):
    toks, heads, width = query_rows.shape
    count = global_pos.shape[0]
    devices = lax.axis_size("ctx")
    slots = max(16, 2 * count // devices)
    scale = width ** (-0.5)
    scale2 = scale * LOG2E
    bits = devices.bit_length() - 1
    stages = [
        [mask << low for mask in range(1, 1 << min(2, bits - low))] for low in range(1, bits, 2)
    ] + [[1]]
    order = [0]
    for stage in stages:
        order = order + [one ^ mask for mask in stage for one in order]
    pos_row = global_pos.reshape(1, count)
    q_flat, k_flat, v_flat, g_flat = (
        x.reshape(toks * heads, width) for x in (query_rows, key_rows, value_rows, out_grad)
    )

    def swap(value, mask):
        return lax.ppermute(value, "ctx", [(i, i ^ mask) for i in range(devices)])

    def from_low(value):
        return lax.ppermute(value, "ctx", [(i, i + 1) for i in range(devices - 1)])

    def from_high(value):
        return lax.ppermute(value, "ctx", [(i + 1, i) for i in range(devices - 1)])

    def after(value, earlier):
        return lax.optimization_barrier((value, earlier))[0]

    pair_shape = (2, heads, toks, width)
    slot_shape = (4, heads, slots, width)
    steps = 1
    flat_spec = pl.BlockSpec((toks * heads // steps, width), lambda i: (i, 0))
    pair_spec = pl.BlockSpec((2, heads, toks // steps, width), lambda i: (0, 0, i, 0))
    wide_pair = pltpu.VMEM((2, toks * heads // steps, width), F32)
    halves = 2 if heads % 2 == 0 else 1
    group = heads // halves
    part_shape = (2, group, toks, width)
    kv, *kv_parts = pl.pallas_call(
        functools.partial(pack_keys_kernel, heads),
        out_shape=[struct(pair_shape, BF)] + [struct(part_shape, BF)] * halves,
        scratch_shapes=[wide_pair],
        compiler_params=params(),
        name="pack_keys",
    )(k_flat, v_flat)

    qd, slot_rows = pl.pallas_call(
        functools.partial(pack_queries_kernel, heads, slots),
        grid=(steps,),
        in_specs=[flat_spec, flat_spec, pair_spec, whole((1, count))],
        out_specs=(pair_spec, whole(slot_shape)),
        out_shape=(struct(pair_shape, BF), struct(slot_shape, BF)),
        scratch_shapes=[wide_pair, pltpu.VMEM(slot_shape, F32)],
        compiler_params=params(),
        name="pack_queries",
    )(q_flat, g_flat, kv, pos_row)

    span = toks + 2 * HALF
    bias, compact, expand, place = pl.pallas_call(
        functools.partial(mask_kernel, order, slots, toks * devices),
        out_shape=(
            struct((span, 128), F32),
            struct((count, devices * slots), BF),
            struct((devices * slots, count), BF),
            struct((toks, slots), BF),
        ),
        compiler_params=params(),
        name="masks",
    )(pos_row)

    lows, highs = [], []
    for part in kv_parts:
        if lows:
            part = after(part, (lows[-1], highs[-1]))
        lows.append(from_low(part))
        highs.append(from_high(part))
    held = [slot_rows[None]]
    for stage in stages:
        send = jnp.concatenate(held, axis=0) if len(held) > 1 else held[0]
        if stage == [1]:
            send = after(send, (lows[0], highs[0], place))
        held += [swap(send, mask) for mask in stage]

    row_shape = (4, heads, count, width)
    rows, stats = pl.pallas_call(
        functools.partial(stats_kernel, scale2),
        grid=(heads,),
        in_specs=[whole(compact.shape)]
        + [per_head(part.shape, 2) for part in held]
        + [per_head(pair_shape, 1)],
        out_specs=(per_head(row_shape, 1), per_head((1, heads, 3, count), 1)),
        out_shape=(struct(row_shape, BF), struct((1, heads, 3, count), F32)),
        compiler_params=params(),
        cost_estimate=cost(1e6, 1e6),
        name="global_stats",
    )(compact, *held, kv)

    kv_done = (lows, highs)
    stats = after(stats, kv_done)
    stats = jnp.broadcast_to(stats, (devices,) + stats.shape[1:])
    stats = lax.all_to_all(stats, "ctx", 0, 0, tiled=True)
    qd_late = after(qd, (kv_done, rows))
    qd_low, qd_high = from_low(qd_late), from_high(qd_late)

    def half_head(part):
        return pl.BlockSpec(
            (2, 1, toks, width), lambda head: (0, jnp.clip(head - part * group, 0, group - 1), 0, 0)
        )

    ends_shape = (devices, 2, heads, slots, width)
    out, log_dot, dq, dkv, sums = pl.pallas_call(
        functools.partial(local_kernel, scale, scale2, halves, group),
        grid=(heads,),
        in_specs=[per_head(pair_shape, 1)] * 2
        + [half_head(part) for part in range(halves)] * 2
        + [per_head(row_shape, 1), whole(bias.shape), whole(expand.shape)],
        out_specs=(
            per_head((heads, toks, width), 0),
            per_head((heads, 2, toks), 0),
            per_head((heads, toks, width), 0),
            per_head(pair_shape, 1),
            per_head(ends_shape, 2),
        ),
        out_shape=(
            struct((heads, toks, width), BF),
            struct((heads, 2, toks), F32),
            struct((heads, toks, width), F32),
            struct(pair_shape, F32),
            struct(ends_shape, BF),
        ),
        scratch_shapes=[
            pltpu.VMEM((span + count, width), BF),
            pltpu.VMEM((span + count, width), BF),
            pltpu.VMEM((toks // TILE, 2 * HALF + TILE + count, TILE), F32),
            pltpu.VMEM((span + count, toks), BF),
            pltpu.VMEM((span + count, toks), BF),
        ],
        compiler_params=params(),
        cost_estimate=cost(1e6, 1e6),
        name="local",
    )(qd, kv, *lows, *highs, rows, bias, expand)
    log_late = after(log_dot, (qd_low, qd_high))
    log_low, log_high = from_low(log_late), from_high(log_late)

    extra, ends = pl.pallas_call(
        functools.partial(global_kernel, scale, scale2),
        grid=(heads,),
        in_specs=[per_head(pair_shape, 1), per_head(row_shape, 1)]
        + [per_head(stats.shape, 1), whole(expand.shape)],
        out_specs=(per_head(pair_shape, 1), per_head(ends_shape, 2)),
        out_shape=(struct(pair_shape, F32), struct(ends_shape, BF)),
        compiler_params=params(),
        cost_estimate=cost(2e9, 5e6, 1e6),
        name="global_queries",
    )(kv, rows, after(stats, log_dot), expand)
    ends = lax.all_to_all(ends, "ctx", 0, 0, tiled=True)
    sums = lax.all_to_all(sums, "ctx", 0, 0, tiled=True)

    dkv = pl.pallas_call(
        functools.partial(rim_kernel, scale, scale2),
        grid=(heads,),
        in_specs=[per_head(pair_shape, 1), whole(bias.shape)]
        + [per_head(pair_shape, 1)] * 2
        + [per_head(log_dot.shape, 0)] * 2
        + [per_head(pair_shape, 1)],
        out_specs=per_head(pair_shape, 1),
        out_shape=struct(pair_shape, F32),
        scratch_shapes=[
            pltpu.VMEM((toks, toks + TILE), BF),
            pltpu.VMEM((toks, toks + TILE), BF),
        ],
        compiler_params=params(),
        cost_estimate=cost(4e9, 8e6, 2e6),
        name="rim",
    )(kv, bias, qd_low, qd_high, log_low, log_high, dkv)

    flat_shape = (toks * heads, width)
    steps = 2
    outs = pl.pallas_call(
        final_kernel,
        grid=(steps,),
        in_specs=[
            pl.BlockSpec((toks // steps, slots), lambda i: (i, 0)),
            pl.BlockSpec((heads, toks // steps, width), lambda i: (0, i, 0)),
            whole(ends_shape),
            whole(ends_shape),
            pl.BlockSpec((heads, toks // steps, width), lambda i: (0, i, 0)),
            pl.BlockSpec((2, heads, toks // steps, width), lambda i: (0, 0, i, 0)),
            pl.BlockSpec((2, heads, toks // steps, width), lambda i: (0, 0, i, 0)),
        ],
        out_specs=[pl.BlockSpec((toks * heads // steps, width), lambda i: (i, 0))] * 4,
        out_shape=[struct(flat_shape, kind) for kind in (BF, F32, F32, F32)],
        scratch_shapes=[pltpu.VMEM((toks * heads // steps, width), F32)],
        compiler_params=params(),
        name="final",
    )(place, out, ends, sums, dq, dkv, extra)
    return tuple(x.reshape(toks, heads, width) for x in outs)


def solution(mesh):
    spec = P("ctx", "head", None)
    return jax.shard_map(
        shards,
        mesh=mesh,
        in_specs=(spec, spec, spec, spec, P()),
        out_specs=(spec, spec, spec, spec),
        check_vma=False,
    )
```

profile of v0, /device:TPU:1, one launch (start us, length us, event | category | flops | bytes accessed | tf_op | source)
XLA Modules:
  0.0 134.3 jit_solution(12191338435346055153)
XLA Ops:
  0.6 2.7 %pack_keys.1 = (bf16[2,4,512,128]{3,2,1,0:T(8,128)(2,1)}, bf16[2,2,512,128]{3,2,1,0:T(8,128)(2,1)}, bf16[2,2,512,128]{3,2,1,0:T(8,128)(2,1)}) custom-call(bf16[2048,128]{1,0:T(8,128)(2,1)} %bitcast.16, bf16[2048,128]{1,0:T(8,128)(2,1)} %bitcast.17), custom_call_target="tpu_custom_call" | custom-call | tf_op jit(solution)/shard_map/pack_keys/pallas_call | solution.py:396
  3.4 2.0 %collective-permute-start.1 = (bf16[2,2,512,128]{3,2,1,0:T(8,128)(2,1)}, bf16[2,2,512,128]{3,2,1,0:T(8,128)(2,1)}, u32[]{:S(2)}, u32[]{:S(2)}) collective-permute-start(bf16[2,2,512,128]{3,2,1,0:T(8,128)(2,1)} %get-tuple-element.35), channel_id=1, source_target_pairs={{4,0},{8,4},{12,8},{16,12},{20,16},{24,20},{28,24},{5,1},{9,5},{13... | collective-permute-start | bytes 1572872 | tf_op jit(solution)/shard_map/ppermute | solution.py:382
  5.3 4.5 %collective-permute-start = (bf16[2,2,512,128]{3,2,1,0:T(8,128)(2,1)}, bf16[2,2,512,128]{3,2,1,0:T(8,128)(2,1)}, u32[]{:S(2)}, u32[]{:S(2)}) collective-permute-start(bf16[2,2,512,128]{3,2,1,0:T(8,128)(2,1)} %get-tuple-element.35), channel_id=1, source_target_pairs={{0,4},{4,8},{8,12},{12,16},{16,20},{20,24},{24,28},{1,5},{5,9},{9,... | collective-permute-start | bytes 1572872 | tf_op jit(solution)/shard_map/ppermute | solution.py:379
  9.8 3.4 %pack_queries.1 = (bf16[2,4,512,128]{3,2,1,0:T(8,128)(2,1)}, bf16[4,4,64,128]{3,2,1,0:T(8,128)(2,1)}) custom-call(bf16[2048,128]{1,0:T(8,128)(2,1)} %bitcast.18, bf16[2048,128]{1,0:T(8,128)(2,1)} %bitcast.19, bf16[2,4,512,128]{3,2,1,0:T(8,128)(2,1)} %get-tuple-element.33.kv.refs_5_, s32[1,256]{1,0:T(1,128)} %bitcast.21), custom_call_target="tpu_custom_call" | custom-call | tf_op jit(solution)/shard_map/pack_queries/pallas_call | solution.py:404
  13.2 1.2 collective-permute-start.6
  14.5 2.0 %collective-permute-start.5 = (bf16[1,4,4,64,128]{4,3,2,1,0:T(8,128)(2,1)}, bf16[1,4,4,64,128]{4,3,2,1,0:T(8,128)(2,1)S(1)}, u32[]{:S(2)}, u32[]{:S(2)}) collective-permute-start(bf16[1,4,4,64,128]{4,3,2,1,0:T(8,128)(2,1)} %bitcast.12), channel_id=1, source_target_pairs={{0,16},{4,20},{8,24},{12,28},{16,0},{20,4},{24,8},{28,12},{1,17},{... | collective-permute-start | bytes 786440 | tf_op jit(solution)/shard_map/ppermute | solution.py:376
  16.5 0.0 collective-permute-start.4
  16.5 2.5 %masks.1 = (f32[1536,128]{1,0:T(8,128)}, bf16[256,512]{1,0:T(8,128)(2,1)}, bf16[512,256]{1,0:T(8,128)(2,1)}, bf16[512,64]{1,0:T(8,128)(2,1)}) custom-call(s32[1,256]{1,0:T(1,128)} %bitcast.22), custom_call_target="tpu_custom_call" | custom-call | tf_op jit(solution)/shard_map/masks/pallas_call | solution.py:416
  19.0 3.6 %collective-permute-done.6.refs_3_ = bf16[1,4,4,64,128]{4,3,2,1,0:T(8,128)(2,1)S(1)} collective-permute-done((bf16[1,4,4,64,128]{4,3,2,1,0:T(8,128)(2,1)}, bf16[1,4,4,64,128]{4,3,2,1,0:T(8,128)(2,1)S(1)}, u32[]{:S(2)}, u32[]{:S(2)}) %collective-permute-start.6) | collective-permute-done | bytes 262176 | tf_op jit(solution)/shard_map/ppermute | solution.py:376
  22.5 8.7 %collective-permute-done.5.refs_2_ = bf16[1,4,4,64,128]{4,3,2,1,0:T(8,128)(2,1)S(1)} collective-permute-done((bf16[1,4,4,64,128]{4,3,2,1,0:T(8,128)(2,1)}, bf16[1,4,4,64,128]{4,3,2,1,0:T(8,128)(2,1)S(1)}, u32[]{:S(2)}, u32[]{:S(2)}) %collective-permute-start.5) | collective-permute-done | bytes 262176 | tf_op jit(solution)/shard_map/ppermute | solution.py:376
  31.2 0.6 collective-permute-done.4.refs_1_
  31.8 1.2 pad_maximum_fusion
  33.0 0.0 collective-permute-done.1.refs_2_
  33.0 0.0 collective-permute-done.refs_0_
  33.0 0.1 collective-permute-start.7
  33.1 2.4 %collective-permute-start.3 = (bf16[2,2,512,128]{3,2,1,0:T(8,128)(2,1)}, bf16[2,2,512,128]{3,2,1,0:T(8,128)(2,1)}, u32[]{:S(2)}, u32[]{:S(2)}) collective-permute-start(bf16[2,2,512,128]{3,2,1,0:T(8,128)(2,1)} %get-tuple-element.37), channel_id=1, source_target_pairs={{4,0},{8,4},{12,8},{16,12},{20,16},{24,20},{28,24},{5,1},{9,5},{13... | collective-permute-start | bytes 1572872 | tf_op jit(solution)/shard_map/ppermute | solution.py:382
  35.5 3.2 %collective-permute-start.2 = (bf16[2,2,512,128]{3,2,1,0:T(8,128)(2,1)}, bf16[2,2,512,128]{3,2,1,0:T(8,128)(2,1)}, u32[]{:S(2)}, u32[]{:S(2)}) collective-permute-start(bf16[2,2,512,128]{3,2,1,0:T(8,128)(2,1)} %get-tuple-element.37), channel_id=1, source_target_pairs={{0,4},{4,8},{8,12},{12,16},{16,20},{20,24},{24,28},{1,5},{5,9},{9,... | collective-permute-start | bytes 1572872 | tf_op jit(solution)/shard_map/ppermute | solution.py:379
  38.7 0.0 collective-permute-done.7.refs_4_
  38.7 0.0 copy-done
  38.7 0.0 copy-done.1
  38.7 0.0 copy-done.2
  38.7 5.5 %global_stats.1 = (bf16[4,4,256,128]{3,2,1,0:T(8,128)(2,1)}, f32[1,4,3,256]{3,2,1,0:T(4,128)}) custom-call(bf16[256,512]{1,0:T(8,128)(2,1)} %get-tuple-element.38.compact, bf16[1,4,4,64,128]{4,3,2,1,0:T(8,128)(2,1)} %bitcast.15, bf16[1,4,4,64,128]{4,3,2,1,0:T(8,128)(2,1)} %copy-done.2, bf16[1,4,4,64,128]{4,3,2,1,0:T(8,128)(2,1)} %copy-done.1, ...), custom_call_target="tpu_custom_call" | custom-call | flops 1000000 | bytes 1000000 | tf_op jit(solution)/shard_map/global_stats/pallas_call | solution.py:442
  44.2 2.3 %collective-permute-done.3.refs_3_ = bf16[2,2,512,128]{3,2,1,0:T(8,128)(2,1)} collective-permute-done((bf16[2,2,512,128]{3,2,1,0:T(8,128)(2,1)}, bf16[2,2,512,128]{3,2,1,0:T(8,128)(2,1)}, u32[]{:S(2)}, u32[]{:S(2)}) %collective-permute-start.3) | collective-permute-done | bytes 524320 | tf_op jit(solution)/shard_map/ppermute | solution.py:382
  46.6 0.0 collective-permute-done.2.refs_1_
  46.6 0.7 copy.9
  47.3 0.7 broadcast_in_dim.12
  48.0 6.5 %all-to-all-start = ((f32[8,4,3,256]{3,1,2,0:T(4,128)}), f32[8,4,3,256]{3,1,2,0:T(4,128)S(1)}, u32[]{:S(2)}, u32[]{:S(2)}) async-start(f32[8,4,3,256]{3,1,2,0:T(4,128)} %broadcast_in_dim.12), calls=%async_computation | async-start | bytes 196608 | tf_op jit(solution)/shard_map/all_to_all | solution.py:458
  54.5 14.5 %local.1 = (bf16[4,512,128]{2,1,0:T(8,128)(2,1)}, f32[4,2,512]{2,1,0:T(2,128)}, f32[4,512,128]{2,1,0:T(8,128)}, f32[2,4,512,128]{3,2,1,0:T(8,128)}, bf16[8,2,4,64,128]{4,3,2,1,0:T(8,128)(2,1)}) custom-call(bf16[2,4,512,128]{3,2,1,0:T(8,128)(2,1)} %get-tuple-element.52.qd, bf16[2,4,512,128]{3,2,1,0:T(8,128)(2,1)} %get-tuple-element.33.kv.refs_5_, ...), custom_call_target="tpu_custom_call" | custom-call | flops 1000000 | bytes 1000000 | tf_op jit(solution)/shard_map/local/pallas_call | solution.py:468
  68.9 0.0 all-to-all-done
  68.9 4.2 %all-to-all-start.2 = ((bf16[8,2,4,64,128]{4,3,2,1,0:T(8,128)(2,1)}), bf16[8,2,4,64,128]{4,3,2,1,0:T(8,128)(2,1)}, u32[]{:S(2)}, u32[]{:S(2)}) async-start(bf16[8,2,4,64,128]{4,3,2,1,0:T(8,128)(2,1)} %get-tuple-element.50), calls=%async_computation.2 | async-start | bytes 2097152 | tf_op jit(solution)/shard_map/all_to_all | solution.py:514
  73.2 1.9 %collective-permute-start.9 = (bf16[2,4,512,128]{3,2,1,0:T(8,128)(2,1)}, bf16[2,4,512,128]{3,2,1,0:T(8,128)(2,1)}, u32[]{:S(2)}, u32[]{:S(2)}) collective-permute-start(bf16[2,4,512,128]{3,2,1,0:T(8,128)(2,1)} %get-tuple-element.52.qd), channel_id=1, source_target_pairs={{4,0},{8,4},{12,8},{16,12},{20,16},{24,20},{28,24},{5,1},{9,5},{13... | collective-permute-start | bytes 3145736 | tf_op jit(solution)/shard_map/ppermute | solution.py:382
  75.1 3.6 %collective-permute-start.8 = (bf16[2,4,512,128]{3,2,1,0:T(8,128)(2,1)}, bf16[2,4,512,128]{3,2,1,0:T(8,128)(2,1)}, u32[]{:S(2)}, u32[]{:S(2)}) collective-permute-start(bf16[2,4,512,128]{3,2,1,0:T(8,128)(2,1)} %get-tuple-element.52.qd), channel_id=1, source_target_pairs={{0,4},{4,8},{8,12},{12,16},{16,20},{20,24},{24,28},{1,5},{5,9},{9,... | collective-permute-start | bytes 3145736 | tf_op jit(solution)/shard_map/ppermute | solution.py:379
  78.7 0.7 copy.10.stats
  79.4 6.5 %global_queries.1 = (f32[2,4,512,128]{3,2,1,0:T(8,128)}, bf16[8,2,4,64,128]{4,3,2,1,0:T(8,128)(2,1)}) custom-call(bf16[2,4,512,128]{3,2,1,0:T(8,128)(2,1)} %get-tuple-element.33.kv.refs_5_, bf16[4,4,256,128]{3,2,1,0:T(8,128)(2,1)} %get-tuple-element.41.refs_4_.rows, f32[8,4,3,256]{3,2,1,0:T(4,128)} %copy.10.stats, ...), custom_call_target="tpu_custom_call" | custom-call | flops 2000000000 | bytes 5000000 | tf_op jit(solution)/shard_map/global_queries/pallas_call | solution.py:502
  85.9 0.0 all-to-all-done.2.sums
  86.0 6.8 %all-to-all-start.1 = ((bf16[8,2,4,64,128]{4,3,2,1,0:T(8,128)(2,1)}), bf16[8,2,4,64,128]{4,3,2,1,0:T(8,128)(2,1)}, u32[]{:S(2)}, u32[]{:S(2)}) async-start(bf16[8,2,4,64,128]{4,3,2,1,0:T(8,128)(2,1)} %get-tuple-element.49), calls=%async_computation.1 | async-start | bytes 2097152 | tf_op jit(solution)/shard_map/all_to_all | solution.py:513
  92.8 17.5 %collective-permute-done.9.qd_high = bf16[2,4,512,128]{3,2,1,0:T(8,128)(2,1)} collective-permute-done((bf16[2,4,512,128]{3,2,1,0:T(8,128)(2,1)}, bf16[2,4,512,128]{3,2,1,0:T(8,128)(2,1)}, u32[]{:S(2)}, u32[]{:S(2)}) %collective-permute-start.9) | collective-permute-done | bytes 1048608 | tf_op jit(solution)/shard_map/ppermute | solution.py:382
  110.3 0.0 collective-permute-done.8.qd_low
  110.3 0.0 copy-done.3
  110.3 1.9 %collective-permute-start.11 = (f32[4,2,512]{2,1,0:T(2,128)S(1)}, f32[4,2,512]{2,1,0:T(2,128)S(1)}, u32[]{:S(2)}, u32[]{:S(2)}) collective-permute-start(f32[4,2,512]{2,1,0:T(2,128)S(1)} %copy-done.3), channel_id=1, source_target_pairs={{4,0},{8,4},{12,8},{16,12},{20,16},{24,20},{28,24},{5,1},{9,5},{13... | collective-permute-start | bytes 49160 | tf_op jit(solution)/shard_map/ppermute | solution.py:382
  112.2 3.6 %collective-permute-start.10 = (f32[4,2,512]{2,1,0:T(2,128)S(1)}, f32[4,2,512]{2,1,0:T(2,128)S(1)}, u32[]{:S(2)}, u32[]{:S(2)}) collective-permute-start(f32[4,2,512]{2,1,0:T(2,128)S(1)} %copy-done.3), channel_id=1, source_target_pairs={{0,4},{4,8},{8,12},{12,16},{16,20},{20,24},{24,28},{1,5},{5,9},{9,... | collective-permute-start | bytes 49160 | tf_op jit(solution)/shard_map/ppermute | solution.py:379
  115.9 5.1 %collective-permute-done.11.log_high = f32[4,2,512]{2,1,0:T(2,128)S(1)} collective-permute-done((f32[4,2,512]{2,1,0:T(2,128)S(1)}, f32[4,2,512]{2,1,0:T(2,128)S(1)}, u32[]{:S(2)}, u32[]{:S(2)}) %collective-permute-start.11) | collective-permute-done | bytes 16416 | tf_op jit(solution)/shard_map/ppermute | solution.py:382
  121.0 0.0 collective-permute-done.10.log_low
  121.0 0.6 copy-done.4
  121.6 0.0 copy-done.5
  121.6 7.5 %rim.1.dkv = f32[2,4,512,128]{3,2,1,0:T(8,128)} custom-call(bf16[2,4,512,128]{3,2,1,0:T(8,128)(2,1)} %get-tuple-element.33.kv.refs_5_, f32[1536,128]{1,0:T(8,128)} %get-tuple-element.42.refs_5_.bias, bf16[2,4,512,128]{3,2,1,0:T(8,128)(2,1)} %collective-permute-done.8.qd_low, bf16[2,4,512,128]{3,2,1,0:T(8,128)(2,1)} %collective-permute-done.9.qd_high, ...), custom_call_target="tpu_custom_call" | custom-call | flops 4000000000 | bytes 8000000 | tf_op jit(solution)/shard_map/rim/pallas_call | solution.py:516
  129.1 0.0 all-to-all-done.1.ends
  129.1 5.2 %final.1 = (bf16[2048,128]{1,0:T(8,128)(2,1)}, f32[2048,128]{1,0:T(8,128)}, f32[2048,128]{1,0:T(8,128)}, f32[2048,128]{1,0:T(8,128)}) custom-call(bf16[512,64]{1,0:T(8,128)(2,1)} %get-tuple-element.32.place, bf16[4,512,128]{2,1,0:T(8,128)(2,1)} %get-tuple-element.44.out, bf16[8,2,4,64,128]{4,3,2,1,0:T(8,128)(2,1)} %all-to-all-done.1.ends, ...), custom_call_target="tpu_custom_call" | custom-call | tf_op jit(solution)/shard_map/final/pallas_call | solution.py:536
  (6 shorter events, 0.0 us)
Async XLA Ops:
  3.4 29.6 %collective-permute-start.1 = (bf16[2,2,512,128]{3,2,1,0:T(8,128)(2,1)}, bf16[2,2,512,128]{3,2,1,0:T(8,128)(2,1)}, u32[]{:S(2)}, u32[]{:S(2)}) collective-permute-start(bf16[2,2,512,128]{3,2,1,0:T(8,128)(2,1)} %get-tuple-element.35), channel_id=1, source_target_pairs={{4,0},{8,4},{12,8},{16,12},{20,16},{24,20},{28,24},{5,1},{9,5},{13... | collective-permute-start | bytes 1572872 | tf_op jit(solution)/shard_map/ppermute | solution.py:382
  5.3 27.7 %collective-permute-start = (bf16[2,2,512,128]{3,2,1,0:T(8,128)(2,1)}, bf16[2,2,512,128]{3,2,1,0:T(8,128)(2,1)}, u32[]{:S(2)}, u32[]{:S(2)}) collective-permute-start(bf16[2,2,512,128]{3,2,1,0:T(8,128)(2,1)} %get-tuple-element.35), channel_id=1, source_target_pairs={{0,4},{4,8},{8,12},{12,16},{16,20},{20,24},{24,28},{1,5},{5,9},{9,... | collective-permute-start | bytes 1572872 | tf_op jit(solution)/shard_map/ppermute | solution.py:379
  13.2 9.3 %collective-permute-start.6 = (bf16[1,4,4,64,128]{4,3,2,1,0:T(8,128)(2,1)}, bf16[1,4,4,64,128]{4,3,2,1,0:T(8,128)(2,1)S(1)}, u32[]{:S(2)}, u32[]{:S(2)}) collective-permute-start(bf16[1,4,4,64,128]{4,3,2,1,0:T(8,128)(2,1)} %bitcast.11), channel_id=1, source_target_pairs={{0,24},{4,28},{8,16},{12,20},{16,8},{20,12},{24,0},{28,4},{1,25},{... | collective-permute-start | bytes 786440 | tf_op jit(solution)/shard_map/ppermute | solution.py:376
  14.5 16.7 %collective-permute-start.5 = (bf16[1,4,4,64,128]{4,3,2,1,0:T(8,128)(2,1)}, bf16[1,4,4,64,128]{4,3,2,1,0:T(8,128)(2,1)S(1)}, u32[]{:S(2)}, u32[]{:S(2)}) collective-permute-start(bf16[1,4,4,64,128]{4,3,2,1,0:T(8,128)(2,1)} %bitcast.12), channel_id=1, source_target_pairs={{0,16},{4,20},{8,24},{12,28},{16,0},{20,4},{24,8},{28,12},{1,17},{... | collective-permute-start | bytes 786440 | tf_op jit(solution)/shard_map/ppermute | solution.py:376
  16.5 15.3 %collective-permute-start.4 = (bf16[1,4,4,64,128]{4,3,2,1,0:T(8,128)(2,1)}, bf16[1,4,4,64,128]{4,3,2,1,0:T(8,128)(2,1)S(1)}, u32[]{:S(2)}, u32[]{:S(2)}) collective-permute-start(bf16[1,4,4,64,128]{4,3,2,1,0:T(8,128)(2,1)} %bitcast.13), channel_id=1, source_target_pairs={{0,8},{4,12},{8,0},{12,4},{16,24},{20,28},{24,16},{28,20},{1,9},{5... | collective-permute-start | bytes 786440 | tf_op jit(solution)/shard_map/ppermute | solution.py:376
  22.5 16.2 %copy-start = (bf16[1,4,4,64,128]{4,3,2,1,0:T(8,128)(2,1)}, bf16[1,4,4,64,128]{4,3,2,1,0:T(8,128)(2,1)S(1)}, u32[]{:S(2)}) copy-start(bf16[1,4,4,64,128]{4,3,2,1,0:T(8,128)(2,1)S(1)} %collective-permute-done.6.refs_3_) | copy-start | bytes 786436
  31.2 7.5 %copy-start.1 = (bf16[1,4,4,64,128]{4,3,2,1,0:T(8,128)(2,1)}, bf16[1,4,4,64,128]{4,3,2,1,0:T(8,128)(2,1)S(1)}, u32[]{:S(2)}) copy-start(bf16[1,4,4,64,128]{4,3,2,1,0:T(8,128)(2,1)S(1)} %collective-permute-done.5.refs_2_) | copy-start | bytes 786436
  31.8 6.9 %copy-start.2 = (bf16[1,4,4,64,128]{4,3,2,1,0:T(8,128)(2,1)}, bf16[1,4,4,64,128]{4,3,2,1,0:T(8,128)(2,1)S(1)}, u32[]{:S(2)}) copy-start(bf16[1,4,4,64,128]{4,3,2,1,0:T(8,128)(2,1)S(1)} %collective-permute-done.4.refs_1_) | copy-start | bytes 786436
  33.0 5.7 %collective-permute-start.7 = (bf16[4,4,4,64,128]{4,3,2,1,0:T(8,128)(2,1)S(1)}, bf16[4,4,4,64,128]{4,3,2,1,0:T(8,128)(2,1)}, u32[]{:S(2)}, u32[]{:S(2)}) collective-permute-start(bf16[4,4,4,64,128]{4,3,2,1,0:T(8,128)(2,1)S(1)} %pad_maximum_fusion), channel_id=1, source_target_pairs={{0,4},{4,0},{8,12},{12,8},{16,20},{20,16},{24,28},{28,24},{1,5},{5... | collective-permute-start | bytes 3145736 | tf_op jit(solution)/shard_map/ppermute | solution.py:376
  33.1 13.4 %collective-permute-start.3 = (bf16[2,2,512,128]{3,2,1,0:T(8,128)(2,1)}, bf16[2,2,512,128]{3,2,1,0:T(8,128)(2,1)}, u32[]{:S(2)}, u32[]{:S(2)}) collective-permute-start(bf16[2,2,512,128]{3,2,1,0:T(8,128)(2,1)} %get-tuple-element.37), channel_id=1, source_target_pairs={{4,0},{8,4},{12,8},{16,12},{20,16},{24,20},{28,24},{5,1},{9,5},{13... | collective-permute-start | bytes 1572872 | tf_op jit(solution)/shard_map/ppermute | solution.py:382
  35.5 11.1 %collective-permute-start.2 = (bf16[2,2,512,128]{3,2,1,0:T(8,128)(2,1)}, bf16[2,2,512,128]{3,2,1,0:T(8,128)(2,1)}, u32[]{:S(2)}, u32[]{:S(2)}) collective-permute-start(bf16[2,2,512,128]{3,2,1,0:T(8,128)(2,1)} %get-tuple-element.37), channel_id=1, source_target_pairs={{0,4},{4,8},{8,12},{12,16},{16,20},{20,24},{24,28},{1,5},{5,9},{9,... | collective-permute-start | bytes 1572872 | tf_op jit(solution)/shard_map/ppermute | solution.py:379
  48.0 21.0 %all-to-all-start = ((f32[8,4,3,256]{3,1,2,0:T(4,128)}), f32[8,4,3,256]{3,1,2,0:T(4,128)S(1)}, u32[]{:S(2)}, u32[]{:S(2)}) async-start(f32[8,4,3,256]{3,1,2,0:T(4,128)} %broadcast_in_dim.12), calls=%async_computation | async-start | bytes 196608 | tf_op jit(solution)/shard_map/all_to_all | solution.py:458
  68.9 17.0 %all-to-all-start.2 = ((bf16[8,2,4,64,128]{4,3,2,1,0:T(8,128)(2,1)}), bf16[8,2,4,64,128]{4,3,2,1,0:T(8,128)(2,1)}, u32[]{:S(2)}, u32[]{:S(2)}) async-start(bf16[8,2,4,64,128]{4,3,2,1,0:T(8,128)(2,1)} %get-tuple-element.50), calls=%async_computation.2 | async-start | bytes 2097152 | tf_op jit(solution)/shard_map/all_to_all | solution.py:514
  73.2 37.1 %collective-permute-start.9 = (bf16[2,4,512,128]{3,2,1,0:T(8,128)(2,1)}, bf16[2,4,512,128]{3,2,1,0:T(8,128)(2,1)}, u32[]{:S(2)}, u32[]{:S(2)}) collective-permute-start(bf16[2,4,512,128]{3,2,1,0:T(8,128)(2,1)} %get-tuple-element.52.qd), channel_id=1, source_target_pairs={{4,0},{8,4},{12,8},{16,12},{20,16},{24,20},{28,24},{5,1},{9,5},{13... | collective-permute-start | bytes 3145736 | tf_op jit(solution)/shard_map/ppermute | solution.py:382
  75.1 35.2 %collective-permute-start.8 = (bf16[2,4,512,128]{3,2,1,0:T(8,128)(2,1)}, bf16[2,4,512,128]{3,2,1,0:T(8,128)(2,1)}, u32[]{:S(2)}, u32[]{:S(2)}) collective-permute-start(bf16[2,4,512,128]{3,2,1,0:T(8,128)(2,1)} %get-tuple-element.52.qd), channel_id=1, source_target_pairs={{0,4},{4,8},{8,12},{12,16},{16,20},{20,24},{24,28},{1,5},{5,9},{9,... | collective-permute-start | bytes 3145736 | tf_op jit(solution)/shard_map/ppermute | solution.py:379
  85.9 24.4 %copy-start.3 = (f32[4,2,512]{2,1,0:T(2,128)S(1)}, f32[4,2,512]{2,1,0:T(2,128)}, u32[]{:S(2)}) copy-start(f32[4,2,512]{2,1,0:T(2,128)} %get-tuple-element.53) | copy-start | bytes 49156
  86.0 43.1 %all-to-all-start.1 = ((bf16[8,2,4,64,128]{4,3,2,1,0:T(8,128)(2,1)}), bf16[8,2,4,64,128]{4,3,2,1,0:T(8,128)(2,1)}, u32[]{:S(2)}, u32[]{:S(2)}) async-start(bf16[8,2,4,64,128]{4,3,2,1,0:T(8,128)(2,1)} %get-tuple-element.49), calls=%async_computation.1 | async-start | bytes 2097152 | tf_op jit(solution)/shard_map/all_to_all | solution.py:513
  110.3 10.7 %collective-permute-start.11 = (f32[4,2,512]{2,1,0:T(2,128)S(1)}, f32[4,2,512]{2,1,0:T(2,128)S(1)}, u32[]{:S(2)}, u32[]{:S(2)}) collective-permute-start(f32[4,2,512]{2,1,0:T(2,128)S(1)} %copy-done.3), channel_id=1, source_target_pairs={{4,0},{8,4},{12,8},{16,12},{20,16},{24,20},{28,24},{5,1},{9,5},{13... | collective-permute-start | bytes 49160 | tf_op jit(solution)/shard_map/ppermute | solution.py:382
  112.2 8.8 %collective-permute-start.10 = (f32[4,2,512]{2,1,0:T(2,128)S(1)}, f32[4,2,512]{2,1,0:T(2,128)S(1)}, u32[]{:S(2)}, u32[]{:S(2)}) collective-permute-start(f32[4,2,512]{2,1,0:T(2,128)S(1)} %copy-done.3), channel_id=1, source_target_pairs={{0,4},{4,8},{8,12},{12,16},{16,20},{20,24},{24,28},{1,5},{5,9},{9,... | collective-permute-start | bytes 49160 | tf_op jit(solution)/shard_map/ppermute | solution.py:379
  121.0 0.6 copy-start.4
  121.0 0.6 copy-start.5
where the time goes:
time: 135 us; the launch traced here: 134 us
  Pallas kernels  47.8 us (35%)
  starting transfers between devices  44 us (33%)
  waiting for transfers between devices  37.9 us (28%)
  local copies, waits for them, and re-layouts  2.69 us (2%)
    ppermute x4, waiting for transfers between devices, from_high(): return lax.ppermute(value, 'ctx', [(i + 1, i) for i in range(devices - 1)])  25 us
    ppermute x4, starting transfers between devices, from_low(): return lax.ppermute(value, 'ctx', [(i, i + 1) for i in range(devices - 1)])  14.9 us
    pallas_call x1, Pallas kernels, shards(): pl.pallas_call(functools.partial(local_kernel, scale, scale2, halves, gro...  14.5 us
    ppermute x4, waiting for transfers between devices, swap(): return lax.ppermute(value, 'ctx', [(i, i ^ mask) for i in range(devices)])  12.9 us
    ppermute x4, starting transfers between devices, from_high(): return lax.ppermute(value, 'ctx', [(i + 1, i) for i in range(devices - 1)])  8.18 us
    pallas_call x1, Pallas kernels, shards(): pl.pallas_call(functools.partial(rim_kernel, scale, scale2), grid=(heads,...  7.46 us
    all_to_all x1, starting transfers between devices, shards(): ends = lax.all_to_all(ends, 'ctx', 0, 0, tiled=True)  6.83 us
    pallas_call x1, Pallas kernels, shards(): pl.pallas_call(functools.partial(global_kernel, scale, scale2), grid=(hea...  6.52 us
  transfers between devices with their start and end apart: 15, of which 6 were waited for; matrix products, arithmetic and copies ran while one was open for 1% of the time, Pallas kernels for 30%

commit v1 on v0

--- a/solution.py
+++ b/solution.py
@@ -139,20 +139,17 @@
     scores = nt(kv[0, 0], queries) * scale2
     top = jnp.max(scores, axis=0, keepdims=True)
     weights = jnp.exp2(scores - top)
-    stats[0, 0, 0:1, :] = top
-    stats[0, 0, 1:2, :] = jnp.sum(weights, axis=0, keepdims=True)
-    stats[0, 0, 2:3, :] = jnp.sum(weights * nt(kv[1, 0], grads), axis=0, keepdims=True)
+    total = jnp.sum(weights, axis=0, keepdims=True)
+    dot = jnp.sum(weights * nt(kv[1, 0], grads), axis=0, keepdims=True)
+    line = iota(stats.shape[2:], 0)
+    found = jnp.where(line == 0, top, jnp.where(line == 1, total, dot))
+    for device in range(stats.shape[0]):
+        stats[device, 0] = found
 
 
 def band(scores, low):
     rows, columns = iota(scores.shape, 0), iota(scores.shape, 1)
     return jnp.where(rows <= columns if low else rows >= columns, scores, NEG)
-
-
-def join(blocks, number, buf):
-    toks = blocks[0].shape[2]
-    for place, block in enumerate(blocks):
-        buf[place * toks : (place + 1) * toks, :] = block[number, 0]
 
 
 def put_in_slots(expand, tables, sums):
@@ -165,7 +162,7 @@
             ]
 
 
-def global_kernel(scale, scale2, kv, rows, stats, expand, dkv, ends):
+def global_kernel(scale, scale2, kv, rows, stats, expand, before, dkv, ends):
     g_query, g_grad = rows[0, 0], rows[3, 0]
     tops = stats[:, 0, 0:1, :]
     top = jnp.max(tops, axis=0)
@@ -176,25 +173,28 @@
     weights = jnp.exp2(nt(kv[0, 0], g_query) * scale2 - g_log)
     narrow = weights.astype(BF)
     slopes = (weights * (nt(kv[1, 0], g_grad) - g_dot)).astype(BF)
-    dkv[0, 0] = (nt(g_query.T, slopes) * scale).T
-    dkv[1, 0] = nt(g_grad.T, narrow).T
+    dkv[0, 0] = before[0, 0] + nn(slopes, g_query) * scale
+    dkv[1, 0] = before[1, 0] + nn(narrow, g_grad)
     out = nn(kv[1, 0].T, narrow).T.astype(BF)
     dq = (nn(kv[0, 0].T, slopes) * scale).T.astype(BF)
     put_in_slots(expand[...], (out, dq), ends)
 
 
 def local_kernel(scale, scale2, halves, group, qd, kv, *refs):
-    lows, highs, refs = refs[:halves], refs[halves : 2 * halves], refs[2 * halves :]
+    nears, fars, refs = refs[:halves], refs[halves : 2 * halves], refs[2 * halves :]
     rows, bias, expand, out, log_dot, dq, dkv, sums, keys, values, score_buf, probs, slopes = refs
     toks = kv.shape[2]
     reach = 2 * HALF + TILE
     span = keys.shape[0] - rows.shape[2]
+    near = 2 * (1 - lax.axis_index("ctx") % 2)
     for part in range(halves):
 
         @pl.when(pl.program_id(0) // group == part)
         def _():
-            join((lows[part], kv, highs[part]), 0, keys)
-            join((lows[part], kv, highs[part]), 1, values)
+            for block, place in ((nears[part], near), (kv, 1), (fars[part], 2 - near)):
+                spot = pl.ds(pl.multiple_of(place * toks, toks), toks)
+                keys[spot, :] = block[0, 0]
+                values[spot, :] = block[1, 0]
 
     keys[span:, :] = rows[1, 0]
     values[span:, :] = rows[2, 0]
@@ -277,12 +277,17 @@
 
 
 def rim_kernel(
-    scale, scale2, kv, bias, qd_low, qd_high, log_low, log_high, partial, dkv, probs, slopes
+    scale, scale2, kv, bias, qd_near, qd_far, log_near, log_far, partial, dkv,
+    queries, grads, logs, probs, slopes,
 ):
     toks = kv.shape[2]
     reach = toks + TILE
-    query_t = jnp.concatenate([qd_low[0, 0].T, qd_high[0, 0].T], axis=1)
-    grad_t = jnp.concatenate([qd_low[1, 0].T, qd_high[1, 0].T], axis=1)
+    near = 1 - lax.axis_index("ctx") % 2
+    for qd, log_dot, place in ((qd_near, log_near, near), (qd_far, log_far, 1 - near)):
+        spot = pl.ds(pl.multiple_of(place * toks, toks), toks)
+        queries[spot, :] = qd[0, 0]
+        grads[spot, :] = qd[1, 0]
+        logs[place] = log_dot[0]
     for k_tile in range(toks // TILE):
         span = slice(k_tile * TILE, (k_tile + 1) * TILE)
         key = kv[0, 0, span, :]
@@ -290,28 +295,24 @@
         key_bias = wide(bias[HALF + k_tile * TILE : HALF + (k_tile + 1) * TILE, :], TILE)
         for piece in range(reach // TILE):
             start = (k_tile + piece) * TILE
-            log_dot, offset = (log_low, start) if start < toks else (log_high, start - toks)
-            lanes = slice(offset, offset + TILE)
-            scores = nn(key, query_t[:, start : start + TILE]) * scale2 + key_bias
+            side, lanes = start // toks, slice(start % toks, start % toks + TILE)
+            scores = nt(key, queries[start : start + TILE, :]) * scale2 + key_bias
             if piece == 0:
                 scores = band(scores, True)
             elif piece == reach // TILE - 1:
                 scores = band(scores, False)
-            weights = jnp.exp2(scores - log_dot[0, 0:1, lanes])
-            rise = nn(value, grad_t[:, start : start + TILE]) - log_dot[0, 1:2, lanes]
+            weights = jnp.exp2(scores - logs[side, 0:1, lanes])
+            slope = weights * (nt(value, grads[start : start + TILE, :]) - logs[side, 1:2, lanes])
             spot = slice(piece * TILE, (piece + 1) * TILE)
             probs[span, spot] = weights.astype(BF)
-            slopes[span, spot] = (weights * rise).astype(BF)
-    for k_tile in range(toks // TILE):
-        span = slice(k_tile * TILE, (k_tile + 1) * TILE)
+            slopes[span, spot] = slope.astype(BF)
         window = slice(k_tile * TILE, k_tile * TILE + reach)
-        dk = (nt(query_t[:, window], slopes[span, :]) * scale).T
-        dkv[0, 0, span, :] = partial[0, 0, span, :] + dk
-        dkv[1, 0, span, :] = partial[1, 0, span, :] + nt(grad_t[:, window], probs[span, :]).T
+        dkv[0, 0, span, :] = partial[0, 0, span, :] + nn(slopes[span, :], queries[window, :]) * scale
+        dkv[1, 0, span, :] = partial[1, 0, span, :] + nn(probs[span, :], grads[window, :])
 
 
 def final_kernel(
-    place, out, ends, sums, dq, dkv, extra, attn, query_grad, key_grad, value_grad, wide_rows
+    place, out, ends, sums, dq, dkv, attn, query_grad, key_grad, value_grad, wide_rows
 ):
     heads, toks = out.shape[0], out.shape[1]
     hot = place[...]
@@ -329,8 +330,8 @@
         added = [added[:, i * width : (i + 1) * width] for i in range(4)]
         wide_rows[rows, :] = jnp.where(is_global, added[0], out[head].astype(F32))
         query_grad[rows, :] = dq[head] + added[1]
-        key_grad[rows, :] = dkv[0, head] + extra[0, head] + added[2]
-        value_grad[rows, :] = dkv[1, head] + extra[1, head] + added[3]
+        key_grad[rows, :] = dkv[0, head] + added[2]
+        value_grad[rows, :] = dkv[1, head] + added[3]
     attn[...] = wide_rows[...].astype(BF)
 
 
@@ -375,11 +376,12 @@
     def swap(value, mask):
         return lax.ppermute(value, "ctx", [(i, i ^ mask) for i in range(devices)])
 
-    def from_low(value):
-        return lax.ppermute(value, "ctx", [(i, i + 1) for i in range(devices - 1)])
-
-    def from_high(value):
-        return lax.ppermute(value, "ctx", [(i + 1, i) for i in range(devices - 1)])
+    def from_near(value):
+        return swap(value, 1)
+
+    def from_far(value):
+        pairs = [(i, i + 1) for i in range(1, devices - 1, 2)]
+        return lax.ppermute(value, "ctx", pairs + [(j, i) for i, j in pairs])
 
     def after(value, earlier):
         return lax.optimization_barrier((value, earlier))[0]
@@ -425,17 +427,17 @@
         name="masks",
     )(pos_row)
 
-    lows, highs = [], []
+    nears, fars = [], []
     for part in kv_parts:
-        if lows:
-            part = after(part, (lows[-1], highs[-1]))
-        lows.append(from_low(part))
-        highs.append(from_high(part))
+        if fars:
+            part = after(part, (nears[-1], fars[-1]))
+        fars.append(from_far(part))
+        nears.append(from_near(part))
     held = [slot_rows[None]]
     for stage in stages:
         send = jnp.concatenate(held, axis=0) if len(held) > 1 else held[0]
         if stage == [1]:
-            send = after(send, (lows[0], highs[0], place))
+            send = after(send, (nears[0], fars[0], place))
         held += [swap(send, mask) for mask in stage]
 
     row_shape = (4, heads, count, width)
@@ -445,19 +447,18 @@
         in_specs=[whole(compact.shape)]
         + [per_head(part.shape, 2) for part in held]
         + [per_head(pair_shape, 1)],
-        out_specs=(per_head(row_shape, 1), per_head((1, heads, 3, count), 1)),
-        out_shape=(struct(row_shape, BF), struct((1, heads, 3, count), F32)),
+        out_specs=(per_head(row_shape, 1), per_head((devices, heads, 8, count), 1)),
+        out_shape=(struct(row_shape, BF), struct((devices, heads, 8, count), F32)),
         compiler_params=params(),
         cost_estimate=cost(1e6, 1e6),
         name="global_stats",
     )(compact, *held, kv)
 
-    kv_done = (lows, highs)
+    kv_done = (nears, fars)
     stats = after(stats, kv_done)
-    stats = jnp.broadcast_to(stats, (devices,) + stats.shape[1:])
     stats = lax.all_to_all(stats, "ctx", 0, 0, tiled=True)
     qd_late = after(qd, (kv_done, rows))
-    qd_low, qd_high = from_low(qd_late), from_high(qd_late)
+    qd_far, qd_near = from_far(qd_late), from_near(qd_late)
 
     def half_head(part):
         return pl.BlockSpec(
@@ -495,21 +496,21 @@
         compiler_params=params(),
         cost_estimate=cost(1e6, 1e6),
         name="local",
-    )(qd, kv, *lows, *highs, rows, bias, expand)
-    log_late = after(log_dot, (qd_low, qd_high))
-    log_low, log_high = from_low(log_late), from_high(log_late)
-
-    extra, ends = pl.pallas_call(
+    )(qd, kv, *nears, *fars, rows, bias, expand)
+    log_far, log_near = from_far(log_dot), from_near(log_dot)
+
+    dkv, ends = pl.pallas_call(
         functools.partial(global_kernel, scale, scale2),
         grid=(heads,),
         in_specs=[per_head(pair_shape, 1), per_head(row_shape, 1)]
-        + [per_head(stats.shape, 1), whole(expand.shape)],
+        + [per_head(stats.shape, 1), whole(expand.shape), per_head(pair_shape, 1)],
         out_specs=(per_head(pair_shape, 1), per_head(ends_shape, 2)),
         out_shape=(struct(pair_shape, F32), struct(ends_shape, BF)),
-        compiler_params=params(),
-        cost_estimate=cost(2e9, 5e6, 1e6),
+        input_output_aliases={4: 0},
+        compiler_params=params(),
+        cost_estimate=cost(1e6, 1e6),
         name="global_queries",
-    )(kv, rows, after(stats, log_dot), expand)
+    )(kv, rows, after(stats, (qd_near, qd_far)), expand, dkv)
     ends = lax.all_to_all(ends, "ctx", 0, 0, tiled=True)
     sums = lax.all_to_all(sums, "ctx", 0, 0, tiled=True)
 
@@ -523,13 +524,16 @@
         out_specs=per_head(pair_shape, 1),
         out_shape=struct(pair_shape, F32),
         scratch_shapes=[
+            pltpu.VMEM((2 * toks, width), BF),
+            pltpu.VMEM((2 * toks, width), BF),
+            pltpu.VMEM((2, 2, toks), F32),
             pltpu.VMEM((toks, toks + TILE), BF),
             pltpu.VMEM((toks, toks + TILE), BF),
         ],
         compiler_params=params(),
-        cost_estimate=cost(4e9, 8e6, 2e6),
+        cost_estimate=cost(1e6, 1e6),
         name="rim",
-    )(kv, bias, qd_low, qd_high, log_low, log_high, dkv)
+    )(kv, bias, qd_near, qd_far, log_near, log_far, dkv)
 
     flat_shape = (toks * heads, width)
     steps = 2
@@ -543,14 +547,13 @@
             whole(ends_shape),
             pl.BlockSpec((heads, toks // steps, width), lambda i: (0, i, 0)),
             pl.BlockSpec((2, heads, toks // steps, width), lambda i: (0, 0, i, 0)),
-            pl.BlockSpec((2, heads, toks // steps, width), lambda i: (0, 0, i, 0)),
         ],
         out_specs=[pl.BlockSpec((toks * heads // steps, width), lambda i: (i, 0))] * 4,
         out_shape=[struct(flat_shape, kind) for kind in (BF, F32, F32, F32)],
         scratch_shapes=[pltpu.VMEM((toks * heads // steps, width), F32)],
         compiler_params=params(),
         name="final",
-    )(place, out, ends, sums, dq, dkv, extra)
+    )(place, out, ends, sums, dq, dkv)
     return tuple(x.reshape(toks, heads, width) for x in outs)
 
 

time: 135 us -> 125 us (0.926)
  starting transfers between devices: 44 us -> 39.8 us
  waiting for transfers between devices: 37.9 us -> 33.9 us
  local copies, waits for them, and re-layouts: 2.69 us -> 0.63 us
    ppermute x8 -> x4, starting transfers between devices: 23.1 us -> 19.5 us  [from_far(): return lax.ppermute(value, 'ctx', pairs + [(j, i) for i, j in pairs])]
    all_to_all x1, starting transfers between devices: 6.51 us -> 3.36 us  [shards(): stats = lax.all_to_all(stats, 'ctx', 0, 0, tiled=True)]
    ppermute x8 -> x4, waiting for transfers between devices: 25 us -> 22.9 us  [from_far(): return lax.ppermute(value, 'ctx', pairs + [(j, i) for i, j in pairs])]
    all_to_all x1, starting transfers between devices: 6.83 us -> 8.8 us  [shards(): ends = lax.all_to_all(ends, 'ctx', 0, 0, tiled=True)]
    ppermute x4 -> x8, waiting for transfers between devices: 12.9 us -> 10.9 us  [swap(): return lax.ppermute(value, 'ctx', [(i, i ^ mask) for i in range(devices)])]
    broadcast_in_dim x2 -> x0, local copies, waits for them, and re-layouts: 1.38 us -> none  [shards(): stats = jnp.broadcast_to(stats, (devices,) + stats.shape[1:])]
    ppermute x4 -> x8, starting transfers between devices: 3.33 us -> 3.96 us  [swap(): return lax.ppermute(value, 'ctx', [(i, i ^ mask) for i in range(devices)])]
  transfers between devices with their start and end apart: 15 -> 15, of which waited for: 6 -> 4; matrix products, arithmetic and copies ran while one was open for 1% -> 1% of each run, Pallas kernels for 30% -> 32%
where the time goes in v1:
time: 125 us; the launch traced here: 124 us
  Pallas kernels  47.2 us (38%)
  starting transfers between devices  39.8 us (32%)
  waiting for transfers between devices  33.9 us (27%)
  other arithmetic  1.29 us (1%)
    ppermute x4, waiting for transfers between devices, from_far(): return lax.ppermute(value, 'ctx', pairs + [(j, i) for i, j in pairs])  22.9 us
    ppermute x4, starting transfers between devices, from_far(): return lax.ppermute(value, 'ctx', pairs + [(j, i) for i, j in pairs])  19.5 us
    pallas_call x1, Pallas kernels, shards(): pl.pallas_call(functools.partial(local_kernel, scale, scale2, halves, gro...  14.5 us
    ppermute x8, waiting for transfers between devices, swap(): return lax.ppermute(value, 'ctx', [(i, i ^ mask) for i in range(devices)])  10.9 us
    all_to_all x1, starting transfers between devices, shards(): ends = lax.all_to_all(ends, 'ctx', 0, 0, tiled=True)  8.8 us
    pallas_call x1, Pallas kernels, shards(): pl.pallas_call(functools.partial(rim_kernel, scale, scale2), grid=(heads,...  7.17 us
    pallas_call x1, Pallas kernels, shards(): pl.pallas_call(functools.partial(global_kernel, scale, scale2), grid=(hea...  6.6 us
    pallas_call x1, Pallas kernels, shards(): pl.pallas_call(functools.partial(stats_kernel, scale2), grid=(heads,), in...  5.51 us
  transfers between devices with their start and end apart: 15, of which 4 were waited for; matrix products, arithmetic and copies ran while one was open for 1% of the time, Pallas kernels for 32%

profile of v1, /device:TPU:1, one launch (start us, length us, event | category | flops | bytes accessed | tf_op | source)
XLA Modules:
  0.0 123.6 jit_solution(11723245585868176905)
XLA Ops:
  0.6 2.7 %pack_keys.1 = (bf16[2,4,512,128]{3,2,1,0:T(8,128)(2,1)}, bf16[2,2,512,128]{3,2,1,0:T(8,128)(2,1)}, bf16[2,2,512,128]{3,2,1,0:T(8,128)(2,1)}) custom-call(bf16[2048,128]{1,0:T(8,128)(2,1)} %bitcast.15, bf16[2048,128]{1,0:T(8,128)(2,1)} %bitcast.16), custom_call_target="tpu_custom_call" | custom-call | tf_op jit(solution)/shard_map/pack_keys/pallas_call | solution.py:398
  3.4 0.1 collective-permute-start
  3.4 4.4 %collective-permute-start.1 = (bf16[2,2,512,128]{3,2,1,0:T(8,128)(2,1)}, bf16[2,2,512,128]{3,2,1,0:T(8,128)(2,1)}, u32[]{:S(2)}, u32[]{:S(2)}) collective-permute-start(bf16[2,2,512,128]{3,2,1,0:T(8,128)(2,1)} %get-tuple-element.34), channel_id=1, source_target_pairs={{4,8},{12,16},{20,24},{8,4},{16,12},{24,20},{5,9},{13,17},{21,25},... | collective-permute-start | bytes 1572872 | tf_op jit(solution)/shard_map/ppermute | solution.py:384
  7.9 3.4 %pack_queries.1 = (bf16[2,4,512,128]{3,2,1,0:T(8,128)(2,1)}, bf16[4,4,64,128]{3,2,1,0:T(8,128)(2,1)}) custom-call(bf16[2048,128]{1,0:T(8,128)(2,1)} %bitcast.17, bf16[2048,128]{1,0:T(8,128)(2,1)} %bitcast.18, bf16[2,4,512,128]{3,2,1,0:T(8,128)(2,1)} %get-tuple-element.32.kv.refs_5_, s32[1,256]{1,0:T(1,128)} %bitcast.19), custom_call_target="tpu_custom_call" | custom-call | tf_op jit(solution)/shard_map/pack_queries/pallas_call | solution.py:406
  11.3 1.2 collective-permute-start.4
  12.5 0.0 collective-permute-start.5
  12.5 1.4 %collective-permute-start.6 = (bf16[1,4,4,64,128]{4,3,2,1,0:T(8,128)(2,1)}, bf16[1,4,4,64,128]{4,3,2,1,0:T(8,128)(2,1)S(1)}, u32[]{:S(2)}, u32[]{:S(2)}) collective-permute-start(bf16[1,4,4,64,128]{4,3,2,1,0:T(8,128)(2,1)} %bitcast.12), channel_id=1, source_target_pairs={{0,24},{4,28},{8,16},{12,20},{16,8},{20,12},{24,0},{28,4},{1,25},{... | collective-permute-start | bytes 786440 | tf_op jit(solution)/shard_map/ppermute | solution.py:377
  13.9 2.5 %masks.1 = (f32[1536,128]{1,0:T(8,128)}, bf16[256,512]{1,0:T(8,128)(2,1)}, bf16[512,256]{1,0:T(8,128)(2,1)}, bf16[512,64]{1,0:T(8,128)(2,1)}) custom-call(s32[1,256]{1,0:T(1,128)} %bitcast.20), custom_call_target="tpu_custom_call" | custom-call | tf_op jit(solution)/shard_map/masks/pallas_call | solution.py:418
  16.5 10.9 %collective-permute-done.4.refs_1_ = bf16[1,4,4,64,128]{4,3,2,1,0:T(8,128)(2,1)S(1)} collective-permute-done((bf16[1,4,4,64,128]{4,3,2,1,0:T(8,128)(2,1)}, bf16[1,4,4,64,128]{4,3,2,1,0:T(8,128)(2,1)S(1)}, u32[]{:S(2)}, u32[]{:S(2)}) %collective-permute-start.4) | collective-permute-done | bytes 262176 | tf_op jit(solution)/shard_map/ppermute | solution.py:377
  27.4 0.0 collective-permute-done.5.refs_2_
  27.4 0.0 collective-permute-done.6.refs_3_
  27.4 0.0 copy-start.3
  27.4 1.3 %pad_maximum_fusion = bf16[4,4,4,64,128]{4,3,2,1,0:T(8,128)(2,1)S(1)} fusion(bf16[1,4,4,64,128]{4,3,2,1,0:T(8,128)(2,1)S(1)} %collective-permute-done.6.refs_3_, bf16[1,4,4,64,128]{4,3,2,1,0:T(8,128)(2,1)S(1)} %collective-permute-done.5.refs_2_, bf16[1,4,4,64,128]{4,3,2,1,0:T(8,128)(2,1)S(1)} %collective-permute-done.4.refs_1_, ...), kind=kLoop, calls=%fused_computation | loop fusion | flops 1572864 | bytes 2097152 | tf_op jit(solution)/shard_map/concatenate | solution.py:438
  28.7 0.0 collective-permute-done.refs_0_
  28.7 0.0 collective-permute-done.1.refs_2_
  28.7 1.0 collective-permute-start.7
  29.7 0.1 collective-permute-start.2
  29.8 8.4 %collective-permute-start.3 = (bf16[2,2,512,128]{3,2,1,0:T(8,128)(2,1)}, bf16[2,2,512,128]{3,2,1,0:T(8,128)(2,1)}, u32[]{:S(2)}, u32[]{:S(2)}) collective-permute-start(bf16[2,2,512,128]{3,2,1,0:T(8,128)(2,1)} %get-tuple-element.36), channel_id=1, source_target_pairs={{4,8},{12,16},{20,24},{8,4},{16,12},{24,20},{5,9},{13,17},{21,25},... | collective-permute-start | bytes 1572872 | tf_op jit(solution)/shard_map/ppermute | solution.py:384
  38.2 0.0 collective-permute-done.7.refs_4_
  38.2 0.0 copy-done.1
  38.2 0.0 copy-done.2
  38.2 0.0 copy-done.3
  38.2 5.5 %global_stats.1 = (bf16[4,4,256,128]{3,2,1,0:T(8,128)(2,1)}, f32[8,4,8,256]{3,2,1,0:T(8,128)}) custom-call(bf16[256,512]{1,0:T(8,128)(2,1)} %get-tuple-element.37.compact, bf16[1,4,4,64,128]{4,3,2,1,0:T(8,128)(2,1)} %bitcast.14, bf16[1,4,4,64,128]{4,3,2,1,0:T(8,128)(2,1)} %copy-done.1, bf16[1,4,4,64,128]{4,3,2,1,0:T(8,128)(2,1)} %copy-done.2, ...), custom_call_target="tpu_custom_call" | custom-call | flops 1000000 | bytes 1000000 | tf_op jit(solution)/shard_map/global_stats/pallas_call | solution.py:444
  43.7 0.0 collective-permute-done.2.refs_1_
  43.7 6.6 %collective-permute-done.3.refs_3_ = bf16[2,2,512,128]{3,2,1,0:T(8,128)(2,1)} collective-permute-done((bf16[2,2,512,128]{3,2,1,0:T(8,128)(2,1)}, bf16[2,2,512,128]{3,2,1,0:T(8,128)(2,1)}, u32[]{:S(2)}, u32[]{:S(2)}) %collective-permute-start.3) | collective-permute-done | bytes 524320 | tf_op jit(solution)/shard_map/ppermute | solution.py:384
  50.3 3.4 %all-to-all-start = ((f32[8,4,8,256]{3,2,1,0:T(8,128)}), f32[8,4,8,256]{3,2,1,0:T(8,128)S(1)}, u32[]{:S(2)}, u32[]{:S(2)}) async-start(f32[8,4,8,256]{3,2,1,0:T(8,128)} %get-tuple-element.45), calls=%async_computation | async-start | bytes 524288 | tf_op jit(solution)/shard_map/all_to_all | solution.py:459
  53.7 0.1 collective-permute-start.8
  53.8 3.1 %collective-permute-start.9 = (bf16[2,4,512,128]{3,2,1,0:T(8,128)(2,1)}, bf16[2,4,512,128]{3,2,1,0:T(8,128)(2,1)}, u32[]{:S(2)}, u32[]{:S(2)}) collective-permute-start(bf16[2,4,512,128]{3,2,1,0:T(8,128)(2,1)} %get-tuple-element.46.qd), channel_id=1, source_target_pairs={{4,8},{12,16},{20,24},{8,4},{16,12},{24,20},{5,9},{13,17},{21,25},... | collective-permute-start | bytes 3145736 | tf_op jit(solution)/shard_map/ppermute | solution.py:384
  56.9 14.5 %local.1 = (bf16[4,512,128]{2,1,0:T(8,128)(2,1)}, f32[4,2,512]{2,1,0:T(2,128)}, f32[4,512,128]{2,1,0:T(8,128)}, f32[2,4,512,128]{3,2,1,0:T(8,128)}, bf16[8,2,4,64,128]{4,3,2,1,0:T(8,128)(2,1)}) custom-call(bf16[2,4,512,128]{3,2,1,0:T(8,128)(2,1)} %get-tuple-element.46.qd, bf16[2,4,512,128]{3,2,1,0:T(8,128)(2,1)} %get-tuple-element.32.kv.refs_5_, ...), custom_call_target="tpu_custom_call" | custom-call | flops 1000000 | bytes 1000000 | tf_op jit(solution)/shard_map/local/pallas_call | solution.py:469
  71.4 0.0 all-to-all-done.stats
  71.4 0.0 copy-start
  71.4 4.2 %all-to-all-start.2 = ((bf16[8,2,4,64,128]{4,3,2,1,0:T(8,128)(2,1)}), bf16[8,2,4,64,128]{4,3,2,1,0:T(8,128)(2,1)}, u32[]{:S(2)}, u32[]{:S(2)}) async-start(bf16[8,2,4,64,128]{4,3,2,1,0:T(8,128)(2,1)} %get-tuple-element.50), calls=%async_computation.2 | async-start | bytes 2097152 | tf_op jit(solution)/shard_map/all_to_all | solution.py:515
  75.6 0.0 collective-permute-done.8.qd_near
  75.7 5.5 %collective-permute-done.9.qd_far = bf16[2,4,512,128]{3,2,1,0:T(8,128)(2,1)} collective-permute-done((bf16[2,4,512,128]{3,2,1,0:T(8,128)(2,1)}, bf16[2,4,512,128]{3,2,1,0:T(8,128)(2,1)}, u32[]{:S(2)}, u32[]{:S(2)}) %collective-permute-start.9) | collective-permute-done | bytes 1048608 | tf_op jit(solution)/shard_map/ppermute | solution.py:384
  81.1 0.0 copy-done
  81.1 6.6 %global_queries.1 = (f32[2,4,512,128]{3,2,1,0:T(8,128)}, bf16[8,2,4,64,128]{4,3,2,1,0:T(8,128)(2,1)}) custom-call(bf16[2,4,512,128]{3,2,1,0:T(8,128)(2,1)} %get-tuple-element.32.kv.refs_5_, bf16[4,4,256,128]{3,2,1,0:T(8,128)(2,1)} %get-tuple-element.40.refs_4_.rows, f32[8,4,8,256]{3,2,1,0:T(8,128)} %copy-done, ...), custom_call_target="tpu_custom_call", output_to_operand_aliasing={{0}: (4, {})} | custom-call | flops 1000000 | bytes 1000000 | tf_op jit(solution)/shard_map/global_queries/pallas_call | solution.py:502
  87.7 0.0 all-to-all-done.2.sums
  87.7 8.8 %all-to-all-start.1 = ((bf16[8,2,4,64,128]{4,3,2,1,0:T(8,128)(2,1)}), bf16[8,2,4,64,128]{4,3,2,1,0:T(8,128)(2,1)}, u32[]{:S(2)}, u32[]{:S(2)}) async-start(bf16[8,2,4,64,128]{4,3,2,1,0:T(8,128)(2,1)} %get-tuple-element.49), calls=%async_computation.1 | async-start | bytes 2097152 | tf_op jit(solution)/shard_map/all_to_all | solution.py:514
  96.5 0.0 copy-done.6
  96.5 0.1 collective-permute-start.10
  96.6 3.6 %collective-permute-start.11 = (f32[4,2,512]{2,1,0:T(2,128)S(1)}, f32[4,2,512]{2,1,0:T(2,128)S(1)}, u32[]{:S(2)}, u32[]{:S(2)}) collective-permute-start(f32[4,2,512]{2,1,0:T(2,128)S(1)} %copy-done.6), channel_id=1, source_target_pairs={{4,8},{12,16},{20,24},{8,4},{16,12},{24,20},{5,9},{13,17},{21,25},... | collective-permute-start | bytes 49160 | tf_op jit(solution)/shard_map/ppermute | solution.py:384
  100.2 0.0 collective-permute-done.10.log_near
  100.2 0.0 copy-start.4
  100.2 10.9 %collective-permute-done.11.log_far = f32[4,2,512]{2,1,0:T(2,128)S(1)} collective-permute-done((f32[4,2,512]{2,1,0:T(2,128)S(1)}, f32[4,2,512]{2,1,0:T(2,128)S(1)}, u32[]{:S(2)}, u32[]{:S(2)}) %collective-permute-start.11) | collective-permute-done | bytes 16416 | tf_op jit(solution)/shard_map/ppermute | solution.py:384
  111.1 0.6 copy-done.5
  111.7 7.2 %rim.1.dkv = f32[2,4,512,128]{3,2,1,0:T(8,128)} custom-call(bf16[2,4,512,128]{3,2,1,0:T(8,128)(2,1)} %get-tuple-element.32.kv.refs_5_, f32[1536,128]{1,0:T(8,128)} %get-tuple-element.41.refs_5_.bias, bf16[2,4,512,128]{3,2,1,0:T(8,128)(2,1)} %collective-permute-done.8.qd_near, bf16[2,4,512,128]{3,2,1,0:T(8,128)(2,1)} %collective-permute-done.9.qd_far, ...), custom_call_target="tpu_custom_call" | custom-call | flops 1000000 | bytes 1000000 | tf_op jit(solution)/shard_map/rim/pallas_call | solution.py:517
  118.9 0.0 all-to-all-done.1.ends
  118.9 4.7 %final.1 = (bf16[2048,128]{1,0:T(8,128)(2,1)}, f32[2048,128]{1,0:T(8,128)}, f32[2048,128]{1,0:T(8,128)}, f32[2048,128]{1,0:T(8,128)}) custom-call(bf16[512,64]{1,0:T(8,128)(2,1)} %get-tuple-element.31.place, bf16[4,512,128]{2,1,0:T(8,128)(2,1)} %get-tuple-element.43.out, bf16[8,2,4,64,128]{4,3,2,1,0:T(8,128)(2,1)} %all-to-all-done.1.ends, ...), custom_call_target="tpu_custom_call" | custom-call | tf_op jit(solution)/shard_map/final/pallas_call | solution.py:540
  (5 shorter events, 0.0 us)
Async XLA Ops:
  3.4 25.3 %collective-permute-start = (bf16[2,2,512,128]{3,2,1,0:T(8,128)(2,1)}, bf16[2,2,512,128]{3,2,1,0:T(8,128)(2,1)}, u32[]{:S(2)}, u32[]{:S(2)}) collective-permute-start(bf16[2,2,512,128]{3,2,1,0:T(8,128)(2,1)} %get-tuple-element.34), channel_id=1, source_target_pairs={{0,4},{4,0},{8,12},{12,8},{16,20},{20,16},{24,28},{28,24},{1,5},{5... | collective-permute-start | bytes 1572872 | tf_op jit(solution)/shard_map/ppermute | solution.py:377
  3.4 25.3 %collective-permute-start.1 = (bf16[2,2,512,128]{3,2,1,0:T(8,128)(2,1)}, bf16[2,2,512,128]{3,2,1,0:T(8,128)(2,1)}, u32[]{:S(2)}, u32[]{:S(2)}) collective-permute-start(bf16[2,2,512,128]{3,2,1,0:T(8,128)(2,1)} %get-tuple-element.34), channel_id=1, source_target_pairs={{4,8},{12,16},{20,24},{8,4},{16,12},{24,20},{5,9},{13,17},{21,25},... | collective-permute-start | bytes 1572872 | tf_op jit(solution)/shard_map/ppermute | solution.py:384
  11.3 16.1 %collective-permute-start.4 = (bf16[1,4,4,64,128]{4,3,2,1,0:T(8,128)(2,1)}, bf16[1,4,4,64,128]{4,3,2,1,0:T(8,128)(2,1)S(1)}, u32[]{:S(2)}, u32[]{:S(2)}) collective-permute-start(bf16[1,4,4,64,128]{4,3,2,1,0:T(8,128)(2,1)} %bitcast.10), channel_id=1, source_target_pairs={{0,8},{4,12},{8,0},{12,4},{16,24},{20,28},{24,16},{28,20},{1,9},{5... | collective-permute-start | bytes 786440 | tf_op jit(solution)/shard_map/ppermute | solution.py:377
  12.5 14.9 %collective-permute-start.5 = (bf16[1,4,4,64,128]{4,3,2,1,0:T(8,128)(2,1)}, bf16[1,4,4,64,128]{4,3,2,1,0:T(8,128)(2,1)S(1)}, u32[]{:S(2)}, u32[]{:S(2)}) collective-permute-start(bf16[1,4,4,64,128]{4,3,2,1,0:T(8,128)(2,1)} %bitcast.11), channel_id=1, source_target_pairs={{0,16},{4,20},{8,24},{12,28},{16,0},{20,4},{24,8},{28,12},{1,17},{... | collective-permute-start | bytes 786440 | tf_op jit(solution)/shard_map/ppermute | solution.py:377
  12.5 14.8 %collective-permute-start.6 = (bf16[1,4,4,64,128]{4,3,2,1,0:T(8,128)(2,1)}, bf16[1,4,4,64,128]{4,3,2,1,0:T(8,128)(2,1)S(1)}, u32[]{:S(2)}, u32[]{:S(2)}) collective-permute-start(bf16[1,4,4,64,128]{4,3,2,1,0:T(8,128)(2,1)} %bitcast.12), channel_id=1, source_target_pairs={{0,24},{4,28},{8,16},{12,20},{16,8},{20,12},{24,0},{28,4},{1,25},{... | collective-permute-start | bytes 786440 | tf_op jit(solution)/shard_map/ppermute | solution.py:377
  27.3 10.8 %copy-start.1 = (bf16[1,4,4,64,128]{4,3,2,1,0:T(8,128)(2,1)}, bf16[1,4,4,64,128]{4,3,2,1,0:T(8,128)(2,1)S(1)}, u32[]{:S(2)}) copy-start(bf16[1,4,4,64,128]{4,3,2,1,0:T(8,128)(2,1)S(1)} %collective-permute-done.4.refs_1_) | copy-start | bytes 786436
  27.4 10.8 %copy-start.2 = (bf16[1,4,4,64,128]{4,3,2,1,0:T(8,128)(2,1)}, bf16[1,4,4,64,128]{4,3,2,1,0:T(8,128)(2,1)S(1)}, u32[]{:S(2)}) copy-start(bf16[1,4,4,64,128]{4,3,2,1,0:T(8,128)(2,1)S(1)} %collective-permute-done.5.refs_2_) | copy-start | bytes 786436
  27.4 10.8 %copy-start.3 = (bf16[1,4,4,64,128]{4,3,2,1,0:T(8,128)(2,1)}, bf16[1,4,4,64,128]{4,3,2,1,0:T(8,128)(2,1)S(1)}, u32[]{:S(2)}) copy-start(bf16[1,4,4,64,128]{4,3,2,1,0:T(8,128)(2,1)S(1)} %collective-permute-done.6.refs_3_) | copy-start | bytes 786436
  28.7 9.5 %collective-permute-start.7 = (bf16[4,4,4,64,128]{4,3,2,1,0:T(8,128)(2,1)S(1)}, bf16[4,4,4,64,128]{4,3,2,1,0:T(8,128)(2,1)}, u32[]{:S(2)}, u32[]{:S(2)}) collective-permute-start(bf16[4,4,4,64,128]{4,3,2,1,0:T(8,128)(2,1)S(1)} %pad_maximum_fusion), channel_id=1, source_target_pairs={{0,4},{4,0},{8,12},{12,8},{16,20},{20,16},{24,28},{28,24},{1,5},{5... | collective-permute-start | bytes 3145736 | tf_op jit(solution)/shard_map/ppermute | solution.py:377
  29.7 14.0 %collective-permute-start.2 = (bf16[2,2,512,128]{3,2,1,0:T(8,128)(2,1)}, bf16[2,2,512,128]{3,2,1,0:T(8,128)(2,1)}, u32[]{:S(2)}, u32[]{:S(2)}) collective-permute-start(bf16[2,2,512,128]{3,2,1,0:T(8,128)(2,1)} %get-tuple-element.36), channel_id=1, source_target_pairs={{0,4},{4,0},{8,12},{12,8},{16,20},{20,16},{24,28},{28,24},{1,5},{5... | collective-permute-start | bytes 1572872 | tf_op jit(solution)/shard_map/ppermute | solution.py:377
  29.8 20.5 %collective-permute-start.3 = (bf16[2,2,512,128]{3,2,1,0:T(8,128)(2,1)}, bf16[2,2,512,128]{3,2,1,0:T(8,128)(2,1)}, u32[]{:S(2)}, u32[]{:S(2)}) collective-permute-start(bf16[2,2,512,128]{3,2,1,0:T(8,128)(2,1)} %get-tuple-element.36), channel_id=1, source_target_pairs={{4,8},{12,16},{20,24},{8,4},{16,12},{24,20},{5,9},{13,17},{21,25},... | collective-permute-start | bytes 1572872 | tf_op jit(solution)/shard_map/ppermute | solution.py:384
  50.3 21.1 %all-to-all-start = ((f32[8,4,8,256]{3,2,1,0:T(8,128)}), f32[8,4,8,256]{3,2,1,0:T(8,128)S(1)}, u32[]{:S(2)}, u32[]{:S(2)}) async-start(f32[8,4,8,256]{3,2,1,0:T(8,128)} %get-tuple-element.45), calls=%async_computation | async-start | bytes 524288 | tf_op jit(solution)/shard_map/all_to_all | solution.py:459
  53.7 21.9 %collective-permute-start.8 = (bf16[2,4,512,128]{3,2,1,0:T(8,128)(2,1)}, bf16[2,4,512,128]{3,2,1,0:T(8,128)(2,1)}, u32[]{:S(2)}, u32[]{:S(2)}) collective-permute-start(bf16[2,4,512,128]{3,2,1,0:T(8,128)(2,1)} %get-tuple-element.46.qd), channel_id=1, source_target_pairs={{0,4},{4,0},{8,12},{12,8},{16,20},{20,16},{24,28},{28,24},{1,5},{5... | collective-permute-start | bytes 3145736 | tf_op jit(solution)/shard_map/ppermute | solution.py:377
  53.8 27.3 %collective-permute-start.9 = (bf16[2,4,512,128]{3,2,1,0:T(8,128)(2,1)}, bf16[2,4,512,128]{3,2,1,0:T(8,128)(2,1)}, u32[]{:S(2)}, u32[]{:S(2)}) collective-permute-start(bf16[2,4,512,128]{3,2,1,0:T(8,128)(2,1)} %get-tuple-element.46.qd), channel_id=1, source_target_pairs={{4,8},{12,16},{20,24},{8,4},{16,12},{24,20},{5,9},{13,17},{21,25},... | collective-permute-start | bytes 3145736 | tf_op jit(solution)/shard_map/ppermute | solution.py:384
  71.4 9.7 %copy-start = (f32[8,4,8,256]{3,2,1,0:T(8,128)}, f32[8,4,8,256]{3,2,1,0:T(8,128)S(1)}, u32[]{:S(2)}) copy-start(f32[8,4,8,256]{3,2,1,0:T(8,128)S(1)} %all-to-all-done.stats) | copy-start | bytes 786436
  71.4 16.3 %all-to-all-start.2 = ((bf16[8,2,4,64,128]{4,3,2,1,0:T(8,128)(2,1)}), bf16[8,2,4,64,128]{4,3,2,1,0:T(8,128)(2,1)}, u32[]{:S(2)}, u32[]{:S(2)}) async-start(bf16[8,2,4,64,128]{4,3,2,1,0:T(8,128)(2,1)} %get-tuple-element.50), calls=%async_computation.2 | async-start | bytes 2097152 | tf_op jit(solution)/shard_map/all_to_all | solution.py:515
  87.7 8.8 %copy-start.6 = (f32[4,2,512]{2,1,0:T(2,128)S(1)}, f32[4,2,512]{2,1,0:T(2,128)}, u32[]{:S(2)}) copy-start(f32[4,2,512]{2,1,0:T(2,128)} %get-tuple-element.52) | copy-start | bytes 49156
  87.7 31.2 %all-to-all-start.1 = ((bf16[8,2,4,64,128]{4,3,2,1,0:T(8,128)(2,1)}), bf16[8,2,4,64,128]{4,3,2,1,0:T(8,128)(2,1)}, u32[]{:S(2)}, u32[]{:S(2)}) async-start(bf16[8,2,4,64,128]{4,3,2,1,0:T(8,128)(2,1)} %get-tuple-element.49), calls=%async_computation.1 | async-start | bytes 2097152 | tf_op jit(solution)/shard_map/all_to_all | solution.py:514
  96.5 3.7 %collective-permute-start.10 = (f32[4,2,512]{2,1,0:T(2,128)S(1)}, f32[4,2,512]{2,1,0:T(2,128)S(1)}, u32[]{:S(2)}, u32[]{:S(2)}) collective-permute-start(f32[4,2,512]{2,1,0:T(2,128)S(1)} %copy-done.6), channel_id=1, source_target_pairs={{0,4},{4,0},{8,12},{12,8},{16,20},{20,16},{24,28},{28,24},{1,5},{5... | collective-permute-start | bytes 49160 | tf_op jit(solution)/shard_map/ppermute | solution.py:377
  96.6 14.5 %collective-permute-start.11 = (f32[4,2,512]{2,1,0:T(2,128)S(1)}, f32[4,2,512]{2,1,0:T(2,128)S(1)}, u32[]{:S(2)}, u32[]{:S(2)}) collective-permute-start(f32[4,2,512]{2,1,0:T(2,128)S(1)} %copy-done.6), channel_id=1, source_target_pairs={{4,8},{12,16},{20,24},{8,4},{16,12},{24,20},{5,9},{13,17},{21,25},... | collective-permute-start | bytes 49160 | tf_op jit(solution)/shard_map/ppermute | solution.py:384
  100.2 10.9 %copy-start.4 = (f32[4,2,512]{2,1,0:T(2,128)}, f32[4,2,512]{2,1,0:T(2,128)S(1)}, u32[]{:S(2)}) copy-start(f32[4,2,512]{2,1,0:T(2,128)S(1)} %collective-permute-done.10.log_near) | copy-start | bytes 49156
  111.1 0.6 copy-start.5

commit v2 on v1

--- a/solution.py
+++ b/solution.py
@@ -119,9 +119,7 @@
     for number, relative in enumerate(order):
         owner = jnp.where(part == number, me ^ relative, owner)
     compact[...] = owner_map(column, owner, toks, slots, compact.shape)
-    owner = iota((1, compact.shape[1]), 1) // slots
-    hot = owner_map(column, owner, toks, slots, compact.shape)
-    expand[...] = hot.astype(F32).T.astype(BF)
+    expand[...] = compact[...].astype(F32).T.astype(BF)
 
 
 def stats_kernel(scale2, compact, *refs):
@@ -152,17 +150,23 @@
     return jnp.where(rows <= columns if low else rows >= columns, scores, NEG)
 
 
-def put_in_slots(expand, tables, sums):
-    owners, kinds, _, slots, width = sums.shape
+def put_in_slots(expand, tables, kept, sent):
+    owners, kinds, _, slots, width = kept.shape
     spread = nn(expand, jnp.concatenate(tables, axis=1)).astype(BF)
-    for owner in range(owners):
+    for owner in range(2 * owners):
         for kind in range(kinds):
-            sums[owner, kind, 0] = spread[
+            (kept if owner < owners else sent)[owner % owners, kind, 0] = spread[
                 owner * slots : (owner + 1) * slots, kind * width : (kind + 1) * width
             ]
 
 
-def global_kernel(scale, scale2, kv, rows, stats, expand, before, dkv, ends):
+def fold_kernel(kept_ends, got_ends, kept_sums, got_sums, *outs):
+    for part, out in enumerate(outs):
+        out[0:2] = (kept_ends[part].astype(F32) + got_ends[part].astype(F32)).astype(BF)
+        out[2:4] = (kept_sums[part].astype(F32) + got_sums[part].astype(F32)).astype(BF)
+
+
+def global_kernel(scale, scale2, kv, rows, stats, expand, dkv, kept, sent):
     g_query, g_grad = rows[0, 0], rows[3, 0]
     tops = stats[:, 0, 0:1, :]
     top = jnp.max(tops, axis=0)
@@ -173,16 +177,17 @@
     weights = jnp.exp2(nt(kv[0, 0], g_query) * scale2 - g_log)
     narrow = weights.astype(BF)
     slopes = (weights * (nt(kv[1, 0], g_grad) - g_dot)).astype(BF)
-    dkv[0, 0] = before[0, 0] + nn(slopes, g_query) * scale
-    dkv[1, 0] = before[1, 0] + nn(narrow, g_grad)
+    dkv[0, 0] = nn(slopes, g_query) * scale
+    dkv[1, 0] = nn(narrow, g_grad)
     out = nn(kv[1, 0].T, narrow).T.astype(BF)
     dq = (nn(kv[0, 0].T, slopes) * scale).T.astype(BF)
-    put_in_slots(expand[...], (out, dq), ends)
+    put_in_slots(expand[...], (out, dq), kept, sent)
 
 
 def local_kernel(scale, scale2, halves, group, qd, kv, *refs):
     nears, fars, refs = refs[:halves], refs[halves : 2 * halves], refs[2 * halves :]
-    rows, bias, expand, out, log_dot, dq, dkv, sums, keys, values, score_buf, probs, slopes = refs
+    rows, bias, expand, before, out, log_dot, dq, dkv, kept, sent = refs[:-5]
+    keys, values, score_buf, probs, slopes = refs[-5:]
     toks = kv.shape[2]
     reach = 2 * HALF + TILE
     span = keys.shape[0] - rows.shape[2]
@@ -269,11 +274,11 @@
             attend(step - 1)
     own = slice(HALF, HALF + toks)
     grads = jnp.concatenate(scaled, axis=1)
-    dkv[0, 0] = (nt(query_t, slopes[own, :]) * scale).T
-    dkv[1, 0] = nt(grads, probs[own, :]).T
+    dkv[0, 0] = before[0, 0] + (nt(query_t, slopes[own, :]) * scale).T
+    dkv[1, 0] = before[1, 0] + nt(grads, probs[own, :]).T
     g_dk = (nt(query_t, slopes[span:, :]) * scale).T.astype(BF)
     g_dv = nt(grads, probs[span:, :]).T.astype(BF)
-    put_in_slots(expand[...], (g_dk, g_dv), sums)
+    put_in_slots(expand[...], (g_dk, g_dv), kept, sent)
 
 
 def rim_kernel(
@@ -312,18 +317,20 @@
 
 
 def final_kernel(
-    place, out, ends, sums, dq, dkv, attn, query_grad, key_grad, value_grad, wide_rows
+    sources, place, out, dq, dkv, *refs
 ):
+    parts, refs = refs[:sources], refs[sources:]
+    attn, query_grad, key_grad, value_grad, wide_rows = refs
     heads, toks = out.shape[0], out.shape[1]
     hot = place[...]
     is_global = jnp.sum(hot.astype(F32), axis=1, keepdims=True) > 0
     for head in range(heads):
         rows = pl.ds(head, toks, stride=heads)
         tables = []
-        for source, kind in ((ends, 0), (ends, 1), (sums, 0), (sums, 1)):
-            table = source[0, kind, head].astype(F32)
-            for device in range(1, source.shape[0]):
-                table = table + source[device, kind, head].astype(F32)
+        for kind in range(4):
+            table = parts[0][kind, head].astype(F32)
+            for part in parts[1:]:
+                table = table + part[kind, head].astype(F32)
             tables.append(table.astype(BF))
         width = out.shape[2]
         added = nn(hot, jnp.concatenate(tables, axis=1))
@@ -455,36 +462,52 @@
     )(compact, *held, kv)
 
     kv_done = (nears, fars)
-    stats = after(stats, kv_done)
     stats = lax.all_to_all(stats, "ctx", 0, 0, tiled=True)
-    qd_late = after(qd, (kv_done, rows))
+    qd_late = after(qd, (kv_done, stats))
     qd_far, qd_near = from_far(qd_late), from_near(qd_late)
+
+    sum_shape = (devices // 2, 2, heads, slots, width)
+    sum_struct = struct(sum_shape, BF)
+    extra, kept_ends, sent_ends = pl.pallas_call(
+        functools.partial(global_kernel, scale, scale2),
+        grid=(heads,),
+        in_specs=[per_head(pair_shape, 1), per_head(row_shape, 1)]
+        + [per_head(stats.shape, 1), whole(expand.shape)],
+        out_specs=(per_head(pair_shape, 1), per_head(sum_shape, 2), per_head(sum_shape, 2)),
+        out_shape=(struct(pair_shape, F32), sum_struct, sum_struct),
+        compiler_params=params(),
+        cost_estimate=cost(1e6, 1e6),
+        name="global_queries",
+    )(kv, rows, stats, expand)
+    got_ends = from_near(sent_ends)
 
     def half_head(part):
         return pl.BlockSpec(
             (2, 1, toks, width), lambda head: (0, jnp.clip(head - part * group, 0, group - 1), 0, 0)
         )
 
-    ends_shape = (devices, 2, heads, slots, width)
-    out, log_dot, dq, dkv, sums = pl.pallas_call(
+    out, log_dot, dq, dkv, kept_sums, sent_sums = pl.pallas_call(
         functools.partial(local_kernel, scale, scale2, halves, group),
         grid=(heads,),
         in_specs=[per_head(pair_shape, 1)] * 2
         + [half_head(part) for part in range(halves)] * 2
-        + [per_head(row_shape, 1), whole(bias.shape), whole(expand.shape)],
+        + [per_head(row_shape, 1), whole(bias.shape), whole(expand.shape)]
+        + [per_head(pair_shape, 1)],
         out_specs=(
             per_head((heads, toks, width), 0),
             per_head((heads, 2, toks), 0),
             per_head((heads, toks, width), 0),
             per_head(pair_shape, 1),
-            per_head(ends_shape, 2),
+            per_head(sum_shape, 2),
+            per_head(sum_shape, 2),
         ),
         out_shape=(
             struct((heads, toks, width), BF),
             struct((heads, 2, toks), F32),
             struct((heads, toks, width), F32),
             struct(pair_shape, F32),
-            struct(ends_shape, BF),
+            sum_struct,
+            sum_struct,
         ),
         scratch_shapes=[
             pltpu.VMEM((span + count, width), BF),
@@ -496,23 +519,26 @@
         compiler_params=params(),
         cost_estimate=cost(1e6, 1e6),
         name="local",
-    )(qd, kv, *nears, *fars, rows, bias, expand)
+    )(qd, kv, *nears, *fars, rows, bias, expand, extra)
     log_far, log_near = from_far(log_dot), from_near(log_dot)
 
-    dkv, ends = pl.pallas_call(
-        functools.partial(global_kernel, scale, scale2),
-        grid=(heads,),
-        in_specs=[per_head(pair_shape, 1), per_head(row_shape, 1)]
-        + [per_head(stats.shape, 1), whole(expand.shape), per_head(pair_shape, 1)],
-        out_specs=(per_head(pair_shape, 1), per_head(ends_shape, 2)),
-        out_shape=(struct(pair_shape, F32), struct(ends_shape, BF)),
-        input_output_aliases={4: 0},
-        compiler_params=params(),
-        cost_estimate=cost(1e6, 1e6),
-        name="global_queries",
-    )(kv, rows, after(stats, (qd_near, qd_far)), expand, dkv)
-    ends = lax.all_to_all(ends, "ctx", 0, 0, tiled=True)
-    sums = lax.all_to_all(sums, "ctx", 0, 0, tiled=True)
+    got_sums = from_near(sent_sums)
+    first = stages[0]
+    halos = (qd_near, qd_far, log_near, log_far)
+    parts = pl.pallas_call(
+        fold_kernel,
+        out_shape=[struct((4, heads, slots, width), BF)] * (devices // 2),
+        compiler_params=params(),
+        name="fold",
+    )(kept_ends, got_ends, kept_sums, after(got_sums, halos))
+    for stage in reversed(stages[1:-1]):
+        size = len(parts) // (len(stage) + 1)
+        kept = parts[:size]
+        for number, mask in enumerate(stage):
+            sent = parts[(number + 1) * size : (number + 2) * size]
+            kept = [one + swap(other, mask) for one, other in zip(kept, sent)]
+        parts = kept
+    parts = [parts[0]] + [swap(part, mask) for part, mask in zip(parts[1:], first)]
 
     dkv = pl.pallas_call(
         functools.partial(rim_kernel, scale, scale2),
@@ -538,22 +564,21 @@
     flat_shape = (toks * heads, width)
     steps = 2
     outs = pl.pallas_call(
-        final_kernel,
+        functools.partial(final_kernel, len(parts)),
         grid=(steps,),
         in_specs=[
             pl.BlockSpec((toks // steps, slots), lambda i: (i, 0)),
             pl.BlockSpec((heads, toks // steps, width), lambda i: (0, i, 0)),
-            whole(ends_shape),
-            whole(ends_shape),
             pl.BlockSpec((heads, toks // steps, width), lambda i: (0, i, 0)),
             pl.BlockSpec((2, heads, toks // steps, width), lambda i: (0, 0, i, 0)),
-        ],
+        ]
+        + [whole((4, heads, slots, width))] * len(parts),
         out_specs=[pl.BlockSpec((toks * heads // steps, width), lambda i: (i, 0))] * 4,
         out_shape=[struct(flat_shape, kind) for kind in (BF, F32, F32, F32)],
         scratch_shapes=[pltpu.VMEM((toks * heads // steps, width), F32)],
         compiler_params=params(),
         name="final",
-    )(place, out, ends, sums, dq, dkv)
+    )(place, out, dq, dkv, *parts)
     return tuple(x.reshape(toks, heads, width) for x in outs)
 
 

time: 125 us -> 111 us (0.89)
  waiting for transfers between devices: 33.9 us -> 25.2 us
  starting transfers between devices: 39.8 us -> 32 us
  Pallas kernels: 47.2 us -> 48.7 us
    ppermute x4, waiting for transfers between devices: 22.9 us -> 5.66 us  [from_far(): return lax.ppermute(value, 'ctx', pairs + [(j, i) for i, j in pairs])]
    all_to_all x2 -> x0, starting transfers between devices: 13 us -> none  [the longest x1 8.8 us: shards(): ends = lax.all_to_all(ends, 'ctx', 0, 0, tiled=True)]
    ppermute x8 -> x13, waiting for transfers between devices: 10.9 us -> 18.5 us  [swap(): return lax.ppermute(value, 'ctx', [(i, i ^ mask) for i in range(devices)])]
    ppermute x8 -> x13, starting transfers between devices: 3.96 us -> 9.49 us  [swap(): return lax.ppermute(value, 'ctx', [(i, i ^ mask) for i in range(devices)])]
    pallas_call x1 -> x2, Pallas kernels: 4.69 us -> 6.7 us  [the longest x1 4.17 us: shards(): pl.pallas_call(functools.partial(final_kernel, len(parts)), grid=(steps,)...]
  transfers between devices with their start and end apart: 15 -> 18, of which waited for: 4 -> 6; matrix products, arithmetic and copies ran while one was open for 1% -> 1% of each run, Pallas kernels for 32% -> 36%
where the time goes in v2:
time: 111 us; the launch traced here: 110 us
  Pallas kernels  48.7 us (44%)
  starting transfers between devices  32 us (29%)
  waiting for transfers between devices  25.2 us (23%)
  local copies, waits for them, and re-layouts  1.56 us (1%)
  other arithmetic  1.29 us (1%)
    ppermute x4, starting transfers between devices, from_far(): return lax.ppermute(value, 'ctx', pairs + [(j, i) for i, j in pairs])  19.1 us
    ppermute x13, waiting for transfers between devices, swap(): return lax.ppermute(value, 'ctx', [(i, i ^ mask) for i in range(devices)])  18.5 us
    pallas_call x1, Pallas kernels, shards(): pl.pallas_call(functools.partial(local_kernel, scale, scale2, halves, gro...  14.7 us
    ppermute x13, starting transfers between devices, swap(): return lax.ppermute(value, 'ctx', [(i, i ^ mask) for i in range(devices)])  9.49 us
    pallas_call x1, Pallas kernels, shards(): pl.pallas_call(functools.partial(rim_kernel, scale, scale2), grid=(heads,...  7.16 us
    pallas_call x1, Pallas kernels, shards(): pl.pallas_call(functools.partial(global_kernel, scale, scale2), grid=(hea...  6.22 us
    ppermute x4, waiting for transfers between devices, from_far(): return lax.ppermute(value, 'ctx', pairs + [(j, i) for i, j in pairs])  5.66 us
    pallas_call x1, Pallas kernels, shards(): pl.pallas_call(functools.partial(stats_kernel, scale2), grid=(heads,), in...  5.51 us
  transfers between devices with their start and end apart: 18, of which 6 were waited for; matrix products, arithmetic and copies ran while one was open for 1% of the time, Pallas kernels for 36%

profile of v2, /device:TPU:1, one launch (start us, length us, event | category | flops | bytes accessed | tf_op | source)
XLA Modules:
  0.0 109.6 jit_solution(1855991540306350931)
XLA Ops:
  0.6 2.7 %pack_keys.1 = (bf16[2,4,512,128]{3,2,1,0:T(8,128)(2,1)}, bf16[2,2,512,128]{3,2,1,0:T(8,128)(2,1)}, bf16[2,2,512,128]{3,2,1,0:T(8,128)(2,1)}) custom-call(bf16[2048,128]{1,0:T(8,128)(2,1)} %bitcast.15, bf16[2048,128]{1,0:T(8,128)(2,1)} %bitcast.16), custom_call_target="tpu_custom_call" | custom-call | tf_op jit(solution)/shard_map/pack_keys/pallas_call | solution.py:405
  3.3 0.1 collective-permute-start
  3.4 4.4 %collective-permute-start.1 = (bf16[2,2,512,128]{3,2,1,0:T(8,128)(2,1)}, bf16[2,2,512,128]{3,2,1,0:T(8,128)(2,1)}, u32[]{:S(2)}, u32[]{:S(2)}) collective-permute-start(bf16[2,2,512,128]{3,2,1,0:T(8,128)(2,1)} %get-tuple-element.39), channel_id=1, source_target_pairs={{4,8},{12,16},{20,24},{8,4},{16,12},{24,20},{5,9},{13,17},{21,25},... | collective-permute-start | bytes 1572872 | tf_op jit(solution)/shard_map/ppermute | solution.py:391
  7.9 3.4 %pack_queries.1 = (bf16[2,4,512,128]{3,2,1,0:T(8,128)(2,1)}, bf16[4,4,64,128]{3,2,1,0:T(8,128)(2,1)}) custom-call(bf16[2048,128]{1,0:T(8,128)(2,1)} %bitcast.17, bf16[2048,128]{1,0:T(8,128)(2,1)} %bitcast.18, bf16[2,4,512,128]{3,2,1,0:T(8,128)(2,1)} %get-tuple-element.37.kv.refs_5_, s32[1,256]{1,0:T(1,128)} %bitcast.19), custom_call_target="tpu_custom_call" | custom-call | tf_op jit(solution)/shard_map/pack_queries/pallas_call | solution.py:413
  11.3 1.2 %collective-permute-start.4 = (bf16[1,4,4,64,128]{4,3,2,1,0:T(8,128)(2,1)}, bf16[1,4,4,64,128]{4,3,2,1,0:T(8,128)(2,1)S(1)}, u32[]{:S(2)}, u32[]{:S(2)}) collective-permute-start(bf16[1,4,4,64,128]{4,3,2,1,0:T(8,128)(2,1)} %bitcast.10), channel_id=1, source_target_pairs={{0,8},{4,12},{8,0},{12,4},{16,24},{20,28},{24,16},{28,20},{1,9},{5... | collective-permute-start | bytes 786440 | tf_op jit(solution)/shard_map/ppermute | solution.py:384
  12.5 0.0 collective-permute-start.5
  12.5 1.4 %collective-permute-start.6 = (bf16[1,4,4,64,128]{4,3,2,1,0:T(8,128)(2,1)}, bf16[1,4,4,64,128]{4,3,2,1,0:T(8,128)(2,1)S(1)}, u32[]{:S(2)}, u32[]{:S(2)}) collective-permute-start(bf16[1,4,4,64,128]{4,3,2,1,0:T(8,128)(2,1)} %bitcast.12), channel_id=1, source_target_pairs={{0,24},{4,28},{8,16},{12,20},{16,8},{20,12},{24,0},{28,4},{1,25},{... | collective-permute-start | bytes 786440 | tf_op jit(solution)/shard_map/ppermute | solution.py:384
  13.9 2.3 %masks.1 = (f32[1536,128]{1,0:T(8,128)}, bf16[256,512]{1,0:T(8,128)(2,1)}, bf16[512,256]{1,0:T(8,128)(2,1)}, bf16[512,64]{1,0:T(8,128)(2,1)}) custom-call(s32[1,256]{1,0:T(1,128)} %bitcast.20), custom_call_target="tpu_custom_call" | custom-call | tf_op jit(solution)/shard_map/masks/pallas_call | solution.py:425
  16.2 11.2 %collective-permute-done.4.refs_1_ = bf16[1,4,4,64,128]{4,3,2,1,0:T(8,128)(2,1)S(1)} collective-permute-done((bf16[1,4,4,64,128]{4,3,2,1,0:T(8,128)(2,1)}, bf16[1,4,4,64,128]{4,3,2,1,0:T(8,128)(2,1)S(1)}, u32[]{:S(2)}, u32[]{:S(2)}) %collective-permute-start.4) | collective-permute-done | bytes 262176 | tf_op jit(solution)/shard_map/ppermute | solution.py:384
  27.3 0.0 collective-permute-done.5.refs_2_
  27.3 0.0 collective-permute-done.6.refs_3_
  27.4 1.3 %pad_maximum_fusion = bf16[4,4,4,64,128]{4,3,2,1,0:T(8,128)(2,1)S(1)} fusion(bf16[1,4,4,64,128]{4,3,2,1,0:T(8,128)(2,1)S(1)} %collective-permute-done.6.refs_3_, bf16[1,4,4,64,128]{4,3,2,1,0:T(8,128)(2,1)S(1)} %collective-permute-done.5.refs_2_, bf16[1,4,4,64,128]{4,3,2,1,0:T(8,128)(2,1)S(1)} %collective-permute-done.4.refs_1_, ...), kind=kLoop, calls=%fused_computation | loop fusion | flops 1572864 | bytes 2097152 | tf_op jit(solution)/shard_map/concatenate | solution.py:445
  28.7 0.0 collective-permute-done.refs_0_
  28.7 0.0 collective-permute-done.1.refs_2_
  28.7 1.0 collective-permute-start.7
  29.7 0.1 collective-permute-start.2
  29.8 8.4 %collective-permute-start.3 = (bf16[2,2,512,128]{3,2,1,0:T(8,128)(2,1)}, bf16[2,2,512,128]{3,2,1,0:T(8,128)(2,1)}, u32[]{:S(2)}, u32[]{:S(2)}) collective-permute-start(bf16[2,2,512,128]{3,2,1,0:T(8,128)(2,1)} %get-tuple-element.41), channel_id=1, source_target_pairs={{4,8},{12,16},{20,24},{8,4},{16,12},{24,20},{5,9},{13,17},{21,25},... | collective-permute-start | bytes 1572872 | tf_op jit(solution)/shard_map/ppermute | solution.py:391
  38.1 0.0 collective-permute-done.7.refs_4_
  38.2 5.5 %global_stats.1 = (bf16[4,4,256,128]{3,2,1,0:T(8,128)(2,1)}, f32[8,4,8,256]{3,2,1,0:T(8,128)}) custom-call(bf16[256,512]{1,0:T(8,128)(2,1)} %get-tuple-element.42.compact, bf16[1,4,4,64,128]{4,3,2,1,0:T(8,128)(2,1)} %bitcast.14, bf16[1,4,4,64,128]{4,3,2,1,0:T(8,128)(2,1)} %copy-done.1, bf16[1,4,4,64,128]{4,3,2,1,0:T(8,128)(2,1)} %copy-done.2, ...), custom_call_target="tpu_custom_call" | custom-call | flops 1000000 | bytes 1000000 | tf_op jit(solution)/shard_map/global_stats/pallas_call | solution.py:451
  43.7 3.4 %all-to-all-start = ((f32[8,4,8,256]{3,2,1,0:T(8,128)}), f32[8,4,8,256]{3,2,1,0:T(8,128)S(1)}, u32[]{:S(2)}, u32[]{:S(2)}) async-start(f32[8,4,8,256]{3,2,1,0:T(8,128)} %get-tuple-element.48), calls=%async_computation | async-start | bytes 524288 | tf_op jit(solution)/shard_map/all_to_all | solution.py:465
  47.1 0.0 collective-permute-done.2.refs_1_
  47.1 3.9 %collective-permute-done.3.refs_3_ = bf16[2,2,512,128]{3,2,1,0:T(8,128)(2,1)} collective-permute-done((bf16[2,2,512,128]{3,2,1,0:T(8,128)(2,1)}, bf16[2,2,512,128]{3,2,1,0:T(8,128)(2,1)}, u32[]{:S(2)}, u32[]{:S(2)}) %collective-permute-start.3) | collective-permute-done | bytes 524320 | tf_op jit(solution)/shard_map/ppermute | solution.py:391
  51.0 1.1 %all-to-all-done.stats = f32[8,4,8,256]{3,2,1,0:T(8,128)S(1)} async-done(((f32[8,4,8,256]{3,2,1,0:T(8,128)}), f32[8,4,8,256]{3,2,1,0:T(8,128)S(1)}, u32[]{:S(2)}, u32[]{:S(2)}) %all-to-all-start) | async-done | bytes 262176 | tf_op jit(solution)/shard_map/all_to_all | solution.py:465
  52.1 1.3 %collective-permute-start.8 = (bf16[2,4,512,128]{3,2,1,0:T(8,128)(2,1)}, bf16[2,4,512,128]{3,2,1,0:T(8,128)(2,1)}, u32[]{:S(2)}, u32[]{:S(2)}) collective-permute-start(bf16[2,4,512,128]{3,2,1,0:T(8,128)(2,1)} %get-tuple-element.52.qd), channel_id=1, source_target_pairs={{0,4},{4,0},{8,12},{12,8},{16,20},{20,16},{24,28},{28,24},{1,5},{5... | collective-permute-start | bytes 3145736 | tf_op jit(solution)/shard_map/ppermute | solution.py:384
  53.5 2.1 %collective-permute-start.9 = (bf16[2,4,512,128]{3,2,1,0:T(8,128)(2,1)}, bf16[2,4,512,128]{3,2,1,0:T(8,128)(2,1)}, u32[]{:S(2)}, u32[]{:S(2)}) collective-permute-start(bf16[2,4,512,128]{3,2,1,0:T(8,128)(2,1)} %get-tuple-element.52.qd), channel_id=1, source_target_pairs={{4,8},{12,16},{20,24},{8,4},{16,12},{24,20},{5,9},{13,17},{21,25},... | collective-permute-start | bytes 3145736 | tf_op jit(solution)/shard_map/ppermute | solution.py:391
  55.5 6.2 %global_queries.1 = (f32[2,4,512,128]{3,2,1,0:T(8,128)}, bf16[4,2,4,64,128]{4,3,2,1,0:T(8,128)(2,1)}, bf16[4,2,4,64,128]{4,3,2,1,0:T(8,128)(2,1)}) custom-call(bf16[2,4,512,128]{3,2,1,0:T(8,128)(2,1)} %get-tuple-element.37.kv.refs_5_, bf16[4,4,256,128]{3,2,1,0:T(8,128)(2,1)} %get-tuple-element.45.rows.refs_4_, f32[8,4,8,256]{3,2,1,0:T(8,128)} %copy-done, ...), custom_call_target="tpu_custom_call" | custom-call | flops 1000000 | bytes 1000000 | tf_op jit(solution)/shard_map/global_queries/pallas_call | solution.py:471
  61.8 14.7 %local.1 = (bf16[4,512,128]{2,1,0:T(8,128)(2,1)}, f32[4,2,512]{2,1,0:T(2,128)}, f32[4,512,128]{2,1,0:T(8,128)}, f32[2,4,512,128]{3,2,1,0:T(8,128)}, bf16[4,2,4,6...) custom-call(bf16[2,4,512,128]{3,2,1,0:T(8,128)(2,1)} %get-tuple-element.52.qd, ...), custom_call_target="tpu_custom_call" | custom-call | flops 1000000 | bytes 1000000 | tf_op jit(solution)/shard_map/local/pallas_call | solution.py:489
  76.5 0.1 collective-permute-start.13
  76.6 0.5 collective-permute-start.12
  77.1 0.1 collective-permute-start.10
  77.2 1.6 %collective-permute-done.10.log_near = f32[4,2,512]{2,1,0:T(2,128)S(1)} collective-permute-done((f32[4,2,512]{2,1,0:T(2,128)}, f32[4,2,512]{2,1,0:T(2,128)S(1)}, u32[]{:S(2)}, u32[]{:S(2)}) %collective-permute-start.10) | collective-permute-done | bytes 16416 | tf_op jit(solution)/shard_map/ppermute | solution.py:384
  78.8 4.3 %collective-permute-start.11 = (f32[4,2,512]{2,1,0:T(2,128)}, f32[4,2,512]{2,1,0:T(2,128)S(1)}, u32[]{:S(2)}, u32[]{:S(2)}) collective-permute-start(f32[4,2,512]{2,1,0:T(2,128)} %get-tuple-element.53), channel_id=1, source_target_pairs={{4,8},{12,16},{20,24},{8,4},{16,12},{24,20},{5,9},{13,17},{21,25},... | collective-permute-start | bytes 49160 | tf_op jit(solution)/shard_map/ppermute | solution.py:391
  83.0 1.7 %collective-permute-done.11.log_far = f32[4,2,512]{2,1,0:T(2,128)S(1)} collective-permute-done((f32[4,2,512]{2,1,0:T(2,128)}, f32[4,2,512]{2,1,0:T(2,128)S(1)}, u32[]{:S(2)}, u32[]{:S(2)}) %collective-permute-start.11) | collective-permute-done | bytes 16416 | tf_op jit(solution)/shard_map/ppermute | solution.py:391
  84.7 0.0 collective-permute-done.13.got_sums
  84.7 0.0 collective-permute-done.8.qd_near
  84.7 0.0 collective-permute-done.9.qd_far
  84.8 0.0 collective-permute-done.12.got_ends
  84.8 0.8 copy-done.4
  85.5 2.5 %fold.1 = (bf16[4,4,64,128]{3,2,1,0:T(8,128)(2,1)}, bf16[4,4,64,128]{3,2,1,0:T(8,128)(2,1)}, bf16[4,4,64,128]{3,2,1,0:T(8,128)(2,1)}, bf16[4,4,64,128]{3,2,1,0:T(8,128)(2,1)}) custom-call(bf16[4,2,4,64,128]{4,3,2,1,0:T(8,128)(2,1)} %get-tuple-element.55.kept_ends, bf16[4,2,4,64,128]{4,3,2,1,0:T(8,128)(2,1)} %collective-permute-done.12.got_ends, ...), custom_call_target="tpu_custom_call" | custom-call | tf_op jit(solution)/shard_map/fold/pallas_call | solution.py:528
  88.1 2.5 %collective-permute-start.14 = (bf16[4,4,64,128]{3,2,1,0:T(8,128)(2,1)}, bf16[4,4,64,128]{3,2,1,0:T(8,128)(2,1)S(1)}, u32[]{:S(2)}, u32[]{:S(2)}) collective-permute-start(bf16[4,4,64,128]{3,2,1,0:T(8,128)(2,1)} %get-tuple-element.61), channel_id=1, source_target_pairs={{0,8},{4,12},{8,0},{12,4},{16,24},{20,28},{24,16},{28,20},{1,9},{5... | collective-permute-start | bytes 786440 | tf_op jit(solution)/shard_map/ppermute | solution.py:384
  90.6 0.0 collective-permute-start.15
  90.6 1.2 %collective-permute-start.16 = (bf16[4,4,64,128]{3,2,1,0:T(8,128)(2,1)}, bf16[4,4,64,128]{3,2,1,0:T(8,128)(2,1)S(1)}, u32[]{:S(2)}, u32[]{:S(2)}) collective-permute-start(bf16[4,4,64,128]{3,2,1,0:T(8,128)(2,1)} %get-tuple-element.63), channel_id=1, source_target_pairs={{0,24},{4,28},{8,16},{12,20},{16,8},{20,12},{24,0},{28,4},{1,25},{... | collective-permute-start | bytes 786440 | tf_op jit(solution)/shard_map/ppermute | solution.py:384
  91.8 7.2 %rim.1.dkv = f32[2,4,512,128]{3,2,1,0:T(8,128)} custom-call(bf16[2,4,512,128]{3,2,1,0:T(8,128)(2,1)} %get-tuple-element.37.kv.refs_5_, f32[1536,128]{1,0:T(8,128)} %get-tuple-element.46.refs_5_.bias, bf16[2,4,512,128]{3,2,1,0:T(8,128)(2,1)} %collective-permute-done.8.qd_near, bf16[2,4,512,128]{3,2,1,0:T(8,128)(2,1)} %collective-permute-done.9.qd_far, ...), custom_call_target="tpu_custom_call" | custom-call | flops 1000000 | bytes 1000000 | tf_op jit(solution)/shard_map/rim/pallas_call | solution.py:543
  98.9 0.0 collective-permute-done.14.refs_1_
  99.0 5.7 %collective-permute-done.15.refs_2_ = bf16[4,4,64,128]{3,2,1,0:T(8,128)(2,1)S(1)} collective-permute-done((bf16[4,4,64,128]{3,2,1,0:T(8,128)(2,1)}, bf16[4,4,64,128]{3,2,1,0:T(8,128)(2,1)S(1)}, u32[]{:S(2)}, u32[]{:S(2)}) %collective-permute-start.15) | collective-permute-done | bytes 262176 | tf_op jit(solution)/shard_map/ppermute | solution.py:384
  104.7 0.7 copy-done.6
  105.4 0.1 copy-done.7
  105.5 4.2 %final.1 = (bf16[2048,128]{1,0:T(8,128)(2,1)}, f32[2048,128]{1,0:T(8,128)}, f32[2048,128]{1,0:T(8,128)}, f32[2048,128]{1,0:T(8,128)}) custom-call(bf16[512,64]{1,0:T(8,128)(2,1)} %get-tuple-element.36.place, bf16[4,512,128]{2,1,0:T(8,128)(2,1)} %get-tuple-element.50.out, f32[4,512,128]{2,1,0:T(8,128)} %get-tuple-element.51.dq, f32[2,4,512,128]{3,2,1,0:T(8,128)} %rim.1.dkv, ...), custom_call_target="tpu_custom_call" | custom-call | tf_op jit(solution)/shard_map/final/pallas_call | solution.py:566
  (18 shorter events, 0.0 us)
Async XLA Ops:
  3.3 25.3 %collective-permute-start = (bf16[2,2,512,128]{3,2,1,0:T(8,128)(2,1)}, bf16[2,2,512,128]{3,2,1,0:T(8,128)(2,1)}, u32[]{:S(2)}, u32[]{:S(2)}) collective-permute-start(bf16[2,2,512,128]{3,2,1,0:T(8,128)(2,1)} %get-tuple-element.39), channel_id=1, source_target_pairs={{0,4},{4,0},{8,12},{12,8},{16,20},{20,16},{24,28},{28,24},{1,5},{5... | collective-permute-start | bytes 1572872 | tf_op jit(solution)/shard_map/ppermute | solution.py:384
  3.4 25.3 %collective-permute-start.1 = (bf16[2,2,512,128]{3,2,1,0:T(8,128)(2,1)}, bf16[2,2,512,128]{3,2,1,0:T(8,128)(2,1)}, u32[]{:S(2)}, u32[]{:S(2)}) collective-permute-start(bf16[2,2,512,128]{3,2,1,0:T(8,128)(2,1)} %get-tuple-element.39), channel_id=1, source_target_pairs={{4,8},{12,16},{20,24},{8,4},{16,12},{24,20},{5,9},{13,17},{21,25},... | collective-permute-start | bytes 1572872 | tf_op jit(solution)/shard_map/ppermute | solution.py:391
  11.3 16.1 %collective-permute-start.4 = (bf16[1,4,4,64,128]{4,3,2,1,0:T(8,128)(2,1)}, bf16[1,4,4,64,128]{4,3,2,1,0:T(8,128)(2,1)S(1)}, u32[]{:S(2)}, u32[]{:S(2)}) collective-permute-start(bf16[1,4,4,64,128]{4,3,2,1,0:T(8,128)(2,1)} %bitcast.10), channel_id=1, source_target_pairs={{0,8},{4,12},{8,0},{12,4},{16,24},{20,28},{24,16},{28,20},{1,9},{5... | collective-permute-start | bytes 786440 | tf_op jit(solution)/shard_map/ppermute | solution.py:384
  12.5 14.8 %collective-permute-start.5 = (bf16[1,4,4,64,128]{4,3,2,1,0:T(8,128)(2,1)}, bf16[1,4,4,64,128]{4,3,2,1,0:T(8,128)(2,1)S(1)}, u32[]{:S(2)}, u32[]{:S(2)}) collective-permute-start(bf16[1,4,4,64,128]{4,3,2,1,0:T(8,128)(2,1)} %bitcast.11), channel_id=1, source_target_pairs={{0,16},{4,20},{8,24},{12,28},{16,0},{20,4},{24,8},{28,12},{1,17},{... | collective-permute-start | bytes 786440 | tf_op jit(solution)/shard_map/ppermute | solution.py:384
  12.5 14.8 %collective-permute-start.6 = (bf16[1,4,4,64,128]{4,3,2,1,0:T(8,128)(2,1)}, bf16[1,4,4,64,128]{4,3,2,1,0:T(8,128)(2,1)S(1)}, u32[]{:S(2)}, u32[]{:S(2)}) collective-permute-start(bf16[1,4,4,64,128]{4,3,2,1,0:T(8,128)(2,1)} %bitcast.12), channel_id=1, source_target_pairs={{0,24},{4,28},{8,16},{12,20},{16,8},{20,12},{24,0},{28,4},{1,25},{... | collective-permute-start | bytes 786440 | tf_op jit(solution)/shard_map/ppermute | solution.py:384
  27.3 10.8 %copy-start.1 = (bf16[1,4,4,64,128]{4,3,2,1,0:T(8,128)(2,1)}, bf16[1,4,4,64,128]{4,3,2,1,0:T(8,128)(2,1)S(1)}, u32[]{:S(2)}) copy-start(bf16[1,4,4,64,128]{4,3,2,1,0:T(8,128)(2,1)S(1)} %collective-permute-done.4.refs_1_) | copy-start | bytes 786436
  27.3 10.8 %copy-start.2 = (bf16[1,4,4,64,128]{4,3,2,1,0:T(8,128)(2,1)}, bf16[1,4,4,64,128]{4,3,2,1,0:T(8,128)(2,1)S(1)}, u32[]{:S(2)}) copy-start(bf16[1,4,4,64,128]{4,3,2,1,0:T(8,128)(2,1)S(1)} %collective-permute-done.5.refs_2_) | copy-start | bytes 786436
  27.3 10.8 %copy-start.3 = (bf16[1,4,4,64,128]{4,3,2,1,0:T(8,128)(2,1)}, bf16[1,4,4,64,128]{4,3,2,1,0:T(8,128)(2,1)S(1)}, u32[]{:S(2)}) copy-start(bf16[1,4,4,64,128]{4,3,2,1,0:T(8,128)(2,1)S(1)} %collective-permute-done.6.refs_3_) | copy-start | bytes 786436
  28.7 9.5 %collective-permute-start.7 = (bf16[4,4,4,64,128]{4,3,2,1,0:T(8,128)(2,1)S(1)}, bf16[4,4,4,64,128]{4,3,2,1,0:T(8,128)(2,1)}, u32[]{:S(2)}, u32[]{:S(2)}) collective-permute-start(bf16[4,4,4,64,128]{4,3,2,1,0:T(8,128)(2,1)S(1)} %pad_maximum_fusion), channel_id=1, source_target_pairs={{0,4},{4,0},{8,12},{12,8},{16,20},{20,16},{24,28},{28,24},{1,5},{5... | collective-permute-start | bytes 3145736 | tf_op jit(solution)/shard_map/ppermute | solution.py:384
  29.7 17.4 %collective-permute-start.2 = (bf16[2,2,512,128]{3,2,1,0:T(8,128)(2,1)}, bf16[2,2,512,128]{3,2,1,0:T(8,128)(2,1)}, u32[]{:S(2)}, u32[]{:S(2)}) collective-permute-start(bf16[2,2,512,128]{3,2,1,0:T(8,128)(2,1)} %get-tuple-element.41), channel_id=1, source_target_pairs={{0,4},{4,0},{8,12},{12,8},{16,20},{20,16},{24,28},{28,24},{1,5},{5... | collective-permute-start | bytes 1572872 | tf_op jit(solution)/shard_map/ppermute | solution.py:384
  29.8 21.2 %collective-permute-start.3 = (bf16[2,2,512,128]{3,2,1,0:T(8,128)(2,1)}, bf16[2,2,512,128]{3,2,1,0:T(8,128)(2,1)}, u32[]{:S(2)}, u32[]{:S(2)}) collective-permute-start(bf16[2,2,512,128]{3,2,1,0:T(8,128)(2,1)} %get-tuple-element.41), channel_id=1, source_target_pairs={{4,8},{12,16},{20,24},{8,4},{16,12},{24,20},{5,9},{13,17},{21,25},... | collective-permute-start | bytes 1572872 | tf_op jit(solution)/shard_map/ppermute | solution.py:391
  43.7 8.4 %all-to-all-start = ((f32[8,4,8,256]{3,2,1,0:T(8,128)}), f32[8,4,8,256]{3,2,1,0:T(8,128)S(1)}, u32[]{:S(2)}, u32[]{:S(2)}) async-start(f32[8,4,8,256]{3,2,1,0:T(8,128)} %get-tuple-element.48), calls=%async_computation | async-start | bytes 524288 | tf_op jit(solution)/shard_map/all_to_all | solution.py:465
  52.1 3.4 %copy-start = (f32[8,4,8,256]{3,2,1,0:T(8,128)}, f32[8,4,8,256]{3,2,1,0:T(8,128)S(1)}, u32[]{:S(2)}) copy-start(f32[8,4,8,256]{3,2,1,0:T(8,128)S(1)} %all-to-all-done.stats) | copy-start | bytes 786436
  52.1 32.6 %collective-permute-start.8 = (bf16[2,4,512,128]{3,2,1,0:T(8,128)(2,1)}, bf16[2,4,512,128]{3,2,1,0:T(8,128)(2,1)}, u32[]{:S(2)}, u32[]{:S(2)}) collective-permute-start(bf16[2,4,512,128]{3,2,1,0:T(8,128)(2,1)} %get-tuple-element.52.qd), channel_id=1, source_target_pairs={{0,4},{4,0},{8,12},{12,8},{16,20},{20,16},{24,28},{28,24},{1,5},{5... | collective-permute-start | bytes 3145736 | tf_op jit(solution)/shard_map/ppermute | solution.py:384
  53.5 31.3 %collective-permute-start.9 = (bf16[2,4,512,128]{3,2,1,0:T(8,128)(2,1)}, bf16[2,4,512,128]{3,2,1,0:T(8,128)(2,1)}, u32[]{:S(2)}, u32[]{:S(2)}) collective-permute-start(bf16[2,4,512,128]{3,2,1,0:T(8,128)(2,1)} %get-tuple-element.52.qd), channel_id=1, source_target_pairs={{4,8},{12,16},{20,24},{8,4},{16,12},{24,20},{5,9},{13,17},{21,25},... | collective-permute-start | bytes 3145736 | tf_op jit(solution)/shard_map/ppermute | solution.py:391
  76.5 8.2 %collective-permute-start.13 = (bf16[4,2,4,64,128]{4,3,2,1,0:T(8,128)(2,1)}, bf16[4,2,4,64,128]{4,3,2,1,0:T(8,128)(2,1)S(1)}, u32[]{:S(2)}, u32[]{:S(2)}) collective-permute-start(bf16[4,2,4,64,128]{4,3,2,1,0:T(8,128)(2,1)} %get-tuple-element.58), channel_id=1, source_target_pairs={{0,4},{4,0},{8,12},{12,8},{16,20},{20,16},{24,28},{28,24},{1,5},{5... | collective-permute-start | bytes 1572872 | tf_op jit(solution)/shard_map/ppermute | solution.py:384
  76.6 8.2 %collective-permute-start.12 = (bf16[4,2,4,64,128]{4,3,2,1,0:T(8,128)(2,1)}, bf16[4,2,4,64,128]{4,3,2,1,0:T(8,128)(2,1)}, u32[]{:S(2)}, u32[]{:S(2)}) collective-permute-start(bf16[4,2,4,64,128]{4,3,2,1,0:T(8,128)(2,1)} %get-tuple-element.56), channel_id=1, source_target_pairs={{0,4},{4,0},{8,12},{12,8},{16,20},{20,16},{24,28},{28,24},{1,5},{5... | collective-permute-start | bytes 1572872 | tf_op jit(solution)/shard_map/ppermute | solution.py:384
  77.1 1.7 %collective-permute-start.10 = (f32[4,2,512]{2,1,0:T(2,128)}, f32[4,2,512]{2,1,0:T(2,128)S(1)}, u32[]{:S(2)}, u32[]{:S(2)}) collective-permute-start(f32[4,2,512]{2,1,0:T(2,128)} %get-tuple-element.53), channel_id=1, source_target_pairs={{0,4},{4,0},{8,12},{12,8},{16,20},{20,16},{24,28},{28,24},{1,5},{5... | collective-permute-start | bytes 49160 | tf_op jit(solution)/shard_map/ppermute | solution.py:384
  78.8 13.0 %copy-start.8 = (f32[4,2,512]{2,1,0:T(2,128)}, f32[4,2,512]{2,1,0:T(2,128)S(1)}, u32[]{:S(2)}) copy-start(f32[4,2,512]{2,1,0:T(2,128)S(1)} %collective-permute-done.10.log_near) | copy-start | bytes 49156
  78.8 6.0 %collective-permute-start.11 = (f32[4,2,512]{2,1,0:T(2,128)}, f32[4,2,512]{2,1,0:T(2,128)S(1)}, u32[]{:S(2)}, u32[]{:S(2)}) collective-permute-start(f32[4,2,512]{2,1,0:T(2,128)} %get-tuple-element.53), channel_id=1, source_target_pairs={{4,8},{12,16},{20,24},{8,4},{16,12},{24,20},{5,9},{13,17},{21,25},... | collective-permute-start | bytes 49160 | tf_op jit(solution)/shard_map/ppermute | solution.py:391
  84.7 7.0 %copy-start.9 = (f32[4,2,512]{2,1,0:T(2,128)}, f32[4,2,512]{2,1,0:T(2,128)S(1)}, u32[]{:S(2)}) copy-start(f32[4,2,512]{2,1,0:T(2,128)S(1)} %collective-permute-done.11.log_far) | copy-start | bytes 49156
  84.7 0.8 copy-start.4
  88.1 10.9 %collective-permute-start.14 = (bf16[4,4,64,128]{3,2,1,0:T(8,128)(2,1)}, bf16[4,4,64,128]{3,2,1,0:T(8,128)(2,1)S(1)}, u32[]{:S(2)}, u32[]{:S(2)}) collective-permute-start(bf16[4,4,64,128]{3,2,1,0:T(8,128)(2,1)} %get-tuple-element.61), channel_id=1, source_target_pairs={{0,8},{4,12},{8,0},{12,4},{16,24},{20,28},{24,16},{28,20},{1,9},{5... | collective-permute-start | bytes 786440 | tf_op jit(solution)/shard_map/ppermute | solution.py:384
  90.6 14.1 %collective-permute-start.15 = (bf16[4,4,64,128]{3,2,1,0:T(8,128)(2,1)}, bf16[4,4,64,128]{3,2,1,0:T(8,128)(2,1)S(1)}, u32[]{:S(2)}, u32[]{:S(2)}) collective-permute-start(bf16[4,4,64,128]{3,2,1,0:T(8,128)(2,1)} %get-tuple-element.62), channel_id=1, source_target_pairs={{0,16},{4,20},{8,24},{12,28},{16,0},{20,4},{24,8},{28,12},{1,17},{... | collective-permute-start | bytes 786440 | tf_op jit(solution)/shard_map/ppermute | solution.py:384
  90.6 14.1 %collective-permute-start.16 = (bf16[4,4,64,128]{3,2,1,0:T(8,128)(2,1)}, bf16[4,4,64,128]{3,2,1,0:T(8,128)(2,1)S(1)}, u32[]{:S(2)}, u32[]{:S(2)}) collective-permute-start(bf16[4,4,64,128]{3,2,1,0:T(8,128)(2,1)} %get-tuple-element.63), channel_id=1, source_target_pairs={{0,24},{4,28},{8,16},{12,20},{16,8},{20,12},{24,0},{28,4},{1,25},{... | collective-permute-start | bytes 786440 | tf_op jit(solution)/shard_map/ppermute | solution.py:384
  98.9 5.8 %copy-start.5 = (bf16[4,4,64,128]{3,2,1,0:T(8,128)(2,1)}, bf16[4,4,64,128]{3,2,1,0:T(8,128)(2,1)S(1)}, u32[]{:S(2)}) copy-start(bf16[4,4,64,128]{3,2,1,0:T(8,128)(2,1)S(1)} %collective-permute-done.14.refs_1_) | copy-start | bytes 786436
  104.7 0.7 copy-start.6
  104.7 0.8 copy-start.7

commit v3 on v2

--- a/solution.py
+++ b/solution.py
@@ -41,16 +41,12 @@
     return jnp.broadcast_to(row, (128, row.shape[1])).T[:, :1]
 
 
-def pack_keys_kernel(heads, k, v, kv, *refs):
-    parts, wide_rows = refs[:-1], refs[-1]
-    group = heads // len(parts)
+def pack_keys_kernel(heads, k, v, kv, wide_rows):
     toks = k.shape[0] // heads
     for number, source in enumerate((k, v)):
         wide_rows[number] = source[...].astype(F32)
         for head in range(heads):
-            rows = wide_rows[number, pl.ds(head, toks, stride=heads), :].astype(BF)
-            kv[number, head] = rows
-            parts[head // group][number, head % group] = rows
+            kv[number, head] = wide_rows[number, pl.ds(head, toks, stride=heads), :].astype(BF)
 
 
 def pack_queries_kernel(heads, slots, q, g, kv, pos_row, qd, slot_rows, wide_rows, acc):
@@ -166,7 +162,7 @@
         out[2:4] = (kept_sums[part].astype(F32) + got_sums[part].astype(F32)).astype(BF)
 
 
-def global_kernel(scale, scale2, kv, rows, stats, expand, dkv, kept, sent):
+def global_kernel(scale, scale2, kv, rows, stats, expand, before, dkv, kept, sent):
     g_query, g_grad = rows[0, 0], rows[3, 0]
     tops = stats[:, 0, 0:1, :]
     top = jnp.max(tops, axis=0)
@@ -177,30 +173,25 @@
     weights = jnp.exp2(nt(kv[0, 0], g_query) * scale2 - g_log)
     narrow = weights.astype(BF)
     slopes = (weights * (nt(kv[1, 0], g_grad) - g_dot)).astype(BF)
-    dkv[0, 0] = nn(slopes, g_query) * scale
-    dkv[1, 0] = nn(narrow, g_grad)
+    dkv[0, 0] = before[0, 0] + nn(slopes, g_query) * scale
+    dkv[1, 0] = before[1, 0] + nn(narrow, g_grad)
     out = nn(kv[1, 0].T, narrow).T.astype(BF)
     dq = (nn(kv[0, 0].T, slopes) * scale).T.astype(BF)
     put_in_slots(expand[...], (out, dq), kept, sent)
 
 
-def local_kernel(scale, scale2, halves, group, qd, kv, *refs):
-    nears, fars, refs = refs[:halves], refs[halves : 2 * halves], refs[2 * halves :]
-    rows, bias, expand, before, out, log_dot, dq, dkv, kept, sent = refs[:-5]
-    keys, values, score_buf, probs, slopes = refs[-5:]
+def local_kernel(
+    scale, scale2, qd, kv, kv_near, kv_far, rows, bias, expand,
+    out, log_dot, dq, dkv, kept, sent, keys, values, score_buf, probs, slopes,
+):
     toks = kv.shape[2]
     reach = 2 * HALF + TILE
     span = keys.shape[0] - rows.shape[2]
     near = 2 * (1 - lax.axis_index("ctx") % 2)
-    for part in range(halves):
-
-        @pl.when(pl.program_id(0) // group == part)
-        def _():
-            for block, place in ((nears[part], near), (kv, 1), (fars[part], 2 - near)):
-                spot = pl.ds(pl.multiple_of(place * toks, toks), toks)
-                keys[spot, :] = block[0, 0]
-                values[spot, :] = block[1, 0]
-
+    for block, place in ((kv_near, near), (kv, 1), (kv_far, 2 - near)):
+        spot = pl.ds(pl.multiple_of(place * toks, toks), toks)
+        keys[spot, :] = block[0, 0]
+        values[spot, :] = block[1, 0]
     keys[span:, :] = rows[1, 0]
     values[span:, :] = rows[2, 0]
     key_t, value_t = keys[...].T, values[...].T
@@ -274,8 +265,8 @@
             attend(step - 1)
     own = slice(HALF, HALF + toks)
     grads = jnp.concatenate(scaled, axis=1)
-    dkv[0, 0] = before[0, 0] + (nt(query_t, slopes[own, :]) * scale).T
-    dkv[1, 0] = before[1, 0] + nt(grads, probs[own, :]).T
+    dkv[0, 0] = (nt(query_t, slopes[own, :]) * scale).T
+    dkv[1, 0] = nt(grads, probs[own, :]).T
     g_dk = (nt(query_t, slopes[span:, :]) * scale).T.astype(BF)
     g_dv = nt(grads, probs[span:, :]).T.astype(BF)
     put_in_slots(expand[...], (g_dk, g_dv), kept, sent)
@@ -399,12 +390,9 @@
     flat_spec = pl.BlockSpec((toks * heads // steps, width), lambda i: (i, 0))
     pair_spec = pl.BlockSpec((2, heads, toks // steps, width), lambda i: (0, 0, i, 0))
     wide_pair = pltpu.VMEM((2, toks * heads // steps, width), F32)
-    halves = 2 if heads % 2 == 0 else 1
-    group = heads // halves
-    part_shape = (2, group, toks, width)
-    kv, *kv_parts = pl.pallas_call(
+    kv = pl.pallas_call(
         functools.partial(pack_keys_kernel, heads),
-        out_shape=[struct(pair_shape, BF)] + [struct(part_shape, BF)] * halves,
+        out_shape=struct(pair_shape, BF),
         scratch_shapes=[wide_pair],
         compiler_params=params(),
         name="pack_keys",
@@ -434,17 +422,12 @@
         name="masks",
     )(pos_row)
 
-    nears, fars = [], []
-    for part in kv_parts:
-        if fars:
-            part = after(part, (nears[-1], fars[-1]))
-        fars.append(from_far(part))
-        nears.append(from_near(part))
+    kv_far, kv_near = from_far(kv), from_near(kv)
     held = [slot_rows[None]]
     for stage in stages:
         send = jnp.concatenate(held, axis=0) if len(held) > 1 else held[0]
         if stage == [1]:
-            send = after(send, (nears[0], fars[0], place))
+            send = after(send, (kv_near, kv_far, place))
         held += [swap(send, mask) for mask in stage]
 
     row_shape = (4, heads, count, width)
@@ -461,38 +444,17 @@
         name="global_stats",
     )(compact, *held, kv)
 
-    kv_done = (nears, fars)
     stats = lax.all_to_all(stats, "ctx", 0, 0, tiled=True)
-    qd_late = after(qd, (kv_done, stats))
+    qd_late = after(qd, (kv_near, kv_far))
     qd_far, qd_near = from_far(qd_late), from_near(qd_late)
 
     sum_shape = (devices // 2, 2, heads, slots, width)
     sum_struct = struct(sum_shape, BF)
-    extra, kept_ends, sent_ends = pl.pallas_call(
-        functools.partial(global_kernel, scale, scale2),
+    out, log_dot, dq, dkv, kept_sums, sent_sums = pl.pallas_call(
+        functools.partial(local_kernel, scale, scale2),
         grid=(heads,),
-        in_specs=[per_head(pair_shape, 1), per_head(row_shape, 1)]
-        + [per_head(stats.shape, 1), whole(expand.shape)],
-        out_specs=(per_head(pair_shape, 1), per_head(sum_shape, 2), per_head(sum_shape, 2)),
-        out_shape=(struct(pair_shape, F32), sum_struct, sum_struct),
-        compiler_params=params(),
-        cost_estimate=cost(1e6, 1e6),
-        name="global_queries",
-    )(kv, rows, stats, expand)
-    got_ends = from_near(sent_ends)
-
-    def half_head(part):
-        return pl.BlockSpec(
-            (2, 1, toks, width), lambda head: (0, jnp.clip(head - part * group, 0, group - 1), 0, 0)
-        )
-
-    out, log_dot, dq, dkv, kept_sums, sent_sums = pl.pallas_call(
-        functools.partial(local_kernel, scale, scale2, halves, group),
-        grid=(heads,),
-        in_specs=[per_head(pair_shape, 1)] * 2
-        + [half_head(part) for part in range(halves)] * 2
-        + [per_head(row_shape, 1), whole(bias.shape), whole(expand.shape)]
-        + [per_head(pair_shape, 1)],
+        in_specs=[per_head(pair_shape, 1)] * 4
+        + [per_head(row_shape, 1), whole(bias.shape), whole(expand.shape)],
         out_specs=(
             per_head((heads, toks, width), 0),
             per_head((heads, 2, toks), 0),
@@ -519,18 +481,87 @@
         compiler_params=params(),
         cost_estimate=cost(1e6, 1e6),
         name="local",
-    )(qd, kv, *nears, *fars, rows, bias, expand, extra)
+    )(qd, kv, kv_near, kv_far, rows, bias, expand)
     log_far, log_near = from_far(log_dot), from_near(log_dot)
 
+    dkv, kept_ends, sent_ends = pl.pallas_call(
+        functools.partial(global_kernel, scale, scale2),
+        grid=(heads,),
+        in_specs=[per_head(pair_shape, 1), per_head(row_shape, 1)]
+        + [per_head(stats.shape, 1), whole(expand.shape), per_head(pair_shape, 1)],
+        out_specs=(per_head(pair_shape, 1), per_head(sum_shape, 2), per_head(sum_shape, 2)),
+        out_shape=(struct(pair_shape, F32), sum_struct, sum_struct),
+        input_output_aliases={4: 0},
+        compiler_params=params(),
+        cost_estimate=cost(1e6, 1e6),
+        name="global_queries",
+    )(kv, rows, after(stats, (log_dot, qd_near, qd_far)), expand, dkv)
     got_sums = from_near(sent_sums)
+    got_ends = from_near(after(sent_ends, (log_near, log_far)))
+
+    sum_shape = (devices // 2, 2, heads, slots, width)
+    sum_struct = struct(sum_shape, BF)
+    out, log_dot, dq, dkv, kept_sums, sent_sums = pl.pallas_call(
+        functools.partial(local_kernel, scale, scale2),
+        grid=(heads,),
+        in_specs=[per_head(pair_shape, 1)] * 4
+        + [per_head(row_shape, 1), whole(bias.shape), whole(expand.shape)],
+        out_specs=(
+            per_head((heads, toks, width), 0),
+            per_head((heads, 2, toks), 0),
+            per_head((heads, toks, width), 0),
+            per_head(pair_shape, 1),
+            per_head(sum_shape, 2),
+            per_head(sum_shape, 2),
+        ),
+        out_shape=(
+            struct((heads, toks, width), BF),
+            struct((heads, 2, toks), F32),
+            struct((heads, toks, width), F32),
+            struct(pair_shape, F32),
+            sum_struct,
+            sum_struct,
+        ),
+        scratch_shapes=[
+            pltpu.VMEM((span + count, width), BF),
+            pltpu.VMEM((span + count, width), BF),
+            pltpu.VMEM((toks // TILE, 2 * HALF + TILE + count, TILE), F32),
+            pltpu.VMEM((span + count, toks), BF),
+            pltpu.VMEM((span + count, toks), BF),
+        ],
+        compiler_params=params(),
+        cost_estimate=cost(1e6, 1e6),
+        name="local",
+    )(qd, kv, kv_near, kv_far, rows, bias, expand)
+    log_far, log_near = from_far(log_dot), from_near(log_dot)
+
+    dkv, kept_ends, sent_ends = pl.pallas_call(
+        functools.partial(global_kernel, scale, scale2),
+        grid=(heads,),
+        in_specs=[per_head(pair_shape, 1), per_head(row_shape, 1)]
+        + [per_head(stats.shape, 1), whole(expand.shape), per_head(pair_shape, 1)],
+        out_specs=(per_head(pair_shape, 1), per_head(sum_shape, 2), per_head(sum_shape, 2)),
+        out_shape=(struct(pair_shape, F32), sum_struct, sum_struct),
+        input_output_aliases={4: 0},
+        compiler_params=params(),
+        cost_estimate=cost(1e6, 1e6),
+        name="global_queries",
+    )(kv, rows, after(stats, (log_dot, qd_near, qd_far)), expand, dkv)
+    got_sums = from_near(sent_sums)
+    got_ends = from_near(after(sent_ends, (log_near, log_far)))
+
+    def half_head(part):
+        return pl.BlockSpec(
+            (2, 1, toks, width), lambda head: (0, jnp.clip(head - part * group, 0, group - 1), 0, 0)
+        )
+
     first = stages[0]
-    halos = (qd_near, qd_far, log_near, log_far)
     parts = pl.pallas_call(
         fold_kernel,
         out_shape=[struct((4, heads, slots, width), BF)] * (devices // 2),
         compiler_params=params(),
         name="fold",
-    )(kept_ends, got_ends, kept_sums, after(got_sums, halos))
+    )(kept_ends, got_ends, kept_sums, got_sums)
     for stage in reversed(stages[1:-1]):
         size = len(parts) // (len(stage) + 1)
         kept = parts[:size]

time: 111 us -> 108 us (0.973)
  starting transfers between devices: 32 us -> 20.6 us
  waiting for transfers between devices: 25.2 us -> 34.3 us
    ppermute x13 -> x12, waiting for transfers between devices: 18.5 us -> 34.3 us  [swap(): return lax.ppermute(value, 'ctx', [(i, i ^ mask) for i in range(devices)])]
    ppermute x4 -> x3, starting transfers between devices: 19.1 us -> 9.98 us  [from_far(): return lax.ppermute(value, 'ctx', pairs + [(j, i) for i, j in pairs])]
    ppermute x4 -> x3, waiting for transfers between devices: 5.66 us -> 0.01 us  [from_far(): return lax.ppermute(value, 'ctx', pairs + [(j, i) for i, j in pairs])]
    ppermute x13 -> x12, starting transfers between devices: 9.49 us -> 6.31 us  [swap(): return lax.ppermute(value, 'ctx', [(i, i ^ mask) for i in range(devices)])]
  transfers between devices with their start and end apart: 18 -> 16, of which waited for: 6 -> 5; matrix products, arithmetic and copies ran while one was open for 1% -> 1% of each run, Pallas kernels for 36% -> 37%
where the time goes in v3:
time: 108 us; the launch traced here: 107 us
  Pallas kernels  48.2 us (45%)
  waiting for transfers between devices  34.3 us (32%)
  starting transfers between devices  20.6 us (19%)
  local copies, waits for them, and re-layouts  1.44 us (1%)
  other arithmetic  1.18 us (1%)
    ppermute x12, waiting for transfers between devices, swap(): return lax.ppermute(value, 'ctx', [(i, i ^ mask) for i in range(devices)])  34.3 us
    pallas_call x1, Pallas kernels, shards(): pl.pallas_call(functools.partial(local_kernel, scale, scale2), grid=(head...  14.2 us
    ppermute x3, starting transfers between devices, from_far(): return lax.ppermute(value, 'ctx', pairs + [(j, i) for i, j in pairs])  9.98 us
    pallas_call x1, Pallas kernels, shards(): pl.pallas_call(functools.partial(rim_kernel, scale, scale2), grid=(heads,...  7.14 us
    pallas_call x1, Pallas kernels, shards(): pl.pallas_call(functools.partial(global_kernel, scale, scale2), grid=(hea...  6.59 us
    ppermute x12, starting transfers between devices, swap(): return lax.ppermute(value, 'ctx', [(i, i ^ mask) for i in range(devices)])  6.31 us
    pallas_call x1, Pallas kernels, shards(): pl.pallas_call(functools.partial(stats_kernel, scale2), grid=(heads,), in...  5.52 us
    all_to_all x1, starting transfers between devices, shards(): stats = lax.all_to_all(stats, 'ctx', 0, 0, tiled=True)  4.27 us
  transfers between devices with their start and end apart: 16, of which 5 were waited for; matrix products, arithmetic and copies ran while one was open for 1% of the time, Pallas kernels for 37%

profile of v3, /device:TPU:1, one launch (start us, length us, event | category | flops | bytes accessed | tf_op | source)
XLA Modules:
  0.0 106.5 jit_solution(17105837424217268178)
XLA Ops:
  0.6 2.4 %pack_keys.1.kv.refs_5_ = bf16[2,4,512,128]{3,2,1,0:T(8,128)(2,1)} custom-call(bf16[2048,128]{1,0:T(8,128)(2,1)} %bitcast.15, bf16[2048,128]{1,0:T(8,128)(2,1)} %bitcast.16), custom_call_target="tpu_custom_call" | custom-call | tf_op jit(solution)/shard_map/pack_keys/pallas_call | solution.py:393
  3.1 4.5 %collective-permute-start.1 = (bf16[2,4,512,128]{3,2,1,0:T(8,128)(2,1)}, bf16[2,4,512,128]{3,2,1,0:T(8,128)(2,1)}, u32[]{:S(2)}, u32[]{:S(2)}) collective-permute-start(bf16[2,4,512,128]{3,2,1,0:T(8,128)(2,1)} %pack_keys.1.kv.refs_5_), channel_id=1, source_target_pairs={{4,8},{12,16},{20,24},{8,4},{16,12},{24,20},{5,9},{13,17},{21,25},... | collective-permute-start | bytes 3145736 | tf_op jit(solution)/shard_map/ppermute | solution.py:382
  7.6 0.1 collective-permute-start
  7.7 3.4 %pack_queries.1 = (bf16[2,4,512,128]{3,2,1,0:T(8,128)(2,1)}, bf16[4,4,64,128]{3,2,1,0:T(8,128)(2,1)}) custom-call(bf16[2048,128]{1,0:T(8,128)(2,1)} %bitcast.17, bf16[2048,128]{1,0:T(8,128)(2,1)} %bitcast.18, bf16[2,4,512,128]{3,2,1,0:T(8,128)(2,1)} %pack_keys.1.kv.refs_5_, s32[1,256]{1,0:T(1,128)} %bitcast.19), custom_call_target="tpu_custom_call" | custom-call | tf_op jit(solution)/shard_map/pack_queries/pallas_call | solution.py:401
  11.1 1.1 collective-permute-start.4
  12.1 1.3 %collective-permute-start.3 = (bf16[1,4,4,64,128]{4,3,2,1,0:T(8,128)(2,1)}, bf16[1,4,4,64,128]{4,3,2,1,0:T(8,128)(2,1)S(1)}, u32[]{:S(2)}, u32[]{:S(2)}) collective-permute-start(bf16[1,4,4,64,128]{4,3,2,1,0:T(8,128)(2,1)} %bitcast.11), channel_id=1, source_target_pairs={{0,16},{4,20},{8,24},{12,28},{16,0},{20,4},{24,8},{28,12},{1,17},{... | collective-permute-start | bytes 786440 | tf_op jit(solution)/shard_map/ppermute | solution.py:375
  13.5 0.3 collective-permute-start.2
  13.7 2.2 %masks.1 = (f32[1536,128]{1,0:T(8,128)}, bf16[256,512]{1,0:T(8,128)(2,1)}, bf16[512,256]{1,0:T(8,128)(2,1)}, bf16[512,64]{1,0:T(8,128)(2,1)}) custom-call(s32[1,256]{1,0:T(1,128)} %bitcast.20), custom_call_target="tpu_custom_call" | custom-call | tf_op jit(solution)/shard_map/masks/pallas_call | solution.py:413
  15.9 12.1 %collective-permute-done.4.refs_3_ = bf16[1,4,4,64,128]{4,3,2,1,0:T(8,128)(2,1)S(1)} collective-permute-done((bf16[1,4,4,64,128]{4,3,2,1,0:T(8,128)(2,1)}, bf16[1,4,4,64,128]{4,3,2,1,0:T(8,128)(2,1)S(1)}, u32[]{:S(2)}, u32[]{:S(2)}) %collective-permute-start.4) | collective-permute-done | bytes 262176 | tf_op jit(solution)/shard_map/ppermute | solution.py:375
  28.0 0.0 collective-permute-done.3.refs_2_
  28.0 14.7 %collective-permute-done.2.refs_1_ = bf16[1,4,4,64,128]{4,3,2,1,0:T(8,128)(2,1)S(1)} collective-permute-done((bf16[1,4,4,64,128]{4,3,2,1,0:T(8,128)(2,1)}, bf16[1,4,4,64,128]{4,3,2,1,0:T(8,128)(2,1)S(1)}, u32[]{:S(2)}, u32[]{:S(2)}) %collective-permute-start.2) | collective-permute-done | bytes 262176 | tf_op jit(solution)/shard_map/ppermute | solution.py:375
  42.7 1.2 %pad_maximum_fusion = bf16[4,4,4,64,128]{4,3,2,1,0:T(8,128)(2,1)S(1)} fusion(bf16[1,4,4,64,128]{4,3,2,1,0:T(8,128)(2,1)S(1)} %collective-permute-done.4.refs_3_, bf16[1,4,4,64,128]{4,3,2,1,0:T(8,128)(2,1)S(1)} %collective-permute-done.3.refs_2_, bf16[1,4,4,64,128]{4,3,2,1,0:T(8,128)(2,1)S(1)} %collective-permute-done.2.refs_1_, ...), kind=kLoop, calls=%fused_computation | loop fusion | flops 1572864 | bytes 2097152 | tf_op jit(solution)/shard_map/concatenate | solution.py:428
  43.9 0.0 collective-permute-done.1.kv_far
  43.9 0.0 collective-permute-done.kv_near
  43.9 0.1 collective-permute-start.5
  44.0 1.9 %collective-permute-start.7 = (bf16[2,4,512,128]{3,2,1,0:T(8,128)(2,1)}, bf16[2,4,512,128]{3,2,1,0:T(8,128)(2,1)}, u32[]{:S(2)}, u32[]{:S(2)}) collective-permute-start(bf16[2,4,512,128]{3,2,1,0:T(8,128)(2,1)} %get-tuple-element.43.qd), channel_id=1, source_target_pairs={{4,8},{12,16},{20,24},{8,4},{16,12},{24,20},{5,9},{13,17},{21,25},... | collective-permute-start | bytes 3145736 | tf_op jit(solution)/shard_map/ppermute | solution.py:382
  46.0 0.2 collective-permute-start.6
  46.1 0.7 collective-permute-done.5.refs_4_
  46.8 0.0 copy-done.1
  46.8 5.5 %global_stats.1 = (bf16[4,4,256,128]{3,2,1,0:T(8,128)(2,1)}, f32[8,4,8,256]{3,2,1,0:T(8,128)}) custom-call(bf16[256,512]{1,0:T(8,128)(2,1)} %get-tuple-element.35.compact, bf16[1,4,4,64,128]{4,3,2,1,0:T(8,128)(2,1)} %bitcast.14, bf16[1,4,4,64,128]{4,3,2,1,0:T(8,128)(2,1)} %copy-done.3, bf16[1,4,4,64,128]{4,3,2,1,0:T(8,128)(2,1)} %copy-done.2, ...), custom_call_target="tpu_custom_call" | custom-call | flops 1000000 | bytes 1000000 | tf_op jit(solution)/shard_map/global_stats/pallas_call | solution.py:434
  52.3 4.3 %all-to-all-start = ((f32[8,4,8,256]{3,2,1,0:T(8,128)}), f32[8,4,8,256]{3,2,1,0:T(8,128)S(1)}, u32[]{:S(2)}, u32[]{:S(2)}) async-start(f32[8,4,8,256]{3,2,1,0:T(8,128)} %get-tuple-element.45), calls=%async_computation | async-start | bytes 524288 | tf_op jit(solution)/shard_map/all_to_all | solution.py:447
  56.6 14.2 %local.1 = (bf16[4,512,128]{2,1,0:T(8,128)(2,1)}, f32[4,2,512]{2,1,0:T(2,128)}, f32[4,512,128]{2,1,0:T(8,128)}, f32[2,4,512,128]{3,2,1,0:T(8,128)}, bf16[4,2,4,6...) custom-call(bf16[2,4,512,128]{3,2,1,0:T(8,128)(2,1)} %get-tuple-element.43.qd, ...), custom_call_target="tpu_custom_call" | custom-call | flops 1000000 | bytes 1000000 | tf_op jit(solution)/shard_map/local/pallas_call | solution.py:504
  70.7 3.5 %collective-permute-start.9 = (f32[4,2,512]{2,1,0:T(2,128)}, f32[4,2,512]{2,1,0:T(2,128)S(1)}, u32[]{:S(2)}, u32[]{:S(2)}) collective-permute-start(f32[4,2,512]{2,1,0:T(2,128)} %get-tuple-element.44), channel_id=1, source_target_pairs={{4,8},{12,16},{20,24},{8,4},{16,12},{24,20},{5,9},{13,17},{21,25},... | collective-permute-start | bytes 49160 | tf_op jit(solution)/shard_map/ppermute | solution.py:382
  74.3 0.1 collective-permute-start.8
  74.4 0.5 collective-permute-start.11
  74.9 0.0 collective-permute-done.7.qd_far
  74.9 0.0 collective-permute-done.6.qd_near
  74.9 0.0 all-to-all-done.stats
  74.9 0.7 copy-done
  75.6 6.6 %global_queries.1 = (f32[2,4,512,128]{3,2,1,0:T(8,128)}, bf16[4,2,4,64,128]{4,3,2,1,0:T(8,128)(2,1)}, bf16[4,2,4,64,128]{4,3,2,1,0:T(8,128)(2,1)}) custom-call(bf16[2,4,512,128]{3,2,1,0:T(8,128)(2,1)} %pack_keys.1.kv.refs_5_, bf16[4,4,256,128]{3,2,1,0:T(8,128)(2,1)} %get-tuple-element.38.rows, ...), custom_call_target="tpu_custom_call", output_to_operand_aliasing={{0}: (4, {})} | custom-call | flops 1000000 | bytes 1000000 | tf_op jit(solution)/shard_map/global_queries/pallas_call | solution.py:538
  82.2 0.0 collective-permute-done.9.log_far
  82.2 0.0 collective-permute-done.8.log_near
  82.2 0.1 collective-permute-start.10
  82.4 0.0 collective-permute-done.11.got_sums
  82.4 2.2 %collective-permute-done.10.got_ends = bf16[4,2,4,64,128]{4,3,2,1,0:T(8,128)(2,1)} collective-permute-done((bf16[4,2,4,64,128]{4,3,2,1,0:T(8,128)(2,1)}, bf16[4,2,4,64,128]{4,3,2,1,0:T(8,128)(2,1)}, u32[]{:S(2)}, u32[]{:S(2)}) %collective-permute-start.10) | collective-permute-done | bytes 524320 | tf_op jit(solution)/shard_map/ppermute | solution.py:375
  84.5 2.6 %fold.1 = (bf16[4,4,64,128]{3,2,1,0:T(8,128)(2,1)}, bf16[4,4,64,128]{3,2,1,0:T(8,128)(2,1)}, bf16[4,4,64,128]{3,2,1,0:T(8,128)(2,1)}, bf16[4,4,64,128]{3,2,1,0:T(8,128)(2,1)}) custom-call(bf16[4,2,4,64,128]{4,3,2,1,0:T(8,128)(2,1)} %get-tuple-element.49.kept_ends, bf16[4,2,4,64,128]{4,3,2,1,0:T(8,128)(2,1)} %collective-permute-done.10.got_ends, ...), custom_call_target="tpu_custom_call" | custom-call | tf_op jit(solution)/shard_map/fold/pallas_call | solution.py:559
  87.1 1.3 %collective-permute-start.12 = (bf16[4,4,64,128]{3,2,1,0:T(8,128)(2,1)}, bf16[4,4,64,128]{3,2,1,0:T(8,128)(2,1)S(1)}, u32[]{:S(2)}, u32[]{:S(2)}) collective-permute-start(bf16[4,4,64,128]{3,2,1,0:T(8,128)(2,1)} %get-tuple-element.55), channel_id=1, source_target_pairs={{0,8},{4,12},{8,0},{12,4},{16,24},{20,28},{24,16},{28,20},{1,9},{5... | collective-permute-start | bytes 786440 | tf_op jit(solution)/shard_map/ppermute | solution.py:375
  88.4 0.0 collective-permute-start.13
  88.4 1.4 %collective-permute-start.14 = (bf16[4,4,64,128]{3,2,1,0:T(8,128)(2,1)}, bf16[4,4,64,128]{3,2,1,0:T(8,128)(2,1)S(1)}, u32[]{:S(2)}, u32[]{:S(2)}) collective-permute-start(bf16[4,4,64,128]{3,2,1,0:T(8,128)(2,1)} %get-tuple-element.57), channel_id=1, source_target_pairs={{0,24},{4,28},{8,16},{12,20},{16,8},{20,12},{24,0},{28,4},{1,25},{... | collective-permute-start | bytes 786440 | tf_op jit(solution)/shard_map/ppermute | solution.py:375
  89.8 0.0 copy-done.8
  89.8 7.1 %rim.1.dkv = f32[2,4,512,128]{3,2,1,0:T(8,128)} custom-call(bf16[2,4,512,128]{3,2,1,0:T(8,128)(2,1)} %pack_keys.1.kv.refs_5_, f32[1536,128]{1,0:T(8,128)} %get-tuple-element.39.bias, bf16[2,4,512,128]{3,2,1,0:T(8,128)(2,1)} %collective-permute-done.6.qd_near, bf16[2,4,512,128]{3,2,1,0:T(8,128)(2,1)} %collective-permute-done.7.qd_far, ...), custom_call_target="tpu_custom_call" | custom-call | flops 1000000 | bytes 1000000 | tf_op jit(solution)/shard_map/rim/pallas_call | solution.py:574
  96.9 0.0 collective-permute-done.12.refs_1_
  96.9 0.0 collective-permute-done.13.refs_2_
  96.9 0.0 copy-start.6
  96.9 4.7 %collective-permute-done.14.refs_3_ = bf16[4,4,64,128]{3,2,1,0:T(8,128)(2,1)S(1)} collective-permute-done((bf16[4,4,64,128]{3,2,1,0:T(8,128)(2,1)}, bf16[4,4,64,128]{3,2,1,0:T(8,128)(2,1)S(1)}, u32[]{:S(2)}, u32[]{:S(2)}) %collective-permute-start.14) | collective-permute-done | bytes 262176 | tf_op jit(solution)/shard_map/ppermute | solution.py:375
  101.6 0.0 copy-done.5
  101.6 0.7 copy-done.7
  102.3 4.2 %final.1 = (bf16[2048,128]{1,0:T(8,128)(2,1)}, f32[2048,128]{1,0:T(8,128)}, f32[2048,128]{1,0:T(8,128)}, f32[2048,128]{1,0:T(8,128)}) custom-call(bf16[512,64]{1,0:T(8,128)(2,1)} %get-tuple-element.33.place, bf16[4,512,128]{2,1,0:T(8,128)(2,1)} %get-tuple-element.41.out, f32[4,512,128]{2,1,0:T(8,128)} %get-tuple-element.42.dq, f32[2,4,512,128]{3,2,1,0:T(8,128)} %rim.1.dkv, ...), custom_call_target="tpu_custom_call" | custom-call | tf_op jit(solution)/shard_map/final/pallas_call | solution.py:597
  (14 shorter events, 0.0 us)
Async XLA Ops:
  3.1 40.8 %collective-permute-start.1 = (bf16[2,4,512,128]{3,2,1,0:T(8,128)(2,1)}, bf16[2,4,512,128]{3,2,1,0:T(8,128)(2,1)}, u32[]{:S(2)}, u32[]{:S(2)}) collective-permute-start(bf16[2,4,512,128]{3,2,1,0:T(8,128)(2,1)} %pack_keys.1.kv.refs_5_), channel_id=1, source_target_pairs={{4,8},{12,16},{20,24},{8,4},{16,12},{24,20},{5,9},{13,17},{21,25},... | collective-permute-start | bytes 3145736 | tf_op jit(solution)/shard_map/ppermute | solution.py:382
  7.6 36.3 %collective-permute-start = (bf16[2,4,512,128]{3,2,1,0:T(8,128)(2,1)}, bf16[2,4,512,128]{3,2,1,0:T(8,128)(2,1)}, u32[]{:S(2)}, u32[]{:S(2)}) collective-permute-start(bf16[2,4,512,128]{3,2,1,0:T(8,128)(2,1)} %pack_keys.1.kv.refs_5_), channel_id=1, source_target_pairs={{0,4},{4,0},{8,12},{12,8},{16,20},{20,16},{24,28},{28,24},{1,5},{5... | collective-permute-start | bytes 3145736 | tf_op jit(solution)/shard_map/ppermute | solution.py:375
  11.1 17.0 %collective-permute-start.4 = (bf16[1,4,4,64,128]{4,3,2,1,0:T(8,128)(2,1)}, bf16[1,4,4,64,128]{4,3,2,1,0:T(8,128)(2,1)S(1)}, u32[]{:S(2)}, u32[]{:S(2)}) collective-permute-start(bf16[1,4,4,64,128]{4,3,2,1,0:T(8,128)(2,1)} %bitcast.10), channel_id=1, source_target_pairs={{0,24},{4,28},{8,16},{12,20},{16,8},{20,12},{24,0},{28,4},{1,25},{... | collective-permute-start | bytes 786440 | tf_op jit(solution)/shard_map/ppermute | solution.py:375
  12.1 15.9 %collective-permute-start.3 = (bf16[1,4,4,64,128]{4,3,2,1,0:T(8,128)(2,1)}, bf16[1,4,4,64,128]{4,3,2,1,0:T(8,128)(2,1)S(1)}, u32[]{:S(2)}, u32[]{:S(2)}) collective-permute-start(bf16[1,4,4,64,128]{4,3,2,1,0:T(8,128)(2,1)} %bitcast.11), channel_id=1, source_target_pairs={{0,16},{4,20},{8,24},{12,28},{16,0},{20,4},{24,8},{28,12},{1,17},{... | collective-permute-start | bytes 786440 | tf_op jit(solution)/shard_map/ppermute | solution.py:375
  13.5 29.3 %collective-permute-start.2 = (bf16[1,4,4,64,128]{4,3,2,1,0:T(8,128)(2,1)}, bf16[1,4,4,64,128]{4,3,2,1,0:T(8,128)(2,1)S(1)}, u32[]{:S(2)}, u32[]{:S(2)}) collective-permute-start(bf16[1,4,4,64,128]{4,3,2,1,0:T(8,128)(2,1)} %bitcast.12), channel_id=1, source_target_pairs={{0,8},{4,12},{8,0},{12,4},{16,24},{20,28},{24,16},{28,20},{1,9},{5... | collective-permute-start | bytes 786440 | tf_op jit(solution)/shard_map/ppermute | solution.py:375
  28.0 18.7 %copy-start.1 = (bf16[1,4,4,64,128]{4,3,2,1,0:T(8,128)(2,1)}, bf16[1,4,4,64,128]{4,3,2,1,0:T(8,128)(2,1)S(1)}, u32[]{:S(2)}) copy-start(bf16[1,4,4,64,128]{4,3,2,1,0:T(8,128)(2,1)S(1)} %collective-permute-done.4.refs_3_) | copy-start | bytes 786436
  28.0 18.7 %copy-start.2 = (bf16[1,4,4,64,128]{4,3,2,1,0:T(8,128)(2,1)}, bf16[1,4,4,64,128]{4,3,2,1,0:T(8,128)(2,1)S(1)}, u32[]{:S(2)}) copy-start(bf16[1,4,4,64,128]{4,3,2,1,0:T(8,128)(2,1)S(1)} %collective-permute-done.3.refs_2_) | copy-start | bytes 786436
  42.7 4.1 %copy-start.3 = (bf16[1,4,4,64,128]{4,3,2,1,0:T(8,128)(2,1)}, bf16[1,4,4,64,128]{4,3,2,1,0:T(8,128)(2,1)S(1)}, u32[]{:S(2)}) copy-start(bf16[1,4,4,64,128]{4,3,2,1,0:T(8,128)(2,1)S(1)} %collective-permute-done.2.refs_1_) | copy-start | bytes 786436
  43.9 2.9 %collective-permute-start.5 = (bf16[4,4,4,64,128]{4,3,2,1,0:T(8,128)(2,1)S(1)}, bf16[4,4,4,64,128]{4,3,2,1,0:T(8,128)(2,1)}, u32[]{:S(2)}, u32[]{:S(2)}) collective-permute-start(bf16[4,4,4,64,128]{4,3,2,1,0:T(8,128)(2,1)S(1)} %pad_maximum_fusion), channel_id=1, source_target_pairs={{0,4},{4,0},{8,12},{12,8},{16,20},{20,16},{24,28},{28,24},{1,5},{5... | collective-permute-start | bytes 3145736 | tf_op jit(solution)/shard_map/ppermute | solution.py:375
  44.0 30.9 %collective-permute-start.7 = (bf16[2,4,512,128]{3,2,1,0:T(8,128)(2,1)}, bf16[2,4,512,128]{3,2,1,0:T(8,128)(2,1)}, u32[]{:S(2)}, u32[]{:S(2)}) collective-permute-start(bf16[2,4,512,128]{3,2,1,0:T(8,128)(2,1)} %get-tuple-element.43.qd), channel_id=1, source_target_pairs={{4,8},{12,16},{20,24},{8,4},{16,12},{24,20},{5,9},{13,17},{21,25},... | collective-permute-start | bytes 3145736 | tf_op jit(solution)/shard_map/ppermute | solution.py:382
  46.0 28.9 %collective-permute-start.6 = (bf16[2,4,512,128]{3,2,1,0:T(8,128)(2,1)}, bf16[2,4,512,128]{3,2,1,0:T(8,128)(2,1)}, u32[]{:S(2)}, u32[]{:S(2)}) collective-permute-start(bf16[2,4,512,128]{3,2,1,0:T(8,128)(2,1)} %get-tuple-element.43.qd), channel_id=1, source_target_pairs={{0,4},{4,0},{8,12},{12,8},{16,20},{20,16},{24,28},{28,24},{1,5},{5... | collective-permute-start | bytes 3145736 | tf_op jit(solution)/shard_map/ppermute | solution.py:375
  52.3 22.6 %all-to-all-start = ((f32[8,4,8,256]{3,2,1,0:T(8,128)}), f32[8,4,8,256]{3,2,1,0:T(8,128)S(1)}, u32[]{:S(2)}, u32[]{:S(2)}) async-start(f32[8,4,8,256]{3,2,1,0:T(8,128)} %get-tuple-element.45), calls=%async_computation | async-start | bytes 524288 | tf_op jit(solution)/shard_map/all_to_all | solution.py:447
  70.7 11.4 %collective-permute-start.9 = (f32[4,2,512]{2,1,0:T(2,128)}, f32[4,2,512]{2,1,0:T(2,128)S(1)}, u32[]{:S(2)}, u32[]{:S(2)}) collective-permute-start(f32[4,2,512]{2,1,0:T(2,128)} %get-tuple-element.44), channel_id=1, source_target_pairs={{4,8},{12,16},{20,24},{8,4},{16,12},{24,20},{5,9},{13,17},{21,25},... | collective-permute-start | bytes 49160 | tf_op jit(solution)/shard_map/ppermute | solution.py:382
  74.3 7.9 %collective-permute-start.8 = (f32[4,2,512]{2,1,0:T(2,128)}, f32[4,2,512]{2,1,0:T(2,128)S(1)}, u32[]{:S(2)}, u32[]{:S(2)}) collective-permute-start(f32[4,2,512]{2,1,0:T(2,128)} %get-tuple-element.44), channel_id=1, source_target_pairs={{0,4},{4,0},{8,12},{12,8},{16,20},{20,16},{24,28},{28,24},{1,5},{5... | collective-permute-start | bytes 49160 | tf_op jit(solution)/shard_map/ppermute | solution.py:375
  74.4 8.0 %collective-permute-start.11 = (bf16[4,2,4,64,128]{4,3,2,1,0:T(8,128)(2,1)}, bf16[4,2,4,64,128]{4,3,2,1,0:T(8,128)(2,1)S(1)}, u32[]{:S(2)}, u32[]{:S(2)}) collective-permute-start(bf16[4,2,4,64,128]{4,3,2,1,0:T(8,128)(2,1)} %get-tuple-element.53), channel_id=1, source_target_pairs={{0,4},{4,0},{8,12},{12,8},{16,20},{20,16},{24,28},{28,24},{1,5},{5... | collective-permute-start | bytes 1572872 | tf_op jit(solution)/shard_map/ppermute | solution.py:375
  74.9 0.7 copy-start
  82.2 7.6 %copy-start.8 = (f32[4,2,512]{2,1,0:T(2,128)}, f32[4,2,512]{2,1,0:T(2,128)S(1)}, u32[]{:S(2)}) copy-start(f32[4,2,512]{2,1,0:T(2,128)S(1)} %collective-permute-done.9.log_far) | copy-start | bytes 49156
  82.2 7.6 %copy-start.9 = (f32[4,2,512]{2,1,0:T(2,128)}, f32[4,2,512]{2,1,0:T(2,128)S(1)}, u32[]{:S(2)}) copy-start(f32[4,2,512]{2,1,0:T(2,128)S(1)} %collective-permute-done.8.log_near) | copy-start | bytes 49156
  82.2 2.3 %collective-permute-start.10 = (bf16[4,2,4,64,128]{4,3,2,1,0:T(8,128)(2,1)}, bf16[4,2,4,64,128]{4,3,2,1,0:T(8,128)(2,1)}, u32[]{:S(2)}, u32[]{:S(2)}) collective-permute-start(bf16[4,2,4,64,128]{4,3,2,1,0:T(8,128)(2,1)} %get-tuple-element.51), channel_id=1, source_target_pairs={{0,4},{4,0},{8,12},{12,8},{16,20},{20,16},{24,28},{28,24},{1,5},{5... | collective-permute-start | bytes 1572872 | tf_op jit(solution)/shard_map/ppermute | solution.py:375
  82.4 2.2 %copy-start.4 = (bf16[4,2,4,64,128]{4,3,2,1,0:T(8,128)(2,1)}, bf16[4,2,4,64,128]{4,3,2,1,0:T(8,128)(2,1)S(1)}, u32[]{:S(2)}) copy-start(bf16[4,2,4,64,128]{4,3,2,1,0:T(8,128)(2,1)S(1)} %collective-permute-done.11.got_sums) | copy-start | bytes 1572868
  87.1 9.8 %collective-permute-start.12 = (bf16[4,4,64,128]{3,2,1,0:T(8,128)(2,1)}, bf16[4,4,64,128]{3,2,1,0:T(8,128)(2,1)S(1)}, u32[]{:S(2)}, u32[]{:S(2)}) collective-permute-start(bf16[4,4,64,128]{3,2,1,0:T(8,128)(2,1)} %get-tuple-element.55), channel_id=1, source_target_pairs={{0,8},{4,12},{8,0},{12,4},{16,24},{20,28},{24,16},{28,20},{1,9},{5... | collective-permute-start | bytes 786440 | tf_op jit(solution)/shard_map/ppermute | solution.py:375
  88.4 8.6 %collective-permute-start.13 = (bf16[4,4,64,128]{3,2,1,0:T(8,128)(2,1)}, bf16[4,4,64,128]{3,2,1,0:T(8,128)(2,1)S(1)}, u32[]{:S(2)}, u32[]{:S(2)}) collective-permute-start(bf16[4,4,64,128]{3,2,1,0:T(8,128)(2,1)} %get-tuple-element.56), channel_id=1, source_target_pairs={{0,16},{4,20},{8,24},{12,28},{16,0},{20,4},{24,8},{28,12},{1,17},{... | collective-permute-start | bytes 786440 | tf_op jit(solution)/shard_map/ppermute | solution.py:375
  88.4 13.3 %collective-permute-start.14 = (bf16[4,4,64,128]{3,2,1,0:T(8,128)(2,1)}, bf16[4,4,64,128]{3,2,1,0:T(8,128)(2,1)S(1)}, u32[]{:S(2)}, u32[]{:S(2)}) collective-permute-start(bf16[4,4,64,128]{3,2,1,0:T(8,128)(2,1)} %get-tuple-element.57), channel_id=1, source_target_pairs={{0,24},{4,28},{8,16},{12,20},{16,8},{20,12},{24,0},{28,4},{1,25},{... | collective-permute-start | bytes 786440 | tf_op jit(solution)/shard_map/ppermute | solution.py:375
  96.9 4.7 %copy-start.5 = (bf16[4,4,64,128]{3,2,1,0:T(8,128)(2,1)}, bf16[4,4,64,128]{3,2,1,0:T(8,128)(2,1)S(1)}, u32[]{:S(2)}) copy-start(bf16[4,4,64,128]{3,2,1,0:T(8,128)(2,1)S(1)} %collective-permute-done.12.refs_1_) | copy-start | bytes 786436
  96.9 4.7 %copy-start.6 = (bf16[4,4,64,128]{3,2,1,0:T(8,128)(2,1)}, bf16[4,4,64,128]{3,2,1,0:T(8,128)(2,1)S(1)}, u32[]{:S(2)}) copy-start(bf16[4,4,64,128]{3,2,1,0:T(8,128)(2,1)S(1)} %collective-permute-done.13.refs_2_) | copy-start | bytes 786436
  101.6 0.7 copy-start.7

commit v4 on v2

--- a/solution.py
+++ b/solution.py
@@ -41,16 +41,12 @@
     return jnp.broadcast_to(row, (128, row.shape[1])).T[:, :1]
 
 
-def pack_keys_kernel(heads, k, v, kv, *refs):
-    parts, wide_rows = refs[:-1], refs[-1]
-    group = heads // len(parts)
+def pack_keys_kernel(heads, k, v, kv, wide_rows):
     toks = k.shape[0] // heads
     for number, source in enumerate((k, v)):
         wide_rows[number] = source[...].astype(F32)
         for head in range(heads):
-            rows = wide_rows[number, pl.ds(head, toks, stride=heads), :].astype(BF)
-            kv[number, head] = rows
-            parts[head // group][number, head % group] = rows
+            kv[number, head] = wide_rows[number, pl.ds(head, toks, stride=heads), :].astype(BF)
 
 
 def pack_queries_kernel(heads, slots, q, g, kv, pos_row, qd, slot_rows, wide_rows, acc):
@@ -184,23 +180,18 @@
     put_in_slots(expand[...], (out, dq), kept, sent)
 
 
-def local_kernel(scale, scale2, halves, group, qd, kv, *refs):
-    nears, fars, refs = refs[:halves], refs[halves : 2 * halves], refs[2 * halves :]
-    rows, bias, expand, before, out, log_dot, dq, dkv, kept, sent = refs[:-5]
-    keys, values, score_buf, probs, slopes = refs[-5:]
+def local_kernel(
+    scale, scale2, qd, kv, kv_near, kv_far, rows, bias, expand, before,
+    out, log_dot, dq, dkv, kept, sent, keys, values, score_buf, probs, slopes,
+):
     toks = kv.shape[2]
     reach = 2 * HALF + TILE
     span = keys.shape[0] - rows.shape[2]
     near = 2 * (1 - lax.axis_index("ctx") % 2)
-    for part in range(halves):
-
-        @pl.when(pl.program_id(0) // group == part)
-        def _():
-            for block, place in ((nears[part], near), (kv, 1), (fars[part], 2 - near)):
-                spot = pl.ds(pl.multiple_of(place * toks, toks), toks)
-                keys[spot, :] = block[0, 0]
-                values[spot, :] = block[1, 0]
-
+    for block, place in ((kv_near, near), (kv, 1), (kv_far, 2 - near)):
+        spot = pl.ds(pl.multiple_of(place * toks, toks), toks)
+        keys[spot, :] = block[0, 0]
+        values[spot, :] = block[1, 0]
     keys[span:, :] = rows[1, 0]
     values[span:, :] = rows[2, 0]
     key_t, value_t = keys[...].T, values[...].T
@@ -399,12 +390,9 @@
     flat_spec = pl.BlockSpec((toks * heads // steps, width), lambda i: (i, 0))
     pair_spec = pl.BlockSpec((2, heads, toks // steps, width), lambda i: (0, 0, i, 0))
     wide_pair = pltpu.VMEM((2, toks * heads // steps, width), F32)
-    halves = 2 if heads % 2 == 0 else 1
-    group = heads // halves
-    part_shape = (2, group, toks, width)
-    kv, *kv_parts = pl.pallas_call(
+    kv = pl.pallas_call(
         functools.partial(pack_keys_kernel, heads),
-        out_shape=[struct(pair_shape, BF)] + [struct(part_shape, BF)] * halves,
+        out_shape=struct(pair_shape, BF),
         scratch_shapes=[wide_pair],
         compiler_params=params(),
         name="pack_keys",
@@ -434,18 +422,13 @@
         name="masks",
     )(pos_row)
 
-    nears, fars = [], []
-    for part in kv_parts:
-        if fars:
-            part = after(part, (nears[-1], fars[-1]))
-        fars.append(from_far(part))
-        nears.append(from_near(part))
     held = [slot_rows[None]]
-    for stage in stages:
-        send = jnp.concatenate(held, axis=0) if len(held) > 1 else held[0]
-        if stage == [1]:
-            send = after(send, (nears[0], fars[0], place))
+    for number, stage in enumerate(stages):
+        send = jnp.concatenate(held, axis=0) if number else held[0]
         held += [swap(send, mask) for mask in stage]
+        if not number:
+            kv_late = after(kv, (held, place))
+            kv_far, kv_near = from_far(kv_late), from_near(kv_late)
 
     row_shape = (4, heads, count, width)
     rows, stats = pl.pallas_call(
@@ -461,10 +444,7 @@
         name="global_stats",
     )(compact, *held, kv)
 
-    kv_done = (nears, fars)
     stats = lax.all_to_all(stats, "ctx", 0, 0, tiled=True)
-    qd_late = after(qd, (kv_done, stats))
-    qd_far, qd_near = from_far(qd_late), from_near(qd_late)
 
     sum_shape = (devices // 2, 2, heads, slots, width)
     sum_struct = struct(sum_shape, BF)
@@ -480,17 +460,13 @@
         name="global_queries",
     )(kv, rows, stats, expand)
     got_ends = from_near(sent_ends)
-
-    def half_head(part):
-        return pl.BlockSpec(
-            (2, 1, toks, width), lambda head: (0, jnp.clip(head - part * group, 0, group - 1), 0, 0)
-        )
+    qd_late = after(qd, (kv_near, kv_far, sent_ends))
+    qd_far, qd_near = from_far(qd_late), from_near(qd_late)
 
     out, log_dot, dq, dkv, kept_sums, sent_sums = pl.pallas_call(
-        functools.partial(local_kernel, scale, scale2, halves, group),
+        functools.partial(local_kernel, scale, scale2),
         grid=(heads,),
-        in_specs=[per_head(pair_shape, 1)] * 2
-        + [half_head(part) for part in range(halves)] * 2
+        in_specs=[per_head(pair_shape, 1)] * 4
         + [per_head(row_shape, 1), whole(bias.shape), whole(expand.shape)]
         + [per_head(pair_shape, 1)],
         out_specs=(
@@ -519,18 +495,18 @@
         compiler_params=params(),
         cost_estimate=cost(1e6, 1e6),
         name="local",
-    )(qd, kv, *nears, *fars, rows, bias, expand, extra)
+    )(qd, kv, kv_near, kv_far, rows, bias, expand, extra)
     log_far, log_near = from_far(log_dot), from_near(log_dot)
 
     got_sums = from_near(sent_sums)
+
     first = stages[0]
-    halos = (qd_near, qd_far, log_near, log_far)
     parts = pl.pallas_call(
         fold_kernel,
         out_shape=[struct((4, heads, slots, width), BF)] * (devices // 2),
         compiler_params=params(),
         name="fold",
-    )(kept_ends, got_ends, kept_sums, after(got_sums, halos))
+    )(kept_ends, got_ends, kept_sums, after(got_sums, (qd_near, qd_far)))
     for stage in reversed(stages[1:-1]):
         size = len(parts) // (len(stage) + 1)
         kept = parts[:size]
@@ -538,7 +514,8 @@
             sent = parts[(number + 1) * size : (number + 2) * size]
             kept = [one + swap(other, mask) for one, other in zip(kept, sent)]
         parts = kept
-    parts = [parts[0]] + [swap(part, mask) for part, mask in zip(parts[1:], first)]
+    sent = after(parts[1:], (log_near, log_far))
+    parts = [parts[0]] + [swap(part, mask) for part, mask in zip(sent, first)]
 
     dkv = pl.pallas_call(
         functools.partial(rim_kernel, scale, scale2),

time: 111 us -> 116 us (1.045)
  blocking collectives: 0 us -> 20.6 us
  starting transfers between devices: 32 us -> 19.7 us
  waiting for transfers between devices: 25.2 us -> 22.7 us
    all_to_all x0 -> x1, blocking collectives: none -> 20.6 us  [shards(): stats = lax.all_to_all(stats, 'ctx', 0, 0, tiled=True)]
    ppermute x4 -> x3, starting transfers between devices: 19.1 us -> 9.61 us  [from_far(): return lax.ppermute(value, 'ctx', pairs + [(j, i) for i, j in pairs])]
    all_to_all x1 -> x0, starting transfers between devices: 3.36 us -> none  [shards(): stats = lax.all_to_all(stats, 'ctx', 0, 0, tiled=True)]
    ppermute x4 -> x3, waiting for transfers between devices: 5.66 us -> 4.01 us  [from_far(): return lax.ppermute(value, 'ctx', pairs + [(j, i) for i, j in pairs])]
    ppermute x13 -> x12, starting transfers between devices: 9.49 us -> 10.1 us  [swap(): return lax.ppermute(value, 'ctx', [(i, i ^ mask) for i in range(devices)])]
    ppermute x13 -> x12, waiting for transfers between devices: 18.5 us -> 18.7 us  [swap(): return lax.ppermute(value, 'ctx', [(i, i ^ mask) for i in range(devices)])]
  transfers between devices with their start and end apart: 18 -> 15, of which waited for: 6 -> 6; matrix products, arithmetic and copies ran while one was open for 1% -> 0% of each run, Pallas kernels for 36% -> 33%
where the time goes in v4:
time: 116 us; the launch traced here: 115 us
  Pallas kernels  48.2 us (42%)
  waiting for transfers between devices  22.7 us (20%)
  blocking collectives  20.6 us (18%)
  starting transfers between devices  19.7 us (17%)
  other arithmetic  2.14 us (2%)
    all_to_all x1, blocking collectives, shards(): stats = lax.all_to_all(stats, 'ctx', 0, 0, tiled=True)  20.6 us
    ppermute x12, waiting for transfers between devices, swap(): return lax.ppermute(value, 'ctx', [(i, i ^ mask) for i in range(devices)])  18.7 us
    pallas_call x1, Pallas kernels, shards(): pl.pallas_call(functools.partial(local_kernel, scale, scale2), grid=(head...  14.5 us
    ppermute x12, starting transfers between devices, swap(): return lax.ppermute(value, 'ctx', [(i, i ^ mask) for i in range(devices)])  10.1 us
    ppermute x3, starting transfers between devices, from_far(): return lax.ppermute(value, 'ctx', pairs + [(j, i) for i, j in pairs])  9.61 us
    pallas_call x1, Pallas kernels, shards(): pl.pallas_call(functools.partial(rim_kernel, scale, scale2), grid=(heads,...  7.18 us
    pallas_call x1, Pallas kernels, shards(): pl.pallas_call(functools.partial(global_kernel, scale, scale2), grid=(hea...  6.2 us
    pallas_call x1, Pallas kernels, shards(): pl.pallas_call(functools.partial(stats_kernel, scale2), grid=(heads,), in...  5.54 us
  transfers between devices with their start and end apart: 15, of which 6 were waited for; matrix products, arithmetic and copies ran while one was open for 0% of the time, Pallas kernels for 33%

profile of v4, /device:TPU:1, one launch (start us, length us, event | category | flops | bytes accessed | tf_op | source)
XLA Modules:
  0.0 114.8 jit_solution(6919244122287097792)
XLA Ops:
  0.6 2.4 %pack_keys.1.kv.refs_5_ = bf16[2,4,512,128]{3,2,1,0:T(8,128)(2,1)} custom-call(bf16[2048,128]{1,0:T(8,128)(2,1)} %bitcast.15, bf16[2048,128]{1,0:T(8,128)(2,1)} %bitcast.16), custom_call_target="tpu_custom_call" | custom-call | tf_op jit(solution)/shard_map/pack_keys/pallas_call | solution.py:393
  3.1 3.4 %pack_queries.1 = (bf16[2,4,512,128]{3,2,1,0:T(8,128)(2,1)}, bf16[4,4,64,128]{3,2,1,0:T(8,128)(2,1)}) custom-call(bf16[2048,128]{1,0:T(8,128)(2,1)} %bitcast.17, bf16[2048,128]{1,0:T(8,128)(2,1)} %bitcast.18, bf16[2,4,512,128]{3,2,1,0:T(8,128)(2,1)} %pack_keys.1.kv.refs_5_, s32[1,256]{1,0:T(1,128)} %bitcast.19), custom_call_target="tpu_custom_call" | custom-call | tf_op jit(solution)/shard_map/pack_queries/pallas_call | solution.py:401
  6.5 2.0 %collective-permute-start = (bf16[1,4,4,64,128]{4,3,2,1,0:T(8,128)(2,1)}, bf16[1,4,4,64,128]{4,3,2,1,0:T(8,128)(2,1)S(1)}, u32[]{:S(2)}, u32[]{:S(2)}) collective-permute-start(bf16[1,4,4,64,128]{4,3,2,1,0:T(8,128)(2,1)} %bitcast.10), channel_id=1, source_target_pairs={{0,8},{4,12},{8,0},{12,4},{16,24},{20,28},{24,16},{28,20},{1,9},{5... | collective-permute-start | bytes 786440 | tf_op jit(solution)/shard_map/ppermute | solution.py:375
  8.5 1.2 %collective-permute-start.1 = (bf16[1,4,4,64,128]{4,3,2,1,0:T(8,128)(2,1)}, bf16[1,4,4,64,128]{4,3,2,1,0:T(8,128)(2,1)S(1)}, u32[]{:S(2)}, u32[]{:S(2)}) collective-permute-start(bf16[1,4,4,64,128]{4,3,2,1,0:T(8,128)(2,1)} %bitcast.11), channel_id=1, source_target_pairs={{0,16},{4,20},{8,24},{12,28},{16,0},{20,4},{24,8},{28,12},{1,17},{... | collective-permute-start | bytes 786440 | tf_op jit(solution)/shard_map/ppermute | solution.py:375
  9.8 0.0 collective-permute-start.2
  9.8 5.0 %collective-permute-done.refs_1_ = bf16[1,4,4,64,128]{4,3,2,1,0:T(8,128)(2,1)S(1)} collective-permute-done((bf16[1,4,4,64,128]{4,3,2,1,0:T(8,128)(2,1)}, bf16[1,4,4,64,128]{4,3,2,1,0:T(8,128)(2,1)S(1)}, u32[]{:S(2)}, u32[]{:S(2)}) %collective-permute-start) | collective-permute-done | bytes 262176 | tf_op jit(solution)/shard_map/ppermute | solution.py:375
  14.8 0.8 collective-permute-done.1.refs_2_
  15.6 5.7 %collective-permute-done.2.refs_3_ = bf16[1,4,4,64,128]{4,3,2,1,0:T(8,128)(2,1)S(1)} collective-permute-done((bf16[1,4,4,64,128]{4,3,2,1,0:T(8,128)(2,1)}, bf16[1,4,4,64,128]{4,3,2,1,0:T(8,128)(2,1)S(1)}, u32[]{:S(2)}, u32[]{:S(2)}) %collective-permute-start.2) | collective-permute-done | bytes 262176 | tf_op jit(solution)/shard_map/ppermute | solution.py:375
  21.3 2.1 %pad_maximum_fusion = bf16[4,4,4,64,128]{4,3,2,1,0:T(8,128)(2,1)} fusion(bf16[1,4,4,64,128]{4,3,2,1,0:T(8,128)(2,1)S(1)} %collective-permute-done.2.refs_3_, bf16[1,4,4,64,128]{4,3,2,1,0:T(8,128)(2,1)S(1)} %collective-permute-done.1.refs_2_, bf16[1,4,4,64,128]{4,3,2,1,0:T(8,128)(2,1)S(1)} %collective-permute-done.refs_1_, bf16[1,4,4,64,128]{4,3,2,1,0:T(8,128)(2,1)} %bitcast.13), kind=kLoop, calls=%fused_computation | loop fusion | flops 1572864 | bytes 2097152 | tf_op jit(solution)/shard_map/concatenate | solution.py:427
  23.5 1.8 %collective-permute-start.5 = (bf16[4,4,4,64,128]{4,3,2,1,0:T(8,128)(2,1)}, bf16[4,4,4,64,128]{4,3,2,1,0:T(8,128)(2,1)}, u32[]{:S(2)}, u32[]{:S(2)}) collective-permute-start(bf16[4,4,4,64,128]{4,3,2,1,0:T(8,128)(2,1)} %pad_maximum_fusion), channel_id=1, source_target_pairs={{0,4},{4,0},{8,12},{12,8},{16,20},{20,16},{24,28},{28,24},{1,5},{5... | collective-permute-start | bytes 3145736 | tf_op jit(solution)/shard_map/ppermute | solution.py:375
  25.3 2.2 %masks.1 = (f32[1536,128]{1,0:T(8,128)}, bf16[256,512]{1,0:T(8,128)(2,1)}, bf16[512,256]{1,0:T(8,128)(2,1)}, bf16[512,64]{1,0:T(8,128)(2,1)}) custom-call(s32[1,256]{1,0:T(1,128)} %bitcast.20), custom_call_target="tpu_custom_call" | custom-call | tf_op jit(solution)/shard_map/masks/pallas_call | solution.py:413
  27.5 0.0 collective-permute-start.3
  27.5 3.2 %collective-permute-start.4 = (bf16[2,4,512,128]{3,2,1,0:T(8,128)(2,1)}, bf16[2,4,512,128]{3,2,1,0:T(8,128)(2,1)}, u32[]{:S(2)}, u32[]{:S(2)}) collective-permute-start(bf16[2,4,512,128]{3,2,1,0:T(8,128)(2,1)} %pack_keys.1.kv.refs_5_), channel_id=1, source_target_pairs={{4,8},{12,16},{20,24},{8,4},{16,12},{24,20},{5,9},{13,17},{21,25},... | collective-permute-start | bytes 3145736 | tf_op jit(solution)/shard_map/ppermute | solution.py:382
  30.7 0.0 collective-permute-done.5.refs_4_
  30.7 0.0 copy-done
  30.7 0.0 copy-done.1
  30.8 5.5 %global_stats.1 = (bf16[4,4,256,128]{3,2,1,0:T(8,128)(2,1)}, f32[8,4,8,256]{3,2,1,0:T(8,128)}) custom-call(bf16[256,512]{1,0:T(8,128)(2,1)} %get-tuple-element.39.compact, bf16[1,4,4,64,128]{4,3,2,1,0:T(8,128)(2,1)} %bitcast.14, bf16[1,4,4,64,128]{4,3,2,1,0:T(8,128)(2,1)} %copy-done, bf16[1,4,4,64,128]{4,3,2,1,0:T(8,128)(2,1)} %copy-done.1, ...), custom_call_target="tpu_custom_call" | custom-call | flops 1000000 | bytes 1000000 | tf_op jit(solution)/shard_map/global_stats/pallas_call | solution.py:434
  36.3 20.6 %all_to_all.5.stats = f32[8,4,8,256]{3,2,1,0:T(8,128)} all-to-all(f32[8,4,8,256]{3,2,1,0:T(8,128)} %get-tuple-element.43), channel_id=1, replica_groups=mesh['ctx'=8,'head'=4] {'ctx'}, dimensions={0} | all-to-all | bytes 524288 | tf_op jit(solution)/shard_map/all_to_all | solution.py:447
  56.9 6.2 %global_queries.1 = (f32[2,4,512,128]{3,2,1,0:T(8,128)}, bf16[4,2,4,64,128]{4,3,2,1,0:T(8,128)(2,1)}, bf16[4,2,4,64,128]{4,3,2,1,0:T(8,128)(2,1)}) custom-call(bf16[2,4,512,128]{3,2,1,0:T(8,128)(2,1)} %pack_keys.1.kv.refs_5_, bf16[4,4,256,128]{3,2,1,0:T(8,128)(2,1)} %get-tuple-element.40.rows, f32[8,4,8,256]{3,2,1,0:T(8,128)} %all_to_all.5.stats, ...), custom_call_target="tpu_custom_call" | custom-call | flops 1000000 | bytes 1000000 | tf_op jit(solution)/shard_map/global_queries/pallas_call | solution.py:451
  63.1 0.0 collective-permute-done.3.kv_near
  63.1 0.0 collective-permute-done.4.kv_far
  63.1 1.5 %collective-permute-start.6 = (bf16[2,4,512,128]{3,2,1,0:T(8,128)(2,1)}, bf16[2,4,512,128]{3,2,1,0:T(8,128)(2,1)}, u32[]{:S(2)}, u32[]{:S(2)}) collective-permute-start(bf16[2,4,512,128]{3,2,1,0:T(8,128)(2,1)} %get-tuple-element.48.qd), channel_id=1, source_target_pairs={{0,4},{4,0},{8,12},{12,8},{16,20},{20,16},{24,28},{28,24},{1,5},{5... | collective-permute-start | bytes 3145736 | tf_op jit(solution)/shard_map/ppermute | solution.py:375
  64.6 2.8 %collective-permute-start.7 = (bf16[2,4,512,128]{3,2,1,0:T(8,128)(2,1)}, bf16[2,4,512,128]{3,2,1,0:T(8,128)(2,1)}, u32[]{:S(2)}, u32[]{:S(2)}) collective-permute-start(bf16[2,4,512,128]{3,2,1,0:T(8,128)(2,1)} %get-tuple-element.48.qd), channel_id=1, source_target_pairs={{4,8},{12,16},{20,24},{8,4},{16,12},{24,20},{5,9},{13,17},{21,25},... | collective-permute-start | bytes 3145736 | tf_op jit(solution)/shard_map/ppermute | solution.py:382
  67.5 14.5 %local.1 = (bf16[4,512,128]{2,1,0:T(8,128)(2,1)}, f32[4,2,512]{2,1,0:T(2,128)}, f32[4,512,128]{2,1,0:T(8,128)}, f32[2,4,512,128]{3,2,1,0:T(8,128)}, bf16[4,2,4,6...) custom-call(bf16[2,4,512,128]{3,2,1,0:T(8,128)(2,1)} %get-tuple-element.48.qd, ...), custom_call_target="tpu_custom_call" | custom-call | flops 1000000 | bytes 1000000 | tf_op jit(solution)/shard_map/local/pallas_call | solution.py:466
  81.9 0.1 collective-permute-start.11
  82.0 0.5 collective-permute-start.10
  82.5 0.1 collective-permute-start.8
  82.6 1.5 %collective-permute-done.11.got_sums = bf16[4,2,4,64,128]{4,3,2,1,0:T(8,128)(2,1)S(1)} collective-permute-done((bf16[4,2,4,64,128]{4,3,2,1,0:T(8,128)(2,1)}, bf16[4,2,4,64,128]{4,3,2,1,0:T(8,128)(2,1)S(1)}, u32[]{:S(2)}, u32[]{:S(2)}) %collective-permute-start.11) | collective-permute-done | bytes 524320 | tf_op jit(solution)/shard_map/ppermute | solution.py:375
  84.1 3.6 %collective-permute-start.9 = (f32[4,2,512]{2,1,0:T(2,128)}, f32[4,2,512]{2,1,0:T(2,128)S(1)}, u32[]{:S(2)}, u32[]{:S(2)}) collective-permute-start(f32[4,2,512]{2,1,0:T(2,128)} %get-tuple-element.49), channel_id=1, source_target_pairs={{4,8},{12,16},{20,24},{8,4},{16,12},{24,20},{5,9},{13,17},{21,25},... | collective-permute-start | bytes 49160 | tf_op jit(solution)/shard_map/ppermute | solution.py:382
  87.7 0.0 collective-permute-done.6.qd_near
  87.7 4.0 %collective-permute-done.7.qd_far = bf16[2,4,512,128]{3,2,1,0:T(8,128)(2,1)} collective-permute-done((bf16[2,4,512,128]{3,2,1,0:T(8,128)(2,1)}, bf16[2,4,512,128]{3,2,1,0:T(8,128)(2,1)}, u32[]{:S(2)}, u32[]{:S(2)}) %collective-permute-start.7) | collective-permute-done | bytes 1048608 | tf_op jit(solution)/shard_map/ppermute | solution.py:382
  91.7 0.0 collective-permute-done.10.got_ends
  91.8 0.0 copy-done.3
  91.8 2.5 %fold.1 = (bf16[4,4,64,128]{3,2,1,0:T(8,128)(2,1)}, bf16[4,4,64,128]{3,2,1,0:T(8,128)(2,1)}, bf16[4,4,64,128]{3,2,1,0:T(8,128)(2,1)}, bf16[4,4,64,128]{3,2,1,0:T(8,128)(2,1)}) custom-call(bf16[4,2,4,64,128]{4,3,2,1,0:T(8,128)(2,1)} %get-tuple-element.51.kept_ends, bf16[4,2,4,64,128]{4,3,2,1,0:T(8,128)(2,1)} %collective-permute-done.10.got_ends, ...), custom_call_target="tpu_custom_call" | custom-call | tf_op jit(solution)/shard_map/fold/pallas_call | solution.py:504
  94.3 0.0 collective-permute-done.8.log_near
  94.3 0.0 collective-permute-done.9.log_far
  94.3 0.0 copy-start.8
  94.3 1.5 %collective-permute-start.12 = (bf16[4,4,64,128]{3,2,1,0:T(8,128)(2,1)}, bf16[4,4,64,128]{3,2,1,0:T(8,128)(2,1)S(1)}, u32[]{:S(2)}, u32[]{:S(2)}) collective-permute-start(bf16[4,4,64,128]{3,2,1,0:T(8,128)(2,1)} %get-tuple-element.59), channel_id=1, source_target_pairs={{0,8},{4,12},{8,0},{12,4},{16,24},{20,28},{24,16},{28,20},{1,9},{5... | collective-permute-start | bytes 786440 | tf_op jit(solution)/shard_map/ppermute | solution.py:375
  95.8 0.0 collective-permute-start.13
  95.8 1.3 %collective-permute-start.14 = (bf16[4,4,64,128]{3,2,1,0:T(8,128)(2,1)}, bf16[4,4,64,128]{3,2,1,0:T(8,128)(2,1)S(1)}, u32[]{:S(2)}, u32[]{:S(2)}) collective-permute-start(bf16[4,4,64,128]{3,2,1,0:T(8,128)(2,1)} %get-tuple-element.61), channel_id=1, source_target_pairs={{0,24},{4,28},{8,16},{12,20},{16,8},{20,12},{24,0},{28,4},{1,25},{... | collective-permute-start | bytes 786440 | tf_op jit(solution)/shard_map/ppermute | solution.py:375
  97.1 7.2 %rim.1.dkv = f32[2,4,512,128]{3,2,1,0:T(8,128)} custom-call(bf16[2,4,512,128]{3,2,1,0:T(8,128)(2,1)} %pack_keys.1.kv.refs_5_, f32[1536,128]{1,0:T(8,128)} %get-tuple-element.41.bias, bf16[2,4,512,128]{3,2,1,0:T(8,128)(2,1)} %collective-permute-done.6.qd_near, bf16[2,4,512,128]{3,2,1,0:T(8,128)(2,1)} %collective-permute-done.7.qd_far, ...), custom_call_target="tpu_custom_call" | custom-call | flops 1000000 | bytes 1000000 | tf_op jit(solution)/shard_map/rim/pallas_call | solution.py:520
  104.2 0.0 collective-permute-done.12.refs_1_
  104.2 0.0 copy-start.4
  104.3 5.6 %collective-permute-done.13.refs_2_ = bf16[4,4,64,128]{3,2,1,0:T(8,128)(2,1)S(1)} collective-permute-done((bf16[4,4,64,128]{3,2,1,0:T(8,128)(2,1)}, bf16[4,4,64,128]{3,2,1,0:T(8,128)(2,1)S(1)}, u32[]{:S(2)}, u32[]{:S(2)}) %collective-permute-start.13) | collective-permute-done | bytes 262176 | tf_op jit(solution)/shard_map/ppermute | solution.py:375
  109.9 0.0 collective-permute-done.14.refs_3_
  109.9 0.7 copy-done.5
  110.6 0.1 copy-done.6
  110.7 4.2 %final.1 = (bf16[2048,128]{1,0:T(8,128)(2,1)}, f32[2048,128]{1,0:T(8,128)}, f32[2048,128]{1,0:T(8,128)}, f32[2048,128]{1,0:T(8,128)}) custom-call(bf16[512,64]{1,0:T(8,128)(2,1)} %get-tuple-element.35.place, bf16[4,512,128]{2,1,0:T(8,128)(2,1)} %get-tuple-element.45.out, f32[4,512,128]{2,1,0:T(8,128)} %get-tuple-element.46.dq, f32[2,4,512,128]{3,2,1,0:T(8,128)} %rim.1.dkv, ...), custom_call_target="tpu_custom_call" | custom-call | tf_op jit(solution)/shard_map/final/pallas_call | solution.py:543
  (11 shorter events, 0.0 us)
Async XLA Ops:
  6.5 8.3 %collective-permute-start = (bf16[1,4,4,64,128]{4,3,2,1,0:T(8,128)(2,1)}, bf16[1,4,4,64,128]{4,3,2,1,0:T(8,128)(2,1)S(1)}, u32[]{:S(2)}, u32[]{:S(2)}) collective-permute-start(bf16[1,4,4,64,128]{4,3,2,1,0:T(8,128)(2,1)} %bitcast.10), channel_id=1, source_target_pairs={{0,8},{4,12},{8,0},{12,4},{16,24},{20,28},{24,16},{28,20},{1,9},{5... | collective-permute-start | bytes 786440 | tf_op jit(solution)/shard_map/ppermute | solution.py:375
  8.5 7.1 %collective-permute-start.1 = (bf16[1,4,4,64,128]{4,3,2,1,0:T(8,128)(2,1)}, bf16[1,4,4,64,128]{4,3,2,1,0:T(8,128)(2,1)S(1)}, u32[]{:S(2)}, u32[]{:S(2)}) collective-permute-start(bf16[1,4,4,64,128]{4,3,2,1,0:T(8,128)(2,1)} %bitcast.11), channel_id=1, source_target_pairs={{0,16},{4,20},{8,24},{12,28},{16,0},{20,4},{24,8},{28,12},{1,17},{... | collective-permute-start | bytes 786440 | tf_op jit(solution)/shard_map/ppermute | solution.py:375
  9.8 11.5 %collective-permute-start.2 = (bf16[1,4,4,64,128]{4,3,2,1,0:T(8,128)(2,1)}, bf16[1,4,4,64,128]{4,3,2,1,0:T(8,128)(2,1)S(1)}, u32[]{:S(2)}, u32[]{:S(2)}) collective-permute-start(bf16[1,4,4,64,128]{4,3,2,1,0:T(8,128)(2,1)} %bitcast.12), channel_id=1, source_target_pairs={{0,24},{4,28},{8,16},{12,20},{16,8},{20,12},{24,0},{28,4},{1,25},{... | collective-permute-start | bytes 786440 | tf_op jit(solution)/shard_map/ppermute | solution.py:375
  14.8 15.9 %copy-start = (bf16[1,4,4,64,128]{4,3,2,1,0:T(8,128)(2,1)}, bf16[1,4,4,64,128]{4,3,2,1,0:T(8,128)(2,1)S(1)}, u32[]{:S(2)}) copy-start(bf16[1,4,4,64,128]{4,3,2,1,0:T(8,128)(2,1)S(1)} %collective-permute-done.refs_1_) | copy-start | bytes 786436
  15.6 15.1 %copy-start.1 = (bf16[1,4,4,64,128]{4,3,2,1,0:T(8,128)(2,1)}, bf16[1,4,4,64,128]{4,3,2,1,0:T(8,128)(2,1)S(1)}, u32[]{:S(2)}) copy-start(bf16[1,4,4,64,128]{4,3,2,1,0:T(8,128)(2,1)S(1)} %collective-permute-done.1.refs_2_) | copy-start | bytes 786436
  21.3 9.4 %copy-start.2 = (bf16[1,4,4,64,128]{4,3,2,1,0:T(8,128)(2,1)}, bf16[1,4,4,64,128]{4,3,2,1,0:T(8,128)(2,1)S(1)}, u32[]{:S(2)}) copy-start(bf16[1,4,4,64,128]{4,3,2,1,0:T(8,128)(2,1)S(1)} %collective-permute-done.2.refs_3_) | copy-start | bytes 786436
  23.5 7.2 %collective-permute-start.5 = (bf16[4,4,4,64,128]{4,3,2,1,0:T(8,128)(2,1)}, bf16[4,4,4,64,128]{4,3,2,1,0:T(8,128)(2,1)}, u32[]{:S(2)}, u32[]{:S(2)}) collective-permute-start(bf16[4,4,4,64,128]{4,3,2,1,0:T(8,128)(2,1)} %pad_maximum_fusion), channel_id=1, source_target_pairs={{0,4},{4,0},{8,12},{12,8},{16,20},{20,16},{24,28},{28,24},{1,5},{5... | collective-permute-start | bytes 3145736 | tf_op jit(solution)/shard_map/ppermute | solution.py:375
  27.5 35.5 %collective-permute-start.3 = (bf16[2,4,512,128]{3,2,1,0:T(8,128)(2,1)}, bf16[2,4,512,128]{3,2,1,0:T(8,128)(2,1)}, u32[]{:S(2)}, u32[]{:S(2)}) collective-permute-start(bf16[2,4,512,128]{3,2,1,0:T(8,128)(2,1)} %pack_keys.1.kv.refs_5_), channel_id=1, source_target_pairs={{0,4},{4,0},{8,12},{12,8},{16,20},{20,16},{24,28},{28,24},{1,5},{5... | collective-permute-start | bytes 3145736 | tf_op jit(solution)/shard_map/ppermute | solution.py:375
  27.5 35.5 %collective-permute-start.4 = (bf16[2,4,512,128]{3,2,1,0:T(8,128)(2,1)}, bf16[2,4,512,128]{3,2,1,0:T(8,128)(2,1)}, u32[]{:S(2)}, u32[]{:S(2)}) collective-permute-start(bf16[2,4,512,128]{3,2,1,0:T(8,128)(2,1)} %pack_keys.1.kv.refs_5_), channel_id=1, source_target_pairs={{4,8},{12,16},{20,24},{8,4},{16,12},{24,20},{5,9},{13,17},{21,25},... | collective-permute-start | bytes 3145736 | tf_op jit(solution)/shard_map/ppermute | solution.py:382
  63.1 24.7 %collective-permute-start.6 = (bf16[2,4,512,128]{3,2,1,0:T(8,128)(2,1)}, bf16[2,4,512,128]{3,2,1,0:T(8,128)(2,1)}, u32[]{:S(2)}, u32[]{:S(2)}) collective-permute-start(bf16[2,4,512,128]{3,2,1,0:T(8,128)(2,1)} %get-tuple-element.48.qd), channel_id=1, source_target_pairs={{0,4},{4,0},{8,12},{12,8},{16,20},{20,16},{24,28},{28,24},{1,5},{5... | collective-permute-start | bytes 3145736 | tf_op jit(solution)/shard_map/ppermute | solution.py:375
  64.6 27.1 %collective-permute-start.7 = (bf16[2,4,512,128]{3,2,1,0:T(8,128)(2,1)}, bf16[2,4,512,128]{3,2,1,0:T(8,128)(2,1)}, u32[]{:S(2)}, u32[]{:S(2)}) collective-permute-start(bf16[2,4,512,128]{3,2,1,0:T(8,128)(2,1)} %get-tuple-element.48.qd), channel_id=1, source_target_pairs={{4,8},{12,16},{20,24},{8,4},{16,12},{24,20},{5,9},{13,17},{21,25},... | collective-permute-start | bytes 3145736 | tf_op jit(solution)/shard_map/ppermute | solution.py:382
  81.9 2.2 %collective-permute-start.11 = (bf16[4,2,4,64,128]{4,3,2,1,0:T(8,128)(2,1)}, bf16[4,2,4,64,128]{4,3,2,1,0:T(8,128)(2,1)S(1)}, u32[]{:S(2)}, u32[]{:S(2)}) collective-permute-start(bf16[4,2,4,64,128]{4,3,2,1,0:T(8,128)(2,1)} %get-tuple-element.53), channel_id=1, source_target_pairs={{0,4},{4,0},{8,12},{12,8},{16,20},{20,16},{24,28},{28,24},{1,5},{5... | collective-permute-start | bytes 1572872 | tf_op jit(solution)/shard_map/ppermute | solution.py:375
  82.0 9.7 %collective-permute-start.10 = (bf16[4,2,4,64,128]{4,3,2,1,0:T(8,128)(2,1)}, bf16[4,2,4,64,128]{4,3,2,1,0:T(8,128)(2,1)}, u32[]{:S(2)}, u32[]{:S(2)}) collective-permute-start(bf16[4,2,4,64,128]{4,3,2,1,0:T(8,128)(2,1)} %get-tuple-element.47), channel_id=1, source_target_pairs={{0,4},{4,0},{8,12},{12,8},{16,20},{20,16},{24,28},{28,24},{1,5},{5... | collective-permute-start | bytes 1572872 | tf_op jit(solution)/shard_map/ppermute | solution.py:375
  82.5 11.8 %collective-permute-start.8 = (f32[4,2,512]{2,1,0:T(2,128)}, f32[4,2,512]{2,1,0:T(2,128)S(1)}, u32[]{:S(2)}, u32[]{:S(2)}) collective-permute-start(f32[4,2,512]{2,1,0:T(2,128)} %get-tuple-element.49), channel_id=1, source_target_pairs={{0,4},{4,0},{8,12},{12,8},{16,20},{20,16},{24,28},{28,24},{1,5},{5... | collective-permute-start | bytes 49160 | tf_op jit(solution)/shard_map/ppermute | solution.py:375
  84.1 7.6 %copy-start.3 = (bf16[4,2,4,64,128]{4,3,2,1,0:T(8,128)(2,1)}, bf16[4,2,4,64,128]{4,3,2,1,0:T(8,128)(2,1)S(1)}, u32[]{:S(2)}) copy-start(bf16[4,2,4,64,128]{4,3,2,1,0:T(8,128)(2,1)S(1)} %collective-permute-done.11.got_sums) | copy-start | bytes 1572868
  84.1 10.2 %collective-permute-start.9 = (f32[4,2,512]{2,1,0:T(2,128)}, f32[4,2,512]{2,1,0:T(2,128)S(1)}, u32[]{:S(2)}, u32[]{:S(2)}) collective-permute-start(f32[4,2,512]{2,1,0:T(2,128)} %get-tuple-element.49), channel_id=1, source_target_pairs={{4,8},{12,16},{20,24},{8,4},{16,12},{24,20},{5,9},{13,17},{21,25},... | collective-permute-start | bytes 49160 | tf_op jit(solution)/shard_map/ppermute | solution.py:382
  94.3 2.8 %copy-start.7 = (f32[4,2,512]{2,1,0:T(2,128)}, f32[4,2,512]{2,1,0:T(2,128)S(1)}, u32[]{:S(2)}) copy-start(f32[4,2,512]{2,1,0:T(2,128)S(1)} %collective-permute-done.8.log_near) | copy-start | bytes 49156
  94.3 2.8 %copy-start.8 = (f32[4,2,512]{2,1,0:T(2,128)}, f32[4,2,512]{2,1,0:T(2,128)S(1)}, u32[]{:S(2)}) copy-start(f32[4,2,512]{2,1,0:T(2,128)S(1)} %collective-permute-done.9.log_far) | copy-start | bytes 49156
  94.3 9.9 %collective-permute-start.12 = (bf16[4,4,64,128]{3,2,1,0:T(8,128)(2,1)}, bf16[4,4,64,128]{3,2,1,0:T(8,128)(2,1)S(1)}, u32[]{:S(2)}, u32[]{:S(2)}) collective-permute-start(bf16[4,4,64,128]{3,2,1,0:T(8,128)(2,1)} %get-tuple-element.59), channel_id=1, source_target_pairs={{0,8},{4,12},{8,0},{12,4},{16,24},{20,28},{24,16},{28,20},{1,9},{5... | collective-permute-start | bytes 786440 | tf_op jit(solution)/shard_map/ppermute | solution.py:375
  95.8 14.1 %collective-permute-start.13 = (bf16[4,4,64,128]{3,2,1,0:T(8,128)(2,1)}, bf16[4,4,64,128]{3,2,1,0:T(8,128)(2,1)S(1)}, u32[]{:S(2)}, u32[]{:S(2)}) collective-permute-start(bf16[4,4,64,128]{3,2,1,0:T(8,128)(2,1)} %get-tuple-element.60), channel_id=1, source_target_pairs={{0,16},{4,20},{8,24},{12,28},{16,0},{20,4},{24,8},{28,12},{1,17},{... | collective-permute-start | bytes 786440 | tf_op jit(solution)/shard_map/ppermute | solution.py:375
  95.8 14.1 %collective-permute-start.14 = (bf16[4,4,64,128]{3,2,1,0:T(8,128)(2,1)}, bf16[4,4,64,128]{3,2,1,0:T(8,128)(2,1)S(1)}, u32[]{:S(2)}, u32[]{:S(2)}) collective-permute-start(bf16[4,4,64,128]{3,2,1,0:T(8,128)(2,1)} %get-tuple-element.61), channel_id=1, source_target_pairs={{0,24},{4,28},{8,16},{12,20},{16,8},{20,12},{24,0},{28,4},{1,25},{... | collective-permute-start | bytes 786440 | tf_op jit(solution)/shard_map/ppermute | solution.py:375
  104.2 5.6 %copy-start.4 = (bf16[4,4,64,128]{3,2,1,0:T(8,128)(2,1)}, bf16[4,4,64,128]{3,2,1,0:T(8,128)(2,1)S(1)}, u32[]{:S(2)}) copy-start(bf16[4,4,64,128]{3,2,1,0:T(8,128)(2,1)S(1)} %collective-permute-done.12.refs_1_) | copy-start | bytes 786436
  109.9 0.7 copy-start.5
  109.9 0.8 copy-start.6

commit v5 on v4

--- a/solution.py
+++ b/solution.py
@@ -162,7 +162,7 @@
         out[2:4] = (kept_sums[part].astype(F32) + got_sums[part].astype(F32)).astype(BF)
 
 
-def global_kernel(scale, scale2, kv, rows, stats, expand, dkv, kept, sent):
+def global_kernel(scale, scale2, kv, rows, stats, expand, before, dkv, kept, sent):
     g_query, g_grad = rows[0, 0], rows[3, 0]
     tops = stats[:, 0, 0:1, :]
     top = jnp.max(tops, axis=0)
@@ -173,15 +173,15 @@
     weights = jnp.exp2(nt(kv[0, 0], g_query) * scale2 - g_log)
     narrow = weights.astype(BF)
     slopes = (weights * (nt(kv[1, 0], g_grad) - g_dot)).astype(BF)
-    dkv[0, 0] = nn(slopes, g_query) * scale
-    dkv[1, 0] = nn(narrow, g_grad)
+    dkv[0, 0] = before[0, 0] + nn(slopes, g_query) * scale
+    dkv[1, 0] = before[1, 0] + nn(narrow, g_grad)
     out = nn(kv[1, 0].T, narrow).T.astype(BF)
     dq = (nn(kv[0, 0].T, slopes) * scale).T.astype(BF)
     put_in_slots(expand[...], (out, dq), kept, sent)
 
 
 def local_kernel(
-    scale, scale2, qd, kv, kv_near, kv_far, rows, bias, expand, before,
+    scale, scale2, qd, kv, kv_near, kv_far, rows, bias, expand,
     out, log_dot, dq, dkv, kept, sent, keys, values, score_buf, probs, slopes,
 ):
     toks = kv.shape[2]
@@ -265,8 +265,8 @@
             attend(step - 1)
     own = slice(HALF, HALF + toks)
     grads = jnp.concatenate(scaled, axis=1)
-    dkv[0, 0] = before[0, 0] + (nt(query_t, slopes[own, :]) * scale).T
-    dkv[1, 0] = before[1, 0] + nt(grads, probs[own, :]).T
+    dkv[0, 0] = (nt(query_t, slopes[own, :]) * scale).T
+    dkv[1, 0] = nt(grads, probs[own, :]).T
     g_dk = (nt(query_t, slopes[span:, :]) * scale).T.astype(BF)
     g_dv = nt(grads, probs[span:, :]).T.astype(BF)
     put_in_slots(expand[...], (g_dk, g_dv), kept, sent)
@@ -424,10 +424,10 @@
 
     held = [slot_rows[None]]
     for number, stage in enumerate(stages):
-        send = jnp.concatenate(held, axis=0) if number else held[0]
+        send = jnp.concatenate(after(held, place), axis=0) if number else held[0]
         held += [swap(send, mask) for mask in stage]
         if not number:
-            kv_late = after(kv, (held, place))
+            kv_late = after(kv, held)
             kv_far, kv_near = from_far(kv_late), from_near(kv_late)
 
     row_shape = (4, heads, count, width)
@@ -448,27 +448,14 @@
 
     sum_shape = (devices // 2, 2, heads, slots, width)
     sum_struct = struct(sum_shape, BF)
-    extra, kept_ends, sent_ends = pl.pallas_call(
-        functools.partial(global_kernel, scale, scale2),
-        grid=(heads,),
-        in_specs=[per_head(pair_shape, 1), per_head(row_shape, 1)]
-        + [per_head(stats.shape, 1), whole(expand.shape)],
-        out_specs=(per_head(pair_shape, 1), per_head(sum_shape, 2), per_head(sum_shape, 2)),
-        out_shape=(struct(pair_shape, F32), sum_struct, sum_struct),
-        compiler_params=params(),
-        cost_estimate=cost(1e6, 1e6),
-        name="global_queries",
-    )(kv, rows, stats, expand)
-    got_ends = from_near(sent_ends)
-    qd_late = after(qd, (kv_near, kv_far, sent_ends))
+    qd_late = after(qd, (kv_near, kv_far, rows))
     qd_far, qd_near = from_far(qd_late), from_near(qd_late)
 
     out, log_dot, dq, dkv, kept_sums, sent_sums = pl.pallas_call(
         functools.partial(local_kernel, scale, scale2),
         grid=(heads,),
         in_specs=[per_head(pair_shape, 1)] * 4
-        + [per_head(row_shape, 1), whole(bias.shape), whole(expand.shape)]
-        + [per_head(pair_shape, 1)],
+        + [per_head(row_shape, 1), whole(bias.shape), whole(expand.shape)],
         out_specs=(
             per_head((heads, toks, width), 0),
             per_head((heads, 2, toks), 0),
@@ -495,18 +482,34 @@
         compiler_params=params(),
         cost_estimate=cost(1e6, 1e6),
         name="local",
-    )(qd, kv, kv_near, kv_far, rows, bias, expand, extra)
+    )(qd, kv, kv_near, kv_far, rows, bias, expand)
     log_far, log_near = from_far(log_dot), from_near(log_dot)
 
+    dkv, kept_ends, sent_ends = pl.pallas_call(
+        functools.partial(global_kernel, scale, scale2),
+        grid=(heads,),
+        in_specs=[per_head(pair_shape, 1), per_head(row_shape, 1)]
+        + [per_head(stats.shape, 1), whole(expand.shape), per_head(pair_shape, 1)],
+        out_specs=(per_head(pair_shape, 1), per_head(sum_shape, 2), per_head(sum_shape, 2)),
+        out_shape=(struct(pair_shape, F32), sum_struct, sum_struct),
+        input_output_aliases={4: 0},
+        compiler_params=params(),
+        cost_estimate=cost(1e6, 1e6),
+        name="global_queries",
+    )(kv, rows, after(stats, (log_dot, qd_near, qd_far)), expand, dkv)
     got_sums = from_near(sent_sums)
+    got_ends = from_near(after(sent_ends, (log_near, log_far)))
 
     first = stages[0]
     parts = pl.pallas_call(
         fold_kernel,
+        grid=(heads,),
+        in_specs=[per_head(sum_shape, 2)] * 4,
+        out_specs=[per_head((4, heads, slots, width), 1)] * (devices // 2),
         out_shape=[struct((4, heads, slots, width), BF)] * (devices // 2),
         compiler_params=params(),
         name="fold",
-    )(kept_ends, got_ends, kept_sums, after(got_sums, (qd_near, qd_far)))
+    )(kept_ends, got_ends, kept_sums, got_sums)
     for stage in reversed(stages[1:-1]):
         size = len(parts) // (len(stage) + 1)
         kept = parts[:size]
@@ -514,8 +517,7 @@
             sent = parts[(number + 1) * size : (number + 2) * size]
             kept = [one + swap(other, mask) for one, other in zip(kept, sent)]
         parts = kept
-    sent = after(parts[1:], (log_near, log_far))
-    parts = [parts[0]] + [swap(part, mask) for part, mask in zip(sent, first)]
+    parts = [parts[0]] + [swap(part, mask) for part, mask in zip(parts[1:], first)]
 
     dkv = pl.pallas_call(
         functools.partial(rim_kernel, scale, scale2),

time: 116 us -> 117 us (level)
  blocking collectives: 20.6 us -> 0 us
  waiting for transfers between devices: 22.7 us -> 39.2 us
  starting transfers between devices: 19.7 us -> 22.8 us
  Pallas kernels: 48.2 us -> 49.4 us
    all_to_all x1 -> x0, blocking collectives: 20.6 us -> none  [shards(): stats = lax.all_to_all(stats, 'ctx', 0, 0, tiled=True)]
    ppermute x3, waiting for transfers between devices: 4.01 us -> 18.7 us  [from_far(): return lax.ppermute(value, 'ctx', pairs + [(j, i) for i, j in pairs])]
    all_to_all x0 -> x1, starting transfers between devices: none -> 5.25 us  [shards(): stats = lax.all_to_all(stats, 'ctx', 0, 0, tiled=True)]
    all_to_all x0 -> x1, waiting for transfers between devices: none -> 3.83 us  [shards(): stats = lax.all_to_all(stats, 'ctx', 0, 0, tiled=True)]
    ppermute x12, waiting for transfers between devices: 18.7 us -> 16.7 us  [swap(): return lax.ppermute(value, 'ctx', [(i, i ^ mask) for i in range(devices)])]
    pallas_call x1, Pallas kernels: 2.54 us -> 3.73 us  [shards(): pl.pallas_call(fold_kernel, grid=(heads,), in_specs=[per_head(sum_shape,...]
  transfers between devices with their start and end apart: 15 -> 16, of which waited for: 6 -> 6; matrix products, arithmetic and copies ran while one was open for 0% -> 0% of each run, Pallas kernels for 33% -> 31%
where the time goes in v5:
time: 117 us; the launch traced here: 115 us
  Pallas kernels  49.4 us (42%)
  waiting for transfers between devices  39.2 us (34%)
  starting transfers between devices  22.8 us (19%)
  local copies, waits for them, and re-layouts  1.44 us (1%)
  other arithmetic  1.25 us (1%)
    ppermute x3, waiting for transfers between devices, from_far(): return lax.ppermute(value, 'ctx', pairs + [(j, i) for i, j in pairs])  18.7 us
    ppermute x12, waiting for transfers between devices, swap(): return lax.ppermute(value, 'ctx', [(i, i ^ mask) for i in range(devices)])  16.7 us
    pallas_call x1, Pallas kernels, shards(): pl.pallas_call(functools.partial(local_kernel, scale, scale2), grid=(head...  14.2 us
    ppermute x12, starting transfers between devices, swap(): return lax.ppermute(value, 'ctx', [(i, i ^ mask) for i in range(devices)])  8.99 us
    ppermute x3, starting transfers between devices, from_far(): return lax.ppermute(value, 'ctx', pairs + [(j, i) for i, j in pairs])  8.56 us
    pallas_call x1, Pallas kernels, shards(): pl.pallas_call(functools.partial(rim_kernel, scale, scale2), grid=(heads,...  7.14 us
    pallas_call x1, Pallas kernels, shards(): pl.pallas_call(functools.partial(global_kernel, scale, scale2), grid=(hea...  6.59 us
    pallas_call x1, Pallas kernels, shards(): pl.pallas_call(functools.partial(stats_kernel, scale2), grid=(heads,), in...  5.52 us
  transfers between devices with their start and end apart: 16, of which 6 were waited for; matrix products, arithmetic and copies ran while one was open for 0% of the time, Pallas kernels for 31%

profile of v5, /device:TPU:1, one launch (start us, length us, event | category | flops | bytes accessed | tf_op | source)
XLA Modules:
  0.0 114.9 jit_solution(7821906536806922934)
XLA Ops:
  0.6 2.4 %pack_keys.1.kv.refs_5_ = bf16[2,4,512,128]{3,2,1,0:T(8,128)(2,1)} custom-call(bf16[2048,128]{1,0:T(8,128)(2,1)} %bitcast.15, bf16[2048,128]{1,0:T(8,128)(2,1)} %bitcast.16), custom_call_target="tpu_custom_call" | custom-call | tf_op jit(solution)/shard_map/pack_keys/pallas_call | solution.py:393
  3.1 3.4 %pack_queries.1 = (bf16[2,4,512,128]{3,2,1,0:T(8,128)(2,1)}, bf16[4,4,64,128]{3,2,1,0:T(8,128)(2,1)}) custom-call(bf16[2048,128]{1,0:T(8,128)(2,1)} %bitcast.17, bf16[2048,128]{1,0:T(8,128)(2,1)} %bitcast.18, bf16[2,4,512,128]{3,2,1,0:T(8,128)(2,1)} %pack_keys.1.kv.refs_5_, s32[1,256]{1,0:T(1,128)} %bitcast.19), custom_call_target="tpu_custom_call" | custom-call | tf_op jit(solution)/shard_map/pack_queries/pallas_call | solution.py:401
  6.5 3.0 %collective-permute-start.2 = (bf16[1,4,4,64,128]{4,3,2,1,0:T(8,128)(2,1)}, bf16[1,4,4,64,128]{4,3,2,1,0:T(8,128)(2,1)S(1)}, u32[]{:S(2)}, u32[]{:S(2)}) collective-permute-start(bf16[1,4,4,64,128]{4,3,2,1,0:T(8,128)(2,1)} %bitcast.10), channel_id=1, source_target_pairs={{0,24},{4,28},{8,16},{12,20},{16,8},{20,12},{24,0},{28,4},{1,25},{... | collective-permute-start | bytes 786440 | tf_op jit(solution)/shard_map/ppermute | solution.py:375
  9.5 0.2 collective-permute-start.1
  9.7 0.1 collective-permute-start
  9.8 2.2 %masks.1 = (f32[1536,128]{1,0:T(8,128)}, bf16[256,512]{1,0:T(8,128)(2,1)}, bf16[512,256]{1,0:T(8,128)(2,1)}, bf16[512,64]{1,0:T(8,128)(2,1)}) custom-call(s32[1,256]{1,0:T(1,128)} %bitcast.20), custom_call_target="tpu_custom_call" | custom-call | tf_op jit(solution)/shard_map/masks/pallas_call | solution.py:413
  12.0 3.8 %collective-permute-done.2.refs_3_ = bf16[1,4,4,64,128]{4,3,2,1,0:T(8,128)(2,1)S(1)} collective-permute-done((bf16[1,4,4,64,128]{4,3,2,1,0:T(8,128)(2,1)}, bf16[1,4,4,64,128]{4,3,2,1,0:T(8,128)(2,1)S(1)}, u32[]{:S(2)}, u32[]{:S(2)}) %collective-permute-start.2) | collective-permute-done | bytes 262176 | tf_op jit(solution)/shard_map/ppermute | solution.py:375
  15.8 6.3 %collective-permute-done.1.refs_2_ = bf16[1,4,4,64,128]{4,3,2,1,0:T(8,128)(2,1)S(1)} collective-permute-done((bf16[1,4,4,64,128]{4,3,2,1,0:T(8,128)(2,1)}, bf16[1,4,4,64,128]{4,3,2,1,0:T(8,128)(2,1)S(1)}, u32[]{:S(2)}, u32[]{:S(2)}) %collective-permute-start.1) | collective-permute-done | bytes 262176 | tf_op jit(solution)/shard_map/ppermute | solution.py:375
  22.1 0.0 collective-permute-done.refs_1_
  22.1 1.2 %pad_maximum_fusion = bf16[4,4,4,64,128]{4,3,2,1,0:T(8,128)(2,1)S(1)} fusion(bf16[1,4,4,64,128]{4,3,2,1,0:T(8,128)(2,1)S(1)} %collective-permute-done.2.refs_3_, bf16[1,4,4,64,128]{4,3,2,1,0:T(8,128)(2,1)S(1)} %collective-permute-done.1.refs_2_, bf16[1,4,4,64,128]{4,3,2,1,0:T(8,128)(2,1)S(1)} %collective-permute-done.refs_1_, ...), kind=kLoop, calls=%fused_computation | loop fusion | flops 1572864 | bytes 2097152 | tf_op jit(solution)/shard_map/concatenate | solution.py:427
  23.3 0.8 collective-permute-start.5
  24.1 3.0 %collective-permute-start.4 = (bf16[2,4,512,128]{3,2,1,0:T(8,128)(2,1)}, bf16[2,4,512,128]{3,2,1,0:T(8,128)(2,1)}, u32[]{:S(2)}, u32[]{:S(2)}) collective-permute-start(bf16[2,4,512,128]{3,2,1,0:T(8,128)(2,1)} %pack_keys.1.kv.refs_5_), channel_id=1, source_target_pairs={{4,8},{12,16},{20,24},{8,4},{16,12},{24,20},{5,9},{13,17},{21,25},... | collective-permute-start | bytes 3145736 | tf_op jit(solution)/shard_map/ppermute | solution.py:382
  27.1 0.1 collective-permute-start.3
  27.2 0.0 collective-permute-done.5.refs_4_
  27.2 0.0 copy-done.1
  27.2 0.0 copy-done.2
  27.2 0.0 copy-done.3
  27.3 5.5 %global_stats.1 = (bf16[4,4,256,128]{3,2,1,0:T(8,128)(2,1)}, f32[8,4,8,256]{3,2,1,0:T(8,128)}) custom-call(bf16[256,512]{1,0:T(8,128)(2,1)} %get-tuple-element.41.compact, bf16[1,4,4,64,128]{4,3,2,1,0:T(8,128)(2,1)} %bitcast.14, bf16[1,4,4,64,128]{4,3,2,1,0:T(8,128)(2,1)} %copy-done.3, bf16[1,4,4,64,128]{4,3,2,1,0:T(8,128)(2,1)} %copy-done.2, ...), custom_call_target="tpu_custom_call" | custom-call | flops 1000000 | bytes 1000000 | tf_op jit(solution)/shard_map/global_stats/pallas_call | solution.py:434
  32.8 18.7 %collective-permute-done.4.kv_far = bf16[2,4,512,128]{3,2,1,0:T(8,128)(2,1)} collective-permute-done((bf16[2,4,512,128]{3,2,1,0:T(8,128)(2,1)}, bf16[2,4,512,128]{3,2,1,0:T(8,128)(2,1)}, u32[]{:S(2)}, u32[]{:S(2)}) %collective-permute-start.4) | collective-permute-done | bytes 1048608 | tf_op jit(solution)/shard_map/ppermute | solution.py:382
  51.5 0.0 collective-permute-done.3.kv_near
  51.5 1.9 %collective-permute-start.7 = (bf16[2,4,512,128]{3,2,1,0:T(8,128)(2,1)}, bf16[2,4,512,128]{3,2,1,0:T(8,128)(2,1)}, u32[]{:S(2)}, u32[]{:S(2)}) collective-permute-start(bf16[2,4,512,128]{3,2,1,0:T(8,128)(2,1)} %get-tuple-element.51.qd), channel_id=1, source_target_pairs={{4,8},{12,16},{20,24},{8,4},{16,12},{24,20},{5,9},{13,17},{21,25},... | collective-permute-start | bytes 3145736 | tf_op jit(solution)/shard_map/ppermute | solution.py:382
  53.4 0.1 collective-permute-start.6
  53.5 5.2 %all-to-all-start = ((f32[8,4,8,256]{3,2,1,0:T(8,128)}), f32[8,4,8,256]{3,2,1,0:T(8,128)S(1)}, u32[]{:S(2)}, u32[]{:S(2)}) async-start(f32[8,4,8,256]{3,2,1,0:T(8,128)} %get-tuple-element.53), calls=%async_computation | async-start | bytes 524288 | tf_op jit(solution)/shard_map/all_to_all | solution.py:447
  58.7 14.2 %local.1 = (bf16[4,512,128]{2,1,0:T(8,128)(2,1)}, f32[4,2,512]{2,1,0:T(2,128)}, f32[4,512,128]{2,1,0:T(8,128)}, f32[2,4,512,128]{3,2,1,0:T(8,128)}, bf16[4,2,4,6...) custom-call(bf16[2,4,512,128]{3,2,1,0:T(8,128)(2,1)} %get-tuple-element.51.qd, ...), custom_call_target="tpu_custom_call" | custom-call | flops 1000000 | bytes 1000000 | tf_op jit(solution)/shard_map/local/pallas_call | solution.py:454
  72.9 3.6 %collective-permute-start.9 = (f32[4,2,512]{2,1,0:T(2,128)}, f32[4,2,512]{2,1,0:T(2,128)S(1)}, u32[]{:S(2)}, u32[]{:S(2)}) collective-permute-start(f32[4,2,512]{2,1,0:T(2,128)} %get-tuple-element.52), channel_id=1, source_target_pairs={{4,8},{12,16},{20,24},{8,4},{16,12},{24,20},{5,9},{13,17},{21,25},... | collective-permute-start | bytes 49160 | tf_op jit(solution)/shard_map/ppermute | solution.py:382
  76.5 0.1 collective-permute-start.8
  76.6 0.5 collective-permute-start.11
  77.1 3.8 %all-to-all-done.stats = f32[8,4,8,256]{3,2,1,0:T(8,128)S(1)} async-done(((f32[8,4,8,256]{3,2,1,0:T(8,128)}), f32[8,4,8,256]{3,2,1,0:T(8,128)S(1)}, u32[]{:S(2)}, u32[]{:S(2)}) %all-to-all-start) | async-done | bytes 262176 | tf_op jit(solution)/shard_map/all_to_all | solution.py:447
  80.9 0.0 collective-permute-done.7.qd_far
  80.9 0.0 collective-permute-done.6.qd_near
  80.9 0.7 copy-done
  81.7 6.6 %global_queries.1 = (f32[2,4,512,128]{3,2,1,0:T(8,128)}, bf16[4,2,4,64,128]{4,3,2,1,0:T(8,128)(2,1)}, bf16[4,2,4,64,128]{4,3,2,1,0:T(8,128)(2,1)}) custom-call(bf16[2,4,512,128]{3,2,1,0:T(8,128)(2,1)} %pack_keys.1.kv.refs_5_, bf16[4,4,256,128]{3,2,1,0:T(8,128)(2,1)} %get-tuple-element.46.rows, ...), custom_call_target="tpu_custom_call", output_to_operand_aliasing={{0}: (4, {})} | custom-call | flops 1000000 | bytes 1000000 | tf_op jit(solution)/shard_map/global_queries/pallas_call | solution.py:488
  88.2 0.0 collective-permute-done.9.log_far
  88.2 0.0 copy-start.8
  88.3 0.0 collective-permute-done.8.log_near
  88.3 1.5 %collective-permute-start.10 = (bf16[4,2,4,64,128]{4,3,2,1,0:T(8,128)(2,1)}, bf16[4,2,4,64,128]{4,3,2,1,0:T(8,128)(2,1)}, u32[]{:S(2)}, u32[]{:S(2)}) collective-permute-start(bf16[4,2,4,64,128]{4,3,2,1,0:T(8,128)(2,1)} %get-tuple-element.59), channel_id=1, source_target_pairs={{0,4},{4,0},{8,12},{12,8},{16,20},{20,16},{24,28},{28,24},{1,5},{5... | collective-permute-start | bytes 1572872 | tf_op jit(solution)/shard_map/ppermute | solution.py:375
  89.8 0.0 collective-permute-done.11.got_sums
  89.8 1.9 %collective-permute-done.10.got_ends = bf16[4,2,4,64,128]{4,3,2,1,0:T(8,128)(2,1)} collective-permute-done((bf16[4,2,4,64,128]{4,3,2,1,0:T(8,128)(2,1)}, bf16[4,2,4,64,128]{4,3,2,1,0:T(8,128)(2,1)}, u32[]{:S(2)}, u32[]{:S(2)}) %collective-permute-start.10) | collective-permute-done | bytes 524320 | tf_op jit(solution)/shard_map/ppermute | solution.py:375
  91.7 3.7 %fold.1 = (bf16[4,4,64,128]{3,2,1,0:T(8,128)(2,1)}, bf16[4,4,64,128]{3,2,1,0:T(8,128)(2,1)}, bf16[4,4,64,128]{3,2,1,0:T(8,128)(2,1)}, bf16[4,4,64,128]{3,2,1,0:T(8,128)(2,1)}) custom-call(bf16[4,2,4,64,128]{4,3,2,1,0:T(8,128)(2,1)} %get-tuple-element.57.kept_ends, bf16[4,2,4,64,128]{4,3,2,1,0:T(8,128)(2,1)} %collective-permute-done.10.got_ends, ...), custom_call_target="tpu_custom_call" | custom-call | tf_op jit(solution)/shard_map/fold/pallas_call | solution.py:504
  95.4 0.0 collective-permute-start.12
  95.4 1.6 %collective-permute-start.13 = (bf16[4,4,64,128]{3,2,1,0:T(8,128)(2,1)}, bf16[4,4,64,128]{3,2,1,0:T(8,128)(2,1)S(1)}, u32[]{:S(2)}, u32[]{:S(2)}) collective-permute-start(bf16[4,4,64,128]{3,2,1,0:T(8,128)(2,1)} %get-tuple-element.64), channel_id=1, source_target_pairs={{0,16},{4,20},{8,24},{12,28},{16,0},{20,4},{24,8},{28,12},{1,17},{... | collective-permute-start | bytes 786440 | tf_op jit(solution)/shard_map/ppermute | solution.py:375
  97.0 1.1 collective-permute-start.14
  98.1 7.1 %rim.1.dkv = f32[2,4,512,128]{3,2,1,0:T(8,128)} custom-call(bf16[2,4,512,128]{3,2,1,0:T(8,128)(2,1)} %pack_keys.1.kv.refs_5_, f32[1536,128]{1,0:T(8,128)} %get-tuple-element.47.bias, bf16[2,4,512,128]{3,2,1,0:T(8,128)(2,1)} %collective-permute-done.6.qd_near, bf16[2,4,512,128]{3,2,1,0:T(8,128)(2,1)} %collective-permute-done.7.qd_far, ...), custom_call_target="tpu_custom_call" | custom-call | flops 1000000 | bytes 1000000 | tf_op jit(solution)/shard_map/rim/pallas_call | solution.py:522
  105.3 0.0 collective-permute-done.12.refs_1_
  105.3 0.0 collective-permute-done.13.refs_2_
  105.3 4.7 %collective-permute-done.14.refs_3_ = bf16[4,4,64,128]{3,2,1,0:T(8,128)(2,1)S(1)} collective-permute-done((bf16[4,4,64,128]{3,2,1,0:T(8,128)(2,1)}, bf16[4,4,64,128]{3,2,1,0:T(8,128)(2,1)S(1)}, u32[]{:S(2)}, u32[]{:S(2)}) %collective-permute-start.14) | collective-permute-done | bytes 262176 | tf_op jit(solution)/shard_map/ppermute | solution.py:375
  110.0 0.7 copy-done.7
  110.7 4.2 %final.1 = (bf16[2048,128]{1,0:T(8,128)(2,1)}, f32[2048,128]{1,0:T(8,128)}, f32[2048,128]{1,0:T(8,128)}, f32[2048,128]{1,0:T(8,128)}) custom-call(bf16[512,64]{1,0:T(8,128)(2,1)} %get-tuple-element.37.place, bf16[4,512,128]{2,1,0:T(8,128)(2,1)} %get-tuple-element.49.out, f32[4,512,128]{2,1,0:T(8,128)} %get-tuple-element.50.dq, f32[2,4,512,128]{3,2,1,0:T(8,128)} %rim.1.dkv, ...), custom_call_target="tpu_custom_call" | custom-call | tf_op jit(solution)/shard_map/final/pallas_call | solution.py:545
  (14 shorter events, 0.0 us)
Async XLA Ops:
  6.5 9.3 %collective-permute-start.2 = (bf16[1,4,4,64,128]{4,3,2,1,0:T(8,128)(2,1)}, bf16[1,4,4,64,128]{4,3,2,1,0:T(8,128)(2,1)S(1)}, u32[]{:S(2)}, u32[]{:S(2)}) collective-permute-start(bf16[1,4,4,64,128]{4,3,2,1,0:T(8,128)(2,1)} %bitcast.10), channel_id=1, source_target_pairs={{0,24},{4,28},{8,16},{12,20},{16,8},{20,12},{24,0},{28,4},{1,25},{... | collective-permute-start | bytes 786440 | tf_op jit(solution)/shard_map/ppermute | solution.py:375
  9.5 12.6 %collective-permute-start.1 = (bf16[1,4,4,64,128]{4,3,2,1,0:T(8,128)(2,1)}, bf16[1,4,4,64,128]{4,3,2,1,0:T(8,128)(2,1)S(1)}, u32[]{:S(2)}, u32[]{:S(2)}) collective-permute-start(bf16[1,4,4,64,128]{4,3,2,1,0:T(8,128)(2,1)} %bitcast.11), channel_id=1, source_target_pairs={{0,16},{4,20},{8,24},{12,28},{16,0},{20,4},{24,8},{28,12},{1,17},{... | collective-permute-start | bytes 786440 | tf_op jit(solution)/shard_map/ppermute | solution.py:375
  9.7 12.4 %collective-permute-start = (bf16[1,4,4,64,128]{4,3,2,1,0:T(8,128)(2,1)}, bf16[1,4,4,64,128]{4,3,2,1,0:T(8,128)(2,1)S(1)}, u32[]{:S(2)}, u32[]{:S(2)}) collective-permute-start(bf16[1,4,4,64,128]{4,3,2,1,0:T(8,128)(2,1)} %bitcast.12), channel_id=1, source_target_pairs={{0,8},{4,12},{8,0},{12,4},{16,24},{20,28},{24,16},{28,20},{1,9},{5... | collective-permute-start | bytes 786440 | tf_op jit(solution)/shard_map/ppermute | solution.py:375
  15.8 11.5 %copy-start.1 = (bf16[1,4,4,64,128]{4,3,2,1,0:T(8,128)(2,1)}, bf16[1,4,4,64,128]{4,3,2,1,0:T(8,128)(2,1)S(1)}, u32[]{:S(2)}) copy-start(bf16[1,4,4,64,128]{4,3,2,1,0:T(8,128)(2,1)S(1)} %collective-permute-done.2.refs_3_) | copy-start | bytes 786436
  22.1 5.2 %copy-start.2 = (bf16[1,4,4,64,128]{4,3,2,1,0:T(8,128)(2,1)}, bf16[1,4,4,64,128]{4,3,2,1,0:T(8,128)(2,1)S(1)}, u32[]{:S(2)}) copy-start(bf16[1,4,4,64,128]{4,3,2,1,0:T(8,128)(2,1)S(1)} %collective-permute-done.1.refs_2_) | copy-start | bytes 786436
  22.1 5.2 %copy-start.3 = (bf16[1,4,4,64,128]{4,3,2,1,0:T(8,128)(2,1)}, bf16[1,4,4,64,128]{4,3,2,1,0:T(8,128)(2,1)S(1)}, u32[]{:S(2)}) copy-start(bf16[1,4,4,64,128]{4,3,2,1,0:T(8,128)(2,1)S(1)} %collective-permute-done.refs_1_) | copy-start | bytes 786436
  23.3 3.9 %collective-permute-start.5 = (bf16[4,4,4,64,128]{4,3,2,1,0:T(8,128)(2,1)S(1)}, bf16[4,4,4,64,128]{4,3,2,1,0:T(8,128)(2,1)}, u32[]{:S(2)}, u32[]{:S(2)}) collective-permute-start(bf16[4,4,4,64,128]{4,3,2,1,0:T(8,128)(2,1)S(1)} %pad_maximum_fusion), channel_id=1, source_target_pairs={{0,4},{4,0},{8,12},{12,8},{16,20},{20,16},{24,28},{28,24},{1,5},{5... | collective-permute-start | bytes 3145736 | tf_op jit(solution)/shard_map/ppermute | solution.py:375
  24.1 27.4 %collective-permute-start.4 = (bf16[2,4,512,128]{3,2,1,0:T(8,128)(2,1)}, bf16[2,4,512,128]{3,2,1,0:T(8,128)(2,1)}, u32[]{:S(2)}, u32[]{:S(2)}) collective-permute-start(bf16[2,4,512,128]{3,2,1,0:T(8,128)(2,1)} %pack_keys.1.kv.refs_5_), channel_id=1, source_target_pairs={{4,8},{12,16},{20,24},{8,4},{16,12},{24,20},{5,9},{13,17},{21,25},... | collective-permute-start | bytes 3145736 | tf_op jit(solution)/shard_map/ppermute | solution.py:382
  27.1 24.4 %collective-permute-start.3 = (bf16[2,4,512,128]{3,2,1,0:T(8,128)(2,1)}, bf16[2,4,512,128]{3,2,1,0:T(8,128)(2,1)}, u32[]{:S(2)}, u32[]{:S(2)}) collective-permute-start(bf16[2,4,512,128]{3,2,1,0:T(8,128)(2,1)} %pack_keys.1.kv.refs_5_), channel_id=1, source_target_pairs={{0,4},{4,0},{8,12},{12,8},{16,20},{20,16},{24,28},{28,24},{1,5},{5... | collective-permute-start | bytes 3145736 | tf_op jit(solution)/shard_map/ppermute | solution.py:375
  51.5 29.5 %collective-permute-start.7 = (bf16[2,4,512,128]{3,2,1,0:T(8,128)(2,1)}, bf16[2,4,512,128]{3,2,1,0:T(8,128)(2,1)}, u32[]{:S(2)}, u32[]{:S(2)}) collective-permute-start(bf16[2,4,512,128]{3,2,1,0:T(8,128)(2,1)} %get-tuple-element.51.qd), channel_id=1, source_target_pairs={{4,8},{12,16},{20,24},{8,4},{16,12},{24,20},{5,9},{13,17},{21,25},... | collective-permute-start | bytes 3145736 | tf_op jit(solution)/shard_map/ppermute | solution.py:382
  53.4 27.5 %collective-permute-start.6 = (bf16[2,4,512,128]{3,2,1,0:T(8,128)(2,1)}, bf16[2,4,512,128]{3,2,1,0:T(8,128)(2,1)}, u32[]{:S(2)}, u32[]{:S(2)}) collective-permute-start(bf16[2,4,512,128]{3,2,1,0:T(8,128)(2,1)} %get-tuple-element.51.qd), channel_id=1, source_target_pairs={{0,4},{4,0},{8,12},{12,8},{16,20},{20,16},{24,28},{28,24},{1,5},{5... | collective-permute-start | bytes 3145736 | tf_op jit(solution)/shard_map/ppermute | solution.py:375
  53.5 27.4 %all-to-all-start = ((f32[8,4,8,256]{3,2,1,0:T(8,128)}), f32[8,4,8,256]{3,2,1,0:T(8,128)S(1)}, u32[]{:S(2)}, u32[]{:S(2)}) async-start(f32[8,4,8,256]{3,2,1,0:T(8,128)} %get-tuple-element.53), calls=%async_computation | async-start | bytes 524288 | tf_op jit(solution)/shard_map/all_to_all | solution.py:447
  72.9 15.3 %collective-permute-start.9 = (f32[4,2,512]{2,1,0:T(2,128)}, f32[4,2,512]{2,1,0:T(2,128)S(1)}, u32[]{:S(2)}, u32[]{:S(2)}) collective-permute-start(f32[4,2,512]{2,1,0:T(2,128)} %get-tuple-element.52), channel_id=1, source_target_pairs={{4,8},{12,16},{20,24},{8,4},{16,12},{24,20},{5,9},{13,17},{21,25},... | collective-permute-start | bytes 49160 | tf_op jit(solution)/shard_map/ppermute | solution.py:382
  76.5 11.7 %collective-permute-start.8 = (f32[4,2,512]{2,1,0:T(2,128)}, f32[4,2,512]{2,1,0:T(2,128)S(1)}, u32[]{:S(2)}, u32[]{:S(2)}) collective-permute-start(f32[4,2,512]{2,1,0:T(2,128)} %get-tuple-element.52), channel_id=1, source_target_pairs={{0,4},{4,0},{8,12},{12,8},{16,20},{20,16},{24,28},{28,24},{1,5},{5... | collective-permute-start | bytes 49160 | tf_op jit(solution)/shard_map/ppermute | solution.py:375
  76.6 13.2 %collective-permute-start.11 = (bf16[4,2,4,64,128]{4,3,2,1,0:T(8,128)(2,1)}, bf16[4,2,4,64,128]{4,3,2,1,0:T(8,128)(2,1)S(1)}, u32[]{:S(2)}, u32[]{:S(2)}) collective-permute-start(bf16[4,2,4,64,128]{4,3,2,1,0:T(8,128)(2,1)} %get-tuple-element.61), channel_id=1, source_target_pairs={{0,4},{4,0},{8,12},{12,8},{16,20},{20,16},{24,28},{28,24},{1,5},{5... | collective-permute-start | bytes 1572872 | tf_op jit(solution)/shard_map/ppermute | solution.py:375
  80.9 0.7 copy-start
  88.2 9.9 %copy-start.8 = (f32[4,2,512]{2,1,0:T(2,128)}, f32[4,2,512]{2,1,0:T(2,128)S(1)}, u32[]{:S(2)}) copy-start(f32[4,2,512]{2,1,0:T(2,128)S(1)} %collective-permute-done.9.log_far) | copy-start | bytes 49156
  88.3 9.9 %copy-start.9 = (f32[4,2,512]{2,1,0:T(2,128)}, f32[4,2,512]{2,1,0:T(2,128)S(1)}, u32[]{:S(2)}) copy-start(f32[4,2,512]{2,1,0:T(2,128)S(1)} %collective-permute-done.8.log_near) | copy-start | bytes 49156
  88.3 3.4 %collective-permute-start.10 = (bf16[4,2,4,64,128]{4,3,2,1,0:T(8,128)(2,1)}, bf16[4,2,4,64,128]{4,3,2,1,0:T(8,128)(2,1)}, u32[]{:S(2)}, u32[]{:S(2)}) collective-permute-start(bf16[4,2,4,64,128]{4,3,2,1,0:T(8,128)(2,1)} %get-tuple-element.59), channel_id=1, source_target_pairs={{0,4},{4,0},{8,12},{12,8},{16,20},{20,16},{24,28},{28,24},{1,5},{5... | collective-permute-start | bytes 1572872 | tf_op jit(solution)/shard_map/ppermute | solution.py:375
  89.8 1.9 %copy-start.4 = (bf16[4,2,4,64,128]{4,3,2,1,0:T(8,128)(2,1)}, bf16[4,2,4,64,128]{4,3,2,1,0:T(8,128)(2,1)S(1)}, u32[]{:S(2)}) copy-start(bf16[4,2,4,64,128]{4,3,2,1,0:T(8,128)(2,1)S(1)} %collective-permute-done.11.got_sums) | copy-start | bytes 1572868
  95.4 9.9 %collective-permute-start.12 = (bf16[4,4,64,128]{3,2,1,0:T(8,128)(2,1)}, bf16[4,4,64,128]{3,2,1,0:T(8,128)(2,1)S(1)}, u32[]{:S(2)}, u32[]{:S(2)}) collective-permute-start(bf16[4,4,64,128]{3,2,1,0:T(8,128)(2,1)} %get-tuple-element.63), channel_id=1, source_target_pairs={{0,8},{4,12},{8,0},{12,4},{16,24},{20,28},{24,16},{28,20},{1,9},{5... | collective-permute-start | bytes 786440 | tf_op jit(solution)/shard_map/ppermute | solution.py:375
  95.4 9.9 %collective-permute-start.13 = (bf16[4,4,64,128]{3,2,1,0:T(8,128)(2,1)}, bf16[4,4,64,128]{3,2,1,0:T(8,128)(2,1)S(1)}, u32[]{:S(2)}, u32[]{:S(2)}) collective-permute-start(bf16[4,4,64,128]{3,2,1,0:T(8,128)(2,1)} %get-tuple-element.64), channel_id=1, source_target_pairs={{0,16},{4,20},{8,24},{12,28},{16,0},{20,4},{24,8},{28,12},{1,17},{... | collective-permute-start | bytes 786440 | tf_op jit(solution)/shard_map/ppermute | solution.py:375
  97.0 13.0 %collective-permute-start.14 = (bf16[4,4,64,128]{3,2,1,0:T(8,128)(2,1)}, bf16[4,4,64,128]{3,2,1,0:T(8,128)(2,1)S(1)}, u32[]{:S(2)}, u32[]{:S(2)}) collective-permute-start(bf16[4,4,64,128]{3,2,1,0:T(8,128)(2,1)} %get-tuple-element.65), channel_id=1, source_target_pairs={{0,24},{4,28},{8,16},{12,20},{16,8},{20,12},{24,0},{28,4},{1,25},{... | collective-permute-start | bytes 786440 | tf_op jit(solution)/shard_map/ppermute | solution.py:375
  105.3 4.7 %copy-start.5 = (bf16[4,4,64,128]{3,2,1,0:T(8,128)(2,1)}, bf16[4,4,64,128]{3,2,1,0:T(8,128)(2,1)S(1)}, u32[]{:S(2)}) copy-start(bf16[4,4,64,128]{3,2,1,0:T(8,128)(2,1)S(1)} %collective-permute-done.12.refs_1_) | copy-start | bytes 786436
  105.3 4.7 %copy-start.6 = (bf16[4,4,64,128]{3,2,1,0:T(8,128)(2,1)}, bf16[4,4,64,128]{3,2,1,0:T(8,128)(2,1)S(1)}, u32[]{:S(2)}) copy-start(bf16[4,4,64,128]{3,2,1,0:T(8,128)(2,1)S(1)} %collective-permute-done.13.refs_2_) | copy-start | bytes 786436
  110.0 0.7 copy-start.7

commit v6 on v5

--- a/solution.py
+++ b/solution.py
@@ -180,39 +180,34 @@
     put_in_slots(expand[...], (out, dq), kept, sent)
 
 
-def local_kernel(
-    scale, scale2, qd, kv, kv_near, kv_far, rows, bias, expand,
-    out, log_dot, dq, dkv, kept, sent, keys, values, score_buf, probs, slopes,
+def gather_window(kv, kv_near, kv_far, number, buf):
+    toks = kv.shape[2]
+    near = 2 * (1 - lax.axis_index("ctx") % 2)
+    for block, place in ((kv_near, near), (kv, 1), (kv_far, 2 - near)):
+        buf[pl.ds(pl.multiple_of(place * toks, toks), toks), :] = block[number, 0]
+
+
+def window_kernel(
+    scale2, qd, kv, kv_near, kv_far, bias, probs, acc, top_sum, keys, values, score_buf
 ):
     toks = kv.shape[2]
     reach = 2 * HALF + TILE
-    span = keys.shape[0] - rows.shape[2]
-    near = 2 * (1 - lax.axis_index("ctx") % 2)
-    for block, place in ((kv_near, near), (kv, 1), (kv_far, 2 - near)):
-        spot = pl.ds(pl.multiple_of(place * toks, toks), toks)
-        keys[spot, :] = block[0, 0]
-        values[spot, :] = block[1, 0]
-    keys[span:, :] = rows[1, 0]
-    values[span:, :] = rows[2, 0]
-    key_t, value_t = keys[...].T, values[...].T
-    query_t, grad_t = qd[0, 0].T, qd[1, 0].T
+    gather_window(kv, kv_near, kv_far, 0, keys)
+    gather_window(kv, kv_near, kv_far, 1, values)
+    value_t = values[...].T
+    query_t = qd[0, 0].T
     tiles = range(toks // TILE)
     lanes = [slice(tile * TILE, (tile + 1) * TILE) for tile in tiles]
-    windows = [slice(tile * TILE, tile * TILE + reach) for tile in tiles]
-    starts = [
-        list(range(tile * TILE, tile * TILE + reach, TILE)) + list(range(span, keys.shape[0], TILE))
-        for tile in tiles
-    ]
-    best, top, total, scaled, dots = ([None] * len(tiles) for _ in range(5))
+    pieces = range(reach // TILE)
+    best, top, total = ([None] * len(tiles) for _ in range(3))
 
     def score(tile, piece):
-        start = starts[tile][piece]
-        scores = nn(keys[start : start + TILE, :], query_t[:, lanes[tile]]) * scale2
-        if start < span:
-            scores = scores + wide(bias[start : start + TILE, :], TILE)
+        span = slice((tile + piece) * TILE, (tile + piece + 1) * TILE)
+        scores = nn(keys[span, :], query_t[:, lanes[tile]]) * scale2
+        scores = scores + wide(bias[span, :], TILE)
         if piece == 0:
             scores = band(scores, False)
-        elif piece == reach // TILE - 1:
+        elif piece == len(pieces) - 1:
             scores = band(scores, True)
         score_buf[tile, piece * TILE : (piece + 1) * TILE, :] = scores
         part = jnp.max(scores.reshape(TILE // 8, 8, TILE), axis=0)
@@ -221,54 +216,73 @@
     def weigh(tile, piece):
         if top[tile] is None:
             top[tile] = jnp.max(best[tile], axis=0, keepdims=True)
-        start = starts[tile][piece]
+        span = slice((tile + piece) * TILE, (tile + piece + 1) * TILE)
         weights = jnp.exp2(score_buf[tile, piece * TILE : (piece + 1) * TILE, :] - top[tile])
-        probs[start : start + TILE, lanes[tile]] = weights.astype(BF)
+        probs[0, span, lanes[tile]] = weights.astype(BF)
         part = jnp.sum(weights.reshape(TILE // 8, 8, TILE), axis=0)
         total[tile] = part if total[tile] is None else total[tile] + part
 
-    def attend(tile):
-        whole_sum = jnp.sum(total[tile], axis=0, keepdims=True)
-        inverse = 1.0 / whole_sum
-        grads = grad_t[:, lanes[tile]].astype(F32)
-        acc = nn(value_t[:, windows[tile]], probs[windows[tile], lanes[tile]])
-        acc = (acc + nn(value_t[:, span:], probs[span:, lanes[tile]])) * inverse
-        dot = jnp.sum(grads * acc, axis=0, keepdims=True)
-        log_dot[0, 0:1, lanes[tile]] = top[tile] + jnp.log2(whole_sum)
-        log_dot[0, 1:2, lanes[tile]] = dot
-        out[0, lanes[tile], :] = acc.T.astype(BF)
-        scaled[tile] = (grads * inverse).astype(BF)
-        dots[tile] = dot * inverse
-
-    def slope(tile, piece):
-        start = starts[tile][piece]
-        rise = nn(values[start : start + TILE, :], scaled[tile]) - dots[tile]
-        weights = probs[start : start + TILE, lanes[tile]].astype(F32)
-        slopes[start : start + TILE, lanes[tile]] = (weights * rise).astype(BF)
-
-    def query_gradient(tile):
-        acc = nn(key_t[:, windows[tile]], slopes[windows[tile], lanes[tile]])
-        acc = acc + nn(key_t[:, span:], slopes[span:, lanes[tile]])
-        dq[0, lanes[tile], :] = (acc * scale).T
-
-    for step in range(len(tiles) + 2):
-        for piece in range(len(starts[0])):
-            if 0 <= step - 2:
-                slope(step - 2, piece)
-            if 0 <= step - 1 < len(tiles):
+    for step in range(len(tiles) + 1):
+        for piece in pieces:
+            if step:
                 weigh(step - 1, piece)
             if step < len(tiles):
                 score(step, piece)
-        if 0 <= step - 2:
-            query_gradient(step - 2)
-        if 0 <= step - 1 < len(tiles):
-            attend(step - 1)
+        if step:
+            tile = step - 1
+            window = slice(tile * TILE, tile * TILE + reach)
+            acc[0, :, lanes[tile]] = nn(value_t[:, window], probs[0, window, lanes[tile]])
+            top_sum[0, 0:1, lanes[tile]] = top[tile]
+            top_sum[0, 1:2, lanes[tile]] = jnp.sum(total[tile], axis=0, keepdims=True)
+
+
+def local_kernel(
+    scale, scale2, qd, kv, kv_near, kv_far, rows, probs, acc, top_sum, expand,
+    out, log_dot, dq, dkv, kept, sent, keys, values, slopes,
+):
+    toks = kv.shape[2]
+    reach = 2 * HALF + TILE
+    gather_window(kv, kv_near, kv_far, 0, keys)
+    gather_window(kv, kv_near, kv_far, 1, values)
+    key_t = keys[...].T
+    g_keys, g_values = rows[1, 0], rows[2, 0]
+    g_key_t, g_value_t = g_keys.T, g_values.T
+    query_t, grad_t = qd[0, 0].T, qd[1, 0].T
+    grads = grad_t.astype(F32)
+    scores = nn(g_keys, query_t) * scale2
+    old = top_sum[0, 0:1, :]
+    top = jnp.maximum(old, jnp.max(scores, axis=0, keepdims=True))
+    weights = jnp.exp2(scores - top)
+    factor = jnp.exp2(old - top)
+    total = top_sum[0, 1:2, :] * factor + jnp.sum(weights, axis=0, keepdims=True)
+    inverse = 1.0 / total
+    g_probs = weights.astype(BF)
+    result = (acc[0] * factor + nn(g_value_t, g_probs)) * inverse
+    dot = jnp.sum(grads * result, axis=0, keepdims=True)
+    log_dot[0, 0:1, :] = top + jnp.log2(total)
+    log_dot[0, 1:2, :] = dot
+    out[0] = result.T.astype(BF)
+    share = factor * inverse
+    g_grads = (grads * inverse).astype(BF)
+    w_grads = (grads * share).astype(BF)
+    g_slopes = (weights * (nn(g_values, g_grads) - dot * inverse)).astype(BF)
+    dots = dot * share
+    for tile in range(toks // TILE):
+        lanes = slice(tile * TILE, (tile + 1) * TILE)
+        for piece in range(reach // TILE):
+            span = slice((tile + piece) * TILE, (tile + piece + 1) * TILE)
+            rise = nn(values[span, :], w_grads[:, lanes]) - dots[:, lanes]
+            slopes[span, lanes] = (probs[0, span, lanes].astype(F32) * rise).astype(BF)
+    for tile in range(toks // TILE):
+        lanes = slice(tile * TILE, (tile + 1) * TILE)
+        window = slice(tile * TILE, tile * TILE + reach)
+        part = nn(key_t[:, window], slopes[window, lanes]) + nn(g_key_t, g_slopes[:, lanes])
+        dq[0, lanes, :] = (part * scale).T
     own = slice(HALF, HALF + toks)
-    grads = jnp.concatenate(scaled, axis=1)
     dkv[0, 0] = (nt(query_t, slopes[own, :]) * scale).T
-    dkv[1, 0] = nt(grads, probs[own, :]).T
-    g_dk = (nt(query_t, slopes[span:, :]) * scale).T.astype(BF)
-    g_dv = nt(grads, probs[span:, :]).T.astype(BF)
+    dkv[1, 0] = nt(w_grads, probs[0, own, :]).T
+    g_dk = (nt(query_t, g_slopes) * scale).T.astype(BF)
+    g_dv = nt(g_grads, g_probs).T.astype(BF)
     put_in_slots(expand[...], (g_dk, g_dv), kept, sent)
 
 
@@ -422,13 +436,38 @@
         name="masks",
     )(pos_row)
 
+    kv_far, kv_near = from_far(kv), from_near(kv)
+    probs_shape = (heads, span, toks)
+    acc_shape = (heads, width, toks)
+    probs, acc, top_sum = pl.pallas_call(
+        functools.partial(window_kernel, scale2),
+        grid=(heads,),
+        in_specs=[per_head(pair_shape, 1)] * 4 + [whole(bias.shape)],
+        out_specs=(
+            per_head(probs_shape, 0),
+            per_head(acc_shape, 0),
+            per_head((heads, 2, toks), 0),
+        ),
+        out_shape=(
+            struct(probs_shape, BF),
+            struct(acc_shape, F32),
+            struct((heads, 2, toks), F32),
+        ),
+        scratch_shapes=[
+            pltpu.VMEM((span, width), BF),
+            pltpu.VMEM((span, width), BF),
+            pltpu.VMEM((toks // TILE, 2 * HALF + TILE, TILE), F32),
+        ],
+        compiler_params=params(),
+        cost_estimate=cost(1e6, 1e6),
+        name="window",
+    )(qd, kv, kv_near, kv_far, bias)
     held = [slot_rows[None]]
     for number, stage in enumerate(stages):
-        send = jnp.concatenate(after(held, place), axis=0) if number else held[0]
+        if stage == [1]:
+            held = after(held, top_sum)
+        send = jnp.concatenate(held, axis=0) if number else held[0]
         held += [swap(send, mask) for mask in stage]
-        if not number:
-            kv_late = after(kv, held)
-            kv_far, kv_near = from_far(kv_late), from_near(kv_late)
 
     row_shape = (4, heads, count, width)
     rows, stats = pl.pallas_call(
@@ -448,14 +487,15 @@
 
     sum_shape = (devices // 2, 2, heads, slots, width)
     sum_struct = struct(sum_shape, BF)
-    qd_late = after(qd, (kv_near, kv_far, rows))
+    qd_late = after(qd, (kv_near, kv_far))
     qd_far, qd_near = from_far(qd_late), from_near(qd_late)
 
     out, log_dot, dq, dkv, kept_sums, sent_sums = pl.pallas_call(
         functools.partial(local_kernel, scale, scale2),
         grid=(heads,),
         in_specs=[per_head(pair_shape, 1)] * 4
-        + [per_head(row_shape, 1), whole(bias.shape), whole(expand.shape)],
+        + [per_head(row_shape, 1), per_head(probs_shape, 0), per_head(acc_shape, 0)]
+        + [per_head((heads, 2, toks), 0), whole(expand.shape)],
         out_specs=(
             per_head((heads, toks, width), 0),
             per_head((heads, 2, toks), 0),
@@ -473,16 +513,14 @@
             sum_struct,
         ),
         scratch_shapes=[
-            pltpu.VMEM((span + count, width), BF),
-            pltpu.VMEM((span + count, width), BF),
-            pltpu.VMEM((toks // TILE, 2 * HALF + TILE + count, TILE), F32),
-            pltpu.VMEM((span + count, toks), BF),
-            pltpu.VMEM((span + count, toks), BF),
+            pltpu.VMEM((span, width), BF),
+            pltpu.VMEM((span, width), BF),
+            pltpu.VMEM((span, toks), BF),
         ],
         compiler_params=params(),
         cost_estimate=cost(1e6, 1e6),
         name="local",
-    )(qd, kv, kv_near, kv_far, rows, bias, expand)
+    )(qd, kv, kv_near, kv_far, rows, probs, acc, top_sum, expand)
     log_far, log_near = from_far(log_dot), from_near(log_dot)
 
     dkv, kept_ends, sent_ends = pl.pallas_call(
@@ -503,9 +541,6 @@
     first = stages[0]
     parts = pl.pallas_call(
         fold_kernel,
-        grid=(heads,),
-        in_specs=[per_head(sum_shape, 2)] * 4,
-        out_specs=[per_head((4, heads, slots, width), 1)] * (devices // 2),
         out_shape=[struct((4, heads, slots, width), BF)] * (devices // 2),
         compiler_params=params(),
         name="fold",

time: 117 us -> 109 us (0.932)
  waiting for transfers between devices: 39.2 us -> 22.8 us
  Pallas kernels: 49.4 us -> 53.7 us
  starting transfers between devices: 22.8 us -> 26.9 us
    ppermute x12, waiting for transfers between devices: 16.7 us -> 6.59 us  [swap(): return lax.ppermute(value, 'ctx', [(i, i ^ mask) for i in range(devices)])]
    ppermute x3, starting transfers between devices: 8.56 us -> 15.7 us  [from_far(): return lax.ppermute(value, 'ctx', pairs + [(j, i) for i, j in pairs])]
    pallas_call x1 -> x2, Pallas kernels: 3.73 us -> 10.6 us  [the longest x1 8.03 us: shards(): pl.pallas_call(functools.partial(window_kernel, scale2), grid=(heads,), i...]
    ppermute x3, waiting for transfers between devices: 18.7 us -> 15.3 us  [from_far(): return lax.ppermute(value, 'ctx', pairs + [(j, i) for i, j in pairs])]
    all_to_all x1, waiting for transfers between devices: 3.83 us -> 0.89 us  [shards(): stats = lax.all_to_all(stats, 'ctx', 0, 0, tiled=True)]
    pallas_call x1, Pallas kernels: 14.2 us -> 11.6 us  [shards(): pl.pallas_call(functools.partial(local_kernel, scale, scale2), grid=(head...]
    all_to_all x1, starting transfers between devices: 5.25 us -> 3.36 us  [shards(): stats = lax.all_to_all(stats, 'ctx', 0, 0, tiled=True)]
  transfers between devices with their start and end apart: 16 -> 16, of which waited for: 6 -> 5; matrix products, arithmetic and copies ran while one was open for 0% -> 0% of each run, Pallas kernels for 31% -> 42%
where the time goes in v6:
time: 109 us; the launch traced here: 107 us
  Pallas kernels  53.7 us (49%)
  starting transfers between devices  26.9 us (25%)
  waiting for transfers between devices  22.8 us (21%)
  local copies, waits for them, and re-layouts  1.43 us (1%)
  other arithmetic  1.24 us (1%)
    ppermute x3, starting transfers between devices, from_far(): return lax.ppermute(value, 'ctx', pairs + [(j, i) for i, j in pairs])  15.7 us
    ppermute x3, waiting for transfers between devices, from_far(): return lax.ppermute(value, 'ctx', pairs + [(j, i) for i, j in pairs])  15.3 us
    pallas_call x1, Pallas kernels, shards(): pl.pallas_call(functools.partial(local_kernel, scale, scale2), grid=(head...  11.6 us
    pallas_call x1, Pallas kernels, shards(): pl.pallas_call(functools.partial(window_kernel, scale2), grid=(heads,), i...  8.03 us
    ppermute x12, starting transfers between devices, swap(): return lax.ppermute(value, 'ctx', [(i, i ^ mask) for i in range(devices)])  7.85 us
    pallas_call x1, Pallas kernels, shards(): pl.pallas_call(functools.partial(rim_kernel, scale, scale2), grid=(heads,...  7.15 us
    ppermute x12, waiting for transfers between devices, swap(): return lax.ppermute(value, 'ctx', [(i, i ^ mask) for i in range(devices)])  6.59 us
    pallas_call x1, Pallas kernels, shards(): pl.pallas_call(functools.partial(global_kernel, scale, scale2), grid=(hea...  6.59 us
  transfers between devices with their start and end apart: 16, of which 5 were waited for; matrix products, arithmetic and copies ran while one was open for 0% of the time, Pallas kernels for 42%

profile of v6, /device:TPU:1, one launch (start us, length us, event | category | flops | bytes accessed | tf_op | source)
XLA Modules:
  0.0 106.9 jit_solution(4045461036115002433)
XLA Ops:
  0.6 2.4 %pack_keys.1.kv.refs_5_ = bf16[2,4,512,128]{3,2,1,0:T(8,128)(2,1)} custom-call(bf16[2048,128]{1,0:T(8,128)(2,1)} %bitcast.15, bf16[2048,128]{1,0:T(8,128)(2,1)} %bitcast.16), custom_call_target="tpu_custom_call" | custom-call | tf_op jit(solution)/shard_map/pack_keys/pallas_call | solution.py:407
  3.1 0.1 collective-permute-start
  3.1 4.4 %collective-permute-start.1 = (bf16[2,4,512,128]{3,2,1,0:T(8,128)(2,1)}, bf16[2,4,512,128]{3,2,1,0:T(8,128)(2,1)}, u32[]{:S(2)}, u32[]{:S(2)}) collective-permute-start(bf16[2,4,512,128]{3,2,1,0:T(8,128)(2,1)} %pack_keys.1.kv.refs_5_), channel_id=1, source_target_pairs={{4,8},{12,16},{20,24},{8,4},{16,12},{24,20},{5,9},{13,17},{21,25},... | collective-permute-start | bytes 3145736 | tf_op jit(solution)/shard_map/ppermute | solution.py:396
  7.6 3.4 %pack_queries.1 = (bf16[2,4,512,128]{3,2,1,0:T(8,128)(2,1)}, bf16[4,4,64,128]{3,2,1,0:T(8,128)(2,1)}) custom-call(bf16[2048,128]{1,0:T(8,128)(2,1)} %bitcast.17, bf16[2048,128]{1,0:T(8,128)(2,1)} %bitcast.18, bf16[2,4,512,128]{3,2,1,0:T(8,128)(2,1)} %pack_keys.1.kv.refs_5_, s32[1,256]{1,0:T(1,128)} %bitcast.19), custom_call_target="tpu_custom_call" | custom-call | tf_op jit(solution)/shard_map/pack_queries/pallas_call | solution.py:415
  11.0 1.2 %collective-permute-start.2 = (bf16[1,4,4,64,128]{4,3,2,1,0:T(8,128)(2,1)}, bf16[1,4,4,64,128]{4,3,2,1,0:T(8,128)(2,1)S(1)}, u32[]{:S(2)}, u32[]{:S(2)}) collective-permute-start(bf16[1,4,4,64,128]{4,3,2,1,0:T(8,128)(2,1)} %bitcast.10), channel_id=1, source_target_pairs={{0,8},{4,12},{8,0},{12,4},{16,24},{20,28},{24,16},{28,20},{1,9},{5... | collective-permute-start | bytes 786440 | tf_op jit(solution)/shard_map/ppermute | solution.py:389
  12.2 0.0 collective-permute-start.3
  12.2 1.4 %collective-permute-start.4 = (bf16[1,4,4,64,128]{4,3,2,1,0:T(8,128)(2,1)}, bf16[1,4,4,64,128]{4,3,2,1,0:T(8,128)(2,1)}, u32[]{:S(2)}, u32[]{:S(2)}) collective-permute-start(bf16[1,4,4,64,128]{4,3,2,1,0:T(8,128)(2,1)} %bitcast.12), channel_id=1, source_target_pairs={{0,24},{4,28},{8,16},{12,20},{16,8},{20,12},{24,0},{28,4},{1,25},{... | collective-permute-start | bytes 786440 | tf_op jit(solution)/shard_map/ppermute | solution.py:389
  13.6 2.2 %masks.1 = (f32[1536,128]{1,0:T(8,128)}, bf16[256,512]{1,0:T(8,128)(2,1)}, bf16[512,256]{1,0:T(8,128)(2,1)}, bf16[512,64]{1,0:T(8,128)(2,1)}) custom-call(s32[1,256]{1,0:T(1,128)} %bitcast.20), custom_call_target="tpu_custom_call" | custom-call | tf_op jit(solution)/shard_map/masks/pallas_call | solution.py:427
  15.9 0.0 collective-permute-done.kv_near
  15.9 15.1 %collective-permute-done.1.kv_far = bf16[2,4,512,128]{3,2,1,0:T(8,128)(2,1)} collective-permute-done((bf16[2,4,512,128]{3,2,1,0:T(8,128)(2,1)}, bf16[2,4,512,128]{3,2,1,0:T(8,128)(2,1)}, u32[]{:S(2)}, u32[]{:S(2)}) %collective-permute-start.1) | collective-permute-done | bytes 1048608 | tf_op jit(solution)/shard_map/ppermute | solution.py:396
  31.0 8.0 %window.1 = (bf16[4,1536,512]{2,1,0:T(8,128)(2,1)}, f32[4,128,512]{2,1,0:T(8,128)}, f32[4,2,512]{2,1,0:T(2,128)}) custom-call(bf16[2,4,512,128]{3,2,1,0:T(8,128)(2,1)} %get-tuple-element.55.qd, bf16[2,4,512,128]{3,2,1,0:T(8,128)(2,1)} %pack_keys.1.kv.refs_5_, bf16[2,4,512,128]{3,2,1,0:T(8,128)(2,1)} %collective-permute-done.kv_near, ...), custom_call_target="tpu_custom_call" | custom-call | flops 1000000 | bytes 1000000 | tf_op jit(solution)/shard_map/window/pallas_call | solution.py:442
  39.0 0.0 collective-permute-done.2.refs_1_
  39.1 0.0 collective-permute-done.3.refs_2_
  39.1 0.0 collective-permute-done.4.refs_3_
  39.1 1.2 %pad_maximum_fusion = bf16[4,4,4,64,128]{4,3,2,1,0:T(8,128)(2,1)S(1)} fusion(bf16[1,4,4,64,128]{4,3,2,1,0:T(8,128)(2,1)} %collective-permute-done.4.refs_3_, bf16[1,4,4,64,128]{4,3,2,1,0:T(8,128)(2,1)S(1)} %collective-permute-done.3.refs_2_, bf16[1,4,4,64,128]{4,3,2,1,0:T(8,128)(2,1)S(1)} %collective-permute-done.2.refs_1_, ...), kind=kLoop, calls=%fused_computation | loop fusion | flops 1572864 | bytes 2097152 | tf_op jit(solution)/shard_map/concatenate | solution.py:469
  40.3 0.1 collective-permute-start.5
  40.4 0.5 collective-permute-start.6
  40.9 8.2 %collective-permute-start.7 = (bf16[2,4,512,128]{3,2,1,0:T(8,128)(2,1)}, bf16[2,4,512,128]{3,2,1,0:T(8,128)(2,1)}, u32[]{:S(2)}, u32[]{:S(2)}) collective-permute-start(bf16[2,4,512,128]{3,2,1,0:T(8,128)(2,1)} %get-tuple-element.55.qd), channel_id=1, source_target_pairs={{4,8},{12,16},{20,24},{8,4},{16,12},{24,20},{5,9},{13,17},{21,25},... | collective-permute-start | bytes 3145736 | tf_op jit(solution)/shard_map/ppermute | solution.py:396
  49.1 0.0 collective-permute-done.5.refs_4_
  49.1 5.5 %global_stats.1 = (bf16[4,4,256,128]{3,2,1,0:T(8,128)(2,1)}, f32[8,4,8,256]{3,2,1,0:T(8,128)}) custom-call(bf16[256,512]{1,0:T(8,128)(2,1)} %get-tuple-element.41.compact, bf16[1,4,4,64,128]{4,3,2,1,0:T(8,128)(2,1)} %bitcast.13, bf16[1,4,4,64,128]{4,3,2,1,0:T(8,128)(2,1)} %copy-done.2, bf16[1,4,4,64,128]{4,3,2,1,0:T(8,128)(2,1)} %copy-done.3, ...), custom_call_target="tpu_custom_call" | custom-call | flops 1000000 | bytes 1000000 | tf_op jit(solution)/shard_map/global_stats/pallas_call | solution.py:473
  54.6 3.4 %all-to-all-start = ((f32[8,4,8,256]{3,2,1,0:T(8,128)}), f32[8,4,8,256]{3,2,1,0:T(8,128)S(1)}, u32[]{:S(2)}, u32[]{:S(2)}) async-start(f32[8,4,8,256]{3,2,1,0:T(8,128)} %get-tuple-element.57), calls=%async_computation | async-start | bytes 524288 | tf_op jit(solution)/shard_map/all_to_all | solution.py:486
  58.0 11.6 %local.1 = (bf16[4,512,128]{2,1,0:T(8,128)(2,1)}, f32[4,2,512]{2,1,0:T(2,128)}, f32[4,512,128]{2,1,0:T(8,128)}, f32[2,4,512,128]{3,2,1,0:T(8,128)}, bf16[4,2,4,6...) custom-call(bf16[2,4,512,128]{3,2,1,0:T(8,128)(2,1)} %get-tuple-element.55.qd, ...), custom_call_target="tpu_custom_call" | custom-call | flops 1000000 | bytes 1000000 | tf_op jit(solution)/shard_map/local/pallas_call | solution.py:493
  69.6 0.1 collective-permute-start.8
  69.7 3.1 %collective-permute-start.9 = (f32[4,2,512]{2,1,0:T(2,128)}, f32[4,2,512]{2,1,0:T(2,128)S(1)}, u32[]{:S(2)}, u32[]{:S(2)}) collective-permute-start(f32[4,2,512]{2,1,0:T(2,128)} %get-tuple-element.56), channel_id=1, source_target_pairs={{4,8},{12,16},{20,24},{8,4},{16,12},{24,20},{5,9},{13,17},{21,25},... | collective-permute-start | bytes 49160 | tf_op jit(solution)/shard_map/ppermute | solution.py:396
  72.8 0.1 collective-permute-start.11
  72.9 0.0 collective-permute-done.6.qd_near
  72.9 0.2 collective-permute-done.7.qd_far
  73.1 0.9 all-to-all-done.stats
  74.0 0.7 copy-done
  74.7 6.6 %global_queries.1 = (f32[2,4,512,128]{3,2,1,0:T(8,128)}, bf16[4,2,4,64,128]{4,3,2,1,0:T(8,128)(2,1)}, bf16[4,2,4,64,128]{4,3,2,1,0:T(8,128)(2,1)}) custom-call(bf16[2,4,512,128]{3,2,1,0:T(8,128)(2,1)} %pack_keys.1.kv.refs_5_, bf16[4,4,256,128]{3,2,1,0:T(8,128)(2,1)} %get-tuple-element.49.rows, ...), custom_call_target="tpu_custom_call", output_to_operand_aliasing={{0}: (4, {})} | custom-call | flops 1000000 | bytes 1000000 | tf_op jit(solution)/shard_map/global_queries/pallas_call | solution.py:526
  81.2 0.0 collective-permute-done.8.log_near
  81.3 0.0 collective-permute-done.9.log_far
  81.3 0.0 copy-start.9
  81.3 1.7 %collective-permute-start.10 = (bf16[4,2,4,64,128]{4,3,2,1,0:T(8,128)(2,1)}, bf16[4,2,4,64,128]{4,3,2,1,0:T(8,128)(2,1)}, u32[]{:S(2)}, u32[]{:S(2)}) collective-permute-start(bf16[4,2,4,64,128]{4,3,2,1,0:T(8,128)(2,1)} %get-tuple-element.63), channel_id=1, source_target_pairs={{0,4},{4,0},{8,12},{12,8},{16,20},{20,16},{24,28},{28,24},{1,5},{5... | collective-permute-start | bytes 1572872 | tf_op jit(solution)/shard_map/ppermute | solution.py:389
  82.9 0.0 collective-permute-done.11.got_sums
  83.0 1.9 %collective-permute-done.10.got_ends = bf16[4,2,4,64,128]{4,3,2,1,0:T(8,128)(2,1)} collective-permute-done((bf16[4,2,4,64,128]{4,3,2,1,0:T(8,128)(2,1)}, bf16[4,2,4,64,128]{4,3,2,1,0:T(8,128)(2,1)}, u32[]{:S(2)}, u32[]{:S(2)}) %collective-permute-start.10) | collective-permute-done | bytes 524320 | tf_op jit(solution)/shard_map/ppermute | solution.py:389
  84.8 2.6 %fold.1 = (bf16[4,4,64,128]{3,2,1,0:T(8,128)(2,1)}, bf16[4,4,64,128]{3,2,1,0:T(8,128)(2,1)}, bf16[4,4,64,128]{3,2,1,0:T(8,128)(2,1)}, bf16[4,4,64,128]{3,2,1,0:T(8,128)(2,1)}) custom-call(bf16[4,2,4,64,128]{4,3,2,1,0:T(8,128)(2,1)} %get-tuple-element.61.kept_ends, bf16[4,2,4,64,128]{4,3,2,1,0:T(8,128)(2,1)} %collective-permute-done.10.got_ends, ...), custom_call_target="tpu_custom_call" | custom-call | tf_op jit(solution)/shard_map/fold/pallas_call | solution.py:542
  87.4 0.0 collective-permute-start.12
  87.4 1.6 %collective-permute-start.13 = (bf16[4,4,64,128]{3,2,1,0:T(8,128)(2,1)}, bf16[4,4,64,128]{3,2,1,0:T(8,128)(2,1)S(1)}, u32[]{:S(2)}, u32[]{:S(2)}) collective-permute-start(bf16[4,4,64,128]{3,2,1,0:T(8,128)(2,1)} %get-tuple-element.68), channel_id=1, source_target_pairs={{0,16},{4,20},{8,24},{12,28},{16,0},{20,4},{24,8},{28,12},{1,17},{... | collective-permute-start | bytes 786440 | tf_op jit(solution)/shard_map/ppermute | solution.py:389
  89.0 1.2 %collective-permute-start.14 = (bf16[4,4,64,128]{3,2,1,0:T(8,128)(2,1)}, bf16[4,4,64,128]{3,2,1,0:T(8,128)(2,1)S(1)}, u32[]{:S(2)}, u32[]{:S(2)}) collective-permute-start(bf16[4,4,64,128]{3,2,1,0:T(8,128)(2,1)} %get-tuple-element.69), channel_id=1, source_target_pairs={{0,24},{4,28},{8,16},{12,20},{16,8},{20,12},{24,0},{28,4},{1,25},{... | collective-permute-start | bytes 786440 | tf_op jit(solution)/shard_map/ppermute | solution.py:389
  90.2 7.1 %rim.1.dkv = f32[2,4,512,128]{3,2,1,0:T(8,128)} custom-call(bf16[2,4,512,128]{3,2,1,0:T(8,128)(2,1)} %pack_keys.1.kv.refs_5_, f32[1536,128]{1,0:T(8,128)} %get-tuple-element.43.bias, bf16[2,4,512,128]{3,2,1,0:T(8,128)(2,1)} %collective-permute-done.6.qd_near, bf16[2,4,512,128]{3,2,1,0:T(8,128)(2,1)} %collective-permute-done.7.qd_far, ...), custom_call_target="tpu_custom_call" | custom-call | flops 1000000 | bytes 1000000 | tf_op jit(solution)/shard_map/rim/pallas_call | solution.py:557
  97.4 0.0 collective-permute-done.12.refs_1_
  97.4 0.0 copy-start.5
  97.4 0.0 collective-permute-done.13.refs_2_
  97.4 4.7 %collective-permute-done.14.refs_3_ = bf16[4,4,64,128]{3,2,1,0:T(8,128)(2,1)S(1)} collective-permute-done((bf16[4,4,64,128]{3,2,1,0:T(8,128)(2,1)}, bf16[4,4,64,128]{3,2,1,0:T(8,128)(2,1)S(1)}, u32[]{:S(2)}, u32[]{:S(2)}) %collective-permute-start.14) | collective-permute-done | bytes 262176 | tf_op jit(solution)/shard_map/ppermute | solution.py:389
  102.1 0.0 copy-done.6
  102.1 0.7 copy-done.7
  102.8 4.2 %final.1 = (bf16[2048,128]{1,0:T(8,128)(2,1)}, f32[2048,128]{1,0:T(8,128)}, f32[2048,128]{1,0:T(8,128)}, f32[2048,128]{1,0:T(8,128)}) custom-call(bf16[512,64]{1,0:T(8,128)(2,1)} %get-tuple-element.39.place, bf16[4,512,128]{2,1,0:T(8,128)(2,1)} %get-tuple-element.53.out, f32[4,512,128]{2,1,0:T(8,128)} %get-tuple-element.54.dq, f32[2,4,512,128]{3,2,1,0:T(8,128)} %rim.1.dkv, ...), custom_call_target="tpu_custom_call" | custom-call | tf_op jit(solution)/shard_map/final/pallas_call | solution.py:580
  (15 shorter events, 0.0 us)
Async XLA Ops:
  3.1 12.8 %collective-permute-start = (bf16[2,4,512,128]{3,2,1,0:T(8,128)(2,1)}, bf16[2,4,512,128]{3,2,1,0:T(8,128)(2,1)}, u32[]{:S(2)}, u32[]{:S(2)}) collective-permute-start(bf16[2,4,512,128]{3,2,1,0:T(8,128)(2,1)} %pack_keys.1.kv.refs_5_), channel_id=1, source_target_pairs={{0,4},{4,0},{8,12},{12,8},{16,20},{20,16},{24,28},{28,24},{1,5},{5... | collective-permute-start | bytes 3145736 | tf_op jit(solution)/shard_map/ppermute | solution.py:389
  3.1 27.9 %collective-permute-start.1 = (bf16[2,4,512,128]{3,2,1,0:T(8,128)(2,1)}, bf16[2,4,512,128]{3,2,1,0:T(8,128)(2,1)}, u32[]{:S(2)}, u32[]{:S(2)}) collective-permute-start(bf16[2,4,512,128]{3,2,1,0:T(8,128)(2,1)} %pack_keys.1.kv.refs_5_), channel_id=1, source_target_pairs={{4,8},{12,16},{20,24},{8,4},{16,12},{24,20},{5,9},{13,17},{21,25},... | collective-permute-start | bytes 3145736 | tf_op jit(solution)/shard_map/ppermute | solution.py:396
  11.0 28.0 %collective-permute-start.2 = (bf16[1,4,4,64,128]{4,3,2,1,0:T(8,128)(2,1)}, bf16[1,4,4,64,128]{4,3,2,1,0:T(8,128)(2,1)S(1)}, u32[]{:S(2)}, u32[]{:S(2)}) collective-permute-start(bf16[1,4,4,64,128]{4,3,2,1,0:T(8,128)(2,1)} %bitcast.10), channel_id=1, source_target_pairs={{0,8},{4,12},{8,0},{12,4},{16,24},{20,28},{24,16},{28,20},{1,9},{5... | collective-permute-start | bytes 786440 | tf_op jit(solution)/shard_map/ppermute | solution.py:389
  12.2 26.9 %collective-permute-start.3 = (bf16[1,4,4,64,128]{4,3,2,1,0:T(8,128)(2,1)}, bf16[1,4,4,64,128]{4,3,2,1,0:T(8,128)(2,1)S(1)}, u32[]{:S(2)}, u32[]{:S(2)}) collective-permute-start(bf16[1,4,4,64,128]{4,3,2,1,0:T(8,128)(2,1)} %bitcast.11), channel_id=1, source_target_pairs={{0,16},{4,20},{8,24},{12,28},{16,0},{20,4},{24,8},{28,12},{1,17},{... | collective-permute-start | bytes 786440 | tf_op jit(solution)/shard_map/ppermute | solution.py:389
  12.2 26.8 %collective-permute-start.4 = (bf16[1,4,4,64,128]{4,3,2,1,0:T(8,128)(2,1)}, bf16[1,4,4,64,128]{4,3,2,1,0:T(8,128)(2,1)}, u32[]{:S(2)}, u32[]{:S(2)}) collective-permute-start(bf16[1,4,4,64,128]{4,3,2,1,0:T(8,128)(2,1)} %bitcast.12), channel_id=1, source_target_pairs={{0,24},{4,28},{8,16},{12,20},{16,8},{20,12},{24,0},{28,4},{1,25},{... | collective-permute-start | bytes 786440 | tf_op jit(solution)/shard_map/ppermute | solution.py:389
  31.0 8.1 %copy-start.1 = (bf16[4,4,64,128]{3,2,1,0:T(8,128)(2,1)S(1)}, bf16[4,4,64,128]{3,2,1,0:T(8,128)(2,1)}, u32[]{:S(2)}) copy-start(bf16[4,4,64,128]{3,2,1,0:T(8,128)(2,1)} %get-tuple-element.42) | copy-start | bytes 786436
  39.0 10.1 %copy-start.2 = (bf16[1,4,4,64,128]{4,3,2,1,0:T(8,128)(2,1)}, bf16[1,4,4,64,128]{4,3,2,1,0:T(8,128)(2,1)S(1)}, u32[]{:S(2)}) copy-start(bf16[1,4,4,64,128]{4,3,2,1,0:T(8,128)(2,1)S(1)} %collective-permute-done.2.refs_1_) | copy-start | bytes 786436
  39.1 10.1 %copy-start.3 = (bf16[1,4,4,64,128]{4,3,2,1,0:T(8,128)(2,1)}, bf16[1,4,4,64,128]{4,3,2,1,0:T(8,128)(2,1)S(1)}, u32[]{:S(2)}) copy-start(bf16[1,4,4,64,128]{4,3,2,1,0:T(8,128)(2,1)S(1)} %collective-permute-done.3.refs_2_) | copy-start | bytes 786436
  40.3 8.8 %collective-permute-start.5 = (bf16[4,4,4,64,128]{4,3,2,1,0:T(8,128)(2,1)S(1)}, bf16[4,4,4,64,128]{4,3,2,1,0:T(8,128)(2,1)}, u32[]{:S(2)}, u32[]{:S(2)}) collective-permute-start(bf16[4,4,4,64,128]{4,3,2,1,0:T(8,128)(2,1)S(1)} %pad_maximum_fusion), channel_id=1, source_target_pairs={{0,4},{4,0},{8,12},{12,8},{16,20},{20,16},{24,28},{28,24},{1,5},{5... | collective-permute-start | bytes 3145736 | tf_op jit(solution)/shard_map/ppermute | solution.py:389
  40.4 32.4 %collective-permute-start.6 = (bf16[2,4,512,128]{3,2,1,0:T(8,128)(2,1)}, bf16[2,4,512,128]{3,2,1,0:T(8,128)(2,1)}, u32[]{:S(2)}, u32[]{:S(2)}) collective-permute-start(bf16[2,4,512,128]{3,2,1,0:T(8,128)(2,1)} %get-tuple-element.55.qd), channel_id=1, source_target_pairs={{0,4},{4,0},{8,12},{12,8},{16,20},{20,16},{24,28},{28,24},{1,5},{5... | collective-permute-start | bytes 3145736 | tf_op jit(solution)/shard_map/ppermute | solution.py:389
  40.9 32.1 %collective-permute-start.7 = (bf16[2,4,512,128]{3,2,1,0:T(8,128)(2,1)}, bf16[2,4,512,128]{3,2,1,0:T(8,128)(2,1)}, u32[]{:S(2)}, u32[]{:S(2)}) collective-permute-start(bf16[2,4,512,128]{3,2,1,0:T(8,128)(2,1)} %get-tuple-element.55.qd), channel_id=1, source_target_pairs={{4,8},{12,16},{20,24},{8,4},{16,12},{24,20},{5,9},{13,17},{21,25},... | collective-permute-start | bytes 3145736 | tf_op jit(solution)/shard_map/ppermute | solution.py:396
  54.6 19.3 %all-to-all-start = ((f32[8,4,8,256]{3,2,1,0:T(8,128)}), f32[8,4,8,256]{3,2,1,0:T(8,128)S(1)}, u32[]{:S(2)}, u32[]{:S(2)}) async-start(f32[8,4,8,256]{3,2,1,0:T(8,128)} %get-tuple-element.57), calls=%async_computation | async-start | bytes 524288 | tf_op jit(solution)/shard_map/all_to_all | solution.py:486
  69.6 11.7 %collective-permute-start.8 = (f32[4,2,512]{2,1,0:T(2,128)}, f32[4,2,512]{2,1,0:T(2,128)S(1)}, u32[]{:S(2)}, u32[]{:S(2)}) collective-permute-start(f32[4,2,512]{2,1,0:T(2,128)} %get-tuple-element.56), channel_id=1, source_target_pairs={{0,4},{4,0},{8,12},{12,8},{16,20},{20,16},{24,28},{28,24},{1,5},{5... | collective-permute-start | bytes 49160 | tf_op jit(solution)/shard_map/ppermute | solution.py:389
  69.7 11.6 %collective-permute-start.9 = (f32[4,2,512]{2,1,0:T(2,128)}, f32[4,2,512]{2,1,0:T(2,128)S(1)}, u32[]{:S(2)}, u32[]{:S(2)}) collective-permute-start(f32[4,2,512]{2,1,0:T(2,128)} %get-tuple-element.56), channel_id=1, source_target_pairs={{4,8},{12,16},{20,24},{8,4},{16,12},{24,20},{5,9},{13,17},{21,25},... | collective-permute-start | bytes 49160 | tf_op jit(solution)/shard_map/ppermute | solution.py:396
  72.8 10.2 %collective-permute-start.11 = (bf16[4,2,4,64,128]{4,3,2,1,0:T(8,128)(2,1)}, bf16[4,2,4,64,128]{4,3,2,1,0:T(8,128)(2,1)S(1)}, u32[]{:S(2)}, u32[]{:S(2)}) collective-permute-start(bf16[4,2,4,64,128]{4,3,2,1,0:T(8,128)(2,1)} %get-tuple-element.65), channel_id=1, source_target_pairs={{0,4},{4,0},{8,12},{12,8},{16,20},{20,16},{24,28},{28,24},{1,5},{5... | collective-permute-start | bytes 1572872 | tf_op jit(solution)/shard_map/ppermute | solution.py:389
  73.9 0.7 copy-start
  81.3 9.0 %copy-start.8 = (f32[4,2,512]{2,1,0:T(2,128)}, f32[4,2,512]{2,1,0:T(2,128)S(1)}, u32[]{:S(2)}) copy-start(f32[4,2,512]{2,1,0:T(2,128)S(1)} %collective-permute-done.8.log_near) | copy-start | bytes 49156
  81.3 8.9 %copy-start.9 = (f32[4,2,512]{2,1,0:T(2,128)}, f32[4,2,512]{2,1,0:T(2,128)S(1)}, u32[]{:S(2)}) copy-start(f32[4,2,512]{2,1,0:T(2,128)S(1)} %collective-permute-done.9.log_far) | copy-start | bytes 49156
  81.3 3.5 %collective-permute-start.10 = (bf16[4,2,4,64,128]{4,3,2,1,0:T(8,128)(2,1)}, bf16[4,2,4,64,128]{4,3,2,1,0:T(8,128)(2,1)}, u32[]{:S(2)}, u32[]{:S(2)}) collective-permute-start(bf16[4,2,4,64,128]{4,3,2,1,0:T(8,128)(2,1)} %get-tuple-element.63), channel_id=1, source_target_pairs={{0,4},{4,0},{8,12},{12,8},{16,20},{20,16},{24,28},{28,24},{1,5},{5... | collective-permute-start | bytes 1572872 | tf_op jit(solution)/shard_map/ppermute | solution.py:389
  83.0 1.9 %copy-start.4 = (bf16[4,2,4,64,128]{4,3,2,1,0:T(8,128)(2,1)}, bf16[4,2,4,64,128]{4,3,2,1,0:T(8,128)(2,1)S(1)}, u32[]{:S(2)}) copy-start(bf16[4,2,4,64,128]{4,3,2,1,0:T(8,128)(2,1)S(1)} %collective-permute-done.11.got_sums) | copy-start | bytes 1572868
  87.4 9.9 %collective-permute-start.12 = (bf16[4,4,64,128]{3,2,1,0:T(8,128)(2,1)}, bf16[4,4,64,128]{3,2,1,0:T(8,128)(2,1)S(1)}, u32[]{:S(2)}, u32[]{:S(2)}) collective-permute-start(bf16[4,4,64,128]{3,2,1,0:T(8,128)(2,1)} %get-tuple-element.67), channel_id=1, source_target_pairs={{0,8},{4,12},{8,0},{12,4},{16,24},{20,28},{24,16},{28,20},{1,9},{5... | collective-permute-start | bytes 786440 | tf_op jit(solution)/shard_map/ppermute | solution.py:389
  87.4 9.9 %collective-permute-start.13 = (bf16[4,4,64,128]{3,2,1,0:T(8,128)(2,1)}, bf16[4,4,64,128]{3,2,1,0:T(8,128)(2,1)S(1)}, u32[]{:S(2)}, u32[]{:S(2)}) collective-permute-start(bf16[4,4,64,128]{3,2,1,0:T(8,128)(2,1)} %get-tuple-element.68), channel_id=1, source_target_pairs={{0,16},{4,20},{8,24},{12,28},{16,0},{20,4},{24,8},{28,12},{1,17},{... | collective-permute-start | bytes 786440 | tf_op jit(solution)/shard_map/ppermute | solution.py:389
  89.0 13.1 %collective-permute-start.14 = (bf16[4,4,64,128]{3,2,1,0:T(8,128)(2,1)}, bf16[4,4,64,128]{3,2,1,0:T(8,128)(2,1)S(1)}, u32[]{:S(2)}, u32[]{:S(2)}) collective-permute-start(bf16[4,4,64,128]{3,2,1,0:T(8,128)(2,1)} %get-tuple-element.69), channel_id=1, source_target_pairs={{0,24},{4,28},{8,16},{12,20},{16,8},{20,12},{24,0},{28,4},{1,25},{... | collective-permute-start | bytes 786440 | tf_op jit(solution)/shard_map/ppermute | solution.py:389
  97.4 4.7 %copy-start.5 = (bf16[4,4,64,128]{3,2,1,0:T(8,128)(2,1)}, bf16[4,4,64,128]{3,2,1,0:T(8,128)(2,1)S(1)}, u32[]{:S(2)}) copy-start(bf16[4,4,64,128]{3,2,1,0:T(8,128)(2,1)S(1)} %collective-permute-done.12.refs_1_) | copy-start | bytes 786436
  97.4 4.7 %copy-start.6 = (bf16[4,4,64,128]{3,2,1,0:T(8,128)(2,1)}, bf16[4,4,64,128]{3,2,1,0:T(8,128)(2,1)S(1)}, u32[]{:S(2)}) copy-start(bf16[4,4,64,128]{3,2,1,0:T(8,128)(2,1)S(1)} %collective-permute-done.13.refs_2_) | copy-start | bytes 786436
  102.1 0.7 copy-start.7

commit v7 on v6

--- a/solution.py
+++ b/solution.py
@@ -162,7 +162,7 @@
         out[2:4] = (kept_sums[part].astype(F32) + got_sums[part].astype(F32)).astype(BF)
 
 
-def global_kernel(scale, scale2, kv, rows, stats, expand, before, dkv, kept, sent):
+def global_kernel(scale, scale2, kv, rows, stats, expand, before, key_t, value_t, dkv, kept, sent):
     g_query, g_grad = rows[0, 0], rows[3, 0]
     tops = stats[:, 0, 0:1, :]
     top = jnp.max(tops, axis=0)
@@ -175,8 +175,8 @@
     slopes = (weights * (nt(kv[1, 0], g_grad) - g_dot)).astype(BF)
     dkv[0, 0] = before[0, 0] + nn(slopes, g_query) * scale
     dkv[1, 0] = before[1, 0] + nn(narrow, g_grad)
-    out = nn(kv[1, 0].T, narrow).T.astype(BF)
-    dq = (nn(kv[0, 0].T, slopes) * scale).T.astype(BF)
+    out = nn(value_t[0, 0], narrow).T.astype(BF)
+    dq = (nn(key_t[0], slopes) * scale).T.astype(BF)
     put_in_slots(expand[...], (out, dq), kept, sent)
 
 
@@ -188,14 +188,18 @@
 
 
 def window_kernel(
-    scale2, qd, kv, kv_near, kv_far, bias, probs, acc, top_sum, keys, values, score_buf
+    scale2, qd, kv, kv_near, kv_far, bias, probs, acc, top_sum, key_t, values, sides, keys, score_buf
 ):
     toks = kv.shape[2]
     reach = 2 * HALF + TILE
     gather_window(kv, kv_near, kv_far, 0, keys)
-    gather_window(kv, kv_near, kv_far, 1, values)
-    value_t = values[...].T
+    gather_window(kv, kv_near, kv_far, 1, values.at[0])
+    key_t[0] = keys[...].T
+    value_t = values[0].T
     query_t = qd[0, 0].T
+    sides[0, 0] = query_t
+    sides[1, 0] = qd[1, 0].T
+    sides[2, 0] = value_t[:, HALF : HALF + toks]
     tiles = range(toks // TILE)
     lanes = [slice(tile * TILE, (tile + 1) * TILE) for tile in tiles]
     pieces = range(reach // TILE)
@@ -237,17 +241,14 @@
 
 
 def local_kernel(
-    scale, scale2, qd, kv, kv_near, kv_far, rows, probs, acc, top_sum, expand,
-    out, log_dot, dq, dkv, kept, sent, keys, values, slopes,
+    scale, scale2, sides, key_t, values, rows, probs, acc, top_sum, expand,
+    out, log_dot, dq, dkv, kept, sent, slopes,
 ):
-    toks = kv.shape[2]
+    toks = acc.shape[2]
     reach = 2 * HALF + TILE
-    gather_window(kv, kv_near, kv_far, 0, keys)
-    gather_window(kv, kv_near, kv_far, 1, values)
-    key_t = keys[...].T
+    query_t, grad_t = sides[0, 0], sides[1, 0]
     g_keys, g_values = rows[1, 0], rows[2, 0]
     g_key_t, g_value_t = g_keys.T, g_values.T
-    query_t, grad_t = qd[0, 0].T, qd[1, 0].T
     grads = grad_t.astype(F32)
     scores = nn(g_keys, query_t) * scale2
     old = top_sum[0, 0:1, :]
@@ -271,12 +272,12 @@
         lanes = slice(tile * TILE, (tile + 1) * TILE)
         for piece in range(reach // TILE):
             span = slice((tile + piece) * TILE, (tile + piece + 1) * TILE)
-            rise = nn(values[span, :], w_grads[:, lanes]) - dots[:, lanes]
+            rise = nn(values[0, span, :], w_grads[:, lanes]) - dots[:, lanes]
             slopes[span, lanes] = (probs[0, span, lanes].astype(F32) * rise).astype(BF)
     for tile in range(toks // TILE):
         lanes = slice(tile * TILE, (tile + 1) * TILE)
         window = slice(tile * TILE, tile * TILE + reach)
-        part = nn(key_t[:, window], slopes[window, lanes]) + nn(g_key_t, g_slopes[:, lanes])
+        part = nn(key_t[0, :, window], slopes[window, lanes]) + nn(g_key_t, g_slopes[:, lanes])
         dq[0, lanes, :] = (part * scale).T
     own = slice(HALF, HALF + toks)
     dkv[0, 0] = (nt(query_t, slopes[own, :]) * scale).T
@@ -439,7 +440,9 @@
     kv_far, kv_near = from_far(kv), from_near(kv)
     probs_shape = (heads, span, toks)
     acc_shape = (heads, width, toks)
-    probs, acc, top_sum = pl.pallas_call(
+    turned_shape = (heads, width, span)
+    sides_shape = (3, heads, width, toks)
+    probs, acc, top_sum, key_t, values, sides = pl.pallas_call(
         functools.partial(window_kernel, scale2),
         grid=(heads,),
         in_specs=[per_head(pair_shape, 1)] * 4 + [whole(bias.shape)],
@@ -447,14 +450,19 @@
             per_head(probs_shape, 0),
             per_head(acc_shape, 0),
             per_head((heads, 2, toks), 0),
+            per_head(turned_shape, 0),
+            per_head((heads, span, width), 0),
+            per_head(sides_shape, 1),
         ),
         out_shape=(
             struct(probs_shape, BF),
             struct(acc_shape, F32),
             struct((heads, 2, toks), F32),
+            struct(turned_shape, BF),
+            struct((heads, span, width), BF),
+            struct(sides_shape, BF),
         ),
         scratch_shapes=[
-            pltpu.VMEM((span, width), BF),
             pltpu.VMEM((span, width), BF),
             pltpu.VMEM((toks // TILE, 2 * HALF + TILE, TILE), F32),
         ],
@@ -493,8 +501,9 @@
     out, log_dot, dq, dkv, kept_sums, sent_sums = pl.pallas_call(
         functools.partial(local_kernel, scale, scale2),
         grid=(heads,),
-        in_specs=[per_head(pair_shape, 1)] * 4
-        + [per_head(row_shape, 1), per_head(probs_shape, 0), per_head(acc_shape, 0)]
+        in_specs=[per_head(sides_shape, 1), per_head(turned_shape, 0)]
+        + [per_head((heads, span, width), 0), per_head(row_shape, 1)]
+        + [per_head(probs_shape, 0), per_head(acc_shape, 0)]
         + [per_head((heads, 2, toks), 0), whole(expand.shape)],
         out_specs=(
             per_head((heads, toks, width), 0),
@@ -513,28 +522,28 @@
             sum_struct,
         ),
         scratch_shapes=[
-            pltpu.VMEM((span, width), BF),
-            pltpu.VMEM((span, width), BF),
             pltpu.VMEM((span, toks), BF),
         ],
         compiler_params=params(),
         cost_estimate=cost(1e6, 1e6),
         name="local",
-    )(qd, kv, kv_near, kv_far, rows, probs, acc, top_sum, expand)
+    )(sides, key_t, values, rows, probs, acc, top_sum, expand)
     log_far, log_near = from_far(log_dot), from_near(log_dot)
 
     dkv, kept_ends, sent_ends = pl.pallas_call(
         functools.partial(global_kernel, scale, scale2),
         grid=(heads,),
         in_specs=[per_head(pair_shape, 1), per_head(row_shape, 1)]
-        + [per_head(stats.shape, 1), whole(expand.shape), per_head(pair_shape, 1)],
+        + [per_head(stats.shape, 1), whole(expand.shape), per_head(pair_shape, 1)]
+        + [pl.BlockSpec((1, width, toks), lambda head: (head, 0, HALF // toks))]
+        + [pl.BlockSpec((1, 1, width, toks), lambda head: (2, head, 0, 0))],
         out_specs=(per_head(pair_shape, 1), per_head(sum_shape, 2), per_head(sum_shape, 2)),
         out_shape=(struct(pair_shape, F32), sum_struct, sum_struct),
         input_output_aliases={4: 0},
         compiler_params=params(),
         cost_estimate=cost(1e6, 1e6),
         name="global_queries",
-    )(kv, rows, after(stats, (log_dot, qd_near, qd_far)), expand, dkv)
+    )(kv, rows, after(stats, (log_dot, qd_near, qd_far)), expand, dkv, key_t, sides)
     got_sums = from_near(sent_sums)
     got_ends = from_near(after(sent_ends, (log_near, log_far)))
 

time: 109 us -> 108 us (level)
  starting transfers between devices: 26.9 us -> 23.4 us
  waiting for transfers between devices: 22.8 us -> 24.8 us
    ppermute x3, starting transfers between devices: 15.7 us -> 10.5 us  [from_far(): return lax.ppermute(value, 'ctx', pairs + [(j, i) for i, j in pairs])]
    ppermute x12, waiting for transfers between devices: 6.59 us -> 9.74 us  [swap(): return lax.ppermute(value, 'ctx', [(i, i ^ mask) for i in range(devices)])]
    pallas_call x1, Pallas kernels: 8.03 us -> 9.16 us  [shards(): pl.pallas_call(functools.partial(window_kernel, scale2), grid=(heads,), i...]
  transfers between devices with their start and end apart: 16 -> 16, of which waited for: 5 -> 6; matrix products, arithmetic and copies ran while one was open for 0% -> 0% of each run, Pallas kernels for 42% -> 43%
where the time goes in v7:
time: 108 us; the launch traced here: 106 us
  Pallas kernels  54.7 us (51%)
  waiting for transfers between devices  24.8 us (23%)
  starting transfers between devices  23.4 us (22%)
  local copies, waits for them, and re-layouts  1.43 us (1%)
  other arithmetic  1.08 us (1%)
    ppermute x3, waiting for transfers between devices, from_far(): return lax.ppermute(value, 'ctx', pairs + [(j, i) for i, j in pairs])  14.8 us
    pallas_call x1, Pallas kernels, shards(): pl.pallas_call(functools.partial(local_kernel, scale, scale2), grid=(head...  11.2 us
    ppermute x3, starting transfers between devices, from_far(): return lax.ppermute(value, 'ctx', pairs + [(j, i) for i, j in pairs])  10.5 us
    ppermute x12, waiting for transfers between devices, swap(): return lax.ppermute(value, 'ctx', [(i, i ^ mask) for i in range(devices)])  9.74 us
    pallas_call x1, Pallas kernels, shards(): pl.pallas_call(functools.partial(window_kernel, scale2), grid=(heads,), i...  9.16 us
    ppermute x12, starting transfers between devices, swap(): return lax.ppermute(value, 'ctx', [(i, i ^ mask) for i in range(devices)])  8.67 us
    pallas_call x1, Pallas kernels, shards(): pl.pallas_call(functools.partial(rim_kernel, scale, scale2), grid=(heads,...  7.15 us
    pallas_call x1, Pallas kernels, shards(): pl.pallas_call(functools.partial(global_kernel, scale, scale2), grid=(hea...  6.77 us
  transfers between devices with their start and end apart: 16, of which 6 were waited for; matrix products, arithmetic and copies ran while one was open for 0% of the time, Pallas kernels for 43%

profile of v7, /device:TPU:1, one launch (start us, length us, event | category | flops | bytes accessed | tf_op | source)
XLA Modules:
  0.0 106.2 jit_solution(7086280613757763456)
XLA Ops:
  0.6 2.4 %pack_keys.1.kv.refs_5_ = bf16[2,4,512,128]{3,2,1,0:T(8,128)(2,1)} custom-call(bf16[2048,128]{1,0:T(8,128)(2,1)} %bitcast.15, bf16[2048,128]{1,0:T(8,128)(2,1)} %bitcast.16), custom_call_target="tpu_custom_call" | custom-call | tf_op jit(solution)/shard_map/pack_keys/pallas_call | solution.py:408
  3.1 4.5 %collective-permute-start.1 = (bf16[2,4,512,128]{3,2,1,0:T(8,128)(2,1)}, bf16[2,4,512,128]{3,2,1,0:T(8,128)(2,1)}, u32[]{:S(2)}, u32[]{:S(2)}) collective-permute-start(bf16[2,4,512,128]{3,2,1,0:T(8,128)(2,1)} %pack_keys.1.kv.refs_5_), channel_id=1, source_target_pairs={{4,8},{12,16},{20,24},{8,4},{16,12},{24,20},{5,9},{13,17},{21,25},... | collective-permute-start | bytes 3145736 | tf_op jit(solution)/shard_map/ppermute | solution.py:397
  7.6 0.1 collective-permute-start
  7.7 3.4 %pack_queries.1 = (bf16[2,4,512,128]{3,2,1,0:T(8,128)(2,1)}, bf16[4,4,64,128]{3,2,1,0:T(8,128)(2,1)}) custom-call(bf16[2048,128]{1,0:T(8,128)(2,1)} %bitcast.17, bf16[2048,128]{1,0:T(8,128)(2,1)} %bitcast.18, bf16[2,4,512,128]{3,2,1,0:T(8,128)(2,1)} %pack_keys.1.kv.refs_5_, s32[1,256]{1,0:T(1,128)} %bitcast.19), custom_call_target="tpu_custom_call" | custom-call | tf_op jit(solution)/shard_map/pack_queries/pallas_call | solution.py:416
  11.1 1.1 %collective-permute-start.4 = (bf16[1,4,4,64,128]{4,3,2,1,0:T(8,128)(2,1)}, bf16[1,4,4,64,128]{4,3,2,1,0:T(8,128)(2,1)S(1)}, u32[]{:S(2)}, u32[]{:S(2)}) collective-permute-start(bf16[1,4,4,64,128]{4,3,2,1,0:T(8,128)(2,1)} %bitcast.10), channel_id=1, source_target_pairs={{0,24},{4,28},{8,16},{12,20},{16,8},{20,12},{24,0},{28,4},{1,25},{... | collective-permute-start | bytes 786440 | tf_op jit(solution)/shard_map/ppermute | solution.py:390
  12.1 1.3 %collective-permute-start.3 = (bf16[1,4,4,64,128]{4,3,2,1,0:T(8,128)(2,1)}, bf16[1,4,4,64,128]{4,3,2,1,0:T(8,128)(2,1)S(1)}, u32[]{:S(2)}, u32[]{:S(2)}) collective-permute-start(bf16[1,4,4,64,128]{4,3,2,1,0:T(8,128)(2,1)} %bitcast.11), channel_id=1, source_target_pairs={{0,16},{4,20},{8,24},{12,28},{16,0},{20,4},{24,8},{28,12},{1,17},{... | collective-permute-start | bytes 786440 | tf_op jit(solution)/shard_map/ppermute | solution.py:390
  13.5 0.3 collective-permute-start.2
  13.7 2.2 %masks.1 = (f32[1536,128]{1,0:T(8,128)}, bf16[256,512]{1,0:T(8,128)(2,1)}, bf16[512,256]{1,0:T(8,128)(2,1)}, bf16[512,64]{1,0:T(8,128)(2,1)}) custom-call(s32[1,256]{1,0:T(1,128)} %bitcast.20), custom_call_target="tpu_custom_call" | custom-call | tf_op jit(solution)/shard_map/masks/pallas_call | solution.py:428
  15.9 14.8 %collective-permute-done.1.kv_far = bf16[2,4,512,128]{3,2,1,0:T(8,128)(2,1)} collective-permute-done((bf16[2,4,512,128]{3,2,1,0:T(8,128)(2,1)}, bf16[2,4,512,128]{3,2,1,0:T(8,128)(2,1)}, u32[]{:S(2)}, u32[]{:S(2)}) %collective-permute-start.1) | collective-permute-done | bytes 1048608 | tf_op jit(solution)/shard_map/ppermute | solution.py:397
  30.7 0.0 collective-permute-done.kv_near
  30.7 9.2 %window.1 = (bf16[4,1536,512]{2,1,0:T(8,128)(2,1)}, f32[4,128,512]{2,1,0:T(8,128)}, f32[4,2,512]{2,1,0:T(2,128)}, bf16[4,128,1536]{2,1,0:T(8,128)(2,1)}, bf16[4,...) custom-call(bf16[2,4,512,128]{3,2,1,0:T(8,128)(2,1)} %get-tuple-element.61.qd, ...), custom_call_target="tpu_custom_call" | custom-call | flops 1000000 | bytes 1000000 | tf_op jit(solution)/shard_map/window/pallas_call | solution.py:445
  39.9 0.0 collective-permute-done.4.refs_3_
  39.9 0.0 copy-start.2
  39.9 0.0 collective-permute-done.3.refs_2_
  39.9 2.9 %collective-permute-done.2.refs_1_ = bf16[1,4,4,64,128]{4,3,2,1,0:T(8,128)(2,1)} collective-permute-done((bf16[1,4,4,64,128]{4,3,2,1,0:T(8,128)(2,1)}, bf16[1,4,4,64,128]{4,3,2,1,0:T(8,128)(2,1)}, u32[]{:S(2)}, u32[]{:S(2)}) %collective-permute-start.2) | collective-permute-done | bytes 262176 | tf_op jit(solution)/shard_map/ppermute | solution.py:390
  42.8 1.1 %pad_maximum_fusion = bf16[4,4,4,64,128]{4,3,2,1,0:T(8,128)(2,1)S(1)} fusion(bf16[1,4,4,64,128]{4,3,2,1,0:T(8,128)(2,1)S(1)} %collective-permute-done.4.refs_3_, bf16[1,4,4,64,128]{4,3,2,1,0:T(8,128)(2,1)S(1)} %collective-permute-done.3.refs_2_, bf16[1,4,4,64,128]{4,3,2,1,0:T(8,128)(2,1)} %collective-permute-done.2.refs_1_, ...), kind=kLoop, calls=%fused_computation | loop fusion | flops 1572864 | bytes 2097152 | tf_op jit(solution)/shard_map/concatenate | solution.py:477
  43.9 0.1 collective-permute-start.5
  44.0 2.5 %collective-permute-start.7 = (bf16[2,4,512,128]{3,2,1,0:T(8,128)(2,1)}, bf16[2,4,512,128]{3,2,1,0:T(8,128)(2,1)}, u32[]{:S(2)}, u32[]{:S(2)}) collective-permute-start(bf16[2,4,512,128]{3,2,1,0:T(8,128)(2,1)} %get-tuple-element.61.qd), channel_id=1, source_target_pairs={{4,8},{12,16},{20,24},{8,4},{16,12},{24,20},{5,9},{13,17},{21,25},... | collective-permute-start | bytes 3145736 | tf_op jit(solution)/shard_map/ppermute | solution.py:397
  46.5 0.1 collective-permute-start.6
  46.5 0.2 collective-permute-done.5.refs_4_
  46.8 0.0 copy-done.2
  46.8 5.5 %global_stats.1 = (bf16[4,4,256,128]{3,2,1,0:T(8,128)(2,1)}, f32[8,4,8,256]{3,2,1,0:T(8,128)}) custom-call(bf16[256,512]{1,0:T(8,128)(2,1)} %get-tuple-element.48.compact, bf16[1,4,4,64,128]{4,3,2,1,0:T(8,128)(2,1)} %bitcast.13, bf16[1,4,4,64,128]{4,3,2,1,0:T(8,128)(2,1)} %collective-permute-done.2.refs_1_, bf16[1,4,4,64,128]{4,3,2,1,0:T(8,128)(2,1)} %copy-done.3, ...), custom_call_target="tpu_custom_call" | custom-call | flops 1000000 | bytes 1000000 | tf_op jit(solution)/shard_map/global_stats/pallas_call | solution.py:481
  52.3 4.3 %all-to-all-start = ((f32[8,4,8,256]{3,2,1,0:T(8,128)}), f32[8,4,8,256]{3,2,1,0:T(8,128)S(1)}, u32[]{:S(2)}, u32[]{:S(2)}) async-start(f32[8,4,8,256]{3,2,1,0:T(8,128)} %get-tuple-element.63), calls=%async_computation | async-start | bytes 524288 | tf_op jit(solution)/shard_map/all_to_all | solution.py:494
  56.6 11.2 %local.1 = (bf16[4,512,128]{2,1,0:T(8,128)(2,1)}, f32[4,2,512]{2,1,0:T(2,128)}, f32[4,512,128]{2,1,0:T(8,128)}, f32[2,4,512,128]{3,2,1,0:T(8,128)}, bf16[4,2,4,6...) custom-call(bf16[3,4,128,512]{3,2,1,0:T(8,128)(2,1)} %get-tuple-element.45.sides.value_t, ...), custom_call_target="tpu_custom_call" | custom-call | flops 1000000 | bytes 1000000 | tf_op jit(solution)/shard_map/local/pallas_call | solution.py:501
  67.8 3.5 %collective-permute-start.9 = (f32[4,2,512]{2,1,0:T(2,128)}, f32[4,2,512]{2,1,0:T(2,128)S(1)}, u32[]{:S(2)}, u32[]{:S(2)}) collective-permute-start(f32[4,2,512]{2,1,0:T(2,128)} %get-tuple-element.62), channel_id=1, source_target_pairs={{4,8},{12,16},{20,24},{8,4},{16,12},{24,20},{5,9},{13,17},{21,25},... | collective-permute-start | bytes 49160 | tf_op jit(solution)/shard_map/ppermute | solution.py:397
  71.4 0.1 collective-permute-start.8
  71.5 0.5 collective-permute-start.11
  72.0 0.0 collective-permute-done.7.qd_far
  72.0 0.0 collective-permute-done.6.qd_near
  72.0 0.3 all-to-all-done.stats
  72.3 0.7 copy-done
  73.0 6.8 %global_queries.1 = (f32[2,4,512,128]{3,2,1,0:T(8,128)}, bf16[4,2,4,64,128]{4,3,2,1,0:T(8,128)(2,1)}, bf16[4,2,4,64,128]{4,3,2,1,0:T(8,128)(2,1)}) custom-call(bf16[2,4,512,128]{3,2,1,0:T(8,128)(2,1)} %pack_keys.1.kv.refs_5_, bf16[4,4,256,128]{3,2,1,0:T(8,128)(2,1)} %get-tuple-element.55.rows, ...), custom_call_target="tpu_custom_call", output_to_operand_aliasing={{0}: (4, {})} | custom-call | flops 1000000 | bytes 1000000 | tf_op jit(solution)/shard_map/global_queries/pallas_call | solution.py:533
  79.7 0.0 collective-permute-done.9.log_far
  79.7 0.0 copy-start.8
  79.8 0.0 collective-permute-done.8.log_near
  79.8 2.2 %collective-permute-start.10 = (bf16[4,2,4,64,128]{4,3,2,1,0:T(8,128)(2,1)}, bf16[4,2,4,64,128]{4,3,2,1,0:T(8,128)(2,1)}, u32[]{:S(2)}, u32[]{:S(2)}) collective-permute-start(bf16[4,2,4,64,128]{4,3,2,1,0:T(8,128)(2,1)} %get-tuple-element.69), channel_id=1, source_target_pairs={{0,4},{4,0},{8,12},{12,8},{16,20},{20,16},{24,28},{28,24},{1,5},{5... | collective-permute-start | bytes 1572872 | tf_op jit(solution)/shard_map/ppermute | solution.py:390
  81.9 0.0 collective-permute-done.11.got_sums
  81.9 1.9 %collective-permute-done.10.got_ends = bf16[4,2,4,64,128]{4,3,2,1,0:T(8,128)(2,1)} collective-permute-done((bf16[4,2,4,64,128]{4,3,2,1,0:T(8,128)(2,1)}, bf16[4,2,4,64,128]{4,3,2,1,0:T(8,128)(2,1)}, u32[]{:S(2)}, u32[]{:S(2)}) %collective-permute-start.10) | collective-permute-done | bytes 524320 | tf_op jit(solution)/shard_map/ppermute | solution.py:390
  83.8 2.6 %fold.1 = (bf16[4,4,64,128]{3,2,1,0:T(8,128)(2,1)}, bf16[4,4,64,128]{3,2,1,0:T(8,128)(2,1)}, bf16[4,4,64,128]{3,2,1,0:T(8,128)(2,1)}, bf16[4,4,64,128]{3,2,1,0:T(8,128)(2,1)}) custom-call(bf16[4,2,4,64,128]{4,3,2,1,0:T(8,128)(2,1)} %get-tuple-element.67.kept_ends, bf16[4,2,4,64,128]{4,3,2,1,0:T(8,128)(2,1)} %collective-permute-done.10.got_ends, ...), custom_call_target="tpu_custom_call" | custom-call | tf_op jit(solution)/shard_map/fold/pallas_call | solution.py:551
  86.4 1.4 %collective-permute-start.12 = (bf16[4,4,64,128]{3,2,1,0:T(8,128)(2,1)}, bf16[4,4,64,128]{3,2,1,0:T(8,128)(2,1)S(1)}, u32[]{:S(2)}, u32[]{:S(2)}) collective-permute-start(bf16[4,4,64,128]{3,2,1,0:T(8,128)(2,1)} %get-tuple-element.73), channel_id=1, source_target_pairs={{0,8},{4,12},{8,0},{12,4},{16,24},{20,28},{24,16},{28,20},{1,9},{5... | collective-permute-start | bytes 786440 | tf_op jit(solution)/shard_map/ppermute | solution.py:390
  87.8 0.8 collective-permute-start.13
  88.6 0.9 collective-permute-start.14
  89.5 7.1 %rim.1.dkv = f32[2,4,512,128]{3,2,1,0:T(8,128)} custom-call(bf16[2,4,512,128]{3,2,1,0:T(8,128)(2,1)} %pack_keys.1.kv.refs_5_, f32[1536,128]{1,0:T(8,128)} %get-tuple-element.44.bias, bf16[2,4,512,128]{3,2,1,0:T(8,128)(2,1)} %collective-permute-done.6.qd_near, bf16[2,4,512,128]{3,2,1,0:T(8,128)(2,1)} %collective-permute-done.7.qd_far, ...), custom_call_target="tpu_custom_call" | custom-call | flops 1000000 | bytes 1000000 | tf_op jit(solution)/shard_map/rim/pallas_call | solution.py:566
  96.6 0.0 collective-permute-done.12.refs_1_
  96.6 0.0 collective-permute-done.13.refs_2_
  96.6 4.7 %collective-permute-done.14.refs_3_ = bf16[4,4,64,128]{3,2,1,0:T(8,128)(2,1)S(1)} collective-permute-done((bf16[4,4,64,128]{3,2,1,0:T(8,128)(2,1)}, bf16[4,4,64,128]{3,2,1,0:T(8,128)(2,1)S(1)}, u32[]{:S(2)}, u32[]{:S(2)}) %collective-permute-start.14) | collective-permute-done | bytes 262176 | tf_op jit(solution)/shard_map/ppermute | solution.py:390
  101.3 0.7 copy-done.7
  102.0 4.2 %final.1 = (bf16[2048,128]{1,0:T(8,128)(2,1)}, f32[2048,128]{1,0:T(8,128)}, f32[2048,128]{1,0:T(8,128)}, f32[2048,128]{1,0:T(8,128)}) custom-call(bf16[512,64]{1,0:T(8,128)(2,1)} %get-tuple-element.42.place, bf16[4,512,128]{2,1,0:T(8,128)(2,1)} %get-tuple-element.59.out, f32[4,512,128]{2,1,0:T(8,128)} %get-tuple-element.60.dq, f32[2,4,512,128]{3,2,1,0:T(8,128)} %rim.1.dkv, ...), custom_call_target="tpu_custom_call" | custom-call | tf_op jit(solution)/shard_map/final/pallas_call | solution.py:589
  (15 shorter events, 0.0 us)
Async XLA Ops:
  3.1 27.6 %collective-permute-start.1 = (bf16[2,4,512,128]{3,2,1,0:T(8,128)(2,1)}, bf16[2,4,512,128]{3,2,1,0:T(8,128)(2,1)}, u32[]{:S(2)}, u32[]{:S(2)}) collective-permute-start(bf16[2,4,512,128]{3,2,1,0:T(8,128)(2,1)} %pack_keys.1.kv.refs_5_), channel_id=1, source_target_pairs={{4,8},{12,16},{20,24},{8,4},{16,12},{24,20},{5,9},{13,17},{21,25},... | collective-permute-start | bytes 3145736 | tf_op jit(solution)/shard_map/ppermute | solution.py:397
  7.6 23.1 %collective-permute-start = (bf16[2,4,512,128]{3,2,1,0:T(8,128)(2,1)}, bf16[2,4,512,128]{3,2,1,0:T(8,128)(2,1)}, u32[]{:S(2)}, u32[]{:S(2)}) collective-permute-start(bf16[2,4,512,128]{3,2,1,0:T(8,128)(2,1)} %pack_keys.1.kv.refs_5_), channel_id=1, source_target_pairs={{0,4},{4,0},{8,12},{12,8},{16,20},{20,16},{24,28},{28,24},{1,5},{5... | collective-permute-start | bytes 3145736 | tf_op jit(solution)/shard_map/ppermute | solution.py:390
  11.1 28.8 %collective-permute-start.4 = (bf16[1,4,4,64,128]{4,3,2,1,0:T(8,128)(2,1)}, bf16[1,4,4,64,128]{4,3,2,1,0:T(8,128)(2,1)S(1)}, u32[]{:S(2)}, u32[]{:S(2)}) collective-permute-start(bf16[1,4,4,64,128]{4,3,2,1,0:T(8,128)(2,1)} %bitcast.10), channel_id=1, source_target_pairs={{0,24},{4,28},{8,16},{12,20},{16,8},{20,12},{24,0},{28,4},{1,25},{... | collective-permute-start | bytes 786440 | tf_op jit(solution)/shard_map/ppermute | solution.py:390
  12.1 27.8 %collective-permute-start.3 = (bf16[1,4,4,64,128]{4,3,2,1,0:T(8,128)(2,1)}, bf16[1,4,4,64,128]{4,3,2,1,0:T(8,128)(2,1)S(1)}, u32[]{:S(2)}, u32[]{:S(2)}) collective-permute-start(bf16[1,4,4,64,128]{4,3,2,1,0:T(8,128)(2,1)} %bitcast.11), channel_id=1, source_target_pairs={{0,16},{4,20},{8,24},{12,28},{16,0},{20,4},{24,8},{28,12},{1,17},{... | collective-permute-start | bytes 786440 | tf_op jit(solution)/shard_map/ppermute | solution.py:390
  13.5 29.4 %collective-permute-start.2 = (bf16[1,4,4,64,128]{4,3,2,1,0:T(8,128)(2,1)}, bf16[1,4,4,64,128]{4,3,2,1,0:T(8,128)(2,1)}, u32[]{:S(2)}, u32[]{:S(2)}) collective-permute-start(bf16[1,4,4,64,128]{4,3,2,1,0:T(8,128)(2,1)} %bitcast.12), channel_id=1, source_target_pairs={{0,8},{4,12},{8,0},{12,4},{16,24},{20,28},{24,16},{28,20},{1,9},{5... | collective-permute-start | bytes 786440 | tf_op jit(solution)/shard_map/ppermute | solution.py:390
  30.7 12.1 %copy-start.1 = (bf16[4,4,64,128]{3,2,1,0:T(8,128)(2,1)S(1)}, bf16[4,4,64,128]{3,2,1,0:T(8,128)(2,1)}, u32[]{:S(2)}) copy-start(bf16[4,4,64,128]{3,2,1,0:T(8,128)(2,1)} %get-tuple-element.49) | copy-start | bytes 786436
  39.9 6.9 %copy-start.2 = (bf16[1,4,4,64,128]{4,3,2,1,0:T(8,128)(2,1)}, bf16[1,4,4,64,128]{4,3,2,1,0:T(8,128)(2,1)S(1)}, u32[]{:S(2)}) copy-start(bf16[1,4,4,64,128]{4,3,2,1,0:T(8,128)(2,1)S(1)} %collective-permute-done.4.refs_3_) | copy-start | bytes 786436
  39.9 6.9 %copy-start.3 = (bf16[1,4,4,64,128]{4,3,2,1,0:T(8,128)(2,1)}, bf16[1,4,4,64,128]{4,3,2,1,0:T(8,128)(2,1)S(1)}, u32[]{:S(2)}) copy-start(bf16[1,4,4,64,128]{4,3,2,1,0:T(8,128)(2,1)S(1)} %collective-permute-done.3.refs_2_) | copy-start | bytes 786436
  43.9 2.9 %collective-permute-start.5 = (bf16[4,4,4,64,128]{4,3,2,1,0:T(8,128)(2,1)S(1)}, bf16[4,4,4,64,128]{4,3,2,1,0:T(8,128)(2,1)}, u32[]{:S(2)}, u32[]{:S(2)}) collective-permute-start(bf16[4,4,4,64,128]{4,3,2,1,0:T(8,128)(2,1)S(1)} %pad_maximum_fusion), channel_id=1, source_target_pairs={{0,4},{4,0},{8,12},{12,8},{16,20},{20,16},{24,28},{28,24},{1,5},{5... | collective-permute-start | bytes 3145736 | tf_op jit(solution)/shard_map/ppermute | solution.py:390
  44.0 28.0 %collective-permute-start.7 = (bf16[2,4,512,128]{3,2,1,0:T(8,128)(2,1)}, bf16[2,4,512,128]{3,2,1,0:T(8,128)(2,1)}, u32[]{:S(2)}, u32[]{:S(2)}) collective-permute-start(bf16[2,4,512,128]{3,2,1,0:T(8,128)(2,1)} %get-tuple-element.61.qd), channel_id=1, source_target_pairs={{4,8},{12,16},{20,24},{8,4},{16,12},{24,20},{5,9},{13,17},{21,25},... | collective-permute-start | bytes 3145736 | tf_op jit(solution)/shard_map/ppermute | solution.py:397
  46.5 25.5 %collective-permute-start.6 = (bf16[2,4,512,128]{3,2,1,0:T(8,128)(2,1)}, bf16[2,4,512,128]{3,2,1,0:T(8,128)(2,1)}, u32[]{:S(2)}, u32[]{:S(2)}) collective-permute-start(bf16[2,4,512,128]{3,2,1,0:T(8,128)(2,1)} %get-tuple-element.61.qd), channel_id=1, source_target_pairs={{0,4},{4,0},{8,12},{12,8},{16,20},{20,16},{24,28},{28,24},{1,5},{5... | collective-permute-start | bytes 3145736 | tf_op jit(solution)/shard_map/ppermute | solution.py:390
  52.3 19.9 %all-to-all-start = ((f32[8,4,8,256]{3,2,1,0:T(8,128)}), f32[8,4,8,256]{3,2,1,0:T(8,128)S(1)}, u32[]{:S(2)}, u32[]{:S(2)}) async-start(f32[8,4,8,256]{3,2,1,0:T(8,128)} %get-tuple-element.63), calls=%async_computation | async-start | bytes 524288 | tf_op jit(solution)/shard_map/all_to_all | solution.py:494
  67.8 11.9 %collective-permute-start.9 = (f32[4,2,512]{2,1,0:T(2,128)}, f32[4,2,512]{2,1,0:T(2,128)S(1)}, u32[]{:S(2)}, u32[]{:S(2)}) collective-permute-start(f32[4,2,512]{2,1,0:T(2,128)} %get-tuple-element.62), channel_id=1, source_target_pairs={{4,8},{12,16},{20,24},{8,4},{16,12},{24,20},{5,9},{13,17},{21,25},... | collective-permute-start | bytes 49160 | tf_op jit(solution)/shard_map/ppermute | solution.py:397
  71.4 8.4 %collective-permute-start.8 = (f32[4,2,512]{2,1,0:T(2,128)}, f32[4,2,512]{2,1,0:T(2,128)S(1)}, u32[]{:S(2)}, u32[]{:S(2)}) collective-permute-start(f32[4,2,512]{2,1,0:T(2,128)} %get-tuple-element.62), channel_id=1, source_target_pairs={{0,4},{4,0},{8,12},{12,8},{16,20},{20,16},{24,28},{28,24},{1,5},{5... | collective-permute-start | bytes 49160 | tf_op jit(solution)/shard_map/ppermute | solution.py:390
  71.5 10.5 %collective-permute-start.11 = (bf16[4,2,4,64,128]{4,3,2,1,0:T(8,128)(2,1)}, bf16[4,2,4,64,128]{4,3,2,1,0:T(8,128)(2,1)S(1)}, u32[]{:S(2)}, u32[]{:S(2)}) collective-permute-start(bf16[4,2,4,64,128]{4,3,2,1,0:T(8,128)(2,1)} %get-tuple-element.71), channel_id=1, source_target_pairs={{0,4},{4,0},{8,12},{12,8},{16,20},{20,16},{24,28},{28,24},{1,5},{5... | collective-permute-start | bytes 1572872 | tf_op jit(solution)/shard_map/ppermute | solution.py:390
  72.3 0.7 copy-start
  79.7 9.7 %copy-start.8 = (f32[4,2,512]{2,1,0:T(2,128)}, f32[4,2,512]{2,1,0:T(2,128)S(1)}, u32[]{:S(2)}) copy-start(f32[4,2,512]{2,1,0:T(2,128)S(1)} %collective-permute-done.9.log_far) | copy-start | bytes 49156
  79.8 9.7 %copy-start.9 = (f32[4,2,512]{2,1,0:T(2,128)}, f32[4,2,512]{2,1,0:T(2,128)S(1)}, u32[]{:S(2)}) copy-start(f32[4,2,512]{2,1,0:T(2,128)S(1)} %collective-permute-done.8.log_near) | copy-start | bytes 49156
  79.8 4.0 %collective-permute-start.10 = (bf16[4,2,4,64,128]{4,3,2,1,0:T(8,128)(2,1)}, bf16[4,2,4,64,128]{4,3,2,1,0:T(8,128)(2,1)}, u32[]{:S(2)}, u32[]{:S(2)}) collective-permute-start(bf16[4,2,4,64,128]{4,3,2,1,0:T(8,128)(2,1)} %get-tuple-element.69), channel_id=1, source_target_pairs={{0,4},{4,0},{8,12},{12,8},{16,20},{20,16},{24,28},{28,24},{1,5},{5... | collective-permute-start | bytes 1572872 | tf_op jit(solution)/shard_map/ppermute | solution.py:390
  81.9 1.9 %copy-start.4 = (bf16[4,2,4,64,128]{4,3,2,1,0:T(8,128)(2,1)}, bf16[4,2,4,64,128]{4,3,2,1,0:T(8,128)(2,1)S(1)}, u32[]{:S(2)}) copy-start(bf16[4,2,4,64,128]{4,3,2,1,0:T(8,128)(2,1)S(1)} %collective-permute-done.11.got_sums) | copy-start | bytes 1572868
  86.4 10.2 %collective-permute-start.12 = (bf16[4,4,64,128]{3,2,1,0:T(8,128)(2,1)}, bf16[4,4,64,128]{3,2,1,0:T(8,128)(2,1)S(1)}, u32[]{:S(2)}, u32[]{:S(2)}) collective-permute-start(bf16[4,4,64,128]{3,2,1,0:T(8,128)(2,1)} %get-tuple-element.73), channel_id=1, source_target_pairs={{0,8},{4,12},{8,0},{12,4},{16,24},{20,28},{24,16},{28,20},{1,9},{5... | collective-permute-start | bytes 786440 | tf_op jit(solution)/shard_map/ppermute | solution.py:390
  87.8 8.8 %collective-permute-start.13 = (bf16[4,4,64,128]{3,2,1,0:T(8,128)(2,1)}, bf16[4,4,64,128]{3,2,1,0:T(8,128)(2,1)S(1)}, u32[]{:S(2)}, u32[]{:S(2)}) collective-permute-start(bf16[4,4,64,128]{3,2,1,0:T(8,128)(2,1)} %get-tuple-element.74), channel_id=1, source_target_pairs={{0,16},{4,20},{8,24},{12,28},{16,0},{20,4},{24,8},{28,12},{1,17},{... | collective-permute-start | bytes 786440 | tf_op jit(solution)/shard_map/ppermute | solution.py:390
  88.6 12.7 %collective-permute-start.14 = (bf16[4,4,64,128]{3,2,1,0:T(8,128)(2,1)}, bf16[4,4,64,128]{3,2,1,0:T(8,128)(2,1)S(1)}, u32[]{:S(2)}, u32[]{:S(2)}) collective-permute-start(bf16[4,4,64,128]{3,2,1,0:T(8,128)(2,1)} %get-tuple-element.75), channel_id=1, source_target_pairs={{0,24},{4,28},{8,16},{12,20},{16,8},{20,12},{24,0},{28,4},{1,25},{... | collective-permute-start | bytes 786440 | tf_op jit(solution)/shard_map/ppermute | solution.py:390
  96.6 4.7 %copy-start.5 = (bf16[4,4,64,128]{3,2,1,0:T(8,128)(2,1)}, bf16[4,4,64,128]{3,2,1,0:T(8,128)(2,1)S(1)}, u32[]{:S(2)}) copy-start(bf16[4,4,64,128]{3,2,1,0:T(8,128)(2,1)S(1)} %collective-permute-done.12.refs_1_) | copy-start | bytes 786436
  96.6 4.7 %copy-start.6 = (bf16[4,4,64,128]{3,2,1,0:T(8,128)(2,1)}, bf16[4,4,64,128]{3,2,1,0:T(8,128)(2,1)S(1)}, u32[]{:S(2)}) copy-start(bf16[4,4,64,128]{3,2,1,0:T(8,128)(2,1)S(1)} %collective-permute-done.13.refs_2_) | copy-start | bytes 786436
  101.3 0.7 copy-start.7

commit v8 on v5

--- a/solution.py
+++ b/solution.py
@@ -422,13 +422,15 @@
         name="masks",
     )(pos_row)
 
+    kv_near = from_near(kv)
     held = [slot_rows[None]]
-    for number, stage in enumerate(stages):
-        send = jnp.concatenate(after(held, place), axis=0) if number else held[0]
-        held += [swap(send, mask) for mask in stage]
-        if not number:
-            kv_late = after(kv, held)
-            kv_far, kv_near = from_far(kv_late), from_near(kv_late)
+    for bit in range(1, bits):
+        if bit == 2:
+            kv_far = from_far(after(kv, held[1]))
+            held = after(held, place)
+        send = jnp.concatenate(held, axis=0) if bit > 1 else held[0]
+        held = list(held) + [swap(send, 1 << bit)]
+    held += [from_near(part) for part in held]
 
     row_shape = (4, heads, count, width)
     rows, stats = pl.pallas_call(
@@ -444,7 +446,7 @@
         name="global_stats",
     )(compact, *held, kv)
 
-    stats = lax.all_to_all(stats, "ctx", 0, 0, tiled=True)
+    stats = lax.all_to_all(after(stats, (kv_near, kv_far)), "ctx", 0, 0, tiled=True)
 
     sum_shape = (devices // 2, 2, heads, slots, width)
     sum_struct = struct(sum_shape, BF)
@@ -503,9 +505,6 @@
     first = stages[0]
     parts = pl.pallas_call(
         fold_kernel,
-        grid=(heads,),
-        in_specs=[per_head(sum_shape, 2)] * 4,
-        out_specs=[per_head((4, heads, slots, width), 1)] * (devices // 2),
         out_shape=[struct((4, heads, slots, width), BF)] * (devices // 2),
         compiler_params=params(),
         name="fold",

time: 117 us -> 110 us (0.940)
  waiting for transfers between devices: 39.2 us -> 25.3 us
  starting transfers between devices: 22.8 us -> 29.5 us
  local copies, waits for them, and re-layouts: 1.44 us -> 3.01 us
    ppermute x3, waiting for transfers between devices: 18.7 us -> 0.01 us  [from_far(): return lax.ppermute(value, 'ctx', pairs + [(j, i) for i, j in pairs])]
    ppermute x12 -> x13, starting transfers between devices: 8.99 us -> 15.3 us  [swap(): return lax.ppermute(value, 'ctx', [(i, i ^ mask) for i in range(devices)])]
    ppermute x12 -> x13, waiting for transfers between devices: 16.7 us -> 21.8 us  [swap(): return lax.ppermute(value, 'ctx', [(i, i ^ mask) for i in range(devices)])]
    unnamed x20 -> x24, local copies, waits for them, and re-layouts: 1.44 us -> 3.01 us
    pallas_call x1, Pallas kernels: 3.73 us -> 2.56 us  [shards(): pl.pallas_call(fold_kernel, out_shape=[struct((4, heads, slots, width), B...]
  transfers between devices with their start and end apart: 16 -> 17, of which waited for: 6 -> 6; matrix products, arithmetic and copies ran while one was open for 0% -> 0% of each run, Pallas kernels for 31% -> 33%
where the time goes in v8:
time: 110 us; the launch traced here: 108 us
  Pallas kernels  48.4 us (44%)
  starting transfers between devices  29.5 us (27%)
  waiting for transfers between devices  25.3 us (23%)
  local copies, waits for them, and re-layouts  3.01 us (3%)
    ppermute x13, waiting for transfers between devices, swap(): return lax.ppermute(value, 'ctx', [(i, i ^ mask) for i in range(devices)])  21.8 us
    ppermute x13, starting transfers between devices, swap(): return lax.ppermute(value, 'ctx', [(i, i ^ mask) for i in range(devices)])  15.3 us
    pallas_call x1, Pallas kernels, shards(): pl.pallas_call(functools.partial(local_kernel, scale, scale2), grid=(head...  14.2 us
    ppermute x3, starting transfers between devices, from_far(): return lax.ppermute(value, 'ctx', pairs + [(j, i) for i, j in pairs])  8.54 us
    pallas_call x1, Pallas kernels, shards(): pl.pallas_call(functools.partial(rim_kernel, scale, scale2), grid=(heads,...  7.13 us
    pallas_call x1, Pallas kernels, shards(): pl.pallas_call(functools.partial(global_kernel, scale, scale2), grid=(hea...  6.59 us
    all_to_all x1, starting transfers between devices, shards(): lax.all_to_all(after(stats, (kv_near, kv_far)), 'ctx', 0, 0, tiled=True)  5.65 us
    pallas_call x1, Pallas kernels, shards(): pl.pallas_call(functools.partial(stats_kernel, scale2), grid=(heads,), in...  5.58 us
  transfers between devices with their start and end apart: 17, of which 6 were waited for; matrix products, arithmetic and copies ran while one was open for 0% of the time, Pallas kernels for 33%

profile of v8, /device:TPU:1, one launch (start us, length us, event | category | flops | bytes accessed | tf_op | source)
XLA Modules:
  0.0 108.1 jit_solution(12336866694383133367)
XLA Ops:
  0.6 2.4 %pack_keys.1.kv.refs_6_ = bf16[2,4,512,128]{3,2,1,0:T(8,128)(2,1)} custom-call(bf16[2048,128]{1,0:T(8,128)(2,1)} %bitcast.14, bf16[2048,128]{1,0:T(8,128)(2,1)} %bitcast.15), custom_call_target="tpu_custom_call" | custom-call | tf_op jit(solution)/shard_map/pack_keys/pallas_call | solution.py:393
  3.1 3.4 %pack_queries.1 = (bf16[2,4,512,128]{3,2,1,0:T(8,128)(2,1)}, bf16[4,4,64,128]{3,2,1,0:T(8,128)(2,1)}) custom-call(bf16[2048,128]{1,0:T(8,128)(2,1)} %bitcast.16, bf16[2048,128]{1,0:T(8,128)(2,1)} %bitcast.17, bf16[2,4,512,128]{3,2,1,0:T(8,128)(2,1)} %pack_keys.1.kv.refs_6_, s32[1,256]{1,0:T(1,128)} %bitcast.18), custom_call_target="tpu_custom_call" | custom-call | tf_op jit(solution)/shard_map/pack_queries/pallas_call | solution.py:401
  6.5 2.0 %collective-permute-start.1 = (bf16[1,4,4,64,128]{4,3,2,1,0:T(8,128)(2,1)}, bf16[1,4,4,64,128]{4,3,2,1,0:T(8,128)(2,1)S(1)}, u32[]{:S(2)}, u32[]{:S(2)}) collective-permute-start(bf16[1,4,4,64,128]{4,3,2,1,0:T(8,128)(2,1)} %bitcast.10), channel_id=1, source_target_pairs={{0,8},{4,12},{8,0},{12,4},{16,24},{20,28},{24,16},{28,20},{1,9},{5... | collective-permute-start | bytes 786440 | tf_op jit(solution)/shard_map/ppermute | solution.py:375
  8.5 2.3 %masks.1 = (f32[1536,128]{1,0:T(8,128)}, bf16[256,512]{1,0:T(8,128)(2,1)}, bf16[512,256]{1,0:T(8,128)(2,1)}, bf16[512,64]{1,0:T(8,128)(2,1)}) custom-call(s32[1,256]{1,0:T(1,128)} %bitcast.19), custom_call_target="tpu_custom_call" | custom-call | tf_op jit(solution)/shard_map/masks/pallas_call | solution.py:413
  10.8 3.9 %collective-permute-done.1.refs_1_ = bf16[1,4,4,64,128]{4,3,2,1,0:T(8,128)(2,1)S(1)} collective-permute-done((bf16[1,4,4,64,128]{4,3,2,1,0:T(8,128)(2,1)}, bf16[1,4,4,64,128]{4,3,2,1,0:T(8,128)(2,1)S(1)}, u32[]{:S(2)}, u32[]{:S(2)}) %collective-permute-start.1) | collective-permute-done | bytes 262176 | tf_op jit(solution)/shard_map/ppermute | solution.py:375
  14.8 1.1 %pad_maximum_fusion = bf16[2,4,4,64,128]{4,3,2,1,0:T(8,128)(2,1)S(1)} fusion(bf16[1,4,4,64,128]{4,3,2,1,0:T(8,128)(2,1)S(1)} %collective-permute-done.1.refs_1_, bf16[1,4,4,64,128]{4,3,2,1,0:T(8,128)(2,1)} %bitcast.11), kind=kLoop, calls=%fused_computation | loop fusion | flops 262144 | bytes 1048576 | tf_op jit(solution)/shard_map/concatenate | solution.py:431
  15.9 1.2 %collective-permute-start.3 = (bf16[2,4,4,64,128]{4,3,2,1,0:T(8,128)(2,1)S(1)}, bf16[2,4,4,64,128]{4,3,2,1,0:T(8,128)(2,1)S(1)}, u32[]{:S(2)}, u32[]{:S(2)}) collective-permute-start(bf16[2,4,4,64,128]{4,3,2,1,0:T(8,128)(2,1)S(1)} %pad_maximum_fusion), channel_id=1, source_target_pairs={{0,16},{4,20},{8,24},{12,28},{16,0},{20,4},{24,8},{28,12},{1,17},{... | collective-permute-start | bytes 1572872 | tf_op jit(solution)/shard_map/ppermute | solution.py:375
  17.1 1.8 %collective-permute-start = (bf16[2,4,512,128]{3,2,1,0:T(8,128)(2,1)}, bf16[2,4,512,128]{3,2,1,0:T(8,128)(2,1)}, u32[]{:S(2)}, u32[]{:S(2)}) collective-permute-start(bf16[2,4,512,128]{3,2,1,0:T(8,128)(2,1)} %pack_keys.1.kv.refs_6_), channel_id=1, source_target_pairs={{0,4},{4,0},{8,12},{12,8},{16,20},{20,16},{24,28},{28,24},{1,5},{5... | collective-permute-start | bytes 3145736 | tf_op jit(solution)/shard_map/ppermute | solution.py:375
  18.9 3.0 %collective-permute-start.2 = (bf16[2,4,512,128]{3,2,1,0:T(8,128)(2,1)}, bf16[2,4,512,128]{3,2,1,0:T(8,128)(2,1)}, u32[]{:S(2)}, u32[]{:S(2)}) collective-permute-start(bf16[2,4,512,128]{3,2,1,0:T(8,128)(2,1)} %pack_keys.1.kv.refs_6_), channel_id=1, source_target_pairs={{4,8},{12,16},{20,24},{8,4},{16,12},{24,20},{5,9},{13,17},{21,25},... | collective-permute-start | bytes 3145736 | tf_op jit(solution)/shard_map/ppermute | solution.py:382
  22.0 9.4 %collective-permute-done.3.refs_2_ = bf16[2,4,4,64,128]{4,3,2,1,0:T(8,128)(2,1)S(1)} collective-permute-done((bf16[2,4,4,64,128]{4,3,2,1,0:T(8,128)(2,1)S(1)}, bf16[2,4,4,64,128]{4,3,2,1,0:T(8,128)(2,1)S(1)}, u32[]{:S(2)}, u32[]{:S(2)}) %collective-permute-start.3) | collective-permute-done | bytes 524320 | tf_op jit(solution)/shard_map/ppermute | solution.py:375
  31.4 4.9 %collective-permute-start.6 = (bf16[2,4,4,64,128]{4,3,2,1,0:T(8,128)(2,1)S(1)}, bf16[2,4,4,64,128]{4,3,2,1,0:T(8,128)(2,1)S(1)}, u32[]{:S(2)}, u32[]{:S(2)}) collective-permute-start(bf16[2,4,4,64,128]{4,3,2,1,0:T(8,128)(2,1)S(1)} %collective-permute-done.3.refs_2_), channel_id=1, source_target_pairs={{0,4},{4,0},{8,12},{12,8},{16,20},{20,16},{24,28},{28,24},{1,5},{5... | collective-permute-start | bytes 1572872 | tf_op jit(solution)/shard_map/ppermute | solution.py:375
  36.3 0.0 collective-permute-start.4
  36.3 0.5 collective-permute-start.5
  36.8 1.9 %collective-permute-done.4.refs_3_ = bf16[1,4,4,64,128]{4,3,2,1,0:T(8,128)(2,1)S(1)} collective-permute-done((bf16[1,4,4,64,128]{4,3,2,1,0:T(8,128)(2,1)}, bf16[1,4,4,64,128]{4,3,2,1,0:T(8,128)(2,1)S(1)}, u32[]{:S(2)}, u32[]{:S(2)}) %collective-permute-start.4) | collective-permute-done | bytes 262176 | tf_op jit(solution)/shard_map/ppermute | solution.py:375
  38.6 0.0 collective-permute-done.5.refs_4_
  38.6 0.0 collective-permute-done.6.refs_5_
  38.6 0.7 copy-done.8
  39.3 0.1 copy-done.9
  39.4 0.8 copy-done.4
  40.2 5.6 %global_stats.1 = (bf16[4,4,256,128]{3,2,1,0:T(8,128)(2,1)}, f32[8,4,8,256]{3,2,1,0:T(8,128)}) custom-call(bf16[256,512]{1,0:T(8,128)(2,1)} %get-tuple-element.40.compact, bf16[1,4,4,64,128]{4,3,2,1,0:T(8,128)(2,1)} %bitcast.13, bf16[1,4,4,64,128]{4,3,2,1,0:T(8,128)(2,1)} %copy-done.1, bf16[2,4,4,64,128]{4,3,2,1,0:T(8,128)(2,1)} %copy-done.3, ...), custom_call_target="tpu_custom_call" | custom-call | flops 1000000 | bytes 1000000 | tf_op jit(solution)/shard_map/global_stats/pallas_call | solution.py:436
  45.8 0.0 collective-permute-done.kv_near
  45.8 0.0 collective-permute-done.2.kv_far
  45.8 1.9 %collective-permute-start.8 = (bf16[2,4,512,128]{3,2,1,0:T(8,128)(2,1)}, bf16[2,4,512,128]{3,2,1,0:T(8,128)(2,1)}, u32[]{:S(2)}, u32[]{:S(2)}) collective-permute-start(bf16[2,4,512,128]{3,2,1,0:T(8,128)(2,1)} %get-tuple-element.48.qd), channel_id=1, source_target_pairs={{4,8},{12,16},{20,24},{8,4},{16,12},{24,20},{5,9},{13,17},{21,25},... | collective-permute-start | bytes 3145736 | tf_op jit(solution)/shard_map/ppermute | solution.py:382
  47.8 0.1 collective-permute-start.7
  47.8 5.6 %all-to-all-start = ((f32[8,4,8,256]{3,2,1,0:T(8,128)}), f32[8,4,8,256]{3,2,1,0:T(8,128)S(1)}, u32[]{:S(2)}, u32[]{:S(2)}) async-start(f32[8,4,8,256]{3,2,1,0:T(8,128)} %get-tuple-element.51), calls=%async_computation | async-start | bytes 524288 | tf_op jit(solution)/shard_map/all_to_all | solution.py:449
  53.5 14.2 %local.1 = (bf16[4,512,128]{2,1,0:T(8,128)(2,1)}, f32[4,2,512]{2,1,0:T(2,128)}, f32[4,512,128]{2,1,0:T(8,128)}, f32[2,4,512,128]{3,2,1,0:T(8,128)}, bf16[4,2,4,6...) custom-call(bf16[2,4,512,128]{3,2,1,0:T(8,128)(2,1)} %get-tuple-element.48.qd, ...), custom_call_target="tpu_custom_call" | custom-call | flops 1000000 | bytes 1000000 | tf_op jit(solution)/shard_map/local/pallas_call | solution.py:456
  67.7 3.6 %collective-permute-start.10 = (f32[4,2,512]{2,1,0:T(2,128)}, f32[4,2,512]{2,1,0:T(2,128)S(1)}, u32[]{:S(2)}, u32[]{:S(2)}) collective-permute-start(f32[4,2,512]{2,1,0:T(2,128)} %get-tuple-element.49), channel_id=1, source_target_pairs={{4,8},{12,16},{20,24},{8,4},{16,12},{24,20},{5,9},{13,17},{21,25},... | collective-permute-start | bytes 49160 | tf_op jit(solution)/shard_map/ppermute | solution.py:382
  71.3 0.1 collective-permute-start.9
  71.4 0.5 collective-permute-start.12
  71.9 3.4 %all-to-all-done.stats = f32[8,4,8,256]{3,2,1,0:T(8,128)S(1)} async-done(((f32[8,4,8,256]{3,2,1,0:T(8,128)}), f32[8,4,8,256]{3,2,1,0:T(8,128)S(1)}, u32[]{:S(2)}, u32[]{:S(2)}) %all-to-all-start) | async-done | bytes 262176 | tf_op jit(solution)/shard_map/all_to_all | solution.py:449
  75.3 0.0 collective-permute-done.8.qd_far
  75.3 0.0 collective-permute-done.7.qd_near
  75.3 0.7 copy-done
  76.0 6.6 %global_queries.1 = (f32[2,4,512,128]{3,2,1,0:T(8,128)}, bf16[4,2,4,64,128]{4,3,2,1,0:T(8,128)(2,1)}, bf16[4,2,4,64,128]{4,3,2,1,0:T(8,128)(2,1)}) custom-call(bf16[2,4,512,128]{3,2,1,0:T(8,128)(2,1)} %pack_keys.1.kv.refs_6_, bf16[4,4,256,128]{3,2,1,0:T(8,128)(2,1)} %get-tuple-element.43.rows, ...), custom_call_target="tpu_custom_call", output_to_operand_aliasing={{0}: (4, {})} | custom-call | flops 1000000 | bytes 1000000 | tf_op jit(solution)/shard_map/global_queries/pallas_call | solution.py:490
  82.6 0.0 collective-permute-done.10.log_far
  82.6 0.0 collective-permute-done.9.log_near
  82.7 1.5 %collective-permute-start.11 = (bf16[4,2,4,64,128]{4,3,2,1,0:T(8,128)(2,1)}, bf16[4,2,4,64,128]{4,3,2,1,0:T(8,128)(2,1)}, u32[]{:S(2)}, u32[]{:S(2)}) collective-permute-start(bf16[4,2,4,64,128]{4,3,2,1,0:T(8,128)(2,1)} %get-tuple-element.57), channel_id=1, source_target_pairs={{0,4},{4,0},{8,12},{12,8},{16,20},{20,16},{24,28},{28,24},{1,5},{5... | collective-permute-start | bytes 1572872 | tf_op jit(solution)/shard_map/ppermute | solution.py:375
  84.1 0.0 collective-permute-done.12.got_sums
  84.1 1.9 %collective-permute-done.11.got_ends = bf16[4,2,4,64,128]{4,3,2,1,0:T(8,128)(2,1)} collective-permute-done((bf16[4,2,4,64,128]{4,3,2,1,0:T(8,128)(2,1)}, bf16[4,2,4,64,128]{4,3,2,1,0:T(8,128)(2,1)}, u32[]{:S(2)}, u32[]{:S(2)}) %collective-permute-start.11) | collective-permute-done | bytes 524320 | tf_op jit(solution)/shard_map/ppermute | solution.py:375
  86.0 2.6 %fold.1 = (bf16[4,4,64,128]{3,2,1,0:T(8,128)(2,1)}, bf16[4,4,64,128]{3,2,1,0:T(8,128)(2,1)}, bf16[4,4,64,128]{3,2,1,0:T(8,128)(2,1)}, bf16[4,4,64,128]{3,2,1,0:T(8,128)(2,1)}) custom-call(bf16[4,2,4,64,128]{4,3,2,1,0:T(8,128)(2,1)} %get-tuple-element.55.kept_ends, bf16[4,2,4,64,128]{4,3,2,1,0:T(8,128)(2,1)} %collective-permute-done.11.got_ends, ...), custom_call_target="tpu_custom_call" | custom-call | tf_op jit(solution)/shard_map/fold/pallas_call | solution.py:506
  88.6 1.5 %collective-permute-start.13 = (bf16[4,4,64,128]{3,2,1,0:T(8,128)(2,1)}, bf16[4,4,64,128]{3,2,1,0:T(8,128)(2,1)S(1)}, u32[]{:S(2)}, u32[]{:S(2)}) collective-permute-start(bf16[4,4,64,128]{3,2,1,0:T(8,128)(2,1)} %get-tuple-element.61), channel_id=1, source_target_pairs={{0,8},{4,12},{8,0},{12,4},{16,24},{20,28},{24,16},{28,20},{1,9},{5... | collective-permute-start | bytes 786440 | tf_op jit(solution)/shard_map/ppermute | solution.py:375
  90.1 0.6 collective-permute-start.14
  90.7 0.6 collective-permute-start.15
  91.3 7.1 %rim.1.dkv = f32[2,4,512,128]{3,2,1,0:T(8,128)} custom-call(bf16[2,4,512,128]{3,2,1,0:T(8,128)(2,1)} %pack_keys.1.kv.refs_6_, f32[1536,128]{1,0:T(8,128)} %get-tuple-element.44.bias, bf16[2,4,512,128]{3,2,1,0:T(8,128)(2,1)} %collective-permute-done.7.qd_near, bf16[2,4,512,128]{3,2,1,0:T(8,128)(2,1)} %collective-permute-done.8.qd_far, ...), custom_call_target="tpu_custom_call" | custom-call | flops 1000000 | bytes 1000000 | tf_op jit(solution)/shard_map/rim/pallas_call | solution.py:521
  98.4 0.0 collective-permute-done.14.refs_2_
  98.5 4.7 %collective-permute-done.15.refs_3_ = bf16[4,4,64,128]{3,2,1,0:T(8,128)(2,1)S(1)} collective-permute-done((bf16[4,4,64,128]{3,2,1,0:T(8,128)(2,1)}, bf16[4,4,64,128]{3,2,1,0:T(8,128)(2,1)S(1)}, u32[]{:S(2)}, u32[]{:S(2)}) %collective-permute-start.15) | collective-permute-done | bytes 262176 | tf_op jit(solution)/shard_map/ppermute | solution.py:375
  103.2 0.7 copy-done.7
  103.9 4.2 %final.1 = (bf16[2048,128]{1,0:T(8,128)(2,1)}, f32[2048,128]{1,0:T(8,128)}, f32[2048,128]{1,0:T(8,128)}, f32[2048,128]{1,0:T(8,128)}) custom-call(bf16[512,64]{1,0:T(8,128)(2,1)} %get-tuple-element.36.place, bf16[4,512,128]{2,1,0:T(8,128)(2,1)} %get-tuple-element.46.out, f32[4,512,128]{2,1,0:T(8,128)} %get-tuple-element.47.dq, f32[2,4,512,128]{3,2,1,0:T(8,128)} %rim.1.dkv, ...), custom_call_target="tpu_custom_call" | custom-call | tf_op jit(solution)/shard_map/final/pallas_call | solution.py:544
  (20 shorter events, 0.0 us)
Async XLA Ops:
  6.5 8.3 %collective-permute-start.1 = (bf16[1,4,4,64,128]{4,3,2,1,0:T(8,128)(2,1)}, bf16[1,4,4,64,128]{4,3,2,1,0:T(8,128)(2,1)S(1)}, u32[]{:S(2)}, u32[]{:S(2)}) collective-permute-start(bf16[1,4,4,64,128]{4,3,2,1,0:T(8,128)(2,1)} %bitcast.10), channel_id=1, source_target_pairs={{0,8},{4,12},{8,0},{12,4},{16,24},{20,28},{24,16},{28,20},{1,9},{5... | collective-permute-start | bytes 786440 | tf_op jit(solution)/shard_map/ppermute | solution.py:375
  14.8 25.4 %copy-start.1 = (bf16[1,4,4,64,128]{4,3,2,1,0:T(8,128)(2,1)}, bf16[1,4,4,64,128]{4,3,2,1,0:T(8,128)(2,1)S(1)}, u32[]{:S(2)}) copy-start(bf16[1,4,4,64,128]{4,3,2,1,0:T(8,128)(2,1)S(1)} %collective-permute-done.1.refs_1_) | copy-start | bytes 786436
  15.9 15.5 %collective-permute-start.3 = (bf16[2,4,4,64,128]{4,3,2,1,0:T(8,128)(2,1)S(1)}, bf16[2,4,4,64,128]{4,3,2,1,0:T(8,128)(2,1)S(1)}, u32[]{:S(2)}, u32[]{:S(2)}) collective-permute-start(bf16[2,4,4,64,128]{4,3,2,1,0:T(8,128)(2,1)S(1)} %pad_maximum_fusion), channel_id=1, source_target_pairs={{0,16},{4,20},{8,24},{12,28},{16,0},{20,4},{24,8},{28,12},{1,17},{... | collective-permute-start | bytes 1572872 | tf_op jit(solution)/shard_map/ppermute | solution.py:375
  17.1 28.7 %collective-permute-start = (bf16[2,4,512,128]{3,2,1,0:T(8,128)(2,1)}, bf16[2,4,512,128]{3,2,1,0:T(8,128)(2,1)}, u32[]{:S(2)}, u32[]{:S(2)}) collective-permute-start(bf16[2,4,512,128]{3,2,1,0:T(8,128)(2,1)} %pack_keys.1.kv.refs_6_), channel_id=1, source_target_pairs={{0,4},{4,0},{8,12},{12,8},{16,20},{20,16},{24,28},{28,24},{1,5},{5... | collective-permute-start | bytes 3145736 | tf_op jit(solution)/shard_map/ppermute | solution.py:375
  18.9 26.9 %collective-permute-start.2 = (bf16[2,4,512,128]{3,2,1,0:T(8,128)(2,1)}, bf16[2,4,512,128]{3,2,1,0:T(8,128)(2,1)}, u32[]{:S(2)}, u32[]{:S(2)}) collective-permute-start(bf16[2,4,512,128]{3,2,1,0:T(8,128)(2,1)} %pack_keys.1.kv.refs_6_), channel_id=1, source_target_pairs={{4,8},{12,16},{20,24},{8,4},{16,12},{24,20},{5,9},{13,17},{21,25},... | collective-permute-start | bytes 3145736 | tf_op jit(solution)/shard_map/ppermute | solution.py:382
  31.4 8.9 %copy-start.3 = (bf16[2,4,4,64,128]{4,3,2,1,0:T(8,128)(2,1)}, bf16[2,4,4,64,128]{4,3,2,1,0:T(8,128)(2,1)S(1)}, u32[]{:S(2)}) copy-start(bf16[2,4,4,64,128]{4,3,2,1,0:T(8,128)(2,1)S(1)} %collective-permute-done.3.refs_2_) | copy-start | bytes 1572868
  31.4 7.3 %collective-permute-start.6 = (bf16[2,4,4,64,128]{4,3,2,1,0:T(8,128)(2,1)S(1)}, bf16[2,4,4,64,128]{4,3,2,1,0:T(8,128)(2,1)S(1)}, u32[]{:S(2)}, u32[]{:S(2)}) collective-permute-start(bf16[2,4,4,64,128]{4,3,2,1,0:T(8,128)(2,1)S(1)} %collective-permute-done.3.refs_2_), channel_id=1, source_target_pairs={{0,4},{4,0},{8,12},{12,8},{16,20},{20,16},{24,28},{28,24},{1,5},{5... | collective-permute-start | bytes 1572872 | tf_op jit(solution)/shard_map/ppermute | solution.py:375
  36.3 2.4 %collective-permute-start.4 = (bf16[1,4,4,64,128]{4,3,2,1,0:T(8,128)(2,1)}, bf16[1,4,4,64,128]{4,3,2,1,0:T(8,128)(2,1)S(1)}, u32[]{:S(2)}, u32[]{:S(2)}) collective-permute-start(bf16[1,4,4,64,128]{4,3,2,1,0:T(8,128)(2,1)} %bitcast.12), channel_id=1, source_target_pairs={{0,4},{4,0},{8,12},{12,8},{16,20},{20,16},{24,28},{28,24},{1,5},{5... | collective-permute-start | bytes 786440 | tf_op jit(solution)/shard_map/ppermute | solution.py:375
  36.3 2.4 %collective-permute-start.5 = (bf16[1,4,4,64,128]{4,3,2,1,0:T(8,128)(2,1)S(1)}, bf16[1,4,4,64,128]{4,3,2,1,0:T(8,128)(2,1)S(1)}, u32[]{:S(2)}, u32[]{:S(2)}) collective-permute-start(bf16[1,4,4,64,128]{4,3,2,1,0:T(8,128)(2,1)S(1)} %collective-permute-done.1.refs_1_), channel_id=1, source_target_pairs={{0,4},{4,0},{8,12},{12,8},{16,20},{20,16},{24,28},{28,24},{1,5},{5... | collective-permute-start | bytes 786440 | tf_op jit(solution)/shard_map/ppermute | solution.py:375
  38.6 0.7 copy-start.8
  38.6 0.8 copy-start.9
  39.4 0.8 copy-start.4
  45.8 29.5 %collective-permute-start.8 = (bf16[2,4,512,128]{3,2,1,0:T(8,128)(2,1)}, bf16[2,4,512,128]{3,2,1,0:T(8,128)(2,1)}, u32[]{:S(2)}, u32[]{:S(2)}) collective-permute-start(bf16[2,4,512,128]{3,2,1,0:T(8,128)(2,1)} %get-tuple-element.48.qd), channel_id=1, source_target_pairs={{4,8},{12,16},{20,24},{8,4},{16,12},{24,20},{5,9},{13,17},{21,25},... | collective-permute-start | bytes 3145736 | tf_op jit(solution)/shard_map/ppermute | solution.py:382
  47.8 27.6 %collective-permute-start.7 = (bf16[2,4,512,128]{3,2,1,0:T(8,128)(2,1)}, bf16[2,4,512,128]{3,2,1,0:T(8,128)(2,1)}, u32[]{:S(2)}, u32[]{:S(2)}) collective-permute-start(bf16[2,4,512,128]{3,2,1,0:T(8,128)(2,1)} %get-tuple-element.48.qd), channel_id=1, source_target_pairs={{0,4},{4,0},{8,12},{12,8},{16,20},{20,16},{24,28},{28,24},{1,5},{5... | collective-permute-start | bytes 3145736 | tf_op jit(solution)/shard_map/ppermute | solution.py:375
  47.8 27.5 %all-to-all-start = ((f32[8,4,8,256]{3,2,1,0:T(8,128)}), f32[8,4,8,256]{3,2,1,0:T(8,128)S(1)}, u32[]{:S(2)}, u32[]{:S(2)}) async-start(f32[8,4,8,256]{3,2,1,0:T(8,128)} %get-tuple-element.51), calls=%async_computation | async-start | bytes 524288 | tf_op jit(solution)/shard_map/all_to_all | solution.py:449
  67.7 14.9 %collective-permute-start.10 = (f32[4,2,512]{2,1,0:T(2,128)}, f32[4,2,512]{2,1,0:T(2,128)S(1)}, u32[]{:S(2)}, u32[]{:S(2)}) collective-permute-start(f32[4,2,512]{2,1,0:T(2,128)} %get-tuple-element.49), channel_id=1, source_target_pairs={{4,8},{12,16},{20,24},{8,4},{16,12},{24,20},{5,9},{13,17},{21,25},... | collective-permute-start | bytes 49160 | tf_op jit(solution)/shard_map/ppermute | solution.py:382
  71.3 11.3 %collective-permute-start.9 = (f32[4,2,512]{2,1,0:T(2,128)}, f32[4,2,512]{2,1,0:T(2,128)S(1)}, u32[]{:S(2)}, u32[]{:S(2)}) collective-permute-start(f32[4,2,512]{2,1,0:T(2,128)} %get-tuple-element.49), channel_id=1, source_target_pairs={{0,4},{4,0},{8,12},{12,8},{16,20},{20,16},{24,28},{28,24},{1,5},{5... | collective-permute-start | bytes 49160 | tf_op jit(solution)/shard_map/ppermute | solution.py:375
  71.4 12.7 %collective-permute-start.12 = (bf16[4,2,4,64,128]{4,3,2,1,0:T(8,128)(2,1)}, bf16[4,2,4,64,128]{4,3,2,1,0:T(8,128)(2,1)S(1)}, u32[]{:S(2)}, u32[]{:S(2)}) collective-permute-start(bf16[4,2,4,64,128]{4,3,2,1,0:T(8,128)(2,1)} %get-tuple-element.59), channel_id=1, source_target_pairs={{0,4},{4,0},{8,12},{12,8},{16,20},{20,16},{24,28},{28,24},{1,5},{5... | collective-permute-start | bytes 1572872 | tf_op jit(solution)/shard_map/ppermute | solution.py:375
  75.3 0.7 copy-start
  82.6 8.6 %copy-start.10 = (f32[4,2,512]{2,1,0:T(2,128)}, f32[4,2,512]{2,1,0:T(2,128)S(1)}, u32[]{:S(2)}) copy-start(f32[4,2,512]{2,1,0:T(2,128)S(1)} %collective-permute-done.10.log_far) | copy-start | bytes 49156
  82.7 8.6 %copy-start.11 = (f32[4,2,512]{2,1,0:T(2,128)}, f32[4,2,512]{2,1,0:T(2,128)S(1)}, u32[]{:S(2)}) copy-start(f32[4,2,512]{2,1,0:T(2,128)S(1)} %collective-permute-done.9.log_near) | copy-start | bytes 49156
  82.7 3.3 %collective-permute-start.11 = (bf16[4,2,4,64,128]{4,3,2,1,0:T(8,128)(2,1)}, bf16[4,2,4,64,128]{4,3,2,1,0:T(8,128)(2,1)}, u32[]{:S(2)}, u32[]{:S(2)}) collective-permute-start(bf16[4,2,4,64,128]{4,3,2,1,0:T(8,128)(2,1)} %get-tuple-element.57), channel_id=1, source_target_pairs={{0,4},{4,0},{8,12},{12,8},{16,20},{20,16},{24,28},{28,24},{1,5},{5... | collective-permute-start | bytes 1572872 | tf_op jit(solution)/shard_map/ppermute | solution.py:375
  84.1 1.9 %copy-start.2 = (bf16[4,2,4,64,128]{4,3,2,1,0:T(8,128)(2,1)}, bf16[4,2,4,64,128]{4,3,2,1,0:T(8,128)(2,1)S(1)}, u32[]{:S(2)}) copy-start(bf16[4,2,4,64,128]{4,3,2,1,0:T(8,128)(2,1)S(1)} %collective-permute-done.12.got_sums) | copy-start | bytes 1572868
  88.6 9.9 %collective-permute-start.13 = (bf16[4,4,64,128]{3,2,1,0:T(8,128)(2,1)}, bf16[4,4,64,128]{3,2,1,0:T(8,128)(2,1)S(1)}, u32[]{:S(2)}, u32[]{:S(2)}) collective-permute-start(bf16[4,4,64,128]{3,2,1,0:T(8,128)(2,1)} %get-tuple-element.61), channel_id=1, source_target_pairs={{0,8},{4,12},{8,0},{12,4},{16,24},{20,28},{24,16},{28,20},{1,9},{5... | collective-permute-start | bytes 786440 | tf_op jit(solution)/shard_map/ppermute | solution.py:375
  90.1 8.4 %collective-permute-start.14 = (bf16[4,4,64,128]{3,2,1,0:T(8,128)(2,1)}, bf16[4,4,64,128]{3,2,1,0:T(8,128)(2,1)S(1)}, u32[]{:S(2)}, u32[]{:S(2)}) collective-permute-start(bf16[4,4,64,128]{3,2,1,0:T(8,128)(2,1)} %get-tuple-element.62), channel_id=1, source_target_pairs={{0,16},{4,20},{8,24},{12,28},{16,0},{20,4},{24,8},{28,12},{1,17},{... | collective-permute-start | bytes 786440 | tf_op jit(solution)/shard_map/ppermute | solution.py:375
  90.7 12.5 %collective-permute-start.15 = (bf16[4,4,64,128]{3,2,1,0:T(8,128)(2,1)}, bf16[4,4,64,128]{3,2,1,0:T(8,128)(2,1)S(1)}, u32[]{:S(2)}, u32[]{:S(2)}) collective-permute-start(bf16[4,4,64,128]{3,2,1,0:T(8,128)(2,1)} %get-tuple-element.63), channel_id=1, source_target_pairs={{0,24},{4,28},{8,16},{12,20},{16,8},{20,12},{24,0},{28,4},{1,25},{... | collective-permute-start | bytes 786440 | tf_op jit(solution)/shard_map/ppermute | solution.py:375
  98.4 4.8 %copy-start.5 = (bf16[4,4,64,128]{3,2,1,0:T(8,128)(2,1)}, bf16[4,4,64,128]{3,2,1,0:T(8,128)(2,1)S(1)}, u32[]{:S(2)}) copy-start(bf16[4,4,64,128]{3,2,1,0:T(8,128)(2,1)S(1)} %collective-permute-done.13.refs_1_) | copy-start | bytes 786436
  98.4 4.8 %copy-start.6 = (bf16[4,4,64,128]{3,2,1,0:T(8,128)(2,1)}, bf16[4,4,64,128]{3,2,1,0:T(8,128)(2,1)S(1)}, u32[]{:S(2)}) copy-start(bf16[4,4,64,128]{3,2,1,0:T(8,128)(2,1)S(1)} %collective-permute-done.14.refs_2_) | copy-start | bytes 786436
  103.2 0.7 copy-start.7

commit v9 on v7

--- a/solution.py
+++ b/solution.py
@@ -12,7 +12,7 @@
 TILE = 256
 NEG = -1e30
 LOG2E = 1.0 / math.log(2.0)
-VMEM_BYTES = 63 * 1024 * 1024
+VMEM_BYTES = int(63.75 * 1024 * 1024)
 BF = jnp.bfloat16
 F32 = jnp.float32
 
@@ -303,7 +303,7 @@
         span = slice(k_tile * TILE, (k_tile + 1) * TILE)
         key = kv[0, 0, span, :]
         value = kv[1, 0, span, :]
-        key_bias = wide(bias[HALF + k_tile * TILE : HALF + (k_tile + 1) * TILE, :], TILE)
+        key_bias = wide(bias[span, :], TILE)
         for piece in range(reach // TILE):
             start = (k_tile + piece) * TILE
             side, lanes = start // toks, slice(start % toks, start % toks + TILE)
@@ -322,24 +322,25 @@
         dkv[1, 0, span, :] = partial[1, 0, span, :] + nn(probs[span, :], grads[window, :])
 
 
-def final_kernel(
-    sources, place, out, dq, dkv, *refs
-):
+def final_kernel(sources, place, out, dq, dkv, *refs):
     parts, refs = refs[:sources], refs[sources:]
-    attn, query_grad, key_grad, value_grad, wide_rows = refs
-    heads, toks = out.shape[0], out.shape[1]
+    attn, query_grad, key_grad, value_grad, wide_rows, tables = refs
+    heads, toks, width = out.shape
+
+    @pl.when(pl.program_id(0) == 0)
+    def _():
+        for head in range(heads):
+            for kind in range(4):
+                table = parts[0][kind, head].astype(F32)
+                for part in parts[1:]:
+                    table = table + part[kind, head].astype(F32)
+                tables[head, :, kind * width : (kind + 1) * width] = table.astype(BF)
+
     hot = place[...]
     is_global = jnp.sum(hot.astype(F32), axis=1, keepdims=True) > 0
     for head in range(heads):
         rows = pl.ds(head, toks, stride=heads)
-        tables = []
-        for kind in range(4):
-            table = parts[0][kind, head].astype(F32)
-            for part in parts[1:]:
-                table = table + part[kind, head].astype(F32)
-            tables.append(table.astype(BF))
-        width = out.shape[2]
-        added = nn(hot, jnp.concatenate(tables, axis=1))
+        added = nn(hot, tables[head])
         added = [added[:, i * width : (i + 1) * width] for i in range(4)]
         wide_rows[rows, :] = jnp.where(is_global, added[0], out[head].astype(F32))
         query_grad[rows, :] = dq[head] + added[1]
@@ -566,7 +567,7 @@
     dkv = pl.pallas_call(
         functools.partial(rim_kernel, scale, scale2),
         grid=(heads,),
-        in_specs=[per_head(pair_shape, 1), whole(bias.shape)]
+        in_specs=[per_head(pair_shape, 1), pl.BlockSpec((toks, 128), lambda head: (HALF // toks, 0))]
         + [per_head(pair_shape, 1)] * 2
         + [per_head(log_dot.shape, 0)] * 2
         + [per_head(pair_shape, 1)],
@@ -585,7 +586,7 @@
     )(kv, bias, qd_near, qd_far, log_near, log_far, dkv)
 
     flat_shape = (toks * heads, width)
-    steps = 2
+    steps = 4
     outs = pl.pallas_call(
         functools.partial(final_kernel, len(parts)),
         grid=(steps,),
@@ -598,7 +599,10 @@
         + [whole((4, heads, slots, width))] * len(parts),
         out_specs=[pl.BlockSpec((toks * heads // steps, width), lambda i: (i, 0))] * 4,
         out_shape=[struct(flat_shape, kind) for kind in (BF, F32, F32, F32)],
-        scratch_shapes=[pltpu.VMEM((toks * heads // steps, width), F32)],
+        scratch_shapes=[
+            pltpu.VMEM((toks * heads // steps, width), F32),
+            pltpu.VMEM((heads, slots, 4 * width), BF),
+        ],
         compiler_params=params(),
         name="final",
     )(place, out, dq, dkv, *parts)

time: 108 us -> 109 us (level)
  local copies, waits for them, and re-layouts: 1.43 us -> 0.01 us
    unnamed x20 -> x4, local copies, waits for them, and re-layouts: 1.43 us -> 0.01 us
    pallas_call x1, Pallas kernels: 4.17 us -> 5.49 us  [shards(): pl.pallas_call(functools.partial(final_kernel, len(parts)), grid=(steps,)...]
where the time goes in v9:
time: 109 us; the launch traced here: 107 us
  Pallas kernels  55.7 us (51%)
  waiting for transfers between devices  25.5 us (23%)
  starting transfers between devices  23.2 us (21%)
  other arithmetic  1.32 us (1%)
    ppermute x3, waiting for transfers between devices, from_far(): return lax.ppermute(value, 'ctx', pairs + [(j, i) for i, j in pairs])  14.8 us
    pallas_call x1, Pallas kernels, shards(): pl.pallas_call(functools.partial(local_kernel, scale, scale2), grid=(head...  11.3 us
    ppermute x12, waiting for transfers between devices, swap(): return lax.ppermute(value, 'ctx', [(i, i ^ mask) for i in range(devices)])  10.3 us
    ppermute x3, starting transfers between devices, from_far(): return lax.ppermute(value, 'ctx', pairs + [(j, i) for i, j in pairs])  10.3 us
    pallas_call x1, Pallas kernels, shards(): pl.pallas_call(functools.partial(window_kernel, scale2), grid=(heads,), i...  9.13 us
    ppermute x12, starting transfers between devices, swap(): return lax.ppermute(value, 'ctx', [(i, i ^ mask) for i in range(devices)])  8.66 us
    pallas_call x1, Pallas kernels, shards(): pl.pallas_call(functools.partial(rim_kernel, scale, scale2), grid=(heads,...  6.95 us
    pallas_call x1, Pallas kernels, shards(): pl.pallas_call(functools.partial(global_kernel, scale, scale2), grid=(hea...  6.77 us
  transfers between devices with their start and end apart: 16, of which 6 were waited for; matrix products, arithmetic and copies ran while one was open for 0% of the time, Pallas kernels for 43%

profile of v9, /device:TPU:1, one launch (start us, length us, event | category | flops | bytes accessed | tf_op | source)
XLA Modules:
  0.0 106.5 jit_solution(11367457291547383421)
XLA Ops:
  0.6 2.4 %pack_keys.1.kv.refs_5_ = bf16[2,4,512,128]{3,2,1,0:T(8,128)(2,1)} custom-call(bf16[2048,128]{1,0:T(8,128)(2,1)} %bitcast.15, bf16[2048,128]{1,0:T(8,128)(2,1)} %bitcast.16), custom_call_target="tpu_custom_call" | custom-call | tf_op jit(solution)/shard_map/pack_keys/pallas_call | solution.py:409
  3.1 4.5 %collective-permute-start.1 = (bf16[2,4,512,128]{3,2,1,0:T(8,128)(2,1)}, bf16[2,4,512,128]{3,2,1,0:T(8,128)(2,1)}, u32[]{:S(2)}, u32[]{:S(2)}) collective-permute-start(bf16[2,4,512,128]{3,2,1,0:T(8,128)(2,1)} %pack_keys.1.kv.refs_5_), channel_id=1, source_target_pairs={{4,8},{12,16},{20,24},{8,4},{16,12},{24,20},{5,9},{13,17},{21,25},... | collective-permute-start | bytes 3145736 | tf_op jit(solution)/shard_map/ppermute | solution.py:398
  7.6 0.1 collective-permute-start
  7.7 3.4 %pack_queries.1 = (bf16[2,4,512,128]{3,2,1,0:T(8,128)(2,1)}, bf16[4,4,64,128]{3,2,1,0:T(8,128)(2,1)}) custom-call(bf16[2048,128]{1,0:T(8,128)(2,1)} %bitcast.17, bf16[2048,128]{1,0:T(8,128)(2,1)} %bitcast.18, bf16[2,4,512,128]{3,2,1,0:T(8,128)(2,1)} %pack_keys.1.kv.refs_5_, s32[1,256]{1,0:T(1,128)} %bitcast.19), custom_call_target="tpu_custom_call" | custom-call | tf_op jit(solution)/shard_map/pack_queries/pallas_call | solution.py:417
  11.1 1.1 collective-permute-start.4
  12.1 1.3 %collective-permute-start.3 = (bf16[1,4,4,64,128]{4,3,2,1,0:T(8,128)(2,1)}, bf16[1,4,4,64,128]{4,3,2,1,0:T(8,128)(2,1)}, u32[]{:S(2)}, u32[]{:S(2)}) collective-permute-start(bf16[1,4,4,64,128]{4,3,2,1,0:T(8,128)(2,1)} %bitcast.11), channel_id=1, source_target_pairs={{0,16},{4,20},{8,24},{12,28},{16,0},{20,4},{24,8},{28,12},{1,17},{... | collective-permute-start | bytes 786440 | tf_op jit(solution)/shard_map/ppermute | solution.py:391
  13.5 0.3 collective-permute-start.2
  13.7 2.2 %masks.1 = (f32[1536,128]{1,0:T(8,128)}, bf16[256,512]{1,0:T(8,128)(2,1)}, bf16[512,256]{1,0:T(8,128)(2,1)}, bf16[512,64]{1,0:T(8,128)(2,1)}) custom-call(s32[1,256]{1,0:T(1,128)} %bitcast.20), custom_call_target="tpu_custom_call" | custom-call | tf_op jit(solution)/shard_map/masks/pallas_call | solution.py:429
  15.9 14.8 %collective-permute-done.1.kv_far = bf16[2,4,512,128]{3,2,1,0:T(8,128)(2,1)} collective-permute-done((bf16[2,4,512,128]{3,2,1,0:T(8,128)(2,1)}, bf16[2,4,512,128]{3,2,1,0:T(8,128)(2,1)}, u32[]{:S(2)}, u32[]{:S(2)}) %collective-permute-start.1) | collective-permute-done | bytes 1048608 | tf_op jit(solution)/shard_map/ppermute | solution.py:398
  30.7 0.0 collective-permute-done.kv_near
  30.7 9.1 %window.1 = (bf16[4,1536,512]{2,1,0:T(8,128)(2,1)}, f32[4,128,512]{2,1,0:T(8,128)}, f32[4,2,512]{2,1,0:T(2,128)}, bf16[4,128,1536]{2,1,0:T(8,128)(2,1)}, bf16[4,...) custom-call(bf16[2,4,512,128]{3,2,1,0:T(8,128)(2,1)} %get-tuple-element.61.qd, ...), custom_call_target="tpu_custom_call" | custom-call | flops 1000000 | bytes 1000000 | tf_op jit(solution)/shard_map/window/pallas_call | solution.py:446
  39.8 0.0 collective-permute-done.4.refs_3_
  39.8 0.0 collective-permute-done.3.refs_2_
  39.9 3.0 %collective-permute-done.2.refs_1_ = bf16[1,4,4,64,128]{4,3,2,1,0:T(8,128)(2,1)} collective-permute-done((bf16[1,4,4,64,128]{4,3,2,1,0:T(8,128)(2,1)}, bf16[1,4,4,64,128]{4,3,2,1,0:T(8,128)(2,1)}, u32[]{:S(2)}, u32[]{:S(2)}) %collective-permute-start.2) | collective-permute-done | bytes 262176 | tf_op jit(solution)/shard_map/ppermute | solution.py:391
  42.8 1.3 %pad_maximum_fusion = bf16[4,4,4,64,128]{4,3,2,1,0:T(8,128)(2,1)S(1)} fusion(bf16[1,4,4,64,128]{4,3,2,1,0:T(8,128)(2,1)} %collective-permute-done.4.refs_3_, bf16[1,4,4,64,128]{4,3,2,1,0:T(8,128)(2,1)} %collective-permute-done.3.refs_2_, bf16[1,4,4,64,128]{4,3,2,1,0:T(8,128)(2,1)} %collective-permute-done.2.refs_1_, bf16[1,4,4,64,128]{4,3,2,1,0:T(8,128)(2,1)} %bitcast.13), kind=kLoop, calls=%fused_computation | loop fusion | flops 1572864 | bytes 2097152 | tf_op jit(solution)/shard_map/concatenate | solution.py:478
  44.2 0.1 collective-permute-start.5
  44.2 2.2 %collective-permute-start.7 = (bf16[2,4,512,128]{3,2,1,0:T(8,128)(2,1)}, bf16[2,4,512,128]{3,2,1,0:T(8,128)(2,1)}, u32[]{:S(2)}, u32[]{:S(2)}) collective-permute-start(bf16[2,4,512,128]{3,2,1,0:T(8,128)(2,1)} %get-tuple-element.61.qd), channel_id=1, source_target_pairs={{4,8},{12,16},{20,24},{8,4},{16,12},{24,20},{5,9},{13,17},{21,25},... | collective-permute-start | bytes 3145736 | tf_op jit(solution)/shard_map/ppermute | solution.py:398
  46.5 0.1 collective-permute-start.6
  46.6 0.5 collective-permute-done.5.refs_4_
  47.0 5.5 %global_stats.1 = (bf16[4,4,256,128]{3,2,1,0:T(8,128)(2,1)}, f32[8,4,8,256]{3,2,1,0:T(8,128)}) custom-call(bf16[256,512]{1,0:T(8,128)(2,1)} %get-tuple-element.48.compact, bf16[1,4,4,64,128]{4,3,2,1,0:T(8,128)(2,1)} %bitcast.14, bf16[1,4,4,64,128]{4,3,2,1,0:T(8,128)(2,1)} %collective-permute-done.2.refs_1_, ...), custom_call_target="tpu_custom_call" | custom-call | flops 1000000 | bytes 1000000 | tf_op jit(solution)/shard_map/global_stats/pallas_call | solution.py:482
  52.5 4.3 %all-to-all-start = ((f32[8,4,8,256]{3,2,1,0:T(8,128)}), f32[8,4,8,256]{3,2,1,0:T(8,128)}, u32[]{:S(2)}, u32[]{:S(2)}) async-start(f32[8,4,8,256]{3,2,1,0:T(8,128)} %get-tuple-element.63), calls=%async_computation | async-start | bytes 524288 | tf_op jit(solution)/shard_map/all_to_all | solution.py:495
  56.8 11.3 %local.1 = (bf16[4,512,128]{2,1,0:T(8,128)(2,1)}, f32[4,2,512]{2,1,0:T(2,128)}, f32[4,512,128]{2,1,0:T(8,128)}, f32[2,4,512,128]{3,2,1,0:T(8,128)}, bf16[4,2,4,6...) custom-call(bf16[3,4,128,512]{3,2,1,0:T(8,128)(2,1)} %get-tuple-element.45.sides.value_t, ...), custom_call_target="tpu_custom_call" | custom-call | flops 1000000 | bytes 1000000 | tf_op jit(solution)/shard_map/local/pallas_call | solution.py:502
  68.1 3.5 %collective-permute-start.9 = (f32[4,2,512]{2,1,0:T(2,128)}, f32[4,2,512]{2,1,0:T(2,128)S(1)}, u32[]{:S(2)}, u32[]{:S(2)}) collective-permute-start(f32[4,2,512]{2,1,0:T(2,128)} %get-tuple-element.62), channel_id=1, source_target_pairs={{4,8},{12,16},{20,24},{8,4},{16,12},{24,20},{5,9},{13,17},{21,25},... | collective-permute-start | bytes 49160 | tf_op jit(solution)/shard_map/ppermute | solution.py:398
  71.6 0.1 collective-permute-start.8
  71.7 0.5 collective-permute-start.11
  72.2 0.0 collective-permute-done.7.qd_far
  72.2 0.0 collective-permute-done.6.qd_near
  72.2 0.4 all-to-all-done.stats
  72.6 6.8 %global_queries.1 = (f32[2,4,512,128]{3,2,1,0:T(8,128)}, bf16[4,2,4,64,128]{4,3,2,1,0:T(8,128)(2,1)}, bf16[4,2,4,64,128]{4,3,2,1,0:T(8,128)(2,1)}) custom-call(bf16[2,4,512,128]{3,2,1,0:T(8,128)(2,1)} %pack_keys.1.kv.refs_5_, bf16[4,4,256,128]{3,2,1,0:T(8,128)(2,1)} %get-tuple-element.55.rows, ...), custom_call_target="tpu_custom_call", output_to_operand_aliasing={{0}: (4, {})} | custom-call | flops 1000000 | bytes 1000000 | tf_op jit(solution)/shard_map/global_queries/pallas_call | solution.py:534
  79.4 0.0 collective-permute-done.9.log_far
  79.4 0.0 copy-start
  79.4 0.0 collective-permute-done.8.log_near
  79.4 0.0 copy-start.1
  79.4 2.2 %collective-permute-start.10 = (bf16[4,2,4,64,128]{4,3,2,1,0:T(8,128)(2,1)}, bf16[4,2,4,64,128]{4,3,2,1,0:T(8,128)(2,1)}, u32[]{:S(2)}, u32[]{:S(2)}) collective-permute-start(bf16[4,2,4,64,128]{4,3,2,1,0:T(8,128)(2,1)} %get-tuple-element.69), channel_id=1, source_target_pairs={{0,4},{4,0},{8,12},{12,8},{16,20},{20,16},{24,28},{28,24},{1,5},{5... | collective-permute-start | bytes 1572872 | tf_op jit(solution)/shard_map/ppermute | solution.py:391
  81.6 0.0 collective-permute-done.11.got_sums
  81.6 1.9 %collective-permute-done.10.got_ends = bf16[4,2,4,64,128]{4,3,2,1,0:T(8,128)(2,1)} collective-permute-done((bf16[4,2,4,64,128]{4,3,2,1,0:T(8,128)(2,1)}, bf16[4,2,4,64,128]{4,3,2,1,0:T(8,128)(2,1)}, u32[]{:S(2)}, u32[]{:S(2)}) %collective-permute-start.10) | collective-permute-done | bytes 524320 | tf_op jit(solution)/shard_map/ppermute | solution.py:391
  83.5 2.5 %fold.1 = (bf16[4,4,64,128]{3,2,1,0:T(8,128)(2,1)}, bf16[4,4,64,128]{3,2,1,0:T(8,128)(2,1)}, bf16[4,4,64,128]{3,2,1,0:T(8,128)(2,1)}, bf16[4,4,64,128]{3,2,1,0:T(8,128)(2,1)}) custom-call(bf16[4,2,4,64,128]{4,3,2,1,0:T(8,128)(2,1)} %get-tuple-element.67.kept_ends, bf16[4,2,4,64,128]{4,3,2,1,0:T(8,128)(2,1)} %collective-permute-done.10.got_ends, ...), custom_call_target="tpu_custom_call" | custom-call | tf_op jit(solution)/shard_map/fold/pallas_call | solution.py:552
  86.0 1.2 %collective-permute-start.12 = (bf16[4,4,64,128]{3,2,1,0:T(8,128)(2,1)}, bf16[4,4,64,128]{3,2,1,0:T(8,128)(2,1)}, u32[]{:S(2)}, u32[]{:S(2)}) collective-permute-start(bf16[4,4,64,128]{3,2,1,0:T(8,128)(2,1)} %get-tuple-element.73), channel_id=1, source_target_pairs={{0,8},{4,12},{8,0},{12,4},{16,24},{20,28},{24,16},{28,20},{1,9},{5... | collective-permute-start | bytes 786440 | tf_op jit(solution)/shard_map/ppermute | solution.py:391
  87.2 0.7 collective-permute-start.13
  87.9 1.2 %collective-permute-start.14 = (bf16[4,4,64,128]{3,2,1,0:T(8,128)(2,1)}, bf16[4,4,64,128]{3,2,1,0:T(8,128)(2,1)}, u32[]{:S(2)}, u32[]{:S(2)}) collective-permute-start(bf16[4,4,64,128]{3,2,1,0:T(8,128)(2,1)} %get-tuple-element.75), channel_id=1, source_target_pairs={{0,24},{4,28},{8,16},{12,20},{16,8},{20,12},{24,0},{28,4},{1,25},{... | collective-permute-start | bytes 786440 | tf_op jit(solution)/shard_map/ppermute | solution.py:391
  89.0 0.0 copy-done
  89.1 0.0 copy-done.1
  89.1 6.9 %rim.1.dkv = f32[2,4,512,128]{3,2,1,0:T(8,128)} custom-call(bf16[2,4,512,128]{3,2,1,0:T(8,128)(2,1)} %pack_keys.1.kv.refs_5_, f32[1536,128]{1,0:T(8,128)} %get-tuple-element.44.bias, bf16[2,4,512,128]{3,2,1,0:T(8,128)(2,1)} %collective-permute-done.6.qd_near, bf16[2,4,512,128]{3,2,1,0:T(8,128)(2,1)} %collective-permute-done.7.qd_far, ...), custom_call_target="tpu_custom_call" | custom-call | flops 1000000 | bytes 1000000 | tf_op jit(solution)/shard_map/rim/pallas_call | solution.py:567
  96.0 0.0 collective-permute-done.12.refs_1_
  96.0 0.0 collective-permute-done.13.refs_2_
  96.0 5.0 %collective-permute-done.14.refs_3_ = bf16[4,4,64,128]{3,2,1,0:T(8,128)(2,1)} collective-permute-done((bf16[4,4,64,128]{3,2,1,0:T(8,128)(2,1)}, bf16[4,4,64,128]{3,2,1,0:T(8,128)(2,1)}, u32[]{:S(2)}, u32[]{:S(2)}) %collective-permute-start.14) | collective-permute-done | bytes 262176 | tf_op jit(solution)/shard_map/ppermute | solution.py:391
  101.0 5.5 %final.1 = (bf16[2048,128]{1,0:T(8,128)(2,1)}, f32[2048,128]{1,0:T(8,128)}, f32[2048,128]{1,0:T(8,128)}, f32[2048,128]{1,0:T(8,128)}) custom-call(bf16[512,64]{1,0:T(8,128)(2,1)} %get-tuple-element.42.place, bf16[4,512,128]{2,1,0:T(8,128)(2,1)} %get-tuple-element.59.out, f32[4,512,128]{2,1,0:T(8,128)} %get-tuple-element.60.dq, f32[2,4,512,128]{3,2,1,0:T(8,128)} %rim.1.dkv, ...), custom_call_target="tpu_custom_call" | custom-call | tf_op jit(solution)/shard_map/final/pallas_call | solution.py:590
Async XLA Ops:
  3.1 27.6 %collective-permute-start.1 = (bf16[2,4,512,128]{3,2,1,0:T(8,128)(2,1)}, bf16[2,4,512,128]{3,2,1,0:T(8,128)(2,1)}, u32[]{:S(2)}, u32[]{:S(2)}) collective-permute-start(bf16[2,4,512,128]{3,2,1,0:T(8,128)(2,1)} %pack_keys.1.kv.refs_5_), channel_id=1, source_target_pairs={{4,8},{12,16},{20,24},{8,4},{16,12},{24,20},{5,9},{13,17},{21,25},... | collective-permute-start | bytes 3145736 | tf_op jit(solution)/shard_map/ppermute | solution.py:398
  7.6 23.1 %collective-permute-start = (bf16[2,4,512,128]{3,2,1,0:T(8,128)(2,1)}, bf16[2,4,512,128]{3,2,1,0:T(8,128)(2,1)}, u32[]{:S(2)}, u32[]{:S(2)}) collective-permute-start(bf16[2,4,512,128]{3,2,1,0:T(8,128)(2,1)} %pack_keys.1.kv.refs_5_), channel_id=1, source_target_pairs={{0,4},{4,0},{8,12},{12,8},{16,20},{20,16},{24,28},{28,24},{1,5},{5... | collective-permute-start | bytes 3145736 | tf_op jit(solution)/shard_map/ppermute | solution.py:391
  11.1 28.8 %collective-permute-start.4 = (bf16[1,4,4,64,128]{4,3,2,1,0:T(8,128)(2,1)}, bf16[1,4,4,64,128]{4,3,2,1,0:T(8,128)(2,1)}, u32[]{:S(2)}, u32[]{:S(2)}) collective-permute-start(bf16[1,4,4,64,128]{4,3,2,1,0:T(8,128)(2,1)} %bitcast.10), channel_id=1, source_target_pairs={{0,24},{4,28},{8,16},{12,20},{16,8},{20,12},{24,0},{28,4},{1,25},{... | collective-permute-start | bytes 786440 | tf_op jit(solution)/shard_map/ppermute | solution.py:391
  12.1 27.7 %collective-permute-start.3 = (bf16[1,4,4,64,128]{4,3,2,1,0:T(8,128)(2,1)}, bf16[1,4,4,64,128]{4,3,2,1,0:T(8,128)(2,1)}, u32[]{:S(2)}, u32[]{:S(2)}) collective-permute-start(bf16[1,4,4,64,128]{4,3,2,1,0:T(8,128)(2,1)} %bitcast.11), channel_id=1, source_target_pairs={{0,16},{4,20},{8,24},{12,28},{16,0},{20,4},{24,8},{28,12},{1,17},{... | collective-permute-start | bytes 786440 | tf_op jit(solution)/shard_map/ppermute | solution.py:391
  13.5 29.4 %collective-permute-start.2 = (bf16[1,4,4,64,128]{4,3,2,1,0:T(8,128)(2,1)}, bf16[1,4,4,64,128]{4,3,2,1,0:T(8,128)(2,1)}, u32[]{:S(2)}, u32[]{:S(2)}) collective-permute-start(bf16[1,4,4,64,128]{4,3,2,1,0:T(8,128)(2,1)} %bitcast.12), channel_id=1, source_target_pairs={{0,8},{4,12},{8,0},{12,4},{16,24},{20,28},{24,16},{28,20},{1,9},{5... | collective-permute-start | bytes 786440 | tf_op jit(solution)/shard_map/ppermute | solution.py:391
  44.2 2.9 %collective-permute-start.5 = (bf16[4,4,4,64,128]{4,3,2,1,0:T(8,128)(2,1)S(1)}, bf16[4,4,4,64,128]{4,3,2,1,0:T(8,128)(2,1)}, u32[]{:S(2)}, u32[]{:S(2)}) collective-permute-start(bf16[4,4,4,64,128]{4,3,2,1,0:T(8,128)(2,1)S(1)} %pad_maximum_fusion), channel_id=1, source_target_pairs={{0,4},{4,0},{8,12},{12,8},{16,20},{20,16},{24,28},{28,24},{1,5},{5... | collective-permute-start | bytes 3145736 | tf_op jit(solution)/shard_map/ppermute | solution.py:391
  44.2 28.0 %collective-permute-start.7 = (bf16[2,4,512,128]{3,2,1,0:T(8,128)(2,1)}, bf16[2,4,512,128]{3,2,1,0:T(8,128)(2,1)}, u32[]{:S(2)}, u32[]{:S(2)}) collective-permute-start(bf16[2,4,512,128]{3,2,1,0:T(8,128)(2,1)} %get-tuple-element.61.qd), channel_id=1, source_target_pairs={{4,8},{12,16},{20,24},{8,4},{16,12},{24,20},{5,9},{13,17},{21,25},... | collective-permute-start | bytes 3145736 | tf_op jit(solution)/shard_map/ppermute | solution.py:398
  46.5 25.7 %collective-permute-start.6 = (bf16[2,4,512,128]{3,2,1,0:T(8,128)(2,1)}, bf16[2,4,512,128]{3,2,1,0:T(8,128)(2,1)}, u32[]{:S(2)}, u32[]{:S(2)}) collective-permute-start(bf16[2,4,512,128]{3,2,1,0:T(8,128)(2,1)} %get-tuple-element.61.qd), channel_id=1, source_target_pairs={{0,4},{4,0},{8,12},{12,8},{16,20},{20,16},{24,28},{28,24},{1,5},{5... | collective-permute-start | bytes 3145736 | tf_op jit(solution)/shard_map/ppermute | solution.py:391
  52.5 20.1 %all-to-all-start = ((f32[8,4,8,256]{3,2,1,0:T(8,128)}), f32[8,4,8,256]{3,2,1,0:T(8,128)}, u32[]{:S(2)}, u32[]{:S(2)}) async-start(f32[8,4,8,256]{3,2,1,0:T(8,128)} %get-tuple-element.63), calls=%async_computation | async-start | bytes 524288 | tf_op jit(solution)/shard_map/all_to_all | solution.py:495
  68.1 11.3 %collective-permute-start.9 = (f32[4,2,512]{2,1,0:T(2,128)}, f32[4,2,512]{2,1,0:T(2,128)S(1)}, u32[]{:S(2)}, u32[]{:S(2)}) collective-permute-start(f32[4,2,512]{2,1,0:T(2,128)} %get-tuple-element.62), channel_id=1, source_target_pairs={{4,8},{12,16},{20,24},{8,4},{16,12},{24,20},{5,9},{13,17},{21,25},... | collective-permute-start | bytes 49160 | tf_op jit(solution)/shard_map/ppermute | solution.py:398
  71.6 7.8 %collective-permute-start.8 = (f32[4,2,512]{2,1,0:T(2,128)}, f32[4,2,512]{2,1,0:T(2,128)S(1)}, u32[]{:S(2)}, u32[]{:S(2)}) collective-permute-start(f32[4,2,512]{2,1,0:T(2,128)} %get-tuple-element.62), channel_id=1, source_target_pairs={{0,4},{4,0},{8,12},{12,8},{16,20},{20,16},{24,28},{28,24},{1,5},{5... | collective-permute-start | bytes 49160 | tf_op jit(solution)/shard_map/ppermute | solution.py:391
  71.7 9.9 %collective-permute-start.11 = (bf16[4,2,4,64,128]{4,3,2,1,0:T(8,128)(2,1)}, bf16[4,2,4,64,128]{4,3,2,1,0:T(8,128)(2,1)}, u32[]{:S(2)}, u32[]{:S(2)}) collective-permute-start(bf16[4,2,4,64,128]{4,3,2,1,0:T(8,128)(2,1)} %get-tuple-element.71), channel_id=1, source_target_pairs={{0,4},{4,0},{8,12},{12,8},{16,20},{20,16},{24,28},{28,24},{1,5},{5... | collective-permute-start | bytes 1572872 | tf_op jit(solution)/shard_map/ppermute | solution.py:391
  79.4 9.7 %copy-start = (f32[4,2,512]{2,1,0:T(2,128)}, f32[4,2,512]{2,1,0:T(2,128)S(1)}, u32[]{:S(2)}) copy-start(f32[4,2,512]{2,1,0:T(2,128)S(1)} %collective-permute-done.9.log_far) | copy-start | bytes 49156
  79.4 9.7 %copy-start.1 = (f32[4,2,512]{2,1,0:T(2,128)}, f32[4,2,512]{2,1,0:T(2,128)S(1)}, u32[]{:S(2)}) copy-start(f32[4,2,512]{2,1,0:T(2,128)S(1)} %collective-permute-done.8.log_near) | copy-start | bytes 49156
  79.4 4.0 %collective-permute-start.10 = (bf16[4,2,4,64,128]{4,3,2,1,0:T(8,128)(2,1)}, bf16[4,2,4,64,128]{4,3,2,1,0:T(8,128)(2,1)}, u32[]{:S(2)}, u32[]{:S(2)}) collective-permute-start(bf16[4,2,4,64,128]{4,3,2,1,0:T(8,128)(2,1)} %get-tuple-element.69), channel_id=1, source_target_pairs={{0,4},{4,0},{8,12},{12,8},{16,20},{20,16},{24,28},{28,24},{1,5},{5... | collective-permute-start | bytes 1572872 | tf_op jit(solution)/shard_map/ppermute | solution.py:391
  86.0 10.0 %collective-permute-start.12 = (bf16[4,4,64,128]{3,2,1,0:T(8,128)(2,1)}, bf16[4,4,64,128]{3,2,1,0:T(8,128)(2,1)}, u32[]{:S(2)}, u32[]{:S(2)}) collective-permute-start(bf16[4,4,64,128]{3,2,1,0:T(8,128)(2,1)} %get-tuple-element.73), channel_id=1, source_target_pairs={{0,8},{4,12},{8,0},{12,4},{16,24},{20,28},{24,16},{28,20},{1,9},{5... | collective-permute-start | bytes 786440 | tf_op jit(solution)/shard_map/ppermute | solution.py:391
  87.2 8.8 %collective-permute-start.13 = (bf16[4,4,64,128]{3,2,1,0:T(8,128)(2,1)}, bf16[4,4,64,128]{3,2,1,0:T(8,128)(2,1)}, u32[]{:S(2)}, u32[]{:S(2)}) collective-permute-start(bf16[4,4,64,128]{3,2,1,0:T(8,128)(2,1)} %get-tuple-element.74), channel_id=1, source_target_pairs={{0,16},{4,20},{8,24},{12,28},{16,0},{20,4},{24,8},{28,12},{1,17},{... | collective-permute-start | bytes 786440 | tf_op jit(solution)/shard_map/ppermute | solution.py:391
  87.9 13.2 %collective-permute-start.14 = (bf16[4,4,64,128]{3,2,1,0:T(8,128)(2,1)}, bf16[4,4,64,128]{3,2,1,0:T(8,128)(2,1)}, u32[]{:S(2)}, u32[]{:S(2)}) collective-permute-start(bf16[4,4,64,128]{3,2,1,0:T(8,128)(2,1)} %get-tuple-element.75), channel_id=1, source_target_pairs={{0,24},{4,28},{8,16},{12,20},{16,8},{20,12},{24,0},{28,4},{1,25},{... | collective-permute-start | bytes 786440 | tf_op jit(solution)/shard_map/ppermute | solution.py:391

commit v10 on v7

--- a/solution.py
+++ b/solution.py
@@ -12,7 +12,7 @@
 TILE = 256
 NEG = -1e30
 LOG2E = 1.0 / math.log(2.0)
-VMEM_BYTES = 63 * 1024 * 1024
+VMEM_BYTES = int(63.75 * 1024 * 1024)
 BF = jnp.bfloat16
 F32 = jnp.float32
 
@@ -303,7 +303,7 @@
         span = slice(k_tile * TILE, (k_tile + 1) * TILE)
         key = kv[0, 0, span, :]
         value = kv[1, 0, span, :]
-        key_bias = wide(bias[HALF + k_tile * TILE : HALF + (k_tile + 1) * TILE, :], TILE)
+        key_bias = wide(bias[span, :], TILE)
         for piece in range(reach // TILE):
             start = (k_tile + piece) * TILE
             side, lanes = start // toks, slice(start % toks, start % toks + TILE)
@@ -566,7 +566,7 @@
     dkv = pl.pallas_call(
         functools.partial(rim_kernel, scale, scale2),
         grid=(heads,),
-        in_specs=[per_head(pair_shape, 1), whole(bias.shape)]
+        in_specs=[per_head(pair_shape, 1), pl.BlockSpec((toks, 128), lambda head: (HALF // toks, 0))]
         + [per_head(pair_shape, 1)] * 2
         + [per_head(log_dot.shape, 0)] * 2
         + [per_head(pair_shape, 1)],

time: 108 us -> 107 us (level)
  local copies, waits for them, and re-layouts: 1.43 us -> 0.01 us
    unnamed x20 -> x4, local copies, waits for them, and re-layouts: 1.43 us -> 0.01 us
where the time goes in v10:
time: 107 us; the launch traced here: 105 us
  Pallas kernels  54.4 us (51%)
  waiting for transfers between devices  25.5 us (24%)
  starting transfers between devices  23.2 us (22%)
  other arithmetic  1.32 us (1%)
    ppermute x3, waiting for transfers between devices, from_far(): return lax.ppermute(value, 'ctx', pairs + [(j, i) for i, j in pairs])  14.8 us
    pallas_call x1, Pallas kernels, shards(): pl.pallas_call(functools.partial(local_kernel, scale, scale2), grid=(head...  11.3 us
    ppermute x12, waiting for transfers between devices, swap(): return lax.ppermute(value, 'ctx', [(i, i ^ mask) for i in range(devices)])  10.3 us
    ppermute x3, starting transfers between devices, from_far(): return lax.ppermute(value, 'ctx', pairs + [(j, i) for i, j in pairs])  10.3 us
    pallas_call x1, Pallas kernels, shards(): pl.pallas_call(functools.partial(window_kernel, scale2), grid=(heads,), i...  9.13 us
    ppermute x12, starting transfers between devices, swap(): return lax.ppermute(value, 'ctx', [(i, i ^ mask) for i in range(devices)])  8.66 us
    pallas_call x1, Pallas kernels, shards(): pl.pallas_call(functools.partial(rim_kernel, scale, scale2), grid=(heads,...  6.95 us
    pallas_call x1, Pallas kernels, shards(): pl.pallas_call(functools.partial(global_kernel, scale, scale2), grid=(hea...  6.77 us
  transfers between devices with their start and end apart: 16, of which 6 were waited for; matrix products, arithmetic and copies ran while one was open for 0% of the time, Pallas kernels for 43%

profile of v10, /device:TPU:1, one launch (start us, length us, event | category | flops | bytes accessed | tf_op | source)
XLA Modules:
  0.0 105.2 jit_solution(2479573006937702130)
XLA Ops:
  0.6 2.4 %pack_keys.1.kv.refs_5_ = bf16[2,4,512,128]{3,2,1,0:T(8,128)(2,1)} custom-call(bf16[2048,128]{1,0:T(8,128)(2,1)} %bitcast.15, bf16[2048,128]{1,0:T(8,128)(2,1)} %bitcast.16), custom_call_target="tpu_custom_call" | custom-call | tf_op jit(solution)/shard_map/pack_keys/pallas_call | solution.py:408
  3.1 4.5 %collective-permute-start.1 = (bf16[2,4,512,128]{3,2,1,0:T(8,128)(2,1)}, bf16[2,4,512,128]{3,2,1,0:T(8,128)(2,1)}, u32[]{:S(2)}, u32[]{:S(2)}) collective-permute-start(bf16[2,4,512,128]{3,2,1,0:T(8,128)(2,1)} %pack_keys.1.kv.refs_5_), channel_id=1, source_target_pairs={{4,8},{12,16},{20,24},{8,4},{16,12},{24,20},{5,9},{13,17},{21,25},... | collective-permute-start | bytes 3145736 | tf_op jit(solution)/shard_map/ppermute | solution.py:397
  7.6 0.1 collective-permute-start
  7.7 3.4 %pack_queries.1 = (bf16[2,4,512,128]{3,2,1,0:T(8,128)(2,1)}, bf16[4,4,64,128]{3,2,1,0:T(8,128)(2,1)}) custom-call(bf16[2048,128]{1,0:T(8,128)(2,1)} %bitcast.17, bf16[2048,128]{1,0:T(8,128)(2,1)} %bitcast.18, bf16[2,4,512,128]{3,2,1,0:T(8,128)(2,1)} %pack_keys.1.kv.refs_5_, s32[1,256]{1,0:T(1,128)} %bitcast.19), custom_call_target="tpu_custom_call" | custom-call | tf_op jit(solution)/shard_map/pack_queries/pallas_call | solution.py:416
  11.1 1.1 %collective-permute-start.4 = (bf16[1,4,4,64,128]{4,3,2,1,0:T(8,128)(2,1)}, bf16[1,4,4,64,128]{4,3,2,1,0:T(8,128)(2,1)}, u32[]{:S(2)}, u32[]{:S(2)}) collective-permute-start(bf16[1,4,4,64,128]{4,3,2,1,0:T(8,128)(2,1)} %bitcast.10), channel_id=1, source_target_pairs={{0,24},{4,28},{8,16},{12,20},{16,8},{20,12},{24,0},{28,4},{1,25},{... | collective-permute-start | bytes 786440 | tf_op jit(solution)/shard_map/ppermute | solution.py:390
  12.1 1.3 %collective-permute-start.3 = (bf16[1,4,4,64,128]{4,3,2,1,0:T(8,128)(2,1)}, bf16[1,4,4,64,128]{4,3,2,1,0:T(8,128)(2,1)}, u32[]{:S(2)}, u32[]{:S(2)}) collective-permute-start(bf16[1,4,4,64,128]{4,3,2,1,0:T(8,128)(2,1)} %bitcast.11), channel_id=1, source_target_pairs={{0,16},{4,20},{8,24},{12,28},{16,0},{20,4},{24,8},{28,12},{1,17},{... | collective-permute-start | bytes 786440 | tf_op jit(solution)/shard_map/ppermute | solution.py:390
  13.5 0.3 collective-permute-start.2
  13.7 2.2 %masks.1 = (f32[1536,128]{1,0:T(8,128)}, bf16[256,512]{1,0:T(8,128)(2,1)}, bf16[512,256]{1,0:T(8,128)(2,1)}, bf16[512,64]{1,0:T(8,128)(2,1)}) custom-call(s32[1,256]{1,0:T(1,128)} %bitcast.20), custom_call_target="tpu_custom_call" | custom-call | tf_op jit(solution)/shard_map/masks/pallas_call | solution.py:428
  15.9 14.8 %collective-permute-done.1.kv_far = bf16[2,4,512,128]{3,2,1,0:T(8,128)(2,1)} collective-permute-done((bf16[2,4,512,128]{3,2,1,0:T(8,128)(2,1)}, bf16[2,4,512,128]{3,2,1,0:T(8,128)(2,1)}, u32[]{:S(2)}, u32[]{:S(2)}) %collective-permute-start.1) | collective-permute-done | bytes 1048608 | tf_op jit(solution)/shard_map/ppermute | solution.py:397
  30.7 0.0 collective-permute-done.kv_near
  30.7 9.1 %window.1 = (bf16[4,1536,512]{2,1,0:T(8,128)(2,1)}, f32[4,128,512]{2,1,0:T(8,128)}, f32[4,2,512]{2,1,0:T(2,128)}, bf16[4,128,1536]{2,1,0:T(8,128)(2,1)}, bf16[4,...) custom-call(bf16[2,4,512,128]{3,2,1,0:T(8,128)(2,1)} %get-tuple-element.61.qd, ...), custom_call_target="tpu_custom_call" | custom-call | flops 1000000 | bytes 1000000 | tf_op jit(solution)/shard_map/window/pallas_call | solution.py:445
  39.8 0.0 collective-permute-done.4.refs_3_
  39.8 0.0 collective-permute-done.3.refs_2_
  39.9 3.0 %collective-permute-done.2.refs_1_ = bf16[1,4,4,64,128]{4,3,2,1,0:T(8,128)(2,1)} collective-permute-done((bf16[1,4,4,64,128]{4,3,2,1,0:T(8,128)(2,1)}, bf16[1,4,4,64,128]{4,3,2,1,0:T(8,128)(2,1)}, u32[]{:S(2)}, u32[]{:S(2)}) %collective-permute-start.2) | collective-permute-done | bytes 262176 | tf_op jit(solution)/shard_map/ppermute | solution.py:390
  42.8 1.3 %pad_maximum_fusion = bf16[4,4,4,64,128]{4,3,2,1,0:T(8,128)(2,1)S(1)} fusion(bf16[1,4,4,64,128]{4,3,2,1,0:T(8,128)(2,1)} %collective-permute-done.4.refs_3_, bf16[1,4,4,64,128]{4,3,2,1,0:T(8,128)(2,1)} %collective-permute-done.3.refs_2_, bf16[1,4,4,64,128]{4,3,2,1,0:T(8,128)(2,1)} %collective-permute-done.2.refs_1_, bf16[1,4,4,64,128]{4,3,2,1,0:T(8,128)(2,1)} %bitcast.13), kind=kLoop, calls=%fused_computation | loop fusion | flops 1572864 | bytes 2097152 | tf_op jit(solution)/shard_map/concatenate | solution.py:477
  44.2 0.1 collective-permute-start.5
  44.2 2.2 %collective-permute-start.7 = (bf16[2,4,512,128]{3,2,1,0:T(8,128)(2,1)}, bf16[2,4,512,128]{3,2,1,0:T(8,128)(2,1)}, u32[]{:S(2)}, u32[]{:S(2)}) collective-permute-start(bf16[2,4,512,128]{3,2,1,0:T(8,128)(2,1)} %get-tuple-element.61.qd), channel_id=1, source_target_pairs={{4,8},{12,16},{20,24},{8,4},{16,12},{24,20},{5,9},{13,17},{21,25},... | collective-permute-start | bytes 3145736 | tf_op jit(solution)/shard_map/ppermute | solution.py:397
  46.5 0.1 collective-permute-start.6
  46.6 0.5 collective-permute-done.5.refs_4_
  47.0 5.5 %global_stats.1 = (bf16[4,4,256,128]{3,2,1,0:T(8,128)(2,1)}, f32[8,4,8,256]{3,2,1,0:T(8,128)}) custom-call(bf16[256,512]{1,0:T(8,128)(2,1)} %get-tuple-element.48.compact, bf16[1,4,4,64,128]{4,3,2,1,0:T(8,128)(2,1)} %bitcast.14, bf16[1,4,4,64,128]{4,3,2,1,0:T(8,128)(2,1)} %collective-permute-done.2.refs_1_, ...), custom_call_target="tpu_custom_call" | custom-call | flops 1000000 | bytes 1000000 | tf_op jit(solution)/shard_map/global_stats/pallas_call | solution.py:481
  52.5 4.3 %all-to-all-start = ((f32[8,4,8,256]{3,2,1,0:T(8,128)}), f32[8,4,8,256]{3,2,1,0:T(8,128)}, u32[]{:S(2)}, u32[]{:S(2)}) async-start(f32[8,4,8,256]{3,2,1,0:T(8,128)} %get-tuple-element.63), calls=%async_computation | async-start | bytes 524288 | tf_op jit(solution)/shard_map/all_to_all | solution.py:494
  56.8 11.3 %local.1 = (bf16[4,512,128]{2,1,0:T(8,128)(2,1)}, f32[4,2,512]{2,1,0:T(2,128)}, f32[4,512,128]{2,1,0:T(8,128)}, f32[2,4,512,128]{3,2,1,0:T(8,128)}, bf16[4,2,4,6...) custom-call(bf16[3,4,128,512]{3,2,1,0:T(8,128)(2,1)} %get-tuple-element.45.sides.value_t, ...), custom_call_target="tpu_custom_call" | custom-call | flops 1000000 | bytes 1000000 | tf_op jit(solution)/shard_map/local/pallas_call | solution.py:501
  68.1 3.5 %collective-permute-start.9 = (f32[4,2,512]{2,1,0:T(2,128)}, f32[4,2,512]{2,1,0:T(2,128)S(1)}, u32[]{:S(2)}, u32[]{:S(2)}) collective-permute-start(f32[4,2,512]{2,1,0:T(2,128)} %get-tuple-element.62), channel_id=1, source_target_pairs={{4,8},{12,16},{20,24},{8,4},{16,12},{24,20},{5,9},{13,17},{21,25},... | collective-permute-start | bytes 49160 | tf_op jit(solution)/shard_map/ppermute | solution.py:397
  71.6 0.1 collective-permute-start.8
  71.7 0.5 collective-permute-start.11
  72.2 0.0 collective-permute-done.7.qd_far
  72.2 0.0 collective-permute-done.6.qd_near
  72.2 0.4 all-to-all-done.stats
  72.6 6.8 %global_queries.1 = (f32[2,4,512,128]{3,2,1,0:T(8,128)}, bf16[4,2,4,64,128]{4,3,2,1,0:T(8,128)(2,1)}, bf16[4,2,4,64,128]{4,3,2,1,0:T(8,128)(2,1)}) custom-call(bf16[2,4,512,128]{3,2,1,0:T(8,128)(2,1)} %pack_keys.1.kv.refs_5_, bf16[4,4,256,128]{3,2,1,0:T(8,128)(2,1)} %get-tuple-element.55.rows, ...), custom_call_target="tpu_custom_call", output_to_operand_aliasing={{0}: (4, {})} | custom-call | flops 1000000 | bytes 1000000 | tf_op jit(solution)/shard_map/global_queries/pallas_call | solution.py:533
  79.4 0.0 collective-permute-done.9.log_far
  79.4 0.0 copy-start
  79.4 0.0 collective-permute-done.8.log_near
  79.4 0.0 copy-start.1
  79.4 2.2 %collective-permute-start.10 = (bf16[4,2,4,64,128]{4,3,2,1,0:T(8,128)(2,1)}, bf16[4,2,4,64,128]{4,3,2,1,0:T(8,128)(2,1)}, u32[]{:S(2)}, u32[]{:S(2)}) collective-permute-start(bf16[4,2,4,64,128]{4,3,2,1,0:T(8,128)(2,1)} %get-tuple-element.69), channel_id=1, source_target_pairs={{0,4},{4,0},{8,12},{12,8},{16,20},{20,16},{24,28},{28,24},{1,5},{5... | collective-permute-start | bytes 1572872 | tf_op jit(solution)/shard_map/ppermute | solution.py:390
  81.6 0.0 collective-permute-done.11.got_sums
  81.6 1.9 %collective-permute-done.10.got_ends = bf16[4,2,4,64,128]{4,3,2,1,0:T(8,128)(2,1)} collective-permute-done((bf16[4,2,4,64,128]{4,3,2,1,0:T(8,128)(2,1)}, bf16[4,2,4,64,128]{4,3,2,1,0:T(8,128)(2,1)}, u32[]{:S(2)}, u32[]{:S(2)}) %collective-permute-start.10) | collective-permute-done | bytes 524320 | tf_op jit(solution)/shard_map/ppermute | solution.py:390
  83.5 2.5 %fold.1 = (bf16[4,4,64,128]{3,2,1,0:T(8,128)(2,1)}, bf16[4,4,64,128]{3,2,1,0:T(8,128)(2,1)}, bf16[4,4,64,128]{3,2,1,0:T(8,128)(2,1)}, bf16[4,4,64,128]{3,2,1,0:T(8,128)(2,1)}) custom-call(bf16[4,2,4,64,128]{4,3,2,1,0:T(8,128)(2,1)} %get-tuple-element.67.kept_ends, bf16[4,2,4,64,128]{4,3,2,1,0:T(8,128)(2,1)} %collective-permute-done.10.got_ends, ...), custom_call_target="tpu_custom_call" | custom-call | tf_op jit(solution)/shard_map/fold/pallas_call | solution.py:551
  86.0 1.2 %collective-permute-start.12 = (bf16[4,4,64,128]{3,2,1,0:T(8,128)(2,1)}, bf16[4,4,64,128]{3,2,1,0:T(8,128)(2,1)}, u32[]{:S(2)}, u32[]{:S(2)}) collective-permute-start(bf16[4,4,64,128]{3,2,1,0:T(8,128)(2,1)} %get-tuple-element.73), channel_id=1, source_target_pairs={{0,8},{4,12},{8,0},{12,4},{16,24},{20,28},{24,16},{28,20},{1,9},{5... | collective-permute-start | bytes 786440 | tf_op jit(solution)/shard_map/ppermute | solution.py:390
  87.2 0.7 collective-permute-start.13
  87.9 1.2 %collective-permute-start.14 = (bf16[4,4,64,128]{3,2,1,0:T(8,128)(2,1)}, bf16[4,4,64,128]{3,2,1,0:T(8,128)(2,1)}, u32[]{:S(2)}, u32[]{:S(2)}) collective-permute-start(bf16[4,4,64,128]{3,2,1,0:T(8,128)(2,1)} %get-tuple-element.75), channel_id=1, source_target_pairs={{0,24},{4,28},{8,16},{12,20},{16,8},{20,12},{24,0},{28,4},{1,25},{... | collective-permute-start | bytes 786440 | tf_op jit(solution)/shard_map/ppermute | solution.py:390
  89.0 0.0 copy-done
  89.1 0.0 copy-done.1
  89.1 6.9 %rim.1.dkv = f32[2,4,512,128]{3,2,1,0:T(8,128)} custom-call(bf16[2,4,512,128]{3,2,1,0:T(8,128)(2,1)} %pack_keys.1.kv.refs_5_, f32[1536,128]{1,0:T(8,128)} %get-tuple-element.44.bias, bf16[2,4,512,128]{3,2,1,0:T(8,128)(2,1)} %collective-permute-done.6.qd_near, bf16[2,4,512,128]{3,2,1,0:T(8,128)(2,1)} %collective-permute-done.7.qd_far, ...), custom_call_target="tpu_custom_call" | custom-call | flops 1000000 | bytes 1000000 | tf_op jit(solution)/shard_map/rim/pallas_call | solution.py:566
  96.0 0.0 collective-permute-done.12.refs_1_
  96.0 0.0 collective-permute-done.13.refs_2_
  96.0 5.0 %collective-permute-done.14.refs_3_ = bf16[4,4,64,128]{3,2,1,0:T(8,128)(2,1)} collective-permute-done((bf16[4,4,64,128]{3,2,1,0:T(8,128)(2,1)}, bf16[4,4,64,128]{3,2,1,0:T(8,128)(2,1)}, u32[]{:S(2)}, u32[]{:S(2)}) %collective-permute-start.14) | collective-permute-done | bytes 262176 | tf_op jit(solution)/shard_map/ppermute | solution.py:390
  101.0 4.2 %final.1 = (bf16[2048,128]{1,0:T(8,128)(2,1)}, f32[2048,128]{1,0:T(8,128)}, f32[2048,128]{1,0:T(8,128)}, f32[2048,128]{1,0:T(8,128)}) custom-call(bf16[512,64]{1,0:T(8,128)(2,1)} %get-tuple-element.42.place, bf16[4,512,128]{2,1,0:T(8,128)(2,1)} %get-tuple-element.59.out, f32[4,512,128]{2,1,0:T(8,128)} %get-tuple-element.60.dq, f32[2,4,512,128]{3,2,1,0:T(8,128)} %rim.1.dkv, ...), custom_call_target="tpu_custom_call" | custom-call | tf_op jit(solution)/shard_map/final/pallas_call | solution.py:589
Async XLA Ops:
  3.1 27.6 %collective-permute-start.1 = (bf16[2,4,512,128]{3,2,1,0:T(8,128)(2,1)}, bf16[2,4,512,128]{3,2,1,0:T(8,128)(2,1)}, u32[]{:S(2)}, u32[]{:S(2)}) collective-permute-start(bf16[2,4,512,128]{3,2,1,0:T(8,128)(2,1)} %pack_keys.1.kv.refs_5_), channel_id=1, source_target_pairs={{4,8},{12,16},{20,24},{8,4},{16,12},{24,20},{5,9},{13,17},{21,25},... | collective-permute-start | bytes 3145736 | tf_op jit(solution)/shard_map/ppermute | solution.py:397
  7.6 23.1 %collective-permute-start = (bf16[2,4,512,128]{3,2,1,0:T(8,128)(2,1)}, bf16[2,4,512,128]{3,2,1,0:T(8,128)(2,1)}, u32[]{:S(2)}, u32[]{:S(2)}) collective-permute-start(bf16[2,4,512,128]{3,2,1,0:T(8,128)(2,1)} %pack_keys.1.kv.refs_5_), channel_id=1, source_target_pairs={{0,4},{4,0},{8,12},{12,8},{16,20},{20,16},{24,28},{28,24},{1,5},{5... | collective-permute-start | bytes 3145736 | tf_op jit(solution)/shard_map/ppermute | solution.py:390
  11.1 28.8 %collective-permute-start.4 = (bf16[1,4,4,64,128]{4,3,2,1,0:T(8,128)(2,1)}, bf16[1,4,4,64,128]{4,3,2,1,0:T(8,128)(2,1)}, u32[]{:S(2)}, u32[]{:S(2)}) collective-permute-start(bf16[1,4,4,64,128]{4,3,2,1,0:T(8,128)(2,1)} %bitcast.10), channel_id=1, source_target_pairs={{0,24},{4,28},{8,16},{12,20},{16,8},{20,12},{24,0},{28,4},{1,25},{... | collective-permute-start | bytes 786440 | tf_op jit(solution)/shard_map/ppermute | solution.py:390
  12.1 27.7 %collective-permute-start.3 = (bf16[1,4,4,64,128]{4,3,2,1,0:T(8,128)(2,1)}, bf16[1,4,4,64,128]{4,3,2,1,0:T(8,128)(2,1)}, u32[]{:S(2)}, u32[]{:S(2)}) collective-permute-start(bf16[1,4,4,64,128]{4,3,2,1,0:T(8,128)(2,1)} %bitcast.11), channel_id=1, source_target_pairs={{0,16},{4,20},{8,24},{12,28},{16,0},{20,4},{24,8},{28,12},{1,17},{... | collective-permute-start | bytes 786440 | tf_op jit(solution)/shard_map/ppermute | solution.py:390
  13.5 29.4 %collective-permute-start.2 = (bf16[1,4,4,64,128]{4,3,2,1,0:T(8,128)(2,1)}, bf16[1,4,4,64,128]{4,3,2,1,0:T(8,128)(2,1)}, u32[]{:S(2)}, u32[]{:S(2)}) collective-permute-start(bf16[1,4,4,64,128]{4,3,2,1,0:T(8,128)(2,1)} %bitcast.12), channel_id=1, source_target_pairs={{0,8},{4,12},{8,0},{12,4},{16,24},{20,28},{24,16},{28,20},{1,9},{5... | collective-permute-start | bytes 786440 | tf_op jit(solution)/shard_map/ppermute | solution.py:390
  44.2 2.9 %collective-permute-start.5 = (bf16[4,4,4,64,128]{4,3,2,1,0:T(8,128)(2,1)S(1)}, bf16[4,4,4,64,128]{4,3,2,1,0:T(8,128)(2,1)}, u32[]{:S(2)}, u32[]{:S(2)}) collective-permute-start(bf16[4,4,4,64,128]{4,3,2,1,0:T(8,128)(2,1)S(1)} %pad_maximum_fusion), channel_id=1, source_target_pairs={{0,4},{4,0},{8,12},{12,8},{16,20},{20,16},{24,28},{28,24},{1,5},{5... | collective-permute-start | bytes 3145736 | tf_op jit(solution)/shard_map/ppermute | solution.py:390
  44.2 28.0 %collective-permute-start.7 = (bf16[2,4,512,128]{3,2,1,0:T(8,128)(2,1)}, bf16[2,4,512,128]{3,2,1,0:T(8,128)(2,1)}, u32[]{:S(2)}, u32[]{:S(2)}) collective-permute-start(bf16[2,4,512,128]{3,2,1,0:T(8,128)(2,1)} %get-tuple-element.61.qd), channel_id=1, source_target_pairs={{4,8},{12,16},{20,24},{8,4},{16,12},{24,20},{5,9},{13,17},{21,25},... | collective-permute-start | bytes 3145736 | tf_op jit(solution)/shard_map/ppermute | solution.py:397
  46.5 25.7 %collective-permute-start.6 = (bf16[2,4,512,128]{3,2,1,0:T(8,128)(2,1)}, bf16[2,4,512,128]{3,2,1,0:T(8,128)(2,1)}, u32[]{:S(2)}, u32[]{:S(2)}) collective-permute-start(bf16[2,4,512,128]{3,2,1,0:T(8,128)(2,1)} %get-tuple-element.61.qd), channel_id=1, source_target_pairs={{0,4},{4,0},{8,12},{12,8},{16,20},{20,16},{24,28},{28,24},{1,5},{5... | collective-permute-start | bytes 3145736 | tf_op jit(solution)/shard_map/ppermute | solution.py:390
  52.5 20.1 %all-to-all-start = ((f32[8,4,8,256]{3,2,1,0:T(8,128)}), f32[8,4,8,256]{3,2,1,0:T(8,128)}, u32[]{:S(2)}, u32[]{:S(2)}) async-start(f32[8,4,8,256]{3,2,1,0:T(8,128)} %get-tuple-element.63), calls=%async_computation | async-start | bytes 524288 | tf_op jit(solution)/shard_map/all_to_all | solution.py:494
  68.1 11.3 %collective-permute-start.9 = (f32[4,2,512]{2,1,0:T(2,128)}, f32[4,2,512]{2,1,0:T(2,128)S(1)}, u32[]{:S(2)}, u32[]{:S(2)}) collective-permute-start(f32[4,2,512]{2,1,0:T(2,128)} %get-tuple-element.62), channel_id=1, source_target_pairs={{4,8},{12,16},{20,24},{8,4},{16,12},{24,20},{5,9},{13,17},{21,25},... | collective-permute-start | bytes 49160 | tf_op jit(solution)/shard_map/ppermute | solution.py:397
  71.6 7.8 %collective-permute-start.8 = (f32[4,2,512]{2,1,0:T(2,128)}, f32[4,2,512]{2,1,0:T(2,128)S(1)}, u32[]{:S(2)}, u32[]{:S(2)}) collective-permute-start(f32[4,2,512]{2,1,0:T(2,128)} %get-tuple-element.62), channel_id=1, source_target_pairs={{0,4},{4,0},{8,12},{12,8},{16,20},{20,16},{24,28},{28,24},{1,5},{5... | collective-permute-start | bytes 49160 | tf_op jit(solution)/shard_map/ppermute | solution.py:390
  71.7 9.9 %collective-permute-start.11 = (bf16[4,2,4,64,128]{4,3,2,1,0:T(8,128)(2,1)}, bf16[4,2,4,64,128]{4,3,2,1,0:T(8,128)(2,1)}, u32[]{:S(2)}, u32[]{:S(2)}) collective-permute-start(bf16[4,2,4,64,128]{4,3,2,1,0:T(8,128)(2,1)} %get-tuple-element.71), channel_id=1, source_target_pairs={{0,4},{4,0},{8,12},{12,8},{16,20},{20,16},{24,28},{28,24},{1,5},{5... | collective-permute-start | bytes 1572872 | tf_op jit(solution)/shard_map/ppermute | solution.py:390
  79.4 9.7 %copy-start = (f32[4,2,512]{2,1,0:T(2,128)}, f32[4,2,512]{2,1,0:T(2,128)S(1)}, u32[]{:S(2)}) copy-start(f32[4,2,512]{2,1,0:T(2,128)S(1)} %collective-permute-done.9.log_far) | copy-start | bytes 49156
  79.4 9.7 %copy-start.1 = (f32[4,2,512]{2,1,0:T(2,128)}, f32[4,2,512]{2,1,0:T(2,128)S(1)}, u32[]{:S(2)}) copy-start(f32[4,2,512]{2,1,0:T(2,128)S(1)} %collective-permute-done.8.log_near) | copy-start | bytes 49156
  79.4 4.0 %collective-permute-start.10 = (bf16[4,2,4,64,128]{4,3,2,1,0:T(8,128)(2,1)}, bf16[4,2,4,64,128]{4,3,2,1,0:T(8,128)(2,1)}, u32[]{:S(2)}, u32[]{:S(2)}) collective-permute-start(bf16[4,2,4,64,128]{4,3,2,1,0:T(8,128)(2,1)} %get-tuple-element.69), channel_id=1, source_target_pairs={{0,4},{4,0},{8,12},{12,8},{16,20},{20,16},{24,28},{28,24},{1,5},{5... | collective-permute-start | bytes 1572872 | tf_op jit(solution)/shard_map/ppermute | solution.py:390
  86.0 10.0 %collective-permute-start.12 = (bf16[4,4,64,128]{3,2,1,0:T(8,128)(2,1)}, bf16[4,4,64,128]{3,2,1,0:T(8,128)(2,1)}, u32[]{:S(2)}, u32[]{:S(2)}) collective-permute-start(bf16[4,4,64,128]{3,2,1,0:T(8,128)(2,1)} %get-tuple-element.73), channel_id=1, source_target_pairs={{0,8},{4,12},{8,0},{12,4},{16,24},{20,28},{24,16},{28,20},{1,9},{5... | collective-permute-start | bytes 786440 | tf_op jit(solution)/shard_map/ppermute | solution.py:390
  87.2 8.8 %collective-permute-start.13 = (bf16[4,4,64,128]{3,2,1,0:T(8,128)(2,1)}, bf16[4,4,64,128]{3,2,1,0:T(8,128)(2,1)}, u32[]{:S(2)}, u32[]{:S(2)}) collective-permute-start(bf16[4,4,64,128]{3,2,1,0:T(8,128)(2,1)} %get-tuple-element.74), channel_id=1, source_target_pairs={{0,16},{4,20},{8,24},{12,28},{16,0},{20,4},{24,8},{28,12},{1,17},{... | collective-permute-start | bytes 786440 | tf_op jit(solution)/shard_map/ppermute | solution.py:390
  87.9 13.2 %collective-permute-start.14 = (bf16[4,4,64,128]{3,2,1,0:T(8,128)(2,1)}, bf16[4,4,64,128]{3,2,1,0:T(8,128)(2,1)}, u32[]{:S(2)}, u32[]{:S(2)}) collective-permute-start(bf16[4,4,64,128]{3,2,1,0:T(8,128)(2,1)} %get-tuple-element.75), channel_id=1, source_target_pairs={{0,24},{4,28},{8,16},{12,20},{16,8},{20,12},{24,0},{28,4},{1,25},{... | collective-permute-start | bytes 786440 | tf_op jit(solution)/shard_map/ppermute | solution.py:390

commit v11 on v10

--- a/solution.py
+++ b/solution.py
@@ -476,6 +476,12 @@
             held = after(held, top_sum)
         send = jnp.concatenate(held, axis=0) if number else held[0]
         held += [swap(send, mask) for mask in stage]
+        if devices == 8 and not number:
+            pairs = [(0, 6), (1, 7), (6, 0), (7, 1)]
+            straight = lax.ppermute(send, "ctx", pairs)
+            turned = lax.ppermute(held[2], "ctx", [(6, 4), (7, 5), (0, 2), (1, 3)])
+            straight, turned = after((straight, turned), top_sum)
+            held[3] = straight + turned
 
     row_shape = (4, heads, count, width)
     rows, stats = pl.pallas_call(

time: 107 us -> 108 us (level)
  waiting for transfers between devices: 25.5 us -> 14.9 us
  starting transfers between devices: 23.2 us -> 32.6 us
    ppermute x3, waiting for transfers between devices: 14.8 us -> 0.28 us  [from_far(): return lax.ppermute(value, 'ctx', pairs + [(j, i) for i, j in pairs])]
    ppermute x0 -> x2, starting transfers between devices: none -> 8.31 us  [the longest x1 5.26 us: shards(): turned = lax.ppermute(held[2], 'ctx', [(6, 4), (7, 5), (0, 2), (1, 3)])]
    ppermute x12 -> x11, waiting for transfers between devices: 10.3 us -> 14.5 us  [swap(): return lax.ppermute(value, 'ctx', [(i, i ^ mask) for i in range(devices)])]
    ppermute x3, starting transfers between devices: 10.3 us -> 11.9 us  [from_far(): return lax.ppermute(value, 'ctx', pairs + [(j, i) for i, j in pairs])]
    add x0 -> x1, other arithmetic: none -> 1.1 us  [shards(): held[3] = straight + turned]
    ppermute x12 -> x11, starting transfers between devices: 8.66 us -> 7.94 us  [swap(): return lax.ppermute(value, 'ctx', [(i, i ^ mask) for i in range(devices)])]
  transfers between devices with their start and end apart: 16 -> 17, of which waited for: 6 -> 5; matrix products, arithmetic and copies ran while one was open for 0% -> 1% of each run, Pallas kernels for 43% -> 43%
where the time goes in v11:
time: 108 us; the launch traced here: 106 us
  Pallas kernels  54.4 us (50%)
  starting transfers between devices  32.6 us (30%)
  waiting for transfers between devices  14.9 us (14%)
  other arithmetic  2.34 us (2%)
    ppermute x11, waiting for transfers between devices, swap(): return lax.ppermute(value, 'ctx', [(i, i ^ mask) for i in range(devices)])  14.5 us
    ppermute x3, starting transfers between devices, from_far(): return lax.ppermute(value, 'ctx', pairs + [(j, i) for i, j in pairs])  11.9 us
    pallas_call x1, Pallas kernels, shards(): pl.pallas_call(functools.partial(local_kernel, scale, scale2), grid=(head...  11.2 us
    pallas_call x1, Pallas kernels, shards(): pl.pallas_call(functools.partial(window_kernel, scale2), grid=(heads,), i...  9.12 us
    ppermute x11, starting transfers between devices, swap(): return lax.ppermute(value, 'ctx', [(i, i ^ mask) for i in range(devices)])  7.94 us
    pallas_call x1, Pallas kernels, shards(): pl.pallas_call(functools.partial(rim_kernel, scale, scale2), grid=(heads,...  6.96 us
    pallas_call x1, Pallas kernels, shards(): pl.pallas_call(functools.partial(global_kernel, scale, scale2), grid=(hea...  6.77 us
    pallas_call x1, Pallas kernels, shards(): pl.pallas_call(functools.partial(stats_kernel, scale2), grid=(heads,), in...  5.56 us
  transfers between devices with their start and end apart: 17, of which 5 were waited for; matrix products, arithmetic and copies ran while one was open for 1% of the time, Pallas kernels for 43%

profile of v11, /device:TPU:1, one launch (start us, length us, event | category | flops | bytes accessed | tf_op | source)
XLA Modules:
  0.0 105.7 jit_solution(300706882022915520)
XLA Ops:
  0.6 2.4 %pack_keys.1.kv.refs_5_ = bf16[2,4,512,128]{3,2,1,0:T(8,128)(2,1)} custom-call(bf16[2048,128]{1,0:T(8,128)(2,1)} %bitcast.15, bf16[2048,128]{1,0:T(8,128)(2,1)} %bitcast.16), custom_call_target="tpu_custom_call" | custom-call | tf_op jit(solution)/shard_map/pack_keys/pallas_call | solution.py:408
  3.1 4.5 %collective-permute-start.1 = (bf16[2,4,512,128]{3,2,1,0:T(8,128)(2,1)}, bf16[2,4,512,128]{3,2,1,0:T(8,128)(2,1)}, u32[]{:S(2)}, u32[]{:S(2)}) collective-permute-start(bf16[2,4,512,128]{3,2,1,0:T(8,128)(2,1)} %pack_keys.1.kv.refs_5_), channel_id=1, source_target_pairs={{4,8},{12,16},{20,24},{8,4},{16,12},{24,20},{5,9},{13,17},{21,25},... | collective-permute-start | bytes 3145736 | tf_op jit(solution)/shard_map/ppermute | solution.py:397
  7.6 0.1 collective-permute-start
  7.7 3.4 %pack_queries.1 = (bf16[2,4,512,128]{3,2,1,0:T(8,128)(2,1)}, bf16[4,4,64,128]{3,2,1,0:T(8,128)(2,1)}) custom-call(bf16[2048,128]{1,0:T(8,128)(2,1)} %bitcast.17, bf16[2048,128]{1,0:T(8,128)(2,1)} %bitcast.18, bf16[2,4,512,128]{3,2,1,0:T(8,128)(2,1)} %pack_keys.1.kv.refs_5_, s32[1,256]{1,0:T(1,128)} %bitcast.19), custom_call_target="tpu_custom_call" | custom-call | tf_op jit(solution)/shard_map/pack_queries/pallas_call | solution.py:416
  11.1 1.2 %collective-permute-start.3 = (bf16[1,4,4,64,128]{4,3,2,1,0:T(8,128)(2,1)}, bf16[1,4,4,64,128]{4,3,2,1,0:T(8,128)(2,1)}, u32[]{:S(2)}, u32[]{:S(2)}) collective-permute-start(bf16[1,4,4,64,128]{4,3,2,1,0:T(8,128)(2,1)} %bitcast.10), channel_id=1, source_target_pairs={{0,16},{4,20},{8,24},{12,28},{16,0},{20,4},{24,8},{28,12},{1,17},{... | collective-permute-start | bytes 786440 | tf_op jit(solution)/shard_map/ppermute | solution.py:390
  12.3 3.0 %collective-permute-start.4 = (bf16[1,4,4,64,128]{4,3,2,1,0:T(8,128)(2,1)}, bf16[1,4,4,64,128]{4,3,2,1,0:T(8,128)(2,1)}, u32[]{:S(2)}, u32[]{:S(2)}) collective-permute-start(bf16[1,4,4,64,128]{4,3,2,1,0:T(8,128)(2,1)} %bitcast.11), channel_id=1, source_target_pairs={{0,24},{4,28},{24,0},{28,4},{1,25},{5,29},{25,1},{29,5},{2,26},{6,... | collective-permute-start | bytes 786440 | tf_op jit(solution)/shard_map/ppermute | solution.py:481
  15.4 7.6 %collective-permute-done.3.refs_2_ = bf16[1,4,4,64,128]{4,3,2,1,0:T(8,128)(2,1)} collective-permute-done((bf16[1,4,4,64,128]{4,3,2,1,0:T(8,128)(2,1)}, bf16[1,4,4,64,128]{4,3,2,1,0:T(8,128)(2,1)}, u32[]{:S(2)}, u32[]{:S(2)}) %collective-permute-start.3) | collective-permute-done | bytes 262176 | tf_op jit(solution)/shard_map/ppermute | solution.py:390
  23.0 5.3 %collective-permute-start.5 = (bf16[1,4,4,64,128]{4,3,2,1,0:T(8,128)(2,1)}, bf16[1,4,4,64,128]{4,3,2,1,0:T(8,128)(2,1)}, u32[]{:S(2)}, u32[]{:S(2)}) collective-permute-start(bf16[1,4,4,64,128]{4,3,2,1,0:T(8,128)(2,1)} %collective-permute-done.3.refs_2_), channel_id=1, source_target_pairs={{24,16},{28,20},{0,8},{4,12},{25,17},{29,21},{1,9},{5,13},{26,18},... | collective-permute-start | bytes 786440 | tf_op jit(solution)/shard_map/ppermute | solution.py:482
  28.2 0.0 collective-permute-start.2
  28.2 2.2 %masks.1 = (f32[1536,128]{1,0:T(8,128)}, bf16[256,512]{1,0:T(8,128)(2,1)}, bf16[512,256]{1,0:T(8,128)(2,1)}, bf16[512,64]{1,0:T(8,128)(2,1)}) custom-call(s32[1,256]{1,0:T(1,128)} %bitcast.20), custom_call_target="tpu_custom_call" | custom-call | tf_op jit(solution)/shard_map/masks/pallas_call | solution.py:428
  30.4 0.3 collective-permute-done.1.kv_far
  30.7 0.0 collective-permute-done.kv_near
  30.7 9.1 %window.1 = (bf16[4,1536,512]{2,1,0:T(8,128)(2,1)}, f32[4,128,512]{2,1,0:T(8,128)}, f32[4,2,512]{2,1,0:T(2,128)}, bf16[4,128,1536]{2,1,0:T(8,128)(2,1)}, bf16[4,...) custom-call(bf16[2,4,512,128]{3,2,1,0:T(8,128)(2,1)} %get-tuple-element.65.qd, ...), custom_call_target="tpu_custom_call" | custom-call | flops 1000000 | bytes 1000000 | tf_op jit(solution)/shard_map/window/pallas_call | solution.py:445
  39.8 0.0 collective-permute-done.4
  39.8 0.0 collective-permute-done.5
  39.8 1.1 %add.3.refs_3_ = bf16[1,4,4,64,128]{4,3,2,1,0:T(8,128)(2,1)S(1)} add(bf16[1,4,4,64,128]{4,3,2,1,0:T(8,128)(2,1)} %collective-permute-done.4, bf16[1,4,4,64,128]{4,3,2,1,0:T(8,128)(2,1)} %collective-permute-done.5) | non-fusion elementwise | flops 131072 | bytes 786432 | tf_op jit(solution)/shard_map/add | solution.py:484
  41.0 0.0 collective-permute-done.2.refs_1_
  41.0 0.7 copy-done
  41.7 1.2 %pad_maximum_fusion = bf16[4,4,4,64,128]{4,3,2,1,0:T(8,128)(2,1)S(1)} fusion(bf16[1,4,4,64,128]{4,3,2,1,0:T(8,128)(2,1)S(1)} %add.3.refs_3_, bf16[1,4,4,64,128]{4,3,2,1,0:T(8,128)(2,1)} %collective-permute-done.3.refs_2_, bf16[1,4,4,64,128]{4,3,2,1,0:T(8,128)(2,1)} %collective-permute-done.2.refs_1_, bf16[1,4,4,64,128]{4,3,2,1,0:T(8,128)(2,1)} %bitcast.13), kind=kLoop, calls=%fused_computation | loop fusion | flops 1572864 | bytes 2097152 | tf_op jit(solution)/shard_map/concatenate | solution.py:477
  42.9 1.4 %collective-permute-start.6 = (bf16[4,4,4,64,128]{4,3,2,1,0:T(8,128)(2,1)S(1)}, bf16[4,4,4,64,128]{4,3,2,1,0:T(8,128)(2,1)}, u32[]{:S(2)}, u32[]{:S(2)}) collective-permute-start(bf16[4,4,4,64,128]{4,3,2,1,0:T(8,128)(2,1)S(1)} %pad_maximum_fusion), channel_id=1, source_target_pairs={{0,4},{4,0},{8,12},{12,8},{16,20},{20,16},{24,28},{28,24},{1,5},{5... | collective-permute-start | bytes 3145736 | tf_op jit(solution)/shard_map/ppermute | solution.py:390
  44.3 3.9 %collective-permute-start.8 = (bf16[2,4,512,128]{3,2,1,0:T(8,128)(2,1)}, bf16[2,4,512,128]{3,2,1,0:T(8,128)(2,1)}, u32[]{:S(2)}, u32[]{:S(2)}) collective-permute-start(bf16[2,4,512,128]{3,2,1,0:T(8,128)(2,1)} %get-tuple-element.65.qd), channel_id=1, source_target_pairs={{4,8},{12,16},{20,24},{8,4},{16,12},{24,20},{5,9},{13,17},{21,25},... | collective-permute-start | bytes 3145736 | tf_op jit(solution)/shard_map/ppermute | solution.py:397
  48.2 0.1 collective-permute-start.7
  48.3 0.0 collective-permute-done.6.refs_4_
  48.3 5.6 %global_stats.1 = (bf16[4,4,256,128]{3,2,1,0:T(8,128)(2,1)}, f32[8,4,8,256]{3,2,1,0:T(8,128)}) custom-call(bf16[256,512]{1,0:T(8,128)(2,1)} %get-tuple-element.50.compact, bf16[1,4,4,64,128]{4,3,2,1,0:T(8,128)(2,1)} %bitcast.14, bf16[1,4,4,64,128]{4,3,2,1,0:T(8,128)(2,1)} %collective-permute-done.2.refs_1_, ...), custom_call_target="tpu_custom_call" | custom-call | flops 1000000 | bytes 1000000 | tf_op jit(solution)/shard_map/global_stats/pallas_call | solution.py:487
  53.8 4.4 %all-to-all-start = ((f32[8,4,8,256]{3,2,1,0:T(8,128)}), f32[8,4,8,256]{3,2,1,0:T(8,128)}, u32[]{:S(2)}, u32[]{:S(2)}) async-start(f32[8,4,8,256]{3,2,1,0:T(8,128)} %get-tuple-element.67), calls=%async_computation | async-start | bytes 524288 | tf_op jit(solution)/shard_map/all_to_all | solution.py:500
  58.2 11.2 %local.1 = (bf16[4,512,128]{2,1,0:T(8,128)(2,1)}, f32[4,2,512]{2,1,0:T(2,128)}, f32[4,512,128]{2,1,0:T(8,128)}, f32[2,4,512,128]{3,2,1,0:T(8,128)}, bf16[4,2,4,6...) custom-call(bf16[3,4,128,512]{3,2,1,0:T(8,128)(2,1)} %get-tuple-element.47.sides.value_t, ...), custom_call_target="tpu_custom_call" | custom-call | flops 1000000 | bytes 1000000 | tf_op jit(solution)/shard_map/local/pallas_call | solution.py:507
  69.5 3.6 %collective-permute-start.10 = (f32[4,2,512]{2,1,0:T(2,128)}, f32[4,2,512]{2,1,0:T(2,128)S(1)}, u32[]{:S(2)}, u32[]{:S(2)}) collective-permute-start(f32[4,2,512]{2,1,0:T(2,128)} %get-tuple-element.66), channel_id=1, source_target_pairs={{4,8},{12,16},{20,24},{8,4},{16,12},{24,20},{5,9},{13,17},{21,25},... | collective-permute-start | bytes 49160 | tf_op jit(solution)/shard_map/ppermute | solution.py:397
  73.0 0.1 collective-permute-start.9
  73.1 0.5 collective-permute-start.12
  73.6 0.0 collective-permute-done.8.qd_far
  73.6 0.0 collective-permute-done.7.qd_near
  73.6 0.1 all-to-all-done.stats
  73.7 6.8 %global_queries.1 = (f32[2,4,512,128]{3,2,1,0:T(8,128)}, bf16[4,2,4,64,128]{4,3,2,1,0:T(8,128)(2,1)}, bf16[4,2,4,64,128]{4,3,2,1,0:T(8,128)(2,1)}) custom-call(bf16[2,4,512,128]{3,2,1,0:T(8,128)(2,1)} %pack_keys.1.kv.refs_5_, bf16[4,4,256,128]{3,2,1,0:T(8,128)(2,1)} %get-tuple-element.59.rows, ...), custom_call_target="tpu_custom_call", output_to_operand_aliasing={{0}: (4, {})} | custom-call | flops 1000000 | bytes 1000000 | tf_op jit(solution)/shard_map/global_queries/pallas_call | solution.py:539
  80.5 0.0 collective-permute-done.10.log_far
  80.5 0.0 collective-permute-done.9.log_near
  80.5 0.0 copy-start.2
  80.5 1.7 %collective-permute-start.11 = (bf16[4,2,4,64,128]{4,3,2,1,0:T(8,128)(2,1)}, bf16[4,2,4,64,128]{4,3,2,1,0:T(8,128)(2,1)}, u32[]{:S(2)}, u32[]{:S(2)}) collective-permute-start(bf16[4,2,4,64,128]{4,3,2,1,0:T(8,128)(2,1)} %get-tuple-element.73), channel_id=1, source_target_pairs={{0,4},{4,0},{8,12},{12,8},{16,20},{20,16},{24,28},{28,24},{1,5},{5... | collective-permute-start | bytes 1572872 | tf_op jit(solution)/shard_map/ppermute | solution.py:390
  82.2 0.0 collective-permute-done.12.got_sums
  82.2 1.9 %collective-permute-done.11.got_ends = bf16[4,2,4,64,128]{4,3,2,1,0:T(8,128)(2,1)} collective-permute-done((bf16[4,2,4,64,128]{4,3,2,1,0:T(8,128)(2,1)}, bf16[4,2,4,64,128]{4,3,2,1,0:T(8,128)(2,1)}, u32[]{:S(2)}, u32[]{:S(2)}) %collective-permute-start.11) | collective-permute-done | bytes 524320 | tf_op jit(solution)/shard_map/ppermute | solution.py:390
  84.1 2.5 %fold.1 = (bf16[4,4,64,128]{3,2,1,0:T(8,128)(2,1)}, bf16[4,4,64,128]{3,2,1,0:T(8,128)(2,1)}, bf16[4,4,64,128]{3,2,1,0:T(8,128)(2,1)}, bf16[4,4,64,128]{3,2,1,0:T(8,128)(2,1)}) custom-call(bf16[4,2,4,64,128]{4,3,2,1,0:T(8,128)(2,1)} %get-tuple-element.71.kept_ends, bf16[4,2,4,64,128]{4,3,2,1,0:T(8,128)(2,1)} %collective-permute-done.11.got_ends, ...), custom_call_target="tpu_custom_call" | custom-call | tf_op jit(solution)/shard_map/fold/pallas_call | solution.py:557
  86.6 1.4 %collective-permute-start.13 = (bf16[4,4,64,128]{3,2,1,0:T(8,128)(2,1)}, bf16[4,4,64,128]{3,2,1,0:T(8,128)(2,1)}, u32[]{:S(2)}, u32[]{:S(2)}) collective-permute-start(bf16[4,4,64,128]{3,2,1,0:T(8,128)(2,1)} %get-tuple-element.77), channel_id=1, source_target_pairs={{0,8},{4,12},{8,0},{12,4},{16,24},{20,28},{24,16},{28,20},{1,9},{5... | collective-permute-start | bytes 786440 | tf_op jit(solution)/shard_map/ppermute | solution.py:390
  88.0 0.6 collective-permute-start.14
  88.7 0.8 collective-permute-start.15
  89.5 7.0 %rim.1.dkv = f32[2,4,512,128]{3,2,1,0:T(8,128)} custom-call(bf16[2,4,512,128]{3,2,1,0:T(8,128)(2,1)} %pack_keys.1.kv.refs_5_, f32[1536,128]{1,0:T(8,128)} %get-tuple-element.46.bias, bf16[2,4,512,128]{3,2,1,0:T(8,128)(2,1)} %collective-permute-done.7.qd_near, bf16[2,4,512,128]{3,2,1,0:T(8,128)(2,1)} %collective-permute-done.8.qd_far, ...), custom_call_target="tpu_custom_call" | custom-call | flops 1000000 | bytes 1000000 | tf_op jit(solution)/shard_map/rim/pallas_call | solution.py:572
  96.5 0.0 collective-permute-done.13.refs_1_
  96.5 0.0 collective-permute-done.14.refs_2_
  96.5 5.0 %collective-permute-done.15.refs_3_ = bf16[4,4,64,128]{3,2,1,0:T(8,128)(2,1)} collective-permute-done((bf16[4,4,64,128]{3,2,1,0:T(8,128)(2,1)}, bf16[4,4,64,128]{3,2,1,0:T(8,128)(2,1)}, u32[]{:S(2)}, u32[]{:S(2)}) %collective-permute-start.15) | collective-permute-done | bytes 262176 | tf_op jit(solution)/shard_map/ppermute | solution.py:390
  101.5 4.2 %final.1 = (bf16[2048,128]{1,0:T(8,128)(2,1)}, f32[2048,128]{1,0:T(8,128)}, f32[2048,128]{1,0:T(8,128)}, f32[2048,128]{1,0:T(8,128)}) custom-call(bf16[512,64]{1,0:T(8,128)(2,1)} %get-tuple-element.44.place, bf16[4,512,128]{2,1,0:T(8,128)(2,1)} %get-tuple-element.63.out, f32[4,512,128]{2,1,0:T(8,128)} %get-tuple-element.64.dq, f32[2,4,512,128]{3,2,1,0:T(8,128)} %rim.1.dkv, ...), custom_call_target="tpu_custom_call" | custom-call | tf_op jit(solution)/shard_map/final/pallas_call | solution.py:595
  (4 shorter events, 0.0 us)
Async XLA Ops:
  3.1 27.6 %collective-permute-start.1 = (bf16[2,4,512,128]{3,2,1,0:T(8,128)(2,1)}, bf16[2,4,512,128]{3,2,1,0:T(8,128)(2,1)}, u32[]{:S(2)}, u32[]{:S(2)}) collective-permute-start(bf16[2,4,512,128]{3,2,1,0:T(8,128)(2,1)} %pack_keys.1.kv.refs_5_), channel_id=1, source_target_pairs={{4,8},{12,16},{20,24},{8,4},{16,12},{24,20},{5,9},{13,17},{21,25},... | collective-permute-start | bytes 3145736 | tf_op jit(solution)/shard_map/ppermute | solution.py:397
  7.6 23.1 %collective-permute-start = (bf16[2,4,512,128]{3,2,1,0:T(8,128)(2,1)}, bf16[2,4,512,128]{3,2,1,0:T(8,128)(2,1)}, u32[]{:S(2)}, u32[]{:S(2)}) collective-permute-start(bf16[2,4,512,128]{3,2,1,0:T(8,128)(2,1)} %pack_keys.1.kv.refs_5_), channel_id=1, source_target_pairs={{0,4},{4,0},{8,12},{12,8},{16,20},{20,16},{24,28},{28,24},{1,5},{5... | collective-permute-start | bytes 3145736 | tf_op jit(solution)/shard_map/ppermute | solution.py:390
  11.1 11.9 %collective-permute-start.3 = (bf16[1,4,4,64,128]{4,3,2,1,0:T(8,128)(2,1)}, bf16[1,4,4,64,128]{4,3,2,1,0:T(8,128)(2,1)}, u32[]{:S(2)}, u32[]{:S(2)}) collective-permute-start(bf16[1,4,4,64,128]{4,3,2,1,0:T(8,128)(2,1)} %bitcast.10), channel_id=1, source_target_pairs={{0,16},{4,20},{8,24},{12,28},{16,0},{20,4},{24,8},{28,12},{1,17},{... | collective-permute-start | bytes 786440 | tf_op jit(solution)/shard_map/ppermute | solution.py:390
  12.3 27.5 %collective-permute-start.4 = (bf16[1,4,4,64,128]{4,3,2,1,0:T(8,128)(2,1)}, bf16[1,4,4,64,128]{4,3,2,1,0:T(8,128)(2,1)}, u32[]{:S(2)}, u32[]{:S(2)}) collective-permute-start(bf16[1,4,4,64,128]{4,3,2,1,0:T(8,128)(2,1)} %bitcast.11), channel_id=1, source_target_pairs={{0,24},{4,28},{24,0},{28,4},{1,25},{5,29},{25,1},{29,5},{2,26},{6,... | collective-permute-start | bytes 786440 | tf_op jit(solution)/shard_map/ppermute | solution.py:481
  23.0 16.9 %collective-permute-start.5 = (bf16[1,4,4,64,128]{4,3,2,1,0:T(8,128)(2,1)}, bf16[1,4,4,64,128]{4,3,2,1,0:T(8,128)(2,1)}, u32[]{:S(2)}, u32[]{:S(2)}) collective-permute-start(bf16[1,4,4,64,128]{4,3,2,1,0:T(8,128)(2,1)} %collective-permute-done.3.refs_2_), channel_id=1, source_target_pairs={{24,16},{28,20},{0,8},{4,12},{25,17},{29,21},{1,9},{5,13},{26,18},... | collective-permute-start | bytes 786440 | tf_op jit(solution)/shard_map/ppermute | solution.py:482
  28.2 12.8 %collective-permute-start.2 = (bf16[1,4,4,64,128]{4,3,2,1,0:T(8,128)(2,1)}, bf16[1,4,4,64,128]{4,3,2,1,0:T(8,128)(2,1)}, u32[]{:S(2)}, u32[]{:S(2)}) collective-permute-start(bf16[1,4,4,64,128]{4,3,2,1,0:T(8,128)(2,1)} %bitcast.12), channel_id=1, source_target_pairs={{0,8},{4,12},{8,0},{12,4},{16,24},{20,28},{24,16},{28,20},{1,9},{5... | collective-permute-start | bytes 786440 | tf_op jit(solution)/shard_map/ppermute | solution.py:390
  41.0 0.7 copy-start
  42.9 5.4 %collective-permute-start.6 = (bf16[4,4,4,64,128]{4,3,2,1,0:T(8,128)(2,1)S(1)}, bf16[4,4,4,64,128]{4,3,2,1,0:T(8,128)(2,1)}, u32[]{:S(2)}, u32[]{:S(2)}) collective-permute-start(bf16[4,4,4,64,128]{4,3,2,1,0:T(8,128)(2,1)S(1)} %pad_maximum_fusion), channel_id=1, source_target_pairs={{0,4},{4,0},{8,12},{12,8},{16,20},{20,16},{24,28},{28,24},{1,5},{5... | collective-permute-start | bytes 3145736 | tf_op jit(solution)/shard_map/ppermute | solution.py:390
  44.3 29.3 %collective-permute-start.8 = (bf16[2,4,512,128]{3,2,1,0:T(8,128)(2,1)}, bf16[2,4,512,128]{3,2,1,0:T(8,128)(2,1)}, u32[]{:S(2)}, u32[]{:S(2)}) collective-permute-start(bf16[2,4,512,128]{3,2,1,0:T(8,128)(2,1)} %get-tuple-element.65.qd), channel_id=1, source_target_pairs={{4,8},{12,16},{20,24},{8,4},{16,12},{24,20},{5,9},{13,17},{21,25},... | collective-permute-start | bytes 3145736 | tf_op jit(solution)/shard_map/ppermute | solution.py:397
  48.2 25.4 %collective-permute-start.7 = (bf16[2,4,512,128]{3,2,1,0:T(8,128)(2,1)}, bf16[2,4,512,128]{3,2,1,0:T(8,128)(2,1)}, u32[]{:S(2)}, u32[]{:S(2)}) collective-permute-start(bf16[2,4,512,128]{3,2,1,0:T(8,128)(2,1)} %get-tuple-element.65.qd), channel_id=1, source_target_pairs={{0,4},{4,0},{8,12},{12,8},{16,20},{20,16},{24,28},{28,24},{1,5},{5... | collective-permute-start | bytes 3145736 | tf_op jit(solution)/shard_map/ppermute | solution.py:390
  53.8 19.9 %all-to-all-start = ((f32[8,4,8,256]{3,2,1,0:T(8,128)}), f32[8,4,8,256]{3,2,1,0:T(8,128)}, u32[]{:S(2)}, u32[]{:S(2)}) async-start(f32[8,4,8,256]{3,2,1,0:T(8,128)} %get-tuple-element.67), calls=%async_computation | async-start | bytes 524288 | tf_op jit(solution)/shard_map/all_to_all | solution.py:500
  69.5 11.1 %collective-permute-start.10 = (f32[4,2,512]{2,1,0:T(2,128)}, f32[4,2,512]{2,1,0:T(2,128)S(1)}, u32[]{:S(2)}, u32[]{:S(2)}) collective-permute-start(f32[4,2,512]{2,1,0:T(2,128)} %get-tuple-element.66), channel_id=1, source_target_pairs={{4,8},{12,16},{20,24},{8,4},{16,12},{24,20},{5,9},{13,17},{21,25},... | collective-permute-start | bytes 49160 | tf_op jit(solution)/shard_map/ppermute | solution.py:397
  73.0 7.5 %collective-permute-start.9 = (f32[4,2,512]{2,1,0:T(2,128)}, f32[4,2,512]{2,1,0:T(2,128)S(1)}, u32[]{:S(2)}, u32[]{:S(2)}) collective-permute-start(f32[4,2,512]{2,1,0:T(2,128)} %get-tuple-element.66), channel_id=1, source_target_pairs={{0,4},{4,0},{8,12},{12,8},{16,20},{20,16},{24,28},{28,24},{1,5},{5... | collective-permute-start | bytes 49160 | tf_op jit(solution)/shard_map/ppermute | solution.py:390
  73.1 9.1 %collective-permute-start.12 = (bf16[4,2,4,64,128]{4,3,2,1,0:T(8,128)(2,1)}, bf16[4,2,4,64,128]{4,3,2,1,0:T(8,128)(2,1)}, u32[]{:S(2)}, u32[]{:S(2)}) collective-permute-start(bf16[4,2,4,64,128]{4,3,2,1,0:T(8,128)(2,1)} %get-tuple-element.75), channel_id=1, source_target_pairs={{0,4},{4,0},{8,12},{12,8},{16,20},{20,16},{24,28},{28,24},{1,5},{5... | collective-permute-start | bytes 1572872 | tf_op jit(solution)/shard_map/ppermute | solution.py:390
  80.5 9.0 %copy-start.1 = (f32[4,2,512]{2,1,0:T(2,128)}, f32[4,2,512]{2,1,0:T(2,128)S(1)}, u32[]{:S(2)}) copy-start(f32[4,2,512]{2,1,0:T(2,128)S(1)} %collective-permute-done.10.log_far) | copy-start | bytes 49156
  80.5 9.0 %copy-start.2 = (f32[4,2,512]{2,1,0:T(2,128)}, f32[4,2,512]{2,1,0:T(2,128)S(1)}, u32[]{:S(2)}) copy-start(f32[4,2,512]{2,1,0:T(2,128)S(1)} %collective-permute-done.9.log_near) | copy-start | bytes 49156
  80.5 3.6 %collective-permute-start.11 = (bf16[4,2,4,64,128]{4,3,2,1,0:T(8,128)(2,1)}, bf16[4,2,4,64,128]{4,3,2,1,0:T(8,128)(2,1)}, u32[]{:S(2)}, u32[]{:S(2)}) collective-permute-start(bf16[4,2,4,64,128]{4,3,2,1,0:T(8,128)(2,1)} %get-tuple-element.73), channel_id=1, source_target_pairs={{0,4},{4,0},{8,12},{12,8},{16,20},{20,16},{24,28},{28,24},{1,5},{5... | collective-permute-start | bytes 1572872 | tf_op jit(solution)/shard_map/ppermute | solution.py:390
  86.6 9.9 %collective-permute-start.13 = (bf16[4,4,64,128]{3,2,1,0:T(8,128)(2,1)}, bf16[4,4,64,128]{3,2,1,0:T(8,128)(2,1)}, u32[]{:S(2)}, u32[]{:S(2)}) collective-permute-start(bf16[4,4,64,128]{3,2,1,0:T(8,128)(2,1)} %get-tuple-element.77), channel_id=1, source_target_pairs={{0,8},{4,12},{8,0},{12,4},{16,24},{20,28},{24,16},{28,20},{1,9},{5... | collective-permute-start | bytes 786440 | tf_op jit(solution)/shard_map/ppermute | solution.py:390
  88.0 8.4 %collective-permute-start.14 = (bf16[4,4,64,128]{3,2,1,0:T(8,128)(2,1)}, bf16[4,4,64,128]{3,2,1,0:T(8,128)(2,1)}, u32[]{:S(2)}, u32[]{:S(2)}) collective-permute-start(bf16[4,4,64,128]{3,2,1,0:T(8,128)(2,1)} %get-tuple-element.78), channel_id=1, source_target_pairs={{0,16},{4,20},{8,24},{12,28},{16,0},{20,4},{24,8},{28,12},{1,17},{... | collective-permute-start | bytes 786440 | tf_op jit(solution)/shard_map/ppermute | solution.py:390
  88.7 12.8 %collective-permute-start.15 = (bf16[4,4,64,128]{3,2,1,0:T(8,128)(2,1)}, bf16[4,4,64,128]{3,2,1,0:T(8,128)(2,1)}, u32[]{:S(2)}, u32[]{:S(2)}) collective-permute-start(bf16[4,4,64,128]{3,2,1,0:T(8,128)(2,1)} %get-tuple-element.79), channel_id=1, source_target_pairs={{0,24},{4,28},{8,16},{12,20},{16,8},{20,12},{24,0},{28,4},{1,25},{... | collective-permute-start | bytes 786440 | tf_op jit(solution)/shard_map/ppermute | solution.py:390

commit v12 on v10

--- a/solution.py
+++ b/solution.py
@@ -545,7 +545,7 @@
         name="global_queries",
     )(kv, rows, after(stats, (log_dot, qd_near, qd_far)), expand, dkv, key_t, sides)
     got_sums = from_near(sent_sums)
-    got_ends = from_near(after(sent_ends, (log_near, log_far)))
+    got_ends = from_near(sent_ends)
 
     first = stages[0]
     parts = pl.pallas_call(

time: 107 us -> 113 us (1.056); the launches traced: 105 us -> 112 us
  waiting for transfers between devices: 25.5 us -> 32.3 us
    ppermute x3, waiting for transfers between devices: 14.8 us -> 26.3 us  [from_far(): return lax.ppermute(value, 'ctx', pairs + [(j, i) for i, j in pairs])]
    ppermute x12, waiting for transfers between devices: 10.3 us -> 5.36 us  [swap(): return lax.ppermute(value, 'ctx', [(i, i ^ mask) for i in range(devices)])]
  transfers between devices with their start and end apart: 16 -> 16, of which waited for: 6 -> 7; matrix products, arithmetic and copies ran while one was open for 0% -> 0% of each run, Pallas kernels for 43% -> 40%
where the time goes in v12:
time: 113 us; the launch traced here: 112 us
  Pallas kernels  54.4 us (48%)
  waiting for transfers between devices  32.3 us (29%)
  starting transfers between devices  23 us (20%)
  other arithmetic  1.32 us (1%)
    ppermute x3, waiting for transfers between devices, from_far(): return lax.ppermute(value, 'ctx', pairs + [(j, i) for i, j in pairs])  26.3 us
    pallas_call x1, Pallas kernels, shards(): pl.pallas_call(functools.partial(local_kernel, scale, scale2), grid=(head...  11.3 us
    ppermute x3, starting transfers between devices, from_far(): return lax.ppermute(value, 'ctx', pairs + [(j, i) for i, j in pairs])  10.5 us
    pallas_call x1, Pallas kernels, shards(): pl.pallas_call(functools.partial(window_kernel, scale2), grid=(heads,), i...  9.11 us
    ppermute x12, starting transfers between devices, swap(): return lax.ppermute(value, 'ctx', [(i, i ^ mask) for i in range(devices)])  8.23 us
    pallas_call x1, Pallas kernels, shards(): pl.pallas_call(functools.partial(rim_kernel, scale, scale2), grid=(heads,...  6.99 us
    pallas_call x1, Pallas kernels, shards(): pl.pallas_call(functools.partial(global_kernel, scale, scale2), grid=(hea...  6.77 us
    pallas_call x1, Pallas kernels, shards(): pl.pallas_call(functools.partial(stats_kernel, scale2), grid=(heads,), in...  5.5 us
  transfers between devices with their start and end apart: 16, of which 7 were waited for; matrix products, arithmetic and copies ran while one was open for 0% of the time, Pallas kernels for 40%

profile of v12, /device:TPU:1, one launch (start us, length us, event | category | flops | bytes accessed | tf_op | source)
XLA Modules:
  0.0 112.4 jit_solution(10448314880156184268)
XLA Ops:
  0.6 2.4 %pack_keys.1.kv.refs_5_ = bf16[2,4,512,128]{3,2,1,0:T(8,128)(2,1)} custom-call(bf16[2048,128]{1,0:T(8,128)(2,1)} %bitcast.15, bf16[2048,128]{1,0:T(8,128)(2,1)} %bitcast.16), custom_call_target="tpu_custom_call" | custom-call | tf_op jit(solution)/shard_map/pack_keys/pallas_call | solution.py:408
  3.1 4.5 %collective-permute-start.1 = (bf16[2,4,512,128]{3,2,1,0:T(8,128)(2,1)}, bf16[2,4,512,128]{3,2,1,0:T(8,128)(2,1)}, u32[]{:S(2)}, u32[]{:S(2)}) collective-permute-start(bf16[2,4,512,128]{3,2,1,0:T(8,128)(2,1)} %pack_keys.1.kv.refs_5_), channel_id=1, source_target_pairs={{4,8},{12,16},{20,24},{8,4},{16,12},{24,20},{5,9},{13,17},{21,25},... | collective-permute-start | bytes 3145736 | tf_op jit(solution)/shard_map/ppermute | solution.py:397
  7.6 0.1 collective-permute-start
  7.7 3.4 %pack_queries.1 = (bf16[2,4,512,128]{3,2,1,0:T(8,128)(2,1)}, bf16[4,4,64,128]{3,2,1,0:T(8,128)(2,1)}) custom-call(bf16[2048,128]{1,0:T(8,128)(2,1)} %bitcast.17, bf16[2048,128]{1,0:T(8,128)(2,1)} %bitcast.18, bf16[2,4,512,128]{3,2,1,0:T(8,128)(2,1)} %pack_keys.1.kv.refs_5_, s32[1,256]{1,0:T(1,128)} %bitcast.19), custom_call_target="tpu_custom_call" | custom-call | tf_op jit(solution)/shard_map/pack_queries/pallas_call | solution.py:416
  11.1 1.1 collective-permute-start.4
  12.1 1.3 %collective-permute-start.3 = (bf16[1,4,4,64,128]{4,3,2,1,0:T(8,128)(2,1)}, bf16[1,4,4,64,128]{4,3,2,1,0:T(8,128)(2,1)}, u32[]{:S(2)}, u32[]{:S(2)}) collective-permute-start(bf16[1,4,4,64,128]{4,3,2,1,0:T(8,128)(2,1)} %bitcast.11), channel_id=1, source_target_pairs={{0,16},{4,20},{8,24},{12,28},{16,0},{20,4},{24,8},{28,12},{1,17},{... | collective-permute-start | bytes 786440 | tf_op jit(solution)/shard_map/ppermute | solution.py:390
  13.5 0.3 collective-permute-start.2
  13.7 2.2 %masks.1 = (f32[1536,128]{1,0:T(8,128)}, bf16[256,512]{1,0:T(8,128)(2,1)}, bf16[512,256]{1,0:T(8,128)(2,1)}, bf16[512,64]{1,0:T(8,128)(2,1)}) custom-call(s32[1,256]{1,0:T(1,128)} %bitcast.20), custom_call_target="tpu_custom_call" | custom-call | tf_op jit(solution)/shard_map/masks/pallas_call | solution.py:428
  15.9 14.8 %collective-permute-done.1.kv_far = bf16[2,4,512,128]{3,2,1,0:T(8,128)(2,1)} collective-permute-done((bf16[2,4,512,128]{3,2,1,0:T(8,128)(2,1)}, bf16[2,4,512,128]{3,2,1,0:T(8,128)(2,1)}, u32[]{:S(2)}, u32[]{:S(2)}) %collective-permute-start.1) | collective-permute-done | bytes 1048608 | tf_op jit(solution)/shard_map/ppermute | solution.py:397
  30.7 0.0 collective-permute-done.kv_near
  30.7 9.1 %window.1 = (bf16[4,1536,512]{2,1,0:T(8,128)(2,1)}, f32[4,128,512]{2,1,0:T(8,128)}, f32[4,2,512]{2,1,0:T(2,128)}, bf16[4,128,1536]{2,1,0:T(8,128)(2,1)}, bf16[4,...) custom-call(bf16[2,4,512,128]{3,2,1,0:T(8,128)(2,1)} %get-tuple-element.60.qd, ...), custom_call_target="tpu_custom_call" | custom-call | flops 1000000 | bytes 1000000 | tf_op jit(solution)/shard_map/window/pallas_call | solution.py:445
  39.8 0.0 collective-permute-done.4.refs_3_
  39.8 0.0 collective-permute-done.3.refs_2_
  39.8 3.0 %collective-permute-done.2.refs_1_ = bf16[1,4,4,64,128]{4,3,2,1,0:T(8,128)(2,1)} collective-permute-done((bf16[1,4,4,64,128]{4,3,2,1,0:T(8,128)(2,1)}, bf16[1,4,4,64,128]{4,3,2,1,0:T(8,128)(2,1)}, u32[]{:S(2)}, u32[]{:S(2)}) %collective-permute-start.2) | collective-permute-done | bytes 262176 | tf_op jit(solution)/shard_map/ppermute | solution.py:390
  42.8 1.3 %pad_maximum_fusion = bf16[4,4,4,64,128]{4,3,2,1,0:T(8,128)(2,1)S(1)} fusion(bf16[1,4,4,64,128]{4,3,2,1,0:T(8,128)(2,1)} %collective-permute-done.4.refs_3_, bf16[1,4,4,64,128]{4,3,2,1,0:T(8,128)(2,1)} %collective-permute-done.3.refs_2_, bf16[1,4,4,64,128]{4,3,2,1,0:T(8,128)(2,1)} %collective-permute-done.2.refs_1_, bf16[1,4,4,64,128]{4,3,2,1,0:T(8,128)(2,1)} %bitcast.13), kind=kLoop, calls=%fused_computation | loop fusion | flops 1572864 | bytes 2097152 | tf_op jit(solution)/shard_map/concatenate | solution.py:477
  44.2 0.1 collective-permute-start.5
  44.2 2.2 %collective-permute-start.7 = (bf16[2,4,512,128]{3,2,1,0:T(8,128)(2,1)}, bf16[2,4,512,128]{3,2,1,0:T(8,128)(2,1)}, u32[]{:S(2)}, u32[]{:S(2)}) collective-permute-start(bf16[2,4,512,128]{3,2,1,0:T(8,128)(2,1)} %get-tuple-element.60.qd), channel_id=1, source_target_pairs={{4,8},{12,16},{20,24},{8,4},{16,12},{24,20},{5,9},{13,17},{21,25},... | collective-permute-start | bytes 3145736 | tf_op jit(solution)/shard_map/ppermute | solution.py:397
  46.5 0.1 collective-permute-start.6
  46.5 0.5 collective-permute-done.5.refs_4_
  47.0 5.5 %global_stats.1 = (bf16[4,4,256,128]{3,2,1,0:T(8,128)(2,1)}, f32[8,4,8,256]{3,2,1,0:T(8,128)}) custom-call(bf16[256,512]{1,0:T(8,128)(2,1)} %get-tuple-element.47.compact, bf16[1,4,4,64,128]{4,3,2,1,0:T(8,128)(2,1)} %bitcast.14, bf16[1,4,4,64,128]{4,3,2,1,0:T(8,128)(2,1)} %collective-permute-done.2.refs_1_, ...), custom_call_target="tpu_custom_call" | custom-call | flops 1000000 | bytes 1000000 | tf_op jit(solution)/shard_map/global_stats/pallas_call | solution.py:481
  52.5 4.3 %all-to-all-start = ((f32[8,4,8,256]{3,2,1,0:T(8,128)}), f32[8,4,8,256]{3,2,1,0:T(8,128)}, u32[]{:S(2)}, u32[]{:S(2)}) async-start(f32[8,4,8,256]{3,2,1,0:T(8,128)} %get-tuple-element.62), calls=%async_computation | async-start | bytes 524288 | tf_op jit(solution)/shard_map/all_to_all | solution.py:494
  56.8 11.3 %local.1 = (bf16[4,512,128]{2,1,0:T(8,128)(2,1)}, f32[4,2,512]{2,1,0:T(2,128)}, f32[4,512,128]{2,1,0:T(8,128)}, f32[2,4,512,128]{3,2,1,0:T(8,128)}, bf16[4,2,4,6...) custom-call(bf16[3,4,128,512]{3,2,1,0:T(8,128)(2,1)} %get-tuple-element.44.sides.value_t, ...), custom_call_target="tpu_custom_call" | custom-call | flops 1000000 | bytes 1000000 | tf_op jit(solution)/shard_map/local/pallas_call | solution.py:501
  68.0 0.1 collective-permute-start.11
  68.1 3.8 %collective-permute-done.7.qd_far = bf16[2,4,512,128]{3,2,1,0:T(8,128)(2,1)} collective-permute-done((bf16[2,4,512,128]{3,2,1,0:T(8,128)(2,1)}, bf16[2,4,512,128]{3,2,1,0:T(8,128)(2,1)}, u32[]{:S(2)}, u32[]{:S(2)}) %collective-permute-start.7) | collective-permute-done | bytes 1048608 | tf_op jit(solution)/shard_map/ppermute | solution.py:397
  71.9 0.0 collective-permute-done.6.qd_near
  71.9 0.7 all-to-all-done.stats
  72.6 6.8 %global_queries.1 = (f32[2,4,512,128]{3,2,1,0:T(8,128)}, bf16[4,2,4,64,128]{4,3,2,1,0:T(8,128)(2,1)}, bf16[4,2,4,64,128]{4,3,2,1,0:T(8,128)(2,1)}) custom-call(bf16[2,4,512,128]{3,2,1,0:T(8,128)(2,1)} %pack_keys.1.kv.refs_5_, bf16[4,4,256,128]{3,2,1,0:T(8,128)(2,1)} %get-tuple-element.54.rows, ...), custom_call_target="tpu_custom_call", output_to_operand_aliasing={{0}: (4, {})} | custom-call | flops 1000000 | bytes 1000000 | tf_op jit(solution)/shard_map/global_queries/pallas_call | solution.py:533
  79.4 0.0 copy-start.2
  79.4 2.2 %collective-permute-start.10 = (bf16[4,2,4,64,128]{4,3,2,1,0:T(8,128)(2,1)}, bf16[4,2,4,64,128]{4,3,2,1,0:T(8,128)(2,1)}, u32[]{:S(2)}, u32[]{:S(2)}) collective-permute-start(bf16[4,2,4,64,128]{4,3,2,1,0:T(8,128)(2,1)} %get-tuple-element.67), channel_id=1, source_target_pairs={{0,4},{4,0},{8,12},{12,8},{16,20},{20,16},{24,28},{28,24},{1,5},{5... | collective-permute-start | bytes 1572872 | tf_op jit(solution)/shard_map/ppermute | solution.py:390
  81.5 0.0 collective-permute-done.11.got_sums
  81.5 1.9 %collective-permute-done.10.got_ends = bf16[4,2,4,64,128]{4,3,2,1,0:T(8,128)(2,1)} collective-permute-done((bf16[4,2,4,64,128]{4,3,2,1,0:T(8,128)(2,1)}, bf16[4,2,4,64,128]{4,3,2,1,0:T(8,128)(2,1)}, u32[]{:S(2)}, u32[]{:S(2)}) %collective-permute-start.10) | collective-permute-done | bytes 524320 | tf_op jit(solution)/shard_map/ppermute | solution.py:390
  83.4 2.5 %fold.1 = (bf16[4,4,64,128]{3,2,1,0:T(8,128)(2,1)}, bf16[4,4,64,128]{3,2,1,0:T(8,128)(2,1)}, bf16[4,4,64,128]{3,2,1,0:T(8,128)(2,1)}, bf16[4,4,64,128]{3,2,1,0:T(8,128)(2,1)}) custom-call(bf16[4,2,4,64,128]{4,3,2,1,0:T(8,128)(2,1)} %get-tuple-element.66.kept_ends, bf16[4,2,4,64,128]{4,3,2,1,0:T(8,128)(2,1)} %collective-permute-done.10.got_ends, ...), custom_call_target="tpu_custom_call" | custom-call | tf_op jit(solution)/shard_map/fold/pallas_call | solution.py:551
  86.0 1.2 %collective-permute-start.12 = (bf16[4,4,64,128]{3,2,1,0:T(8,128)(2,1)}, bf16[4,4,64,128]{3,2,1,0:T(8,128)(2,1)}, u32[]{:S(2)}, u32[]{:S(2)}) collective-permute-start(bf16[4,4,64,128]{3,2,1,0:T(8,128)(2,1)} %get-tuple-element.71), channel_id=1, source_target_pairs={{0,8},{4,12},{8,0},{12,4},{16,24},{20,28},{24,16},{28,20},{1,9},{5... | collective-permute-start | bytes 786440 | tf_op jit(solution)/shard_map/ppermute | solution.py:390
  87.1 0.7 collective-permute-start.13
  87.8 1.2 %collective-permute-start.14 = (bf16[4,4,64,128]{3,2,1,0:T(8,128)(2,1)}, bf16[4,4,64,128]{3,2,1,0:T(8,128)(2,1)}, u32[]{:S(2)}, u32[]{:S(2)}) collective-permute-start(bf16[4,4,64,128]{3,2,1,0:T(8,128)(2,1)} %get-tuple-element.73), channel_id=1, source_target_pairs={{0,24},{4,28},{8,16},{12,20},{16,8},{20,12},{24,0},{28,4},{1,25},{... | collective-permute-start | bytes 786440 | tf_op jit(solution)/shard_map/ppermute | solution.py:390
  89.0 0.0 copy-done.2
  89.0 3.8 %collective-permute-start.9 = (f32[4,2,512]{2,1,0:T(2,128)S(1)}, f32[4,2,512]{2,1,0:T(2,128)S(1)}, u32[]{:S(2)}, u32[]{:S(2)}) collective-permute-start(f32[4,2,512]{2,1,0:T(2,128)S(1)} %copy-done.2), channel_id=1, source_target_pairs={{4,8},{12,16},{20,24},{8,4},{16,12},{24,20},{5,9},{13,17},{21,25},... | collective-permute-start | bytes 49160 | tf_op jit(solution)/shard_map/ppermute | solution.py:397
  92.8 0.1 collective-permute-start.8
  92.9 7.7 %collective-permute-done.9.log_far = f32[4,2,512]{2,1,0:T(2,128)S(1)} collective-permute-done((f32[4,2,512]{2,1,0:T(2,128)S(1)}, f32[4,2,512]{2,1,0:T(2,128)S(1)}, u32[]{:S(2)}, u32[]{:S(2)}) %collective-permute-start.9) | collective-permute-done | bytes 16416 | tf_op jit(solution)/shard_map/ppermute | solution.py:397
  100.6 0.0 copy-start
  100.6 0.0 collective-permute-done.8.log_near
  100.6 0.6 copy-done
  101.2 0.0 copy-done.1
  101.2 7.0 %rim.1.dkv = f32[2,4,512,128]{3,2,1,0:T(8,128)} custom-call(bf16[2,4,512,128]{3,2,1,0:T(8,128)(2,1)} %pack_keys.1.kv.refs_5_, f32[1536,128]{1,0:T(8,128)} %get-tuple-element.43.bias, bf16[2,4,512,128]{3,2,1,0:T(8,128)(2,1)} %collective-permute-done.6.qd_near, bf16[2,4,512,128]{3,2,1,0:T(8,128)(2,1)} %collective-permute-done.7.qd_far, ...), custom_call_target="tpu_custom_call" | custom-call | flops 1000000 | bytes 1000000 | tf_op jit(solution)/shard_map/rim/pallas_call | solution.py:566
  108.2 0.0 collective-permute-done.12.refs_1_
  108.2 0.0 collective-permute-done.13.refs_2_
  108.2 0.0 collective-permute-done.14.refs_3_
  108.2 4.2 %final.1 = (bf16[2048,128]{1,0:T(8,128)(2,1)}, f32[2048,128]{1,0:T(8,128)}, f32[2048,128]{1,0:T(8,128)}, f32[2048,128]{1,0:T(8,128)}) custom-call(bf16[512,64]{1,0:T(8,128)(2,1)} %get-tuple-element.41.place, bf16[4,512,128]{2,1,0:T(8,128)(2,1)} %get-tuple-element.58.out, f32[4,512,128]{2,1,0:T(8,128)} %get-tuple-element.59.dq, f32[2,4,512,128]{3,2,1,0:T(8,128)} %rim.1.dkv, ...), custom_call_target="tpu_custom_call" | custom-call | tf_op jit(solution)/shard_map/final/pallas_call | solution.py:589
  (1 shorter events, 0.0 us)
Async XLA Ops:
  3.1 27.6 %collective-permute-start.1 = (bf16[2,4,512,128]{3,2,1,0:T(8,128)(2,1)}, bf16[2,4,512,128]{3,2,1,0:T(8,128)(2,1)}, u32[]{:S(2)}, u32[]{:S(2)}) collective-permute-start(bf16[2,4,512,128]{3,2,1,0:T(8,128)(2,1)} %pack_keys.1.kv.refs_5_), channel_id=1, source_target_pairs={{4,8},{12,16},{20,24},{8,4},{16,12},{24,20},{5,9},{13,17},{21,25},... | collective-permute-start | bytes 3145736 | tf_op jit(solution)/shard_map/ppermute | solution.py:397
  7.6 23.1 %collective-permute-start = (bf16[2,4,512,128]{3,2,1,0:T(8,128)(2,1)}, bf16[2,4,512,128]{3,2,1,0:T(8,128)(2,1)}, u32[]{:S(2)}, u32[]{:S(2)}) collective-permute-start(bf16[2,4,512,128]{3,2,1,0:T(8,128)(2,1)} %pack_keys.1.kv.refs_5_), channel_id=1, source_target_pairs={{0,4},{4,0},{8,12},{12,8},{16,20},{20,16},{24,28},{28,24},{1,5},{5... | collective-permute-start | bytes 3145736 | tf_op jit(solution)/shard_map/ppermute | solution.py:390
  11.1 28.8 %collective-permute-start.4 = (bf16[1,4,4,64,128]{4,3,2,1,0:T(8,128)(2,1)}, bf16[1,4,4,64,128]{4,3,2,1,0:T(8,128)(2,1)}, u32[]{:S(2)}, u32[]{:S(2)}) collective-permute-start(bf16[1,4,4,64,128]{4,3,2,1,0:T(8,128)(2,1)} %bitcast.10), channel_id=1, source_target_pairs={{0,24},{4,28},{8,16},{12,20},{16,8},{20,12},{24,0},{28,4},{1,25},{... | collective-permute-start | bytes 786440 | tf_op jit(solution)/shard_map/ppermute | solution.py:390
  12.1 27.7 %collective-permute-start.3 = (bf16[1,4,4,64,128]{4,3,2,1,0:T(8,128)(2,1)}, bf16[1,4,4,64,128]{4,3,2,1,0:T(8,128)(2,1)}, u32[]{:S(2)}, u32[]{:S(2)}) collective-permute-start(bf16[1,4,4,64,128]{4,3,2,1,0:T(8,128)(2,1)} %bitcast.11), channel_id=1, source_target_pairs={{0,16},{4,20},{8,24},{12,28},{16,0},{20,4},{24,8},{28,12},{1,17},{... | collective-permute-start | bytes 786440 | tf_op jit(solution)/shard_map/ppermute | solution.py:390
  13.5 29.4 %collective-permute-start.2 = (bf16[1,4,4,64,128]{4,3,2,1,0:T(8,128)(2,1)}, bf16[1,4,4,64,128]{4,3,2,1,0:T(8,128)(2,1)}, u32[]{:S(2)}, u32[]{:S(2)}) collective-permute-start(bf16[1,4,4,64,128]{4,3,2,1,0:T(8,128)(2,1)} %bitcast.12), channel_id=1, source_target_pairs={{0,8},{4,12},{8,0},{12,4},{16,24},{20,28},{24,16},{28,20},{1,9},{5... | collective-permute-start | bytes 786440 | tf_op jit(solution)/shard_map/ppermute | solution.py:390
  44.2 2.9 %collective-permute-start.5 = (bf16[4,4,4,64,128]{4,3,2,1,0:T(8,128)(2,1)S(1)}, bf16[4,4,4,64,128]{4,3,2,1,0:T(8,128)(2,1)}, u32[]{:S(2)}, u32[]{:S(2)}) collective-permute-start(bf16[4,4,4,64,128]{4,3,2,1,0:T(8,128)(2,1)S(1)} %pad_maximum_fusion), channel_id=1, source_target_pairs={{0,4},{4,0},{8,12},{12,8},{16,20},{20,16},{24,28},{28,24},{1,5},{5... | collective-permute-start | bytes 3145736 | tf_op jit(solution)/shard_map/ppermute | solution.py:390
  44.2 27.7 %collective-permute-start.7 = (bf16[2,4,512,128]{3,2,1,0:T(8,128)(2,1)}, bf16[2,4,512,128]{3,2,1,0:T(8,128)(2,1)}, u32[]{:S(2)}, u32[]{:S(2)}) collective-permute-start(bf16[2,4,512,128]{3,2,1,0:T(8,128)(2,1)} %get-tuple-element.60.qd), channel_id=1, source_target_pairs={{4,8},{12,16},{20,24},{8,4},{16,12},{24,20},{5,9},{13,17},{21,25},... | collective-permute-start | bytes 3145736 | tf_op jit(solution)/shard_map/ppermute | solution.py:397
  46.5 25.4 %collective-permute-start.6 = (bf16[2,4,512,128]{3,2,1,0:T(8,128)(2,1)}, bf16[2,4,512,128]{3,2,1,0:T(8,128)(2,1)}, u32[]{:S(2)}, u32[]{:S(2)}) collective-permute-start(bf16[2,4,512,128]{3,2,1,0:T(8,128)(2,1)} %get-tuple-element.60.qd), channel_id=1, source_target_pairs={{0,4},{4,0},{8,12},{12,8},{16,20},{20,16},{24,28},{28,24},{1,5},{5... | collective-permute-start | bytes 3145736 | tf_op jit(solution)/shard_map/ppermute | solution.py:390
  52.5 20.1 %all-to-all-start = ((f32[8,4,8,256]{3,2,1,0:T(8,128)}), f32[8,4,8,256]{3,2,1,0:T(8,128)}, u32[]{:S(2)}, u32[]{:S(2)}) async-start(f32[8,4,8,256]{3,2,1,0:T(8,128)} %get-tuple-element.62), calls=%async_computation | async-start | bytes 524288 | tf_op jit(solution)/shard_map/all_to_all | solution.py:494
  68.0 13.5 %collective-permute-start.11 = (bf16[4,2,4,64,128]{4,3,2,1,0:T(8,128)(2,1)}, bf16[4,2,4,64,128]{4,3,2,1,0:T(8,128)(2,1)}, u32[]{:S(2)}, u32[]{:S(2)}) collective-permute-start(bf16[4,2,4,64,128]{4,3,2,1,0:T(8,128)(2,1)} %get-tuple-element.69), channel_id=1, source_target_pairs={{0,4},{4,0},{8,12},{12,8},{16,20},{20,16},{24,28},{28,24},{1,5},{5... | collective-permute-start | bytes 1572872 | tf_op jit(solution)/shard_map/ppermute | solution.py:390
  79.4 9.6 %copy-start.2 = (f32[4,2,512]{2,1,0:T(2,128)S(1)}, f32[4,2,512]{2,1,0:T(2,128)}, u32[]{:S(2)}) copy-start(f32[4,2,512]{2,1,0:T(2,128)} %get-tuple-element.61) | copy-start | bytes 49156
  79.4 4.0 %collective-permute-start.10 = (bf16[4,2,4,64,128]{4,3,2,1,0:T(8,128)(2,1)}, bf16[4,2,4,64,128]{4,3,2,1,0:T(8,128)(2,1)}, u32[]{:S(2)}, u32[]{:S(2)}) collective-permute-start(bf16[4,2,4,64,128]{4,3,2,1,0:T(8,128)(2,1)} %get-tuple-element.67), channel_id=1, source_target_pairs={{0,4},{4,0},{8,12},{12,8},{16,20},{20,16},{24,28},{28,24},{1,5},{5... | collective-permute-start | bytes 1572872 | tf_op jit(solution)/shard_map/ppermute | solution.py:390
  86.0 22.3 %collective-permute-start.12 = (bf16[4,4,64,128]{3,2,1,0:T(8,128)(2,1)}, bf16[4,4,64,128]{3,2,1,0:T(8,128)(2,1)}, u32[]{:S(2)}, u32[]{:S(2)}) collective-permute-start(bf16[4,4,64,128]{3,2,1,0:T(8,128)(2,1)} %get-tuple-element.71), channel_id=1, source_target_pairs={{0,8},{4,12},{8,0},{12,4},{16,24},{20,28},{24,16},{28,20},{1,9},{5... | collective-permute-start | bytes 786440 | tf_op jit(solution)/shard_map/ppermute | solution.py:390
  87.1 21.1 %collective-permute-start.13 = (bf16[4,4,64,128]{3,2,1,0:T(8,128)(2,1)}, bf16[4,4,64,128]{3,2,1,0:T(8,128)(2,1)}, u32[]{:S(2)}, u32[]{:S(2)}) collective-permute-start(bf16[4,4,64,128]{3,2,1,0:T(8,128)(2,1)} %get-tuple-element.72), channel_id=1, source_target_pairs={{0,16},{4,20},{8,24},{12,28},{16,0},{20,4},{24,8},{28,12},{1,17},{... | collective-permute-start | bytes 786440 | tf_op jit(solution)/shard_map/ppermute | solution.py:390
  87.8 20.4 %collective-permute-start.14 = (bf16[4,4,64,128]{3,2,1,0:T(8,128)(2,1)}, bf16[4,4,64,128]{3,2,1,0:T(8,128)(2,1)}, u32[]{:S(2)}, u32[]{:S(2)}) collective-permute-start(bf16[4,4,64,128]{3,2,1,0:T(8,128)(2,1)} %get-tuple-element.73), channel_id=1, source_target_pairs={{0,24},{4,28},{8,16},{12,20},{16,8},{20,12},{24,0},{28,4},{1,25},{... | collective-permute-start | bytes 786440 | tf_op jit(solution)/shard_map/ppermute | solution.py:390
  89.0 11.6 %collective-permute-start.9 = (f32[4,2,512]{2,1,0:T(2,128)S(1)}, f32[4,2,512]{2,1,0:T(2,128)S(1)}, u32[]{:S(2)}, u32[]{:S(2)}) collective-permute-start(f32[4,2,512]{2,1,0:T(2,128)S(1)} %copy-done.2), channel_id=1, source_target_pairs={{4,8},{12,16},{20,24},{8,4},{16,12},{24,20},{5,9},{13,17},{21,25},... | collective-permute-start | bytes 49160 | tf_op jit(solution)/shard_map/ppermute | solution.py:397
  92.8 7.8 %collective-permute-start.8 = (f32[4,2,512]{2,1,0:T(2,128)S(1)}, f32[4,2,512]{2,1,0:T(2,128)S(1)}, u32[]{:S(2)}, u32[]{:S(2)}) collective-permute-start(f32[4,2,512]{2,1,0:T(2,128)S(1)} %copy-done.2), channel_id=1, source_target_pairs={{0,4},{4,0},{8,12},{12,8},{16,20},{20,16},{24,28},{28,24},{1,5},{5... | collective-permute-start | bytes 49160 | tf_op jit(solution)/shard_map/ppermute | solution.py:390
  100.6 0.6 copy-start
  100.6 0.6 copy-start.1
